TPU v7x, 32 devices: a whole 2x2x4 slice. The times are simulated.
32 devices in a mesh: dp: 4 (over y, x), ctx: 8 (over z, core).
Axes of the slice: x: 2, y: 2, z: 4, core: 2. Of those that a mesh axis runs over, the one named last changes fastest.
Arguments:
- hidden_in: float32 [4, 1024, 640], P('dp', 'ctx'), may hold values from -6 to 6
- positions: int32 [4, 1024], P('dp', 'ctx'), may hold values from 0 to 511, as said below
- w_query: bfloat16 [1024, 640], P(('dp', 'ctx')), may hold values from -0.25 to 0.25
- w_key: bfloat16 [256, 640], P(('dp', 'ctx')), may hold values from -0.25 to 0.25
- w_value: bfloat16 [256, 640], P(('dp', 'ctx')), may hold values from -0.25 to 0.25
- w_output: bfloat16 [1024, 640], P(('dp', 'ctx')), may hold values from -0.1875 to 0.1875
- w_gate: bfloat16 [2048, 640], P(('dp', 'ctx')), may hold values from -0.25 to 0.25
- w_up: bfloat16 [2048, 640], P(('dp', 'ctx')), may hold values from -0.25 to 0.25
- w_down: bfloat16 [2048, 640], P(('dp', 'ctx')), may hold values from -0.125 to 0.125
- norm_scales: bfloat16 [3072], P(('dp', 'ctx')), may hold values from -0.5 to 0.5
- grad_out: float32 [4, 1024, 640], P('dp', 'ctx'), may hold values from -6 to 6
Outputs:
- block_out: float32 [4, 1024, 640], P('dp', 'ctx')
- grad_in: float32 [4, 1024, 640], P('dp', 'ctx')
- grad_w_query: float32 [1024, 640], P(('dp', 'ctx'))
- grad_w_key: float32 [256, 640], P(('dp', 'ctx'))
- grad_w_value: float32 [256, 640], P(('dp', 'ctx'))
- grad_w_output: float32 [1024, 640], P(('dp', 'ctx'))
- grad_w_gate: float32 [2048, 640], P(('dp', 'ctx'))
- grad_w_up: float32 [2048, 640], P(('dp', 'ctx'))
- grad_w_down: float32 [2048, 640], P(('dp', 'ctx'))
- grad_scales: float32 [3072], P(('dp', 'ctx'))
Inputs may be any that keep to these rules, and one draw needn't show every extreme that they name: `positions`: each sequence is a pack of documents in natural order; the first document is the first half of the sequence (512 tokens), the rest are shorter; a token's entry is its distance from the first token of its document, rising by one from token to token within a document, listed in stored order.
All inputs are finite; a program needn't handle non-finite values.
Results may differ from a plain program's by a relative error of at most 0.015.
Values may be sent and summed in bfloat16 or wider, within the bound.
No kernel may reach another device: no remote copies, remote signals or barrier semaphores. Data moves between devices by JAX's collectives and lax.ppermute only.
A program may use at most 192 MiB of HBM per device.

v0:
```python
import jax
import jax.numpy as jnp
from jax import lax
from jax.experimental import pallas as pl
from jax.experimental.pallas import tpu as pltpu
from jax.sharding import PartitionSpec as P

EPS = 1e-06


def rms_scale(vector, scale):
    return (
        vector * lax.rsqrt(jnp.mean(vector * vector, axis=-1, keepdims=True) + EPS) * (1.0 + scale)
    )


def rotate(vector, position):
    half = vector.shape[-1] // 2
    freq_table = 1000000.0 ** (-jnp.arange(half, dtype=jnp.float32) / half)
    angle = position.astype(jnp.float32)[:, None] * freq_table[None, :]
    cosine = jnp.cos(angle)[:, None, :]
    sine = jnp.sin(angle)[:, None, :]
    first = vector[..., :half]
    second = vector[..., half:]
    return jnp.concatenate(
        [first * cosine - second * sine, second * cosine + first * sine], axis=-1
    )


def mid_piece(resid, projected, scale_attn, scale_pre):
    middle = resid + rms_scale(projected, scale_attn)
    return (middle, rms_scale(middle, scale_pre))


def glu_piece(gate, upward):
    return jax.nn.gelu(gate, approximate=True) * upward


def out_piece(middle, ffn, scale_post):
    return middle + rms_scale(ffn, scale_post)


def times_wt(left, weight):
    return lax.dot_general(
        left, weight, (((1,), (1,)), ((), ())), preferred_element_type=jnp.float32
    )


def outer_sum(left, right):
    return lax.dot_general(
        left, right, (((0,), (0,)), ((), ())), preferred_element_type=jnp.float32
    )


def split_scales(norm_scales, width, head_width):
    scales = norm_scales.astype(jnp.float32)
    pieces = [scales[index * width : (index + 1) * width] for index in range(4)]
    offset = 4 * width
    return pieces + [
        scales[offset : offset + head_width],
        scales[offset + head_width : offset + 2 * head_width],
    ]


BF = jnp.bfloat16


def swap_dp(block, bits):
    count = lax.axis_size("dp")
    return lax.ppermute(block, "dp", [(place, place ^ bits) for place in range(count)])


def swap_ctx(block, bits):
    count = lax.axis_size("ctx")
    return lax.ppermute(block, "ctx", [(place, place ^ bits) for place in range(count)])


def swap_z(block, bits):
    return swap_ctx(block, 2 * bits)


def gather_over(block, swap, count):
    if count <= 4:
        return jnp.concatenate([block] + [swap(block, bits) for bits in range(1, count)], axis=0)
    bits = 1
    while bits < count:
        block = jnp.concatenate([block, swap(block, bits)], axis=0)
        bits = 2 * bits
    return block


def add_bf16(first, *others):
    total = first.astype(jnp.float32)
    for other in others:
        total = total + other.astype(jnp.float32)
    return total


def scatter_over(blocks, swap, count):
    if count <= 4:
        return add_bf16(blocks[0], *[swap(blocks[bits], bits) for bits in range(1, count)])
    bits = count // 2
    while bits > 1:
        blocks = add_bf16(blocks[:bits], swap(blocks[bits:], bits)).astype(BF)
        bits = bits // 2
    return add_bf16(blocks[0], swap(blocks[1], 1))


def gather_chip(block):
    groups = lax.axis_size("ctx") // 2
    over_z = gather_over(block[None], swap_z, groups)
    over_dp = gather_over(over_z[None], swap_dp, lax.axis_size("dp"))
    return over_dp.reshape((-1,) + block.shape[1:])


def double(blocks, swap, bits):
    return jnp.concatenate([blocks, swap(blocks, bits)], axis=0)


def double_inner(blocks, swap, bits):
    pair = blocks.reshape((2, 1, -1) + blocks.shape[1:])
    return jnp.concatenate([pair, swap(pair, bits)], axis=1).reshape((-1,) + blocks.shape[1:])


def halve(blocks, swap, bits):
    half = blocks.shape[0] // 2
    return add_bf16(blocks[:half], swap(blocks[half:], bits)).astype(BF)


def halve_inner(blocks, swap, bits):
    quarters = blocks.reshape((2, 2, -1) + blocks.shape[1:])
    half = add_bf16(quarters[:, 0], swap(quarters[:, 1], bits)).astype(BF)
    return half.reshape((-1,) + blocks.shape[1:])


def scatter_chip(blocks):
    groups = lax.axis_size("ctx") // 2
    count = lax.axis_size("dp")
    shaped = blocks.reshape((count, groups, -1) + blocks.shape[1:])
    mid = scatter_over(shaped, swap_dp, count).astype(BF)
    return scatter_over(mid, swap_z, groups)


def scatter_all(first, second):
    return scatter_chip(add_bf16(first, swap_ctx(second, 1)).astype(BF))


def natural_rows(places, block, groups):
    within = jnp.arange(2 * block, dtype=jnp.int32)[None, :]
    early = places[:, None] * block + within
    late = (2 * groups - 1 - places[:, None]) * block + within - block
    return jnp.where(within < block, early, late).reshape(-1)


def row_order(owner_of, rows):
    count = owner_of.shape[0] * rows
    held = (owner_of[:, None] * rows + jnp.arange(rows, dtype=jnp.int32)[None, :]).reshape(1, count)
    return (jnp.arange(count, dtype=jnp.int32)[:, None] == held).astype(BF)


def reorder(order, blocks):
    return jnp.dot(order, blocks, preferred_element_type=jnp.float32).astype(BF)


def reorder_back(order, blocks):
    return outer_sum(order, blocks.astype(BF)).astype(BF)


def rms_back(unit, inverse, grad_scaled):
    return inverse * (grad_scaled - unit * jnp.mean(grad_scaled * unit, axis=-1, keepdims=True))


def dot_nt(left, right):
    return lax.dot_general(left, right, (((1,), (1,)), ((), ())), preferred_element_type=jnp.float32)


def dot_nn(left, right):
    return lax.dot_general(left, right, (((1,), (0,)), ((), ())), preferred_element_type=jnp.float32)


def dot_tn(left, right):
    return lax.dot_general(left, right, (((0,), (0,)), ((), ())), preferred_element_type=jnp.float32)


def unit_of(rows):
    inverse = lax.rsqrt(jnp.mean(rows * rows, axis=-1, keepdims=True) + EPS)
    return rows * inverse, inverse


def turn(rows, cosine, sine):
    half = rows.shape[1] // 2
    first, second = rows[:, :half], rows[:, half:]
    return jnp.concatenate([first * cosine - second * sine, second * cosine + first * sine], axis=1)


def turn_back(rows, cosine, sine):
    half = rows.shape[1] // 2
    first, second = rows[:, :half], rows[:, half:]
    return jnp.concatenate([first * cosine + second * sine, second * cosine - first * sine], axis=1)


def call_kernel(body, out_shapes, scratch, flops, inputs):
    whole = pl.BlockSpec(memory_space=pltpu.VMEM)
    return pl.pallas_call(
        body,
        out_shape=[jax.ShapeDtypeStruct(shape, dtype) for shape, dtype in out_shapes],
        in_specs=[whole] * len(inputs),
        out_specs=[whole] * len(out_shapes),
        scratch_shapes=[pltpu.VMEM(shape, dtype) for shape, dtype in scratch],
        compiler_params=pltpu.CompilerParams(vmem_limit_bytes=52 * 1024 * 1024),
        cost_estimate=pl.CostEstimate(flops=flops, bytes_accessed=20_000_000, transcendentals=0),
    )(*inputs)


def attend_kernel(
    unit_ref, near_ref, far_ref, wq_ref, wk_ref, wv_ref, sin_scale_ref, sq_ref, sk_ref,
    cos_ref, sine_ref, cos_all_ref, sine_all_ref, key_index_ref, row_index_ref,
    normed_ref, normed_all_ref, qraw_ref, kraw_ref, q_ref, k_ref, v_ref, attn_ref, lse_ref,
):
    scale_in = 1.0 + sin_scale_ref[...]
    normed_ref[...] = (unit_ref[...] * scale_in).astype(BF)
    half = near_ref.shape[0]
    normed_all_ref[:half] = (near_ref[...].astype(jnp.float32) * scale_in).astype(BF)
    normed_all_ref[half:] = (far_ref[...].astype(jnp.float32) * scale_in).astype(BF)
    head_width = wk_ref.shape[0]
    heads = wq_ref.shape[0] // head_width
    key_raw = dot_nt(normed_all_ref[...], wk_ref[...])
    kraw_ref[...] = key_raw
    v_ref[...] = dot_nt(normed_all_ref[...], wv_ref[...]).astype(BF)
    key_unit, _ = unit_of(key_raw)
    k_ref[...] = turn(key_unit * (1.0 + sk_ref[...]), cos_all_ref[...], sine_all_ref[...]).astype(BF)
    allowed = key_index_ref[...] <= row_index_ref[...]
    for head in range(heads):
        span = slice(head * head_width, (head + 1) * head_width)
        raw = dot_nt(normed_ref[...], wq_ref[span, :])
        qraw_ref[:, span] = raw
        unit, _ = unit_of(raw)
        turned = turn(unit * (1.0 + sq_ref[...]), cos_ref[...], sine_ref[...])
        query = (turned * head_width ** (-0.5)).astype(BF)
        q_ref[:, span] = query
        scores = jnp.where(allowed, dot_nt(query, k_ref[...]), -1e30)
        top = jnp.max(scores, axis=1, keepdims=True)
        lse = top + jnp.log(jnp.sum(jnp.exp(scores - top), axis=1, keepdims=True))
        lse_ref[:, head : head + 1] = lse
        probs = jnp.exp(scores - lse).astype(BF)
        attn_ref[:, span] = dot_nn(probs, v_ref[...]).astype(BF)


def attend_back_kernel(
    grad_attn_ref, attn_ref, q_ref, k_ref, v_ref, lse_ref, qraw_ref, kraw_ref, wq_ref, wk_ref, wv_ref,
    sq_ref, sk_ref, cos_ref, sine_ref, cos_all_ref, sine_all_ref, key_index_ref, row_index_ref,
    normed_ref, normed_all_ref, unit_ref, near_ref, far_ref,
    gwq_ref, gwk_ref, gwv_ref, gnear_ref, gfar_ref, gq_ref, gsin_ref, gsq_ref, gsk_ref,
    probs_scr, gscores_scr, grows_scr, qrows_scr, gqraw_scr,
):
    head_width = wk_ref.shape[0]
    heads = wq_ref.shape[0] // head_width
    tokens = q_ref.shape[0]
    allowed = key_index_ref[...] <= row_index_ref[...]
    grad_sq = jnp.zeros((1, head_width), jnp.float32)
    for head in range(heads):
        span = slice(head * head_width, (head + 1) * head_width)
        rows = slice(head * tokens, (head + 1) * tokens)
        query = q_ref[:, span]
        grad_rows = grad_attn_ref[:, span]
        delta = jnp.sum(
            grad_rows.astype(jnp.float32) * attn_ref[:, span].astype(jnp.float32),
            axis=1,
            keepdims=True,
        )
        scores = jnp.where(allowed, dot_nt(query, k_ref[...]), -1e30)
        probs = jnp.exp(scores - lse_ref[:, head : head + 1])
        grad_scores = (probs * (dot_nt(grad_rows, v_ref[...]) - delta)).astype(BF)
        probs_scr[rows, :] = probs.astype(BF)
        gscores_scr[rows, :] = grad_scores
        grows_scr[rows, :] = grad_rows
        qrows_scr[rows, :] = query
        grad_query = dot_nn(grad_scores, k_ref[...]) * head_width ** (-0.5)
        grad_query = turn_back(grad_query, cos_ref[...], sine_ref[...])
        unit, inverse = unit_of(qraw_ref[:, span])
        grad_sq = grad_sq + jnp.sum(grad_query * unit, axis=0, keepdims=True)
        grad_raw = rms_back(unit, inverse, grad_query * (1.0 + sq_ref[...]))
        gqraw_scr[:, span] = grad_raw.astype(BF)
    gsq_ref[...] = grad_sq
    grad_key = dot_tn(gscores_scr[...], qrows_scr[...])
    grad_value = dot_tn(probs_scr[...], grows_scr[...]).astype(BF)
    grad_key = turn_back(grad_key, cos_all_ref[...], sine_all_ref[...])
    unit, inverse = unit_of(kraw_ref[...])
    gsk_ref[...] = jnp.sum(grad_key * unit, axis=0, keepdims=True)
    grad_kraw = rms_back(unit, inverse, grad_key * (1.0 + sk_ref[...])).astype(BF)
    half = near_ref.shape[0]
    grad_normed = dot_nn(grad_kraw, wk_ref[...]) + dot_nn(grad_value, wv_ref[...])
    grad_q = dot_nn(gqraw_scr[...], wq_ref[...])
    gq_ref[...] = grad_q
    gsin_ref[...] = (
        jnp.sum(grad_normed[:half] * near_ref[...].astype(jnp.float32), axis=0, keepdims=True)
        + jnp.sum(grad_normed[half:] * far_ref[...].astype(jnp.float32), axis=0, keepdims=True)
        + jnp.sum(grad_q * unit_ref[...], axis=0, keepdims=True)
    )
    gnear_ref[...] = grad_normed[:half].astype(BF)
    gfar_ref[...] = grad_normed[half:].astype(BF)
    gwk_ref[...] = dot_tn(grad_kraw, normed_all_ref[...]).astype(BF)
    gwv_ref[...] = dot_tn(grad_value, normed_all_ref[...]).astype(BF)
    gwq_ref[...] = dot_tn(gqraw_scr[...], normed_ref[...]).astype(BF)


GELU_A = (2.0 / 3.141592653589793) ** 0.5


def mid_kernel(*refs):
    attn_ref, order_ref, resid_ref, gout_ref, sattn_ref, spre_ref, spost_ref = refs[:7]
    a_refs = (refs[7:9], refs[9:11])
    b_refs = (refs[11:13], refs[13:15])
    block_out_ref, gresid_ref, gattn_ref, gsattn_ref, gspre_ref, gspost_ref = refs[15:21]
    ga_refs = (refs[21:23], refs[23:25])
    gb_refs = (refs[25:27], refs[27:29])
    held_scr, ahead_scr, gate_scr, up_scr, inner_scr = refs[29:]
    chips = a_refs[0][0].shape[0] // 2
    width = resid_ref.shape[1]
    rows_f = b_refs[0][0].shape[1] // 2
    rows_o = a_refs[0][0].shape[1] - rows_f
    chunk = chips * rows_f

    def place_a(dp):
        return dp // 2, slice((dp % 2) * chips, (dp % 2 + 1) * chips)

    def place_b(dp):
        return dp % 2, slice((dp // 2) * chips, (dp // 2 + 1) * chips)

    def weights(core, dp):
        piece_a, at_a = place_a(dp)
        piece_b, at_b = place_b(dp)
        gate = a_refs[core][piece_a][at_a, :rows_f, :].reshape(chunk, width)
        up = b_refs[core][piece_b][at_b, :rows_f, :].reshape(chunk, width)
        down = b_refs[core][piece_b][at_b, rows_f:, :].reshape(chunk, width)
        return gate, up, down

    parts = [(core, dp) for core in range(2) for dp in range(4)]
    out_chunk = chips * rows_o
    for number, (core, dp) in enumerate(parts):
        piece, at = place_a(dp)
        held_scr[number * out_chunk : (number + 1) * out_chunk, :] = a_refs[core][piece][
            at, rows_f:, :
        ].reshape(out_chunk, width)
    ahead_scr[...] = dot_nn(attn_ref[...], order_ref[...]).astype(BF)
    projected = dot_nn(ahead_scr[...], held_scr[...])
    unit_a, inverse_a = unit_of(projected)
    middle = resid_ref[...] + unit_a * (1.0 + sattn_ref[...])
    unit_p, inverse_p = unit_of(middle)
    pre = (unit_p * (1.0 + spre_ref[...])).astype(BF)
    ffn = jnp.zeros(middle.shape, jnp.float32)
    for number, (core, dp) in enumerate(parts):
        span = slice(number * chunk, (number + 1) * chunk)
        w_gate, w_up, w_down = weights(core, dp)
        gate = dot_nt(pre, w_gate)
        up = dot_nt(pre, w_up)
        gate_scr[:, span] = gate
        up_scr[:, span] = up
        bent = jnp.tanh(GELU_A * (gate + 0.044715 * (gate * gate * gate)))
        inner = (0.5 * gate * (1.0 + bent) * up).astype(BF)
        inner_scr[:, span] = inner
        ffn = ffn + dot_nn(inner, w_down)
    unit_f, inverse_f = unit_of(ffn)
    block_out_ref[...] = middle + unit_f * (1.0 + spost_ref[...])
    grad_out = gout_ref[...]
    gspost_ref[...] = jnp.sum(grad_out * unit_f, axis=0, keepdims=True)
    grad_ffn = rms_back(unit_f, inverse_f, grad_out * (1.0 + spost_ref[...])).astype(BF)
    grad_pre = jnp.zeros(middle.shape, jnp.float32)
    for number, (core, dp) in enumerate(parts):
        span = slice(number * chunk, (number + 1) * chunk)
        w_gate, w_up, w_down = weights(core, dp)
        grad_inner = dot_nt(grad_ffn, w_down)
        gate = gate_scr[:, span]
        square = gate * gate
        bent = jnp.tanh(GELU_A * (gate + 0.044715 * (square * gate)))
        curve = 0.5 * gate * (1.0 + bent)
        slope = 0.5 * (1.0 + bent) + 0.5 * gate * (1.0 - bent * bent) * (
            GELU_A * (1.0 + 3.0 * 0.044715 * square)
        )
        grad_up = (grad_inner * curve).astype(BF)
        grad_gate = (grad_inner * up_scr[:, span] * slope).astype(BF)
        grad_pre = grad_pre + dot_nn(grad_gate, w_gate) + dot_nn(grad_up, w_up)
        piece_a, at_a = place_a(dp)
        piece_b, at_b = place_b(dp)
        shape = (chips, rows_f, width)
        ga_refs[core][piece_a][at_a, :rows_f, :] = dot_tn(grad_gate, pre).astype(BF).reshape(shape)
        gb_refs[core][piece_b][at_b, :rows_f, :] = dot_tn(grad_up, pre).astype(BF).reshape(shape)
        gb_refs[core][piece_b][at_b, rows_f:, :] = (
            dot_tn(inner_scr[:, span], grad_ffn).astype(BF).reshape(shape)
        )
    gspre_ref[...] = jnp.sum(grad_pre * unit_p, axis=0, keepdims=True)
    grad_middle = grad_out + rms_back(unit_p, inverse_p, grad_pre * (1.0 + spre_ref[...]))
    gresid_ref[...] = grad_middle
    gsattn_ref[...] = jnp.sum(grad_middle * unit_a, axis=0, keepdims=True)
    grad_proj = rms_back(unit_a, inverse_a, grad_middle * (1.0 + sattn_ref[...])).astype(BF)
    grad_held = dot_nt(grad_proj, held_scr[...]).astype(BF)
    gattn_ref[...] = dot_nt(grad_held, order_ref[...]).astype(BF)
    for number, (core, dp) in enumerate(parts):
        piece, at = place_a(dp)
        span = slice(number * out_chunk, (number + 1) * out_chunk)
        ga_refs[core][piece][at, rows_f:, :] = (
            dot_tn(ahead_scr[:, span], grad_proj).astype(BF).reshape(chips, rows_o, width)
        )


def shards_plain(
    hidden_in,
    positions,
    w_query,
    w_key,
    w_value,
    w_output,
    w_gate,
    w_up,
    w_down,
    norm_scales,
    grad_out,
):
    width = hidden_in.shape[2]
    groups = lax.axis_size("ctx")
    count_dp = lax.axis_size("dp")
    chips = groups // 2
    owners = count_dp * groups
    place = lax.axis_index("ctx")
    row = lax.axis_index("dp")
    resid = hidden_in[0]
    posit = positions[0]
    grad_nat = grad_out[0]
    tokens = resid.shape[0]
    block = tokens // 2
    head_width = w_key.shape[0] * owners
    heads = w_query.shape[0] * owners // head_width
    rows_q, rows_k = w_query.shape[0], w_key.shape[0]
    scale_part = norm_scales.shape[0]

    tie = lax.optimization_barrier
    scale_rows = jnp.zeros((8, width), BF).at[0, :scale_part].set(norm_scales)
    first = gather_over(
        jnp.concatenate([w_query, w_key, w_value, scale_rows], axis=0)[None], swap_z, chips
    )
    rows_f = w_gate.shape[0]
    group_a = jnp.concatenate([w_gate, w_output], axis=0)[None]
    group_b = jnp.concatenate([w_up, w_down], axis=0)[None]
    inverse_in = lax.rsqrt(jnp.mean(resid * resid, axis=-1, keepdims=True) + EPS)
    unit_in = resid * inverse_in
    place_rows = jnp.zeros((8, width), BF)
    place_rows = place_rows.at[0, :tokens].set((posit // 64).astype(BF))
    place_rows = place_rows.at[1, :tokens].set((posit % 64).astype(BF))
    seq_part = jnp.concatenate([unit_in.astype(BF), place_rows], axis=0)[None]
    first, group_a, group_b, seq_part = tie((first, group_a, group_b, seq_part))
    first = gather_over(first[None], swap_dp, count_dp)
    group_a = gather_over(group_a, swap_z, chips)
    group_b = gather_over(group_b, swap_z, chips)
    first, group_a, group_b, seq_part = tie((first, group_a, group_b, seq_part))
    first = first.reshape((owners // 2,) + first.shape[2:])
    group_a = double(group_a, swap_dp, 1)
    group_b = double(group_b, swap_dp, 2)
    seq_z = gather_over(seq_part, swap_z, chips)
    first = jnp.concatenate([first, swap_ctx(first, 1)], axis=0)
    first, group_a, group_b, seq_z = tie((first, group_a, group_b, seq_z))
    seq_all = jnp.concatenate([seq_z, swap_ctx(seq_z, 1)], axis=0)
    group_a = double(group_a, swap_dp, 2)
    group_b = double_inner(group_b, swap_dp, 1)
    far_core, far_dp, far_z = (
        jnp.arange(owners, dtype=jnp.int32) // (owners // 2),
        (jnp.arange(owners, dtype=jnp.int32) // chips) % count_dp,
        jnp.arange(owners, dtype=jnp.int32) % chips,
    )
    owner_of = (row ^ far_dp) * groups + (place ^ (2 * far_z + far_core))
    order_q = row_order(owner_of, rows_q)
    order_k = row_order(owner_of, rows_k)
    order_s = row_order(owner_of, 1)
    full_query = reorder(order_q, first[:, :rows_q].reshape(-1, width))
    full_key = reorder(order_k, first[:, rows_q : rows_q + rows_k].reshape(-1, width))
    full_value = reorder(order_k, first[:, rows_q + rows_k : rows_q + 2 * rows_k].reshape(-1, width))
    full_scales = reorder(order_s, first[:, rows_q + 2 * rows_k, :scale_part]).reshape(-1)
    scale_in, scale_attn, scale_pre, scale_post, scale_query, scale_key = split_scales(
        full_scales, width, head_width
    )

    seq_len = groups * tokens
    seq_core, seq_zed = (
        jnp.arange(groups, dtype=jnp.int32) // chips,
        jnp.arange(groups, dtype=jnp.int32) % chips,
    )
    key_index = natural_rows(place ^ (2 * seq_zed + seq_core), block, groups)
    row_index = natural_rows(place[None], block, groups)
    unit_all = seq_all[:, :tokens].reshape(seq_len, width).astype(jnp.float32)
    pos_all = (
        seq_all[:, tokens, :tokens].astype(jnp.int32) * 64
        + seq_all[:, tokens + 1, :tokens].astype(jnp.int32)
    ).reshape(seq_len)
    normed = (unit_in * (1.0 + scale_in)).astype(BF)
    normed_all = (unit_all * (1.0 + scale_in)).astype(BF)

    query_raw = times_wt(normed, full_query).reshape(tokens, heads, head_width)
    key_raw = times_wt(normed_all, full_key)
    value_bf = times_wt(normed_all, full_value).astype(BF)

    def query_piece(raw, scale):
        return rotate(rms_scale(raw, scale), posit) * head_width ** (-0.5)

    def key_piece(raw, scale):
        return rotate(rms_scale(raw, scale)[:, None, :], pos_all)[:, 0, :]

    query_rot, query_back = jax.vjp(query_piece, query_raw, scale_query)
    key_rot, key_back = jax.vjp(key_piece, key_raw, scale_key)
    query_bf = jnp.swapaxes(query_rot.astype(BF), 0, 1).reshape(heads * tokens, head_width)
    key_bf = key_rot.astype(BF)
    allowed = jnp.tile(key_index[None, :] <= row_index[:, None], (heads, 1))
    scores = jnp.where(allowed, times_wt(query_bf, key_bf), -1e30)
    top = jnp.max(scores, axis=1, keepdims=True)
    lse = top + jnp.log(jnp.sum(jnp.exp(scores - top), axis=1, keepdims=True))
    probs = jnp.exp(scores - lse)
    probs_bf = probs.astype(BF)
    mixed = jnp.dot(probs_bf, value_bf, preferred_element_type=jnp.float32).astype(BF)
    attn_bf = jnp.swapaxes(mixed.reshape(heads, tokens, head_width), 0, 1).reshape(tokens, -1)

    group_a, group_b, attn_bf, probs = lax.optimization_barrier((group_a, group_b, attn_bf, probs))
    halves_a = (group_a, swap_ctx(group_a, 1))
    halves_b = (group_b, swap_ctx(group_b, 1))
    gates = [half[:, :rows_f].reshape(-1, width) for half in halves_a]
    ups = [half[:, :rows_f].reshape(-1, width) for half in halves_b]
    downs = [half[:, rows_f:].reshape(-1, width) for half in halves_b]
    out_held = jnp.concatenate([half[:, rows_f:].reshape(-1, width) for half in halves_a], axis=0)
    full_output = reorder(order_q, out_held)
    projected = jnp.dot(attn_bf, full_output, preferred_element_type=jnp.float32)
    (middle, pre_ffn), mid_back = jax.vjp(mid_piece, resid, projected, scale_attn, scale_pre)
    pre_bf = pre_ffn.astype(BF)
    inners, glu_backs = [], []
    for half_no in range(2):
        inner, glu_back = jax.vjp(
            glu_piece, times_wt(pre_bf, gates[half_no]), times_wt(pre_bf, ups[half_no])
        )
        inners.append(inner.astype(BF))
        glu_backs.append(glu_back)
    ffn = sum(
        jnp.dot(inners[half_no], downs[half_no], preferred_element_type=jnp.float32)
        for half_no in range(2)
    )
    block_out, out_back = jax.vjp(out_piece, middle, ffn, scale_post)
    grad_mid, grad_ffn, grad_scale_post = out_back(grad_nat)
    grad_ffn_bf = grad_ffn.astype(BF)
    grad_pre = 0.0
    downs_grad, gates_grad, ups_grad = [], [], []
    for half_no in range(2):
        grad_gate, grad_upward = glu_backs[half_no](times_wt(grad_ffn_bf, downs[half_no]))
        gate_bf = grad_gate.astype(BF)
        upward_bf = grad_upward.astype(BF)
        grad_pre = grad_pre + (
            jnp.dot(gate_bf, gates[half_no], preferred_element_type=jnp.float32)
            + jnp.dot(upward_bf, ups[half_no], preferred_element_type=jnp.float32)
        )
        downs_grad.append(outer_sum(inners[half_no], grad_ffn_bf).astype(BF))
        gates_grad.append(outer_sum(gate_bf, pre_bf).astype(BF))
        ups_grad.append(outer_sum(upward_bf, pre_bf).astype(BF))
    grads_b = [
        jnp.concatenate(
            [
                ups_grad[half_no].reshape(-1, rows_f, width),
                downs_grad[half_no].reshape(-1, rows_f, width),
            ],
            axis=1,
        )
        for half_no in range(2)
    ]
    grads_b = add_bf16(grads_b[0], swap_ctx(grads_b[1], 1)).astype(BF)
    grad_resid_a, grad_proj, grad_scale_attn, grad_scale_pre = mid_back((grad_mid, grad_pre))
    grad_proj_bf = grad_proj.astype(BF)
    grad_attn_bf = times_wt(grad_proj_bf, full_output).astype(BF)
    out_grad = reorder_back(order_q, outer_sum(attn_bf, grad_proj_bf))
    out_grad = out_grad.reshape(2, -1, rows_q, width)
    grads_a = [
        jnp.concatenate([gates_grad[half_no].reshape(-1, rows_f, width), out_grad[half_no]], axis=1)
        for half_no in range(2)
    ]
    grads_a = add_bf16(grads_a[0], swap_ctx(grads_a[1], 1)).astype(BF)
    grads_a, grads_b, grad_attn_bf, pre_bf = lax.optimization_barrier(
        (grads_a, grads_b, grad_attn_bf, pre_bf)
    )
    grads_a = halve(grads_a, swap_dp, 2)
    grads_b = halve_inner(grads_b, swap_dp, 1)

    grad_rows = jnp.swapaxes(grad_attn_bf.reshape(tokens, heads, head_width), 0, 1).reshape(
        heads * tokens, head_width
    )
    delta = jnp.sum(
        grad_rows.astype(jnp.float32) * mixed.astype(jnp.float32), axis=1, keepdims=True
    )
    grad_scores = (probs * (times_wt(grad_rows, value_bf) - delta)).astype(BF)
    grad_query = jnp.dot(grad_scores, key_bf, preferred_element_type=jnp.float32)
    grad_query = jnp.swapaxes(grad_query.reshape(heads, tokens, head_width), 0, 1)
    grad_key = outer_sum(grad_scores, query_bf)
    grad_value_bf = outer_sum(probs_bf, grad_rows).astype(BF)
    grad_qraw, grad_scale_query = query_back(grad_query)
    grad_kraw, grad_scale_key = key_back(grad_key)
    grad_qraw_bf = grad_qraw.reshape(tokens, heads * head_width).astype(BF)
    grad_kraw_bf = grad_kraw.astype(BF)

    grad_normed_q = jnp.dot(grad_qraw_bf, full_query, preferred_element_type=jnp.float32)
    grad_normed = jnp.dot(grad_kraw_bf, full_key, preferred_element_type=jnp.float32) + jnp.dot(
        grad_value_bf, full_value, preferred_element_type=jnp.float32
    )
    grad_scale_in = jnp.sum(grad_normed * unit_all, axis=0) + jnp.sum(
        grad_normed_q * unit_in, axis=0
    )
    far = grad_normed.astype(BF).reshape(2, chips, tokens, width)
    grad_w_query = reorder_back(order_q, outer_sum(grad_qraw_bf, normed))
    grad_w_key = reorder_back(order_k, outer_sum(grad_kraw_bf, normed_all))
    grad_w_value = reorder_back(order_k, outer_sum(grad_value_bf, normed_all))
    grad_scales = jnp.concatenate(
        [
            grad_scale_in,
            grad_scale_attn,
            grad_scale_pre,
            grad_scale_post,
            grad_scale_query,
            grad_scale_key,
        ]
    ).reshape(owners, scale_part)
    scales_back = reorder_back(order_s, grad_scales)
    packed = jnp.concatenate(
        [
            grad_w_query.reshape(owners, rows_q, width),
            grad_w_key.reshape(owners, rows_k, width),
            grad_w_value.reshape(owners, rows_k, width),
            jnp.zeros((owners, 8, width), BF).at[:, 0, :scale_part].set(scales_back),
        ],
        axis=1,
    ).reshape(2, -1, width)
    far_sum = add_bf16(far[0], swap_ctx(far[1], 1)).astype(BF)
    grads_a, grads_b, packed, far_sum = tie((grads_a, grads_b, packed, far_sum))
    grads_a = halve(grads_a, swap_dp, 1)
    grads_b = halve(grads_b, swap_dp, 2)
    own_normed = scatter_over(far_sum, swap_z, chips) + grad_normed_q
    packed = add_bf16(packed[0], swap_ctx(packed[1], 1)).astype(BF)
    grads_a, grads_b, packed, own_normed = tie((grads_a, grads_b, packed, own_normed))
    own_first = scatter_chip(packed)
    sum_a = scatter_over(grads_a, swap_z, chips)
    sum_b = scatter_over(grads_b, swap_z, chips)
    own_gate, own_output = sum_a[:rows_f], sum_a[rows_f:]
    own_up, own_down = sum_b[:rows_f], sum_b[rows_f:]
    own_query = own_first[:rows_q]
    own_key = own_first[rows_q : rows_q + rows_k]
    own_value = own_first[rows_q + rows_k : rows_q + 2 * rows_k]
    own_scales = own_first[rows_q + 2 * rows_k, :scale_part]
    grad_resid = grad_resid_a + rms_back(unit_in, inverse_in, own_normed * (1.0 + scale_in))
    return (
        block_out[None],
        grad_resid[None],
        own_query,
        own_key,
        own_value,
        own_output,
        own_gate,
        own_up,
        own_down,
        own_scales,
    )


def shards(*args):
    hidden_in, w_query, w_gate = args[0], args[2], args[6]
    fits = hidden_in.shape[1] * lax.axis_size("ctx") <= 2048 and lax.axis_size("dp") == 4
    if fits and w_query.shape[0] % 16 == 0 and w_gate.shape[0] % 16 == 0:
        return shards_kernels(*args)
    return shards_plain(*args)


def shards_kernels(
    hidden_in,
    positions,
    w_query,
    w_key,
    w_value,
    w_output,
    w_gate,
    w_up,
    w_down,
    norm_scales,
    grad_out,
):
    width = hidden_in.shape[2]
    groups = lax.axis_size("ctx")
    count_dp = lax.axis_size("dp")
    chips = groups // 2
    owners = count_dp * groups
    place = lax.axis_index("ctx")
    row = lax.axis_index("dp")
    resid = hidden_in[0]
    posit = positions[0]
    tokens = resid.shape[0]
    block = tokens // 2
    seq_len = groups * tokens
    head_width = w_key.shape[0] * owners
    heads = w_query.shape[0] * owners // head_width
    rows_q, rows_k, rows_f = w_query.shape[0], w_key.shape[0], w_gate.shape[0]
    scale_part = norm_scales.shape[0]
    tie = lax.optimization_barrier

    far_core, far_dp, far_z = (
        jnp.arange(owners, dtype=jnp.int32) // (owners // 2),
        (jnp.arange(owners, dtype=jnp.int32) // chips) % count_dp,
        jnp.arange(owners, dtype=jnp.int32) % chips,
    )
    owner_of = (row ^ far_dp) * groups + (place ^ (2 * far_z + far_core))
    order_q = row_order(owner_of, rows_q)
    order_k = row_order(owner_of, rows_k)
    order_s = row_order(owner_of, 1)
    seq_core, seq_zed = (
        jnp.arange(groups, dtype=jnp.int32) // chips,
        jnp.arange(groups, dtype=jnp.int32) % chips,
    )
    key_index = natural_rows(place ^ (2 * seq_zed + seq_core), block, groups).reshape(1, seq_len)
    row_index = natural_rows(place[None], block, groups).reshape(tokens, 1)

    last_rows = jnp.zeros((8, width), BF).at[0, :scale_part].set(norm_scales)
    last_rows = last_rows.at[1, :tokens].set((posit // 64).astype(BF))
    last_rows = last_rows.at[2, :tokens].set((posit % 64).astype(BF))
    first = gather_over(
        jnp.concatenate([w_query, w_key, w_value, last_rows], axis=0)[None], swap_z, chips
    )
    group_a = jnp.concatenate([w_gate, w_output], axis=0)[None]
    group_b = jnp.concatenate([w_up, w_down], axis=0)[None]
    inverse_in = lax.rsqrt(jnp.mean(resid * resid, axis=-1, keepdims=True) + EPS)
    unit_in = resid * inverse_in
    first, group_a, group_b, unit_bf = tie((first, group_a, group_b, unit_in.astype(BF)[None]))
    first = gather_over(first[None], swap_dp, count_dp)
    group_a = gather_over(group_a, swap_z, chips)
    group_b = gather_over(group_b, swap_z, chips)
    first, group_a, group_b, unit_bf = tie((first, group_a, group_b, unit_bf))
    first = first.reshape((owners // 2,) + first.shape[2:])
    a_one = double(group_a, swap_dp, 1)
    b_one = double(group_b, swap_dp, 2)
    near = gather_over(unit_bf, swap_z, chips).reshape(chips * tokens, width)
    first = jnp.concatenate([first, swap_ctx(first, 1)], axis=0)
    full_query = reorder(order_q, first[:, :rows_q].reshape(-1, width))
    full_key = reorder(order_k, first[:, rows_q : rows_q + rows_k].reshape(-1, width))
    full_value = reorder(order_k, first[:, rows_q + rows_k : rows_q + 2 * rows_k].reshape(-1, width))
    last = rows_q + 2 * rows_k
    full_scales = reorder(order_s, first[:, last, :scale_part]).reshape(-1)
    same_seq = first.reshape((2, count_dp, chips) + first.shape[1:])[:, 0, :, last:, :tokens]
    pos_all = same_seq[:, :, 1].astype(jnp.float32) * 64.0 + same_seq[:, :, 2].astype(jnp.float32)
    half = head_width // 2
    freq_table = 1000000.0 ** (-jnp.arange(half, dtype=jnp.float32) / half)
    angle = pos_all.reshape(seq_len)[:, None] * freq_table[None, :]
    cos_all, sine_all = jnp.cos(angle), jnp.sin(angle)
    (a_one, b_one, near, full_query, full_key, full_value, full_scales, cos_all, sine_all) = tie(
        (a_one, b_one, near, full_query, full_key, full_value, full_scales, cos_all, sine_all)
    )
    far = swap_ctx(near, 1)
    a_two = swap_dp(a_one, 2)
    b_two = swap_dp(b_one, 1)
    a_one_far = swap_ctx(a_one, 1)
    b_one_far = swap_ctx(b_one, 1)
    scale_in, scale_attn, scale_pre, scale_post, scale_query, scale_key = [
        scale[None] for scale in split_scales(full_scales, width, head_width)
    ]
    cos_own, sine_own = cos_all[:tokens], sine_all[:tokens]
    f32 = jnp.float32
    normed, normed_all, query_raw, key_raw, query_bf, key_bf, value_bf, attn_bf, lse = call_kernel(
        attend_kernel,
        [
            ((tokens, width), BF),
            ((seq_len, width), BF),
            ((tokens, heads * head_width), f32),
            ((seq_len, head_width), f32),
            ((tokens, heads * head_width), BF),
            ((seq_len, head_width), BF),
            ((seq_len, head_width), BF),
            ((tokens, heads * head_width), BF),
            ((tokens, heads), f32),
        ],
        [],
        20_000_000_000,
        (
            unit_in, near, far, full_query, full_key, full_value, scale_in, scale_query, scale_key,
            cos_own, sine_own, cos_all, sine_all, key_index, row_index,
        ),
    )
    a_one_far, b_one_far, a_two, b_two, attn_bf = tie((a_one_far, b_one_far, a_two, b_two, attn_bf))
    a_two_far = swap_ctx(a_two, 1)
    b_two_far = swap_ctx(b_two, 1)

    pieces_a = (a_one, a_two, a_one_far, a_two_far)
    pieces_b = (b_one, b_two, b_one_far, b_two_far)
    held = owners * rows_q
    hidden = owners * rows_f
    outs = call_kernel(
        mid_kernel,
        [((tokens, width), f32), ((tokens, width), f32), ((tokens, heads * head_width), BF)]
        + [((1, width), f32)] * 3
        + [(piece.shape, BF) for piece in pieces_a + pieces_b],
        [
            ((held, width), BF),
            ((tokens, held), BF),
            ((tokens, hidden), f32),
            ((tokens, hidden), f32),
            ((tokens, hidden), BF),
        ],
        20_000_000_000,
        (attn_bf, order_q, resid, grad_out[0], scale_attn, scale_pre, scale_post)
        + pieces_a
        + pieces_b,
    )
    block_out, grad_resid_a, grad_attn_bf, grad_s_attn, grad_s_pre, grad_s_post = outs[:6]
    ga_one, ga_two, ga_one_far, ga_two_far, gb_one, gb_two, gb_one_far, gb_two_far = outs[6:]

    ga_two = add_bf16(ga_two, swap_ctx(ga_two_far, 1)).astype(BF)
    gb_two = add_bf16(gb_two, swap_ctx(gb_two_far, 1)).astype(BF)
    ga_two, gb_two, grad_attn_bf = tie((ga_two, gb_two, grad_attn_bf))
    ga_come = swap_dp(ga_two, 2)
    gb_come = swap_dp(gb_two, 1)
    ga_one = add_bf16(ga_one, swap_ctx(ga_one_far, 1))
    gb_one = add_bf16(gb_one, swap_ctx(gb_one_far, 1))

    (gwq, gwk, gwv, g_near, g_far, grad_normed_q, grad_s_in, grad_s_query, grad_s_key) = call_kernel(
        attend_back_kernel,
        [
            ((heads * head_width, width), BF),
            ((head_width, width), BF),
            ((head_width, width), BF),
            (near.shape, BF),
            (far.shape, BF),
            ((tokens, width), f32),
            ((1, width), f32),
            ((1, head_width), f32),
            ((1, head_width), f32),
        ],
        [
            ((heads * tokens, seq_len), BF),
            ((heads * tokens, seq_len), BF),
            ((heads * tokens, head_width), BF),
            ((heads * tokens, head_width), BF),
            ((tokens, heads * head_width), BF),
        ],
        20_000_000_000,
        (
            grad_attn_bf, attn_bf, query_bf, key_bf, value_bf, lse, query_raw, key_raw,
            full_query, full_key, full_value, scale_query, scale_key, cos_own, sine_own, cos_all,
            sine_all, key_index, row_index, normed, normed_all, unit_in, near, far,
        ),
    )
    far_sum = add_bf16(g_near, swap_ctx(g_far, 1)).astype(BF).reshape(chips, tokens, width)
    grad_scales = jnp.concatenate(
        [grad_s_in, grad_s_attn, grad_s_pre, grad_s_post, grad_s_query, grad_s_key], axis=1
    ).reshape(owners, scale_part)
    scales_back = reorder_back(order_s, grad_scales)
    packed = jnp.concatenate(
        [
            reorder_back(order_q, gwq).reshape(owners, rows_q, width),
            reorder_back(order_k, gwk).reshape(owners, rows_k, width),
            reorder_back(order_k, gwv).reshape(owners, rows_k, width),
            jnp.zeros((owners, 8, width), BF).at[:, 0, :scale_part].set(scales_back),
        ],
        axis=1,
    ).reshape(2, -1, width)
    packed = add_bf16(packed[0], swap_ctx(packed[1], 1)).astype(BF)
    grads_a = add_bf16(ga_one, ga_come).astype(BF)
    grads_b = add_bf16(gb_one, gb_come).astype(BF)
    grads_a, grads_b, packed, far_sum = tie((grads_a, grads_b, packed, far_sum))
    grads_a = halve(grads_a, swap_dp, 1)
    grads_b = halve(grads_b, swap_dp, 2)
    own_normed = scatter_over(far_sum, swap_z, chips) + grad_normed_q
    grads_a, grads_b, packed, own_normed = tie((grads_a, grads_b, packed, own_normed))
    own_first = scatter_chip(packed)
    sum_a = scatter_over(grads_a, swap_z, chips)
    sum_b = scatter_over(grads_b, swap_z, chips)
    grad_resid = grad_resid_a + rms_back(unit_in, inverse_in, own_normed * (1.0 + scale_in))
    return (
        block_out[None],
        grad_resid[None],
        own_first[:rows_q],
        own_first[rows_q : rows_q + rows_k],
        own_first[rows_q + rows_k : last],
        sum_a[rows_f:],
        sum_a[:rows_f],
        sum_b[:rows_f],
        sum_b[rows_f:],
        own_first[last, :scale_part],
    )


def solution(mesh):
    in_specs = (
        P("dp", "ctx", None),
        P("dp", "ctx"),
        P(("dp", "ctx"), None),
        P(("dp", "ctx"), None),
        P(("dp", "ctx"), None),
        P(("dp", "ctx"), None),
        P(("dp", "ctx"), None),
        P(("dp", "ctx"), None),
        P(("dp", "ctx"), None),
        P(("dp", "ctx")),
        P("dp", "ctx", None),
    )
    out_specs = (
        P("dp", "ctx", None),
        P("dp", "ctx", None),
        P(("dp", "ctx"), None),
        P(("dp", "ctx"), None),
        P(("dp", "ctx"), None),
        P(("dp", "ctx"), None),
        P(("dp", "ctx"), None),
        P(("dp", "ctx"), None),
        P(("dp", "ctx"), None),
        P(("dp", "ctx")),
    )
    return jax.shard_map(shards, mesh=mesh, in_specs=in_specs, out_specs=out_specs, check_vma=False)
```

profile of v0, /device:TPU:0, one launch (start us, length us, event | category | flops | bytes accessed | tf_op | source)
XLA Modules:
  0.0 259.6 jit_solution(928457777129872073)
XLA Ops:
  3.1 5.1 %collective-permute-start.2 = (bf16[1,56,640]{2,1,0:T(8,128)(2,1)S(1)}, bf16[1,56,640]{2,1,0:T(8,128)(2,1)S(1)}, u32[]{:S(2)}, u32[]{:S(2)}) collective-permute-start(bf16[1,56,640]{2,1,0:T(8,128)(2,1)S(1)} %maximum_bitcast_fusion.2), channel_id=1, source_target_pairs={{0,6},{1,7},{2,4},{3,5},{4,2},{5,3},{6,0},{7,1},{8,14},{9,15},{10,... | collective-permute-start | bytes 215048 | tf_op jit(solution)/shard_map/ppermute | solution.py:75
  8.8 1.1 multiply_reduce_fusion.1
  9.9 1.1 multiply_convert_fusion
  12.8 1.3 collective-permute-done.1
  14.2 2.8 %collective-permute-start.8 = (bf16[1,96,640]{2,1,0:T(8,128)(2,1)S(1)}, bf16[1,96,640]{2,1,0:T(8,128)(2,1)S(1)}, u32[]{:S(2)}, u32[]{:S(2)}) collective-permute-start(bf16[1,96,640]{2,1,0:T(8,128)(2,1)S(1)} %maximum_bitcast_fusion.1), channel_id=1, source_target_pairs={{0,6},{1,7},{2,4},{3,5},{4,2},{5,3},{6,0},{7,1},{8,14},{9,15},{10,... | collective-permute-start | bytes 368648 | tf_op jit(solution)/shard_map/ppermute | solution.py:75
  17.0 1.7 collective-permute-start.6
  18.7 2.7 %collective-permute-start.11 = (bf16[1,128,640]{2,1,0:T(8,128)(2,1)S(1)}, bf16[1,128,640]{2,1,0:T(8,128)(2,1)S(1)}, u32[]{:S(2)}, u32[]{:S(2)}) collective-permute-start(bf16[1,128,640]{2,1,0:T(8,128)(2,1)S(1)} %maximum_bitcast_fusion), channel_id=1, source_target_pairs={{0,6},{1,7},{2,4},{3,5},{4,2},{5,3},{6,0},{7,1},{8,14},{9,15},{10,... | collective-permute-start | bytes 491528 | tf_op jit(solution)/shard_map/ppermute | solution.py:75
  22.4 5.6 %collective-permute-start.9 = (bf16[1,128,640]{2,1,0:T(8,128)(2,1)S(1)}, bf16[1,128,640]{2,1,0:T(8,128)(2,1)S(1)}, u32[]{:S(2)}, u32[]{:S(2)}) collective-permute-start(bf16[1,128,640]{2,1,0:T(8,128)(2,1)S(1)} %maximum_bitcast_fusion), channel_id=1, source_target_pairs={{0,2},{1,3},{2,0},{3,1},{4,6},{5,7},{6,4},{7,5},{8,10},{9,11},{10,... | collective-permute-start | bytes 491528 | tf_op jit(solution)/shard_map/ppermute | solution.py:75
  28.0 7.6 %collective-permute-done.7 = bf16[1,96,640]{2,1,0:T(8,128)(2,1)S(1)} collective-permute-done((bf16[1,96,640]{2,1,0:T(8,128)(2,1)S(1)}, bf16[1,96,640]{2,1,0:T(8,128)(2,1)S(1)}, u32[]{:S(2)}, u32[]{:S(2)}) %collective-permute-start.7) | collective-permute-done | bytes 122912 | tf_op jit(solution)/shard_map/ppermute | solution.py:75
  35.7 2.4 collective-permute-start.5
  39.3 2.1 collective-permute-done.10
  41.6 3.5 %collective-permute-done.5 = bf16[1,4,56,640]{3,2,1,0:T(8,128)(2,1)S(1)} collective-permute-done((bf16[1,4,56,640]{3,2,1,0:T(8,128)(2,1)S(1)}, bf16[1,4,56,640]{3,2,1,0:T(8,128)(2,1)S(1)}, u32[]{:S(2)}, u32[]{:S(2)}) %collective-permute-start.5) | collective-permute-done | bytes 286752 | tf_op jit(solution)/shard_map/ppermute | solution.py:70
  45.1 3.0 %collective-permute-done.4 = bf16[1,4,56,640]{3,2,1,0:T(8,128)(2,1)S(1)} collective-permute-done((bf16[1,4,56,640]{3,2,1,0:T(8,128)(2,1)S(1)}, bf16[1,4,56,640]{3,2,1,0:T(8,128)(2,1)S(1)}, u32[]{:S(2)}, u32[]{:S(2)}) %collective-permute-start.4) | collective-permute-done | bytes 286752 | tf_op jit(solution)/shard_map/ppermute | solution.py:70
  49.4 1.5 collective-permute-start.12
  52.1 5.7 %collective-permute-done.16 = bf16[1,128,640]{2,1,0:T(8,128)(2,1)S(1)} collective-permute-done((bf16[1,128,640]{2,1,0:T(8,128)(2,1)S(1)}, bf16[1,128,640]{2,1,0:T(8,128)(2,1)S(1)}, u32[]{:S(2)}, u32[]{:S(2)}) %collective-permute-start.16) | collective-permute-done | bytes 163872 | tf_op jit(solution)/shard_map/ppermute | solution.py:75
  57.8 4.8 %collective-permute-start.14 = (bf16[1,128,640]{2,1,0:T(8,128)(2,1)S(1)}, bf16[1,128,640]{2,1,0:T(8,128)(2,1)}, u32[]{:S(2)}, u32[]{:S(2)}) collective-permute-start(bf16[1,128,640]{2,1,0:T(8,128)(2,1)S(1)} %multiply_convert_fusion), channel_id=1, source_target_pairs={{0,2},{1,3},{2,0},{3,1},{4,6},{5,7},{6,4},{7,5},{8,10},{9,11},{10,... | collective-permute-start | bytes 491528 | tf_op jit(solution)/shard_map/ppermute | solution.py:75
  62.7 2.5 collective-permute-done.15
  65.2 3.5 %collective-permute-done.14 = bf16[1,128,640]{2,1,0:T(8,128)(2,1)} collective-permute-done((bf16[1,128,640]{2,1,0:T(8,128)(2,1)S(1)}, bf16[1,128,640]{2,1,0:T(8,128)(2,1)}, u32[]{:S(2)}, u32[]{:S(2)}) %collective-permute-start.14) | collective-permute-done | bytes 163872 | tf_op jit(solution)/shard_map/ppermute | solution.py:75
  68.7 1.9 pad_maximum_fusion.5
  70.7 2.1 pad_maximum_fusion.3.refs_7_
  72.8 2.4 pad_maximum_fusion.1.refs_11_
  76.1 1.5 pad_maximum_fusion
  77.7 1.2 fusion.10
  78.9 3.0 %fusion.8.wq_ref = bf16[1024,640]{1,0:T(8,128)(2,1)} fusion(bf16[1024,640]{1,0:T(8,128)(2,1)S(1)} %bitcast.117, s32[1024]{0:T(1024)S(1)} %add.390), kind=kOutput, calls=%fused_computation.24 | convolution fusion | flops 1343881216 | bytes 2625536 | tf_op jit(solution)/shard_map/dot_general | solution.py:162
  81.9 1.9 multiply_sine_fusion
  83.8 1.5 convolution_convert_fusion.3.wk_ref
  85.3 1.3 convolution_convert_fusion.2.wv_ref
  87.6 1.5 collective-permute-start.21
  90.1 7.4 %shard_map.186 = (bf16[128,640]{1,0:T(8,128)(2,1)S(1)}, bf16[1024,640]{1,0:T(8,128)(2,1)}, f32[128,1024]{1,0:T(8,128)}, f32[1024,256]{1,0:T(8,128)}, bf16[128,10...) custom-call(f32[128,640]{1,0:T(8,128)S(1)} %broadcast_multiply_fusio, ...), custom_call_target="tpu_custom_call" | custom-call | flops 20000000000 | bytes 20000000 | tf_op jit(solution)/shard_map/pallas_call | solution.py:204
  97.5 13.6 %collective-permute-done.20.refs_8_ = bf16[8,96,640]{2,1,0:T(8,128)(2,1)S(1)} collective-permute-done((bf16[8,96,640]{2,1,0:T(8,128)(2,1)S(1)}, bf16[8,96,640]{2,1,0:T(8,128)(2,1)S(1)}, u32[]{:S(2)}, u32[]{:S(2)}) %collective-permute-start.20) | collective-permute-done | bytes 983072 | tf_op jit(solution)/shard_map/ppermute | solution.py:70
  111.0 7.6 %collective-permute-done.21.refs_12_ = bf16[8,128,640]{2,1,0:T(8,128)(2,1)S(1)} collective-permute-done((bf16[8,128,640]{2,1,0:T(8,128)(2,1)S(1)}, bf16[8,128,640]{2,1,0:T(8,128)(2,1)S(1)}, u32[]{:S(2)}, u32[]{:S(2)}) %collective-permute-start.21) | collective-permute-done | bytes 1310752 | tf_op jit(solution)/shard_map/ppermute | solution.py:70
  119.1 2.4 fusion.2.refs_1_
  121.5 1.5 collective-permute-done.23.refs_10_
  124.5 17.4 %shard_map.187 = (f32[128,640]{1,0:T(8,128)}, f32[128,640]{1,0:T(8,128)S(1)}, bf16[128,1024]{1,0:T(8,128)(2,1)S(1)}, f32[1,640]{1,0:T(1,128)S(1)}, f32[1,640]{1,...) custom-call(bf16[128,1024]{1,0:T(8,128)(2,1)S(1)} %get-tuple-element, ...), custom_call_target="tpu_custom_call" | custom-call | flops 20000000000 | bytes 20000000 | tf_op jit(solution)/shard_map/pallas_call | solution.py:204
  142.6 5.4 %collective-permute-done.26 = bf16[8,96,640]{2,1,0:T(8,128)(2,1)S(1)} collective-permute-done((bf16[8,96,640]{2,1,0:T(8,128)(2,1)}, bf16[8,96,640]{2,1,0:T(8,128)(2,1)S(1)}, u32[]{:S(2)}, u32[]{:S(2)}) %collective-permute-start.26) | collective-permute-done | bytes 983072 | tf_op jit(solution)/shard_map/ppermute | solution.py:75
  148.0 2.5 add_convert_fusion.3
  150.6 1.4 add_convert_fusion.1
  152.0 9.7 %shard_map.188 = (bf16[1024,640]{1,0:T(8,128)(2,1)}, bf16[256,640]{1,0:T(8,128)(2,1)S(1)}, bf16[256,640]{1,0:T(8,128)(2,1)S(1)}, bf16[512,640]{1,0:T(8,128)(2,1)...) custom-call(bf16[128,1024]{1,0:T(8,128)(2,1)S(1)} %get-tuple-element, ...), custom_call_target="tpu_custom_call" | custom-call | flops 20000000000 | bytes 20000000 | tf_op jit(solution)/shard_map/pallas_call | solution.py:204
  161.7 3.5 %fusion.9 = bf16[1024,640]{1,0:T(8,128)(2,1)S(1)} fusion(bf16[1024,640]{1,0:T(8,128)(2,1)} %get-tuple-element.168, s32[1024]{0:T(1024)S(1)} %add.390), kind=kOutput, calls=%fused_computation.25 | convolution fusion | flops 1343881216 | bytes 2625536 | tf_op jit(solution)/shard_map/dot_general | solution.py:50
  166.6 1.5 collective-permute-start.28
  170.0 1.5 collective-permute-start.30
  171.7 18.8 %collective-permute-done.28 = bf16[8,96,640]{2,1,0:T(8,128)(2,1)S(1)} collective-permute-done((bf16[8,96,640]{2,1,0:T(8,128)(2,1)S(1)}, bf16[8,96,640]{2,1,0:T(8,128)(2,1)S(1)}, u32[]{:S(2)}, u32[]{:S(2)}) %collective-permute-start.28) | collective-permute-done | bytes 983072 | tf_op jit(solution)/shard_map/ppermute | solution.py:70
  190.5 1.6 add_convert_fusion.2
  192.5 8.3 %collective-permute-done.30 = bf16[8,128,640]{2,1,0:T(8,128)(2,1)S(1)} collective-permute-done((bf16[8,128,640]{2,1,0:T(8,128)(2,1)S(1)}, bf16[8,128,640]{2,1,0:T(8,128)(2,1)S(1)}, u32[]{:S(2)}, u32[]{:S(2)}) %collective-permute-start.30) | collective-permute-done | bytes 1310752 | tf_op jit(solution)/shard_map/ppermute | solution.py:70
  201.4 1.6 collective-permute-start.33
  203.1 2.4 collective-permute-start.37
  205.5 1.1 collective-permute-start.36
  207.3 3.7 %collective-permute-done.35 = bf16[128,640]{1,0:T(8,128)(2,1)S(1)} collective-permute-done((bf16[128,640]{1,0:T(8,128)(2,1)S(1)}, bf16[128,640]{1,0:T(8,128)(2,1)S(1)}, u32[]{:S(2)}, u32[]{:S(2)}) %collective-permute-start.35) | collective-permute-done | bytes 163872 | tf_op jit(solution)/shard_map/ppermute | solution.py:75
  211.0 3.2 %collective-permute-done.37 = bf16[128,640]{1,0:T(8,128)(2,1)S(1)} collective-permute-done((bf16[128,640]{1,0:T(8,128)(2,1)S(1)}, bf16[128,640]{1,0:T(8,128)(2,1)S(1)}, u32[]{:S(2)}, u32[]{:S(2)}) %collective-permute-start.37) | collective-permute-done | bytes 163872 | tf_op jit(solution)/shard_map/ppermute | solution.py:75
  214.2 5.8 %collective-permute-done.36 = bf16[128,640]{1,0:T(8,128)(2,1)S(1)} collective-permute-done((bf16[128,640]{1,0:T(8,128)(2,1)S(1)}, bf16[128,640]{1,0:T(8,128)(2,1)S(1)}, u32[]{:S(2)}, u32[]{:S(2)}) %collective-permute-start.36) | collective-permute-done | bytes 163872 | tf_op jit(solution)/shard_map/ppermute | solution.py:75
  220.2 1.3 collective-permute-done.34
  222.6 1.3 collective-permute-start.44
  223.9 2.4 collective-permute-start.46
  226.3 2.1 collective-permute-start.47
  229.3 2.0 collective-permute-done.44
  231.3 1.4 collective-permute-start.38
  232.7 1.6 collective-permute-start.39
  234.3 1.2 collective-permute-done.45
  235.5 6.1 %collective-permute-start.49 = (bf16[128,640]{1,0:T(8,128)(2,1)S(1)}, bf16[128,640]{1,0:T(8,128)(2,1)S(1)}, u32[]{:S(2)}, u32[]{:S(2)}) collective-permute-start(bf16[128,640]{1,0:T(8,128)(2,1)S(1)} %get-tuple-element.197), channel_id=1, source_target_pairs={{0,6},{1,7},{2,4},{3,5},{4,2},{5,3},{6,0},{7,1},{8,14},{9,15},{10,... | collective-permute-start | bytes 491528 | tf_op jit(solution)/shard_map/ppermute | solution.py:75
  243.0 2.0 collective-permute-done.49
  245.0 3.7 %collective-permute-done.48 = bf16[128,640]{1,0:T(8,128)(2,1)S(1)} collective-permute-done((bf16[128,640]{1,0:T(8,128)(2,1)S(1)}, bf16[128,640]{1,0:T(8,128)(2,1)S(1)}, u32[]{:S(2)}, u32[]{:S(2)}) %collective-permute-start.48) | collective-permute-done | bytes 163872 | tf_op jit(solution)/shard_map/ppermute | solution.py:75
  249.1 2.7 %collective-permute-start.43 = (bf16[56,640]{1,0:T(8,128)(2,1)S(1)}, bf16[56,640]{1,0:T(8,128)(2,1)S(1)}, u32[]{:S(2)}, u32[]{:S(2)}) collective-permute-start(bf16[56,640]{1,0:T(8,128)(2,1)S(1)} %get-tuple-element.208), channel_id=1, source_target_pairs={{0,6},{1,7},{2,4},{3,5},{4,2},{5,3},{6,0},{7,1},{8,14},{9,15},{10,... | collective-permute-start | bytes 215048 | tf_op jit(solution)/shard_map/ppermute | solution.py:75
  253.9 1.5 collective-permute-done.43
  255.4 2.4 collective-permute-done.42
  (182 shorter events, 28.5 us)
Async XLA Ops:
  3.1 9.8 %collective-permute-start.2 = (bf16[1,56,640]{2,1,0:T(8,128)(2,1)S(1)}, bf16[1,56,640]{2,1,0:T(8,128)(2,1)S(1)}, u32[]{:S(2)}, u32[]{:S(2)}) collective-permute-start(bf16[1,56,640]{2,1,0:T(8,128)(2,1)S(1)} %maximum_bitcast_fusion.2), channel_id=1, source_target_pairs={{0,6},{1,7},{2,4},{3,5},{4,2},{5,3},{6,0},{7,1},{8,14},{9,15},{10,... | collective-permute-start | bytes 215048 | tf_op jit(solution)/shard_map/ppermute | solution.py:75
  8.1 6.1 %collective-permute-start.1 = (bf16[1,56,640]{2,1,0:T(8,128)(2,1)S(1)}, bf16[1,56,640]{2,1,0:T(8,128)(2,1)S(1)}, u32[]{:S(2)}, u32[]{:S(2)}) collective-permute-start(bf16[1,56,640]{2,1,0:T(8,128)(2,1)S(1)} %maximum_bitcast_fusion.2), channel_id=1, source_target_pairs={{0,4},{1,5},{2,6},{3,7},{4,0},{5,1},{6,2},{7,3},{8,12},{9,13},{10,... | collective-permute-start | bytes 215048 | tf_op jit(solution)/shard_map/ppermute | solution.py:75
  8.1 6.1 %collective-permute-start = (bf16[1,56,640]{2,1,0:T(8,128)(2,1)S(1)}, bf16[1,56,640]{2,1,0:T(8,128)(2,1)S(1)}, u32[]{:S(2)}, u32[]{:S(2)}) collective-permute-start(bf16[1,56,640]{2,1,0:T(8,128)(2,1)S(1)} %maximum_bitcast_fusion.2), channel_id=1, source_target_pairs={{0,2},{1,3},{2,0},{3,1},{4,6},{5,7},{6,4},{7,5},{8,10},{9,11},{10,... | collective-permute-start | bytes 215048 | tf_op jit(solution)/shard_map/ppermute | solution.py:75
  14.2 8.2 %collective-permute-start.8 = (bf16[1,96,640]{2,1,0:T(8,128)(2,1)S(1)}, bf16[1,96,640]{2,1,0:T(8,128)(2,1)S(1)}, u32[]{:S(2)}, u32[]{:S(2)}) collective-permute-start(bf16[1,96,640]{2,1,0:T(8,128)(2,1)S(1)} %maximum_bitcast_fusion.1), channel_id=1, source_target_pairs={{0,6},{1,7},{2,4},{3,5},{4,2},{5,3},{6,0},{7,1},{8,14},{9,15},{10,... | collective-permute-start | bytes 368648 | tf_op jit(solution)/shard_map/ppermute | solution.py:75
  17.0 18.6 %collective-permute-start.7 = (bf16[1,96,640]{2,1,0:T(8,128)(2,1)S(1)}, bf16[1,96,640]{2,1,0:T(8,128)(2,1)S(1)}, u32[]{:S(2)}, u32[]{:S(2)}) collective-permute-start(bf16[1,96,640]{2,1,0:T(8,128)(2,1)S(1)} %maximum_bitcast_fusion.1), channel_id=1, source_target_pairs={{0,4},{1,5},{2,6},{3,7},{4,0},{5,1},{6,2},{7,3},{8,12},{9,13},{10,... | collective-permute-start | bytes 368648 | tf_op jit(solution)/shard_map/ppermute | solution.py:75
  17.0 21.1 %collective-permute-start.6 = (bf16[1,96,640]{2,1,0:T(8,128)(2,1)S(1)}, bf16[1,96,640]{2,1,0:T(8,128)(2,1)S(1)}, u32[]{:S(2)}, u32[]{:S(2)}) collective-permute-start(bf16[1,96,640]{2,1,0:T(8,128)(2,1)S(1)} %maximum_bitcast_fusion.1), channel_id=1, source_target_pairs={{0,2},{1,3},{2,0},{3,1},{4,6},{5,7},{6,4},{7,5},{8,10},{9,11},{10,... | collective-permute-start | bytes 368648 | tf_op jit(solution)/shard_map/ppermute | solution.py:75
  18.7 19.9 %collective-permute-start.11 = (bf16[1,128,640]{2,1,0:T(8,128)(2,1)S(1)}, bf16[1,128,640]{2,1,0:T(8,128)(2,1)S(1)}, u32[]{:S(2)}, u32[]{:S(2)}) collective-permute-start(bf16[1,128,640]{2,1,0:T(8,128)(2,1)S(1)} %maximum_bitcast_fusion), channel_id=1, source_target_pairs={{0,6},{1,7},{2,4},{3,5},{4,2},{5,3},{6,0},{7,1},{8,14},{9,15},{10,... | collective-permute-start | bytes 491528 | tf_op jit(solution)/shard_map/ppermute | solution.py:75
  21.4 20.0 %collective-permute-start.10 = (bf16[1,128,640]{2,1,0:T(8,128)(2,1)S(1)}, bf16[1,128,640]{2,1,0:T(8,128)(2,1)S(1)}, u32[]{:S(2)}, u32[]{:S(2)}) collective-permute-start(bf16[1,128,640]{2,1,0:T(8,128)(2,1)S(1)} %maximum_bitcast_fusion), channel_id=1, source_target_pairs={{0,4},{1,5},{2,6},{3,7},{4,0},{5,1},{6,2},{7,3},{8,12},{9,13},{10,... | collective-permute-start | bytes 491528 | tf_op jit(solution)/shard_map/ppermute | solution.py:75
  22.4 19.0 %collective-permute-start.9 = (bf16[1,128,640]{2,1,0:T(8,128)(2,1)S(1)}, bf16[1,128,640]{2,1,0:T(8,128)(2,1)S(1)}, u32[]{:S(2)}, u32[]{:S(2)}) collective-permute-start(bf16[1,128,640]{2,1,0:T(8,128)(2,1)S(1)} %maximum_bitcast_fusion), channel_id=1, source_target_pairs={{0,2},{1,3},{2,0},{3,1},{4,6},{5,7},{6,4},{7,5},{8,10},{9,11},{10,... | collective-permute-start | bytes 491528 | tf_op jit(solution)/shard_map/ppermute | solution.py:75
  35.7 9.4 %collective-permute-start.5 = (bf16[1,4,56,640]{3,2,1,0:T(8,128)(2,1)S(1)}, bf16[1,4,56,640]{3,2,1,0:T(8,128)(2,1)S(1)}, u32[]{:S(2)}, u32[]{:S(2)}) collective-permute-start(bf16[1,4,56,640]{3,2,1,0:T(8,128)(2,1)S(1)} %bitcast.119), channel_id=1, source_target_pairs={{0,24},{8,16},{16,8},{24,0},{1,25},{9,17},{17,9},{25,1},{2,26},{10... | collective-permute-start | bytes 860168 | tf_op jit(solution)/shard_map/ppermute | solution.py:70
  38.1 10.0 %collective-permute-start.4 = (bf16[1,4,56,640]{3,2,1,0:T(8,128)(2,1)S(1)}, bf16[1,4,56,640]{3,2,1,0:T(8,128)(2,1)S(1)}, u32[]{:S(2)}, u32[]{:S(2)}) collective-permute-start(bf16[1,4,56,640]{3,2,1,0:T(8,128)(2,1)S(1)} %bitcast.120), channel_id=1, source_target_pairs={{0,16},{8,24},{16,0},{24,8},{1,17},{9,25},{17,1},{25,9},{2,18},{10... | collective-permute-start | bytes 860168 | tf_op jit(solution)/shard_map/ppermute | solution.py:70
  38.6 9.8 %collective-permute-start.3 = (bf16[1,4,56,640]{3,2,1,0:T(8,128)(2,1)S(1)}, bf16[1,4,56,640]{3,2,1,0:T(8,128)(2,1)S(1)}, u32[]{:S(2)}, u32[]{:S(2)}) collective-permute-start(bf16[1,4,56,640]{3,2,1,0:T(8,128)(2,1)S(1)} %bitcast.121), channel_id=1, source_target_pairs={{0,8},{8,0},{16,24},{24,16},{1,9},{9,1},{17,25},{25,17},{2,10},{10... | collective-permute-start | bytes 860168 | tf_op jit(solution)/shard_map/ppermute | solution.py:70
  41.6 7.2 %copy-start = (f32[1,128,640]{2,1,0:T(8,128)S(1)}, f32[1,128,640]{2,1,0:T(8,128)}, u32[]{:S(2)}) copy-start(f32[1,128,640]{2,1,0:T(8,128)} %param.19) | copy-start | bytes 983044
  48.6 26.6 %collective-permute-start.17 = (bf16[16,56,640]{2,1,0:T(8,128)(2,1)S(1)}, bf16[16,56,640]{2,1,0:T(8,128)(2,1)}, u32[]{:S(2)}, u32[]{:S(2)}) collective-permute-start(bf16[16,56,640]{2,1,0:T(8,128)(2,1)S(1)} %bitcast.108), channel_id=1, source_target_pairs={{0,1},{1,0},{2,3},{3,2},{4,5},{5,4},{6,7},{7,6},{8,9},{9,8},{10,11... | collective-permute-start | bytes 3440648 | tf_op jit(solution)/shard_map/ppermute | solution.py:75
  48.8 40.4 %copy-start.3 = (f32[128,640]{1,0:T(8,128)}, f32[128,640]{1,0:T(8,128)S(1)}, u32[]{:S(2)}) copy-start(f32[128,640]{1,0:T(8,128)S(1)} %broadcast_multiply_fusion.unit_ref) | copy-start | bytes 983044
  48.8 9.0 %collective-permute-start.16 = (bf16[1,128,640]{2,1,0:T(8,128)(2,1)S(1)}, bf16[1,128,640]{2,1,0:T(8,128)(2,1)S(1)}, u32[]{:S(2)}, u32[]{:S(2)}) collective-permute-start(bf16[1,128,640]{2,1,0:T(8,128)(2,1)S(1)} %multiply_convert_fusion), channel_id=1, source_target_pairs={{0,6},{1,7},{2,4},{3,5},{4,2},{5,3},{6,0},{7,1},{8,14},{9,15},{10,... | collective-permute-start | bytes 491528 | tf_op jit(solution)/shard_map/ppermute | solution.py:75
  49.4 21.2 %collective-permute-start.12 = (bf16[4,96,640]{2,1,0:T(8,128)(2,1)S(1)}, bf16[4,96,640]{2,1,0:T(8,128)(2,1)}, u32[]{:S(2)}, u32[]{:S(2)}) collective-permute-start(bf16[4,96,640]{2,1,0:T(8,128)(2,1)S(1)} %pad_maximum_fusion.6), channel_id=1, source_target_pairs={{0,8},{8,0},{16,24},{24,16},{1,9},{9,1},{17,25},{25,17},{2,10},{10... | collective-permute-start | bytes 1474568 | tf_op jit(solution)/shard_map/ppermute | solution.py:70
  50.9 21.8 %collective-permute-start.13 = (bf16[4,128,640]{2,1,0:T(8,128)(2,1)S(1)}, bf16[4,128,640]{2,1,0:T(8,128)(2,1)}, u32[]{:S(2)}, u32[]{:S(2)}) collective-permute-start(bf16[4,128,640]{2,1,0:T(8,128)(2,1)S(1)} %pad_maximum_fusion.4), channel_id=1, source_target_pairs={{0,16},{8,24},{16,0},{24,8},{1,17},{9,25},{17,1},{25,9},{2,18},{10... | collective-permute-start | bytes 1966088 | tf_op jit(solution)/shard_map/ppermute | solution.py:70
  51.6 13.6 %collective-permute-start.15 = (bf16[1,128,640]{2,1,0:T(8,128)(2,1)S(1)}, bf16[1,128,640]{2,1,0:T(8,128)(2,1)S(1)}, u32[]{:S(2)}, u32[]{:S(2)}) collective-permute-start(bf16[1,128,640]{2,1,0:T(8,128)(2,1)S(1)} %multiply_convert_fusion), channel_id=1, source_target_pairs={{0,4},{1,5},{2,6},{3,7},{4,0},{5,1},{6,2},{7,3},{8,12},{9,13},{10,... | collective-permute-start | bytes 491528 | tf_op jit(solution)/shard_map/ppermute | solution.py:75
  57.8 10.9 %collective-permute-start.14 = (bf16[1,128,640]{2,1,0:T(8,128)(2,1)S(1)}, bf16[1,128,640]{2,1,0:T(8,128)(2,1)}, u32[]{:S(2)}, u32[]{:S(2)}) collective-permute-start(bf16[1,128,640]{2,1,0:T(8,128)(2,1)S(1)} %multiply_convert_fusion), channel_id=1, source_target_pairs={{0,2},{1,3},{2,0},{3,1},{4,6},{5,7},{6,4},{7,5},{8,10},{9,11},{10,... | collective-permute-start | bytes 491528 | tf_op jit(solution)/shard_map/ppermute | solution.py:75
  83.8 5.4 %copy-start.13 = (f32[1024,128]{1,0:T(8,128)}, f32[1024,128]{1,0:T(8,128)S(1)}, u32[]{:S(2)}) copy-start(f32[1024,128]{1,0:T(8,128)S(1)} %get-tuple-element.138.cos_all_ref) | copy-start | bytes 1572868
  83.8 5.4 %copy-start.12 = (f32[1024,128]{1,0:T(8,128)}, f32[1024,128]{1,0:T(8,128)S(1)}, u32[]{:S(2)}) copy-start(f32[1024,128]{1,0:T(8,128)S(1)} %get-tuple-element.139.sine_all_ref) | copy-start | bytes 1572868
  85.3 4.0 %copy-start.1 = (bf16[256,640]{1,0:T(8,128)(2,1)}, bf16[256,640]{1,0:T(8,128)(2,1)S(1)}, u32[]{:S(2)}) copy-start(bf16[256,640]{1,0:T(8,128)(2,1)S(1)} %convolution_convert_fusion.3.wk_ref) | copy-start | bytes 983044
  86.7 10.8 %copy-start.2 = (bf16[256,640]{1,0:T(8,128)(2,1)}, bf16[256,640]{1,0:T(8,128)(2,1)S(1)}, u32[]{:S(2)}) copy-start(bf16[256,640]{1,0:T(8,128)(2,1)S(1)} %convolution_convert_fusion.2.wv_ref) | copy-start | bytes 983044
  86.7 2.5 collective-permute-start.22
  86.9 24.2 %collective-permute-start.20 = (bf16[8,96,640]{2,1,0:T(8,128)(2,1)S(1)}, bf16[8,96,640]{2,1,0:T(8,128)(2,1)S(1)}, u32[]{:S(2)}, u32[]{:S(2)}) collective-permute-start(bf16[8,96,640]{2,1,0:T(8,128)(2,1)S(1)} %copy-done.9), channel_id=1, source_target_pairs={{0,16},{8,24},{16,0},{24,8},{1,17},{9,25},{17,1},{25,9},{2,18},{10... | collective-permute-start | bytes 2949128 | tf_op jit(solution)/shard_map/ppermute | solution.py:70
  87.4 23.6 %collective-permute-start.18 = (bf16[8,96,640]{2,1,0:T(8,128)(2,1)S(1)}, bf16[8,96,640]{2,1,0:T(8,128)(2,1)}, u32[]{:S(2)}, u32[]{:S(2)}) collective-permute-start(bf16[8,96,640]{2,1,0:T(8,128)(2,1)S(1)} %copy-done.9), channel_id=1, source_target_pairs={{0,1},{1,0},{2,3},{3,2},{4,5},{5,4},{6,7},{7,6},{8,9},{9,8},{10,11... | collective-permute-start | bytes 2949128 | tf_op jit(solution)/shard_map/ppermute | solution.py:75
  87.6 31.0 %collective-permute-start.21 = (bf16[8,128,640]{2,1,0:T(8,128)(2,1)S(1)}, bf16[8,128,640]{2,1,0:T(8,128)(2,1)S(1)}, u32[]{:S(2)}, u32[]{:S(2)}) collective-permute-start(bf16[8,128,640]{2,1,0:T(8,128)(2,1)S(1)} %copy-done.6), channel_id=1, source_target_pairs={{0,8},{8,0},{16,24},{24,16},{1,9},{9,1},{17,25},{25,17},{2,10},{10... | collective-permute-start | bytes 3932168 | tf_op jit(solution)/shard_map/ppermute | solution.py:70
  89.1 29.5 %collective-permute-start.19 = (bf16[8,128,640]{2,1,0:T(8,128)(2,1)S(1)}, bf16[8,128,640]{2,1,0:T(8,128)(2,1)}, u32[]{:S(2)}, u32[]{:S(2)}) collective-permute-start(bf16[8,128,640]{2,1,0:T(8,128)(2,1)S(1)} %copy-done.6), channel_id=1, source_target_pairs={{0,1},{1,0},{2,3},{3,2},{4,5},{5,4},{6,7},{7,6},{8,9},{9,8},{10,11... | collective-permute-start | bytes 3932168 | tf_op jit(solution)/shard_map/ppermute | solution.py:75
  97.5 27.1 %copy-start.4 = (f32[1,128,640]{2,1,0:T(8,128)S(1)}, f32[1,128,640]{2,1,0:T(8,128)}, u32[]{:S(2)}) copy-start(f32[1,128,640]{2,1,0:T(8,128)} %param.29) | copy-start | bytes 983044
  111.0 12.1 %copy-start.20 = (bf16[8,96,640]{2,1,0:T(8,128)(2,1)}, bf16[8,96,640]{2,1,0:T(8,128)(2,1)S(1)}, u32[]{:S(2)}) copy-start(bf16[8,96,640]{2,1,0:T(8,128)(2,1)S(1)} %collective-permute-done.20.refs_8_) | copy-start | bytes 2949124
  118.6 4.5 %copy-start.18 = (bf16[8,128,640]{2,1,0:T(8,128)(2,1)}, bf16[8,128,640]{2,1,0:T(8,128)(2,1)S(1)}, u32[]{:S(2)}) copy-start(bf16[8,128,640]{2,1,0:T(8,128)(2,1)S(1)} %collective-permute-done.21.refs_12_) | copy-start | bytes 3932164
  118.6 4.4 %collective-permute-start.24 = (bf16[8,128,640]{2,1,0:T(8,128)(2,1)S(1)}, bf16[8,128,640]{2,1,0:T(8,128)(2,1)S(1)}, u32[]{:S(2)}, u32[]{:S(2)}) collective-permute-start(bf16[8,128,640]{2,1,0:T(8,128)(2,1)S(1)} %collective-permute-done.21.refs_12_), channel_id=1, source_target_pairs={{0,1},{1,0},{2,3},{3,2},{4,5},{5,4},{6,7},{7,6},{8,9},{9,8},{10,11... | collective-permute-start | bytes 3932168 | tf_op jit(solution)/shard_map/ppermute | solution.py:75
  118.6 4.4 %collective-permute-start.23 = (bf16[8,96,640]{2,1,0:T(8,128)(2,1)S(1)}, bf16[8,96,640]{2,1,0:T(8,128)(2,1)S(1)}, u32[]{:S(2)}, u32[]{:S(2)}) collective-permute-start(bf16[8,96,640]{2,1,0:T(8,128)(2,1)S(1)} %collective-permute-done.20.refs_8_), channel_id=1, source_target_pairs={{0,1},{1,0},{2,3},{3,2},{4,5},{5,4},{6,7},{7,6},{8,9},{9,8},{10,11... | collective-permute-start | bytes 2949128 | tf_op jit(solution)/shard_map/ppermute | solution.py:75
  142.0 8.6 %collective-permute-start.27 = (bf16[8,128,640]{2,1,0:T(8,128)(2,1)}, bf16[8,128,640]{2,1,0:T(8,128)(2,1)S(1)}, u32[]{:S(2)}, u32[]{:S(2)}) collective-permute-start(bf16[8,128,640]{2,1,0:T(8,128)(2,1)} %get-tuple-element.153), channel_id=1, source_target_pairs={{0,1},{1,0},{2,3},{3,2},{4,5},{5,4},{6,7},{7,6},{8,9},{9,8},{10,11... | collective-permute-start | bytes 3932168 | tf_op jit(solution)/shard_map/ppermute | solution.py:75
  142.1 5.9 %collective-permute-start.26 = (bf16[8,96,640]{2,1,0:T(8,128)(2,1)}, bf16[8,96,640]{2,1,0:T(8,128)(2,1)S(1)}, u32[]{:S(2)}, u32[]{:S(2)}) collective-permute-start(bf16[8,96,640]{2,1,0:T(8,128)(2,1)} %get-tuple-element.151), channel_id=1, source_target_pairs={{0,1},{1,0},{2,3},{3,2},{4,5},{5,4},{6,7},{7,6},{8,9},{9,8},{10,11... | collective-permute-start | bytes 2949128 | tf_op jit(solution)/shard_map/ppermute | solution.py:75
  142.5 29.2 %collective-permute-start.25 = (bf16[8,96,640]{2,1,0:T(8,128)(2,1)}, bf16[8,96,640]{2,1,0:T(8,128)(2,1)}, u32[]{:S(2)}, u32[]{:S(2)}) collective-permute-start(bf16[8,96,640]{2,1,0:T(8,128)(2,1)} %get-tuple-element.149), channel_id=1, source_target_pairs={{0,1},{1,0},{2,3},{3,2},{4,5},{5,4},{6,7},{7,6},{8,9},{9,8},{10,11... | collective-permute-start | bytes 2949128 | tf_op jit(solution)/shard_map/ppermute | solution.py:75
  161.7 4.6 %copy-start.23 = (bf16[512,640]{1,0:T(8,128)(2,1)S(1)}, bf16[512,640]{1,0:T(8,128)(2,1)}, u32[]{:S(2)}) copy-start(bf16[512,640]{1,0:T(8,128)(2,1)} %get-tuple-element.178) | copy-start | bytes 1966084
  166.3 3.3 %collective-permute-start.32 = (bf16[512,640]{1,0:T(8,128)(2,1)S(1)}, bf16[512,640]{1,0:T(8,128)(2,1)S(1)}, u32[]{:S(2)}, u32[]{:S(2)}) collective-permute-start(bf16[512,640]{1,0:T(8,128)(2,1)S(1)} %copy-done.23), channel_id=1, source_target_pairs={{0,1},{1,0},{2,3},{3,2},{4,5},{5,4},{6,7},{7,6},{8,9},{9,8},{10,11... | collective-permute-start | bytes 1966088 | tf_op jit(solution)/shard_map/ppermute | solution.py:75
  166.6 23.9 %collective-permute-start.28 = (bf16[8,96,640]{2,1,0:T(8,128)(2,1)S(1)}, bf16[8,96,640]{2,1,0:T(8,128)(2,1)S(1)}, u32[]{:S(2)}, u32[]{:S(2)}) collective-permute-start(bf16[8,96,640]{2,1,0:T(8,128)(2,1)S(1)} %copy-done.10), channel_id=1, source_target_pairs={{0,16},{8,24},{16,0},{24,8},{1,17},{9,25},{17,1},{25,9},{2,18},{10... | collective-permute-start | bytes 2949128 | tf_op jit(solution)/shard_map/ppermute | solution.py:70
  168.3 3.2 %copy-start.15 = (bf16[512,640]{1,0:T(8,128)(2,1)S(1)}, bf16[512,640]{1,0:T(8,128)(2,1)}, u32[]{:S(2)}) copy-start(bf16[512,640]{1,0:T(8,128)(2,1)} %get-tuple-element.177) | copy-start | bytes 1966084
  168.5 22.0 %copy-start.11 = (bf16[8,96,640]{2,1,0:T(8,128)(2,1)S(1)}, bf16[8,96,640]{2,1,0:T(8,128)(2,1)}, u32[]{:S(2)}) copy-start(bf16[8,96,640]{2,1,0:T(8,128)(2,1)} %get-tuple-element.148) | copy-start | bytes 2949124
  168.5 23.6 %collective-permute-start.31 = (bf16[896,640]{1,0:T(8,128)(2,1)S(1)}, bf16[896,640]{1,0:T(8,128)(2,1)S(1)}, u32[]{:S(2)}, u32[]{:S(2)}) collective-permute-start(bf16[896,640]{1,0:T(8,128)(2,1)S(1)} %bitcast.123), channel_id=1, source_target_pairs={{0,1},{1,0},{2,3},{3,2},{4,5},{5,4},{6,7},{7,6},{8,9},{9,8},{10,11... | collective-permute-start | bytes 3440648 | tf_op jit(solution)/shard_map/ppermute | solution.py:75
  169.6 22.9 %collective-permute-start.29 = (bf16[8,128,640]{2,1,0:T(8,128)(2,1)S(1)}, bf16[8,128,640]{2,1,0:T(8,128)(2,1)S(1)}, u32[]{:S(2)}, u32[]{:S(2)}) collective-permute-start(bf16[8,128,640]{2,1,0:T(8,128)(2,1)S(1)} %copy-done.17), channel_id=1, source_target_pairs={{0,1},{1,0},{2,3},{3,2},{4,5},{5,4},{6,7},{7,6},{8,9},{9,8},{10,11... | collective-permute-start | bytes 3932168 | tf_op jit(solution)/shard_map/ppermute | solution.py:75
  170.0 30.8 %collective-permute-start.30 = (bf16[8,128,640]{2,1,0:T(8,128)(2,1)S(1)}, bf16[8,128,640]{2,1,0:T(8,128)(2,1)S(1)}, u32[]{:S(2)}, u32[]{:S(2)}) collective-permute-start(bf16[8,128,640]{2,1,0:T(8,128)(2,1)S(1)} %copy-done.7), channel_id=1, source_target_pairs={{0,8},{8,0},{16,24},{24,16},{1,9},{9,1},{17,25},{25,17},{2,10},{10... | collective-permute-start | bytes 3932168 | tf_op jit(solution)/shard_map/ppermute | solution.py:70
  192.1 8.7 %copy-start.5 = (bf16[8,128,640]{2,1,0:T(8,128)(2,1)S(1)}, bf16[8,128,640]{2,1,0:T(8,128)(2,1)}, u32[]{:S(2)}) copy-start(bf16[8,128,640]{2,1,0:T(8,128)(2,1)} %get-tuple-element.156) | copy-start | bytes 3932164
  201.4 18.5 %copy-start.16 = (f32[128,640]{1,0:T(8,128)S(1)}, f32[128,640]{1,0:T(8,128)}, u32[]{:S(2)}) copy-start(f32[128,640]{1,0:T(8,128)} %get-tuple-element.183) | copy-start | bytes 983044
  201.4 18.6 %collective-permute-start.33 = (bf16[4,96,640]{2,1,0:T(8,128)(2,1)S(1)}, bf16[4,96,640]{2,1,0:T(8,128)(2,1)S(1)}, u32[]{:S(2)}, u32[]{:S(2)}) collective-permute-start(bf16[4,96,640]{2,1,0:T(8,128)(2,1)S(1)} %slice.248), channel_id=1, source_target_pairs={{0,8},{8,0},{16,24},{24,16},{1,9},{9,1},{17,25},{25,17},{2,10},{10... | collective-permute-start | bytes 1474568 | tf_op jit(solution)/shard_map/ppermute | solution.py:70
  203.1 7.9 %collective-permute-start.35 = (bf16[128,640]{1,0:T(8,128)(2,1)S(1)}, bf16[128,640]{1,0:T(8,128)(2,1)S(1)}, u32[]{:S(2)}, u32[]{:S(2)}) collective-permute-start(bf16[128,640]{1,0:T(8,128)(2,1)S(1)} %get-tuple-element.199), channel_id=1, source_target_pairs={{0,2},{1,3},{2,0},{3,1},{4,6},{5,7},{6,4},{7,5},{8,10},{9,11},{10,... | collective-permute-start | bytes 491528 | tf_op jit(solution)/shard_map/ppermute | solution.py:75
  203.1 11.0 %collective-permute-start.37 = (bf16[128,640]{1,0:T(8,128)(2,1)S(1)}, bf16[128,640]{1,0:T(8,128)(2,1)S(1)}, u32[]{:S(2)}, u32[]{:S(2)}) collective-permute-start(bf16[128,640]{1,0:T(8,128)(2,1)S(1)} %get-tuple-element.200), channel_id=1, source_target_pairs={{0,6},{1,7},{2,4},{3,5},{4,2},{5,3},{6,0},{7,1},{8,14},{9,15},{10,... | collective-permute-start | bytes 491528 | tf_op jit(solution)/shard_map/ppermute | solution.py:75
  205.5 14.4 %collective-permute-start.36 = (bf16[128,640]{1,0:T(8,128)(2,1)S(1)}, bf16[128,640]{1,0:T(8,128)(2,1)S(1)}, u32[]{:S(2)}, u32[]{:S(2)}) collective-permute-start(bf16[128,640]{1,0:T(8,128)(2,1)S(1)} %get-tuple-element.201), channel_id=1, source_target_pairs={{0,4},{1,5},{2,6},{3,7},{4,0},{5,1},{6,2},{7,3},{8,12},{9,13},{10,... | collective-permute-start | bytes 491528 | tf_op jit(solution)/shard_map/ppermute | solution.py:75
  206.7 14.9 %collective-permute-start.34 = (bf16[4,128,640]{2,1,0:T(8,128)(2,1)S(1)}, bf16[4,128,640]{2,1,0:T(8,128)(2,1)S(1)}, u32[]{:S(2)}, u32[]{:S(2)}) collective-permute-start(bf16[4,128,640]{2,1,0:T(8,128)(2,1)S(1)} %slice.250), channel_id=1, source_target_pairs={{0,16},{8,24},{16,0},{24,8},{1,17},{9,25},{17,1},{25,9},{2,18},{10... | collective-permute-start | bytes 1966088 | tf_op jit(solution)/shard_map/ppermute | solution.py:70
  222.0 26.7 %collective-permute-start.40 = (bf16[4,56,640]{2,1,0:T(8,128)(2,1)S(1)}, bf16[4,56,640]{2,1,0:T(8,128)(2,1)S(1)}, u32[]{:S(2)}, u32[]{:S(2)}) collective-permute-start(bf16[4,56,640]{2,1,0:T(8,128)(2,1)S(1)} %bitcast.130), channel_id=1, source_target_pairs={{0,24},{8,16},{16,8},{24,0},{1,25},{9,17},{17,9},{25,1},{2,26},{10... | collective-permute-start | bytes 860168 | tf_op jit(solution)/shard_map/ppermute | solution.py:70
  222.6 8.7 %collective-permute-start.44 = (bf16[96,640]{1,0:T(8,128)(2,1)S(1)}, bf16[96,640]{1,0:T(8,128)(2,1)S(1)}, u32[]{:S(2)}, u32[]{:S(2)}) collective-permute-start(bf16[96,640]{1,0:T(8,128)(2,1)S(1)} %get-tuple-element.202), channel_id=1, source_target_pairs={{0,2},{1,3},{2,0},{3,1},{4,6},{5,7},{6,4},{7,5},{8,10},{9,11},{10,... | collective-permute-start | bytes 368648 | tf_op jit(solution)/shard_map/ppermute | solution.py:75
  223.9 8.8 %collective-permute-start.46 = (bf16[96,640]{1,0:T(8,128)(2,1)S(1)}, bf16[96,640]{1,0:T(8,128)(2,1)S(1)}, u32[]{:S(2)}, u32[]{:S(2)}) collective-permute-start(bf16[96,640]{1,0:T(8,128)(2,1)S(1)} %get-tuple-element.203), channel_id=1, source_target_pairs={{0,6},{1,7},{2,4},{3,5},{4,2},{5,3},{6,0},{7,1},{8,14},{9,15},{10,... | collective-permute-start | bytes 368648 | tf_op jit(solution)/shard_map/ppermute | solution.py:75
  226.3 9.2 %collective-permute-start.45 = (bf16[96,640]{1,0:T(8,128)(2,1)S(1)}, bf16[96,640]{1,0:T(8,128)(2,1)S(1)}, u32[]{:S(2)}, u32[]{:S(2)}) collective-permute-start(bf16[96,640]{1,0:T(8,128)(2,1)S(1)} %get-tuple-element.204), channel_id=1, source_target_pairs={{0,4},{1,5},{2,6},{3,7},{4,0},{5,1},{6,2},{7,3},{8,12},{9,13},{10,... | collective-permute-start | bytes 368648 | tf_op jit(solution)/shard_map/ppermute | solution.py:75
  226.3 15.2 %collective-permute-start.47 = (bf16[128,640]{1,0:T(8,128)(2,1)S(1)}, bf16[128,640]{1,0:T(8,128)(2,1)S(1)}, u32[]{:S(2)}, u32[]{:S(2)}) collective-permute-start(bf16[128,640]{1,0:T(8,128)(2,1)S(1)} %get-tuple-element.196), channel_id=1, source_target_pairs={{0,2},{1,3},{2,0},{3,1},{4,6},{5,7},{6,4},{7,5},{8,10},{9,11},{10,... | collective-permute-start | bytes 491528 | tf_op jit(solution)/shard_map/ppermute | solution.py:75
  231.3 17.5 %collective-permute-start.38 = (bf16[4,56,640]{2,1,0:T(8,128)(2,1)S(1)}, bf16[4,56,640]{2,1,0:T(8,128)(2,1)S(1)}, u32[]{:S(2)}, u32[]{:S(2)}) collective-permute-start(bf16[4,56,640]{2,1,0:T(8,128)(2,1)S(1)} %bitcast.129), channel_id=1, source_target_pairs={{0,8},{8,0},{16,24},{24,16},{1,9},{9,1},{17,25},{25,17},{2,10},{10... | collective-permute-start | bytes 860168 | tf_op jit(solution)/shard_map/ppermute | solution.py:70
  232.7 16.1 %collective-permute-start.39 = (bf16[4,56,640]{2,1,0:T(8,128)(2,1)S(1)}, bf16[4,56,640]{2,1,0:T(8,128)(2,1)S(1)}, u32[]{:S(2)}, u32[]{:S(2)}) collective-permute-start(bf16[4,56,640]{2,1,0:T(8,128)(2,1)S(1)} %bitcast.128), channel_id=1, source_target_pairs={{0,16},{8,24},{16,0},{24,8},{1,17},{9,25},{17,1},{25,9},{2,18},{10... | collective-permute-start | bytes 860168 | tf_op jit(solution)/shard_map/ppermute | solution.py:70
  235.5 9.5 %collective-permute-start.49 = (bf16[128,640]{1,0:T(8,128)(2,1)S(1)}, bf16[128,640]{1,0:T(8,128)(2,1)S(1)}, u32[]{:S(2)}, u32[]{:S(2)}) collective-permute-start(bf16[128,640]{1,0:T(8,128)(2,1)S(1)} %get-tuple-element.197), channel_id=1, source_target_pairs={{0,6},{1,7},{2,4},{3,5},{4,2},{5,3},{6,0},{7,1},{8,14},{9,15},{10,... | collective-permute-start | bytes 491528 | tf_op jit(solution)/shard_map/ppermute | solution.py:75
  241.6 7.1 %collective-permute-start.48 = (bf16[128,640]{1,0:T(8,128)(2,1)S(1)}, bf16[128,640]{1,0:T(8,128)(2,1)S(1)}, u32[]{:S(2)}, u32[]{:S(2)}) collective-permute-start(bf16[128,640]{1,0:T(8,128)(2,1)S(1)} %get-tuple-element.198), channel_id=1, source_target_pairs={{0,4},{1,5},{2,6},{3,7},{4,0},{5,1},{6,2},{7,3},{8,12},{9,13},{10,... | collective-permute-start | bytes 491528 | tf_op jit(solution)/shard_map/ppermute | solution.py:75
  249.0 4.9 %collective-permute-start.41 = (bf16[56,640]{1,0:T(8,128)(2,1)S(1)}, bf16[56,640]{1,0:T(8,128)(2,1)S(1)}, u32[]{:S(2)}, u32[]{:S(2)}) collective-permute-start(bf16[56,640]{1,0:T(8,128)(2,1)S(1)} %get-tuple-element.207), channel_id=1, source_target_pairs={{0,2},{1,3},{2,0},{3,1},{4,6},{5,7},{6,4},{7,5},{8,10},{9,11},{10,... | collective-permute-start | bytes 215048 | tf_op jit(solution)/shard_map/ppermute | solution.py:75
  249.1 6.3 %collective-permute-start.43 = (bf16[56,640]{1,0:T(8,128)(2,1)S(1)}, bf16[56,640]{1,0:T(8,128)(2,1)S(1)}, u32[]{:S(2)}, u32[]{:S(2)}) collective-permute-start(bf16[56,640]{1,0:T(8,128)(2,1)S(1)} %get-tuple-element.208), channel_id=1, source_target_pairs={{0,6},{1,7},{2,4},{3,5},{4,2},{5,3},{6,0},{7,1},{8,14},{9,15},{10,... | collective-permute-start | bytes 215048 | tf_op jit(solution)/shard_map/ppermute | solution.py:75
  251.8 6.0 %collective-permute-start.42 = (bf16[56,640]{1,0:T(8,128)(2,1)S(1)}, bf16[56,640]{1,0:T(8,128)(2,1)S(1)}, u32[]{:S(2)}, u32[]{:S(2)}) collective-permute-start(bf16[56,640]{1,0:T(8,128)(2,1)S(1)} %get-tuple-element.209), channel_id=1, source_target_pairs={{0,4},{1,5},{2,6},{3,7},{4,0},{5,1},{6,2},{7,3},{8,12},{9,13},{10,... | collective-permute-start | bytes 215048 | tf_op jit(solution)/shard_map/ppermute | solution.py:75
  (10 other events, 16.8 us)
where the time goes:
time: 260 us
  waiting for transfers between devices  113 us (43%)
  starting transfers between devices  61.7 us (24%)
  Pallas kernels  34.5 us (13%)
  other arithmetic  29.1 us (11%)
  matrix products  10.3 us (4%)
  local copies, waits for them, and re-layouts  9.5 us (4%)
    ppermute x36, waiting for transfers between devices, swap_ctx(): lax.ppermute(block, 'ctx', [(place, place ^ bits) for place in range(coun...  56.8 us
    ppermute x14, waiting for transfers between devices, swap_dp(): lax.ppermute(block, 'dp', [(place, place ^ bits) for place in range(count)])  56.4 us
    ppermute x36, starting transfers between devices, swap_ctx(): lax.ppermute(block, 'ctx', [(place, place ^ bits) for place in range(coun...  45.2 us
    pallas_call x3, Pallas kernels, call_kernel(): pl.pallas_call(body, out_shape=[jax.ShapeDtypeStruct(shape, dtype) for sh...  34.5 us
    ppermute x14, starting transfers between devices, swap_dp(): lax.ppermute(block, 'dp', [(place, place ^ bits) for place in range(count)])  16.5 us
    dot_general x4, matrix products, reorder(): return jnp.dot(order, blocks, preferred_element_type=jnp.float32).astype(BF)  5.96 us
  transfers between devices with their start and end apart: 50, of which 27 were waited for; matrix products, arithmetic and copies ran while one was open for 11% of the time, Pallas kernels for 7%

commit v1 on v0

--- a/solution.py
+++ b/solution.py
@@ -213,29 +213,44 @@
 
 
 def attend_kernel(
-    unit_ref, near_ref, far_ref, wq_ref, wk_ref, wv_ref, sin_scale_ref, sq_ref, sk_ref,
-    cos_ref, sine_ref, cos_all_ref, sine_all_ref, key_index_ref, row_index_ref,
-    normed_ref, normed_all_ref, qraw_ref, kraw_ref, q_ref, k_ref, v_ref, attn_ref, lse_ref,
+    unit_ref, near_ref, far_ref, own_ref, other_ref, order_q_ref, order_kv_ref, sin_scale_ref, sq_ref,
+    sk_ref, cos_all_ref, sine_all_ref, key_index_ref, row_index_ref,
+    wq_ref, wkv_ref, normed_ref, normed_all_ref, qraw_ref, kraw_ref, q_ref, k_ref, v_ref, attn_ref, lse_ref,
+    held_q, held_kv,
 ):
+    places, _, width = own_ref.shape
+    rows_q = held_q.shape[0] // (2 * places)
+    rows_kv = held_kv.shape[0] // (2 * places)
+    for core, ref in enumerate((own_ref, other_ref)):
+        held_q[core * places * rows_q : (core + 1) * places * rows_q, :] = ref[:, :rows_q, :].reshape(
+            places * rows_q, width
+        )
+        held_kv[core * places * rows_kv : (core + 1) * places * rows_kv, :] = ref[
+            :, rows_q : rows_q + rows_kv, :
+        ].reshape(places * rows_kv, width)
+    wq_ref[...] = dot_nn(order_q_ref[...], held_q[...]).astype(BF)
+    wkv_ref[...] = dot_nn(order_kv_ref[...], held_kv[...]).astype(BF)
+    tokens = unit_ref.shape[0]
     scale_in = 1.0 + sin_scale_ref[...]
     normed_ref[...] = (unit_ref[...] * scale_in).astype(BF)
     half = near_ref.shape[0]
     normed_all_ref[:half] = (near_ref[...].astype(jnp.float32) * scale_in).astype(BF)
     normed_all_ref[half:] = (far_ref[...].astype(jnp.float32) * scale_in).astype(BF)
-    head_width = wk_ref.shape[0]
+    head_width = sq_ref.shape[1]
     heads = wq_ref.shape[0] // head_width
-    key_raw = dot_nt(normed_all_ref[...], wk_ref[...])
+    key_raw = dot_nt(normed_all_ref[...], wkv_ref[:head_width, :])
     kraw_ref[...] = key_raw
-    v_ref[...] = dot_nt(normed_all_ref[...], wv_ref[...]).astype(BF)
+    v_ref[...] = dot_nt(normed_all_ref[...], wkv_ref[head_width:, :]).astype(BF)
     key_unit, _ = unit_of(key_raw)
     k_ref[...] = turn(key_unit * (1.0 + sk_ref[...]), cos_all_ref[...], sine_all_ref[...]).astype(BF)
     allowed = key_index_ref[...] <= row_index_ref[...]
+    cosine, sine = cos_all_ref[:tokens, :], sine_all_ref[:tokens, :]
     for head in range(heads):
         span = slice(head * head_width, (head + 1) * head_width)
         raw = dot_nt(normed_ref[...], wq_ref[span, :])
         qraw_ref[:, span] = raw
         unit, _ = unit_of(raw)
-        turned = turn(unit * (1.0 + sq_ref[...]), cos_ref[...], sine_ref[...])
+        turned = turn(unit * (1.0 + sq_ref[...]), cosine, sine)
         query = (turned * head_width ** (-0.5)).astype(BF)
         q_ref[:, span] = query
         scores = jnp.where(allowed, dot_nt(query, k_ref[...]), -1e30)
@@ -246,16 +261,133 @@
         attn_ref[:, span] = dot_nn(probs, v_ref[...]).astype(BF)
 
 
+def project_kernel(
+    attn_ref, order_ref, own_ref, other_ref, resid_ref, sattn_ref, spre_ref,
+    held_ref, ahead_ref, projected_ref, middle_ref, pre_ref,
+):
+    places, rows, width = own_ref.shape
+    held_ref[: places * rows, :] = own_ref[...].reshape(places * rows, width)
+    held_ref[places * rows :, :] = other_ref[...].reshape(places * rows, width)
+    ahead_ref[...] = dot_nn(attn_ref[...], order_ref[...]).astype(BF)
+    projected = dot_nn(ahead_ref[...], held_ref[...])
+    projected_ref[...] = projected
+    unit, _ = unit_of(projected)
+    middle = resid_ref[...] + unit * (1.0 + sattn_ref[...])
+    middle_ref[...] = middle
+    unit, _ = unit_of(middle)
+    pre_ref[...] = (unit * (1.0 + spre_ref[...])).astype(BF)
+
+
+GELU_A = (2.0 / 3.141592653589793) ** 0.5
+
+
+def feed_kernel(*refs):
+    pres, weights = refs[:4], refs[4:12]
+    part_refs = refs[12:16]
+    gate_ref, up_ref, inner_ref, pre_ref, wg_ref, wu_ref, wd_ref = refs[16:]
+    tokens = pres[0].shape[0]
+    rows = weights[0].shape[0] // 3
+    for number, ref in enumerate(pres):
+        pre_ref[number * tokens : (number + 1) * tokens, :] = ref[...]
+    for number, ref in enumerate(weights):
+        span = slice(number * rows, (number + 1) * rows)
+        wg_ref[span, :] = ref[:rows, :]
+        wu_ref[span, :] = ref[rows : 2 * rows, :]
+        wd_ref[span, :] = ref[2 * rows :, :]
+    for number in range(4):
+        at = slice(number * tokens, (number + 1) * tokens)
+        gate = dot_nt(pre_ref[at, :], wg_ref[...])
+        up = dot_nt(pre_ref[at, :], wu_ref[...])
+        gate_ref[at, :] = gate
+        up_ref[at, :] = up
+        bent = jnp.tanh(GELU_A * (gate + 0.044715 * (gate * gate * gate)))
+        inner = (0.5 * gate * (1.0 + bent) * up).astype(BF)
+        inner_ref[at, :] = inner
+        part_refs[number][...] = dot_nn(inner, wd_ref[...]).astype(part_refs[number].dtype)
+
+
+def turning_kernel(
+    own_ref, come1_ref, come2_ref, come3_ref, middle_ref, gout_ref, spost_ref,
+    block_out_ref, gffn_ref, gspost_ref,
+):
+    ffn = own_ref[...]
+    for ref in (come1_ref, come2_ref, come3_ref):
+        ffn = ffn + ref[...].astype(jnp.float32)
+    unit, inverse = unit_of(ffn)
+    grad_out = gout_ref[...]
+    block_out_ref[...] = middle_ref[...] + unit * (1.0 + spost_ref[...])
+    gspost_ref[...] = jnp.sum(grad_out * unit, axis=0, keepdims=True)
+    gffn_ref[...] = rms_back(unit, inverse, grad_out * (1.0 + spost_ref[...])).astype(BF)
+
+
+def feed_back_kernel(*refs):
+    grads = refs[:4]
+    gate_ref, up_ref, inner_ref, pre_ref, wg_ref, wu_ref, wd_ref = refs[4:11]
+    part_refs = refs[11:15]
+    own_ref, other_ref = refs[15:17]
+    gffn_scr, ggate_scr, gup_scr = refs[17:]
+    tokens = grads[0].shape[0]
+    for number, ref in enumerate(grads):
+        at = slice(number * tokens, (number + 1) * tokens)
+        gffn_scr[at, :] = ref[...]
+        grad_inner = dot_nt(ref[...], wd_ref[...])
+        gate = gate_ref[at, :]
+        square = gate * gate
+        bent = jnp.tanh(GELU_A * (gate + 0.044715 * (square * gate)))
+        curve = 0.5 * gate * (1.0 + bent)
+        slope = 0.5 * (1.0 + bent) + 0.5 * gate * (1.0 - bent * bent) * (
+            GELU_A * (1.0 + 3.0 * 0.044715 * square)
+        )
+        grad_up = (grad_inner * curve).astype(BF)
+        grad_gate = (grad_inner * up_ref[at, :] * slope).astype(BF)
+        ggate_scr[at, :] = grad_gate
+        gup_scr[at, :] = grad_up
+        part_refs[number][...] = (dot_nn(grad_gate, wg_ref[...]) + dot_nn(grad_up, wu_ref[...])).astype(
+            part_refs[number].dtype
+        )
+    places, rows, width = own_ref.shape
+    rows = rows // 3
+    shape = (places, rows, width)
+    for core, ref in enumerate((own_ref, other_ref)):
+        span = slice(core * places * rows, (core + 1) * places * rows)
+        ref[:, :rows, :] = dot_tn(ggate_scr[:, span], pre_ref[...]).astype(BF).reshape(shape)
+        ref[:, rows : 2 * rows, :] = dot_tn(gup_scr[:, span], pre_ref[...]).astype(BF).reshape(shape)
+        ref[:, 2 * rows :, :] = dot_tn(inner_ref[:, span], gffn_scr[...]).astype(BF).reshape(shape)
+
+
+def project_back_kernel(
+    own_ref, come1_ref, come2_ref, come3_ref, gout_ref, projected_ref, middle_ref, held_ref, ahead_ref,
+    order_ref, sattn_ref, spre_ref,
+    gresid_ref, gattn_ref, gown_ref, gother_ref, gsattn_ref, gspre_ref,
+):
+    grad_pre = own_ref[...]
+    for ref in (come1_ref, come2_ref, come3_ref):
+        grad_pre = grad_pre + ref[...].astype(jnp.float32)
+    unit_p, inverse_p = unit_of(middle_ref[...])
+    unit_a, inverse_a = unit_of(projected_ref[...])
+    gspre_ref[...] = jnp.sum(grad_pre * unit_p, axis=0, keepdims=True)
+    grad_middle = gout_ref[...] + rms_back(unit_p, inverse_p, grad_pre * (1.0 + spre_ref[...]))
+    gresid_ref[...] = grad_middle
+    gsattn_ref[...] = jnp.sum(grad_middle * unit_a, axis=0, keepdims=True)
+    grad_proj = rms_back(unit_a, inverse_a, grad_middle * (1.0 + sattn_ref[...])).astype(BF)
+    grad_held = dot_nt(grad_proj, held_ref[...]).astype(BF)
+    gattn_ref[...] = dot_nt(grad_held, order_ref[...]).astype(BF)
+    half = held_ref.shape[0] // 2
+    gown_ref[...] = dot_tn(ahead_ref[:, :half], grad_proj).astype(BF).reshape(gown_ref.shape)
+    gother_ref[...] = dot_tn(ahead_ref[:, half:], grad_proj).astype(BF).reshape(gother_ref.shape)
+
+
 def attend_back_kernel(
-    grad_attn_ref, attn_ref, q_ref, k_ref, v_ref, lse_ref, qraw_ref, kraw_ref, wq_ref, wk_ref, wv_ref,
-    sq_ref, sk_ref, cos_ref, sine_ref, cos_all_ref, sine_all_ref, key_index_ref, row_index_ref,
-    normed_ref, normed_all_ref, unit_ref, near_ref, far_ref,
-    gwq_ref, gwk_ref, gwv_ref, gnear_ref, gfar_ref, gq_ref, gsin_ref, gsq_ref, gsk_ref,
-    probs_scr, gscores_scr, grows_scr, qrows_scr, gqraw_scr,
+    grad_attn_ref, attn_ref, q_ref, k_ref, v_ref, lse_ref, qraw_ref, kraw_ref, wq_ref, wkv_ref,
+    sq_ref, sk_ref, cos_all_ref, sine_all_ref, key_index_ref, row_index_ref,
+    normed_ref, normed_all_ref, unit_ref, near_ref, far_ref, order_q_ref, order_kv_ref,
+    own_ref, other_ref, gnear_ref, gfar_ref, gq_ref, gsin_ref, gsq_ref, gsk_ref,
+    probs_scr, gscores_scr, grows_scr, qrows_scr, gqraw_scr, gkv_scr,
 ):
-    head_width = wk_ref.shape[0]
+    head_width = sq_ref.shape[1]
     heads = wq_ref.shape[0] // head_width
     tokens = q_ref.shape[0]
+    cosine, sine = cos_all_ref[:tokens, :], sine_all_ref[:tokens, :]
     allowed = key_index_ref[...] <= row_index_ref[...]
     grad_sq = jnp.zeros((1, head_width), jnp.float32)
     for head in range(heads):
@@ -276,7 +408,7 @@
         grows_scr[rows, :] = grad_rows
         qrows_scr[rows, :] = query
         grad_query = dot_nn(grad_scores, k_ref[...]) * head_width ** (-0.5)
-        grad_query = turn_back(grad_query, cos_ref[...], sine_ref[...])
+        grad_query = turn_back(grad_query, cosine, sine)
         unit, inverse = unit_of(qraw_ref[:, span])
         grad_sq = grad_sq + jnp.sum(grad_query * unit, axis=0, keepdims=True)
         grad_raw = rms_back(unit, inverse, grad_query * (1.0 + sq_ref[...]))
@@ -289,7 +421,9 @@
     gsk_ref[...] = jnp.sum(grad_key * unit, axis=0, keepdims=True)
     grad_kraw = rms_back(unit, inverse, grad_key * (1.0 + sk_ref[...])).astype(BF)
     half = near_ref.shape[0]
-    grad_normed = dot_nn(grad_kraw, wk_ref[...]) + dot_nn(grad_value, wv_ref[...])
+    grad_normed = dot_nn(grad_kraw, wkv_ref[:head_width, :]) + dot_nn(
+        grad_value, wkv_ref[head_width:, :]
+    )
     grad_q = dot_nn(gqraw_scr[...], wq_ref[...])
     gq_ref[...] = grad_q
     gsin_ref[...] = (
@@ -299,108 +433,22 @@
     )
     gnear_ref[...] = grad_normed[:half].astype(BF)
     gfar_ref[...] = grad_normed[half:].astype(BF)
-    gwk_ref[...] = dot_tn(grad_kraw, normed_all_ref[...]).astype(BF)
-    gwv_ref[...] = dot_tn(grad_value, normed_all_ref[...]).astype(BF)
-    gwq_ref[...] = dot_tn(gqraw_scr[...], normed_ref[...]).astype(BF)
-
-
-GELU_A = (2.0 / 3.141592653589793) ** 0.5
-
-
-def mid_kernel(*refs):
-    attn_ref, order_ref, resid_ref, gout_ref, sattn_ref, spre_ref, spost_ref = refs[:7]
-    a_refs = (refs[7:9], refs[9:11])
-    b_refs = (refs[11:13], refs[13:15])
-    block_out_ref, gresid_ref, gattn_ref, gsattn_ref, gspre_ref, gspost_ref = refs[15:21]
-    ga_refs = (refs[21:23], refs[23:25])
-    gb_refs = (refs[25:27], refs[27:29])
-    held_scr, ahead_scr, gate_scr, up_scr, inner_scr = refs[29:]
-    chips = a_refs[0][0].shape[0] // 2
-    width = resid_ref.shape[1]
-    rows_f = b_refs[0][0].shape[1] // 2
-    rows_o = a_refs[0][0].shape[1] - rows_f
-    chunk = chips * rows_f
-
-    def place_a(dp):
-        return dp // 2, slice((dp % 2) * chips, (dp % 2 + 1) * chips)
-
-    def place_b(dp):
-        return dp % 2, slice((dp // 2) * chips, (dp // 2 + 1) * chips)
-
-    def weights(core, dp):
-        piece_a, at_a = place_a(dp)
-        piece_b, at_b = place_b(dp)
-        gate = a_refs[core][piece_a][at_a, :rows_f, :].reshape(chunk, width)
-        up = b_refs[core][piece_b][at_b, :rows_f, :].reshape(chunk, width)
-        down = b_refs[core][piece_b][at_b, rows_f:, :].reshape(chunk, width)
-        return gate, up, down
-
-    parts = [(core, dp) for core in range(2) for dp in range(4)]
-    out_chunk = chips * rows_o
-    for number, (core, dp) in enumerate(parts):
-        piece, at = place_a(dp)
-        held_scr[number * out_chunk : (number + 1) * out_chunk, :] = a_refs[core][piece][
-            at, rows_f:, :
-        ].reshape(out_chunk, width)
-    ahead_scr[...] = dot_nn(attn_ref[...], order_ref[...]).astype(BF)
-    projected = dot_nn(ahead_scr[...], held_scr[...])
-    unit_a, inverse_a = unit_of(projected)
-    middle = resid_ref[...] + unit_a * (1.0 + sattn_ref[...])
-    unit_p, inverse_p = unit_of(middle)
-    pre = (unit_p * (1.0 + spre_ref[...])).astype(BF)
-    ffn = jnp.zeros(middle.shape, jnp.float32)
-    for number, (core, dp) in enumerate(parts):
-        span = slice(number * chunk, (number + 1) * chunk)
-        w_gate, w_up, w_down = weights(core, dp)
-        gate = dot_nt(pre, w_gate)
-        up = dot_nt(pre, w_up)
-        gate_scr[:, span] = gate
-        up_scr[:, span] = up
-        bent = jnp.tanh(GELU_A * (gate + 0.044715 * (gate * gate * gate)))
-        inner = (0.5 * gate * (1.0 + bent) * up).astype(BF)
-        inner_scr[:, span] = inner
-        ffn = ffn + dot_nn(inner, w_down)
-    unit_f, inverse_f = unit_of(ffn)
-    block_out_ref[...] = middle + unit_f * (1.0 + spost_ref[...])
-    grad_out = gout_ref[...]
-    gspost_ref[...] = jnp.sum(grad_out * unit_f, axis=0, keepdims=True)
-    grad_ffn = rms_back(unit_f, inverse_f, grad_out * (1.0 + spost_ref[...])).astype(BF)
-    grad_pre = jnp.zeros(middle.shape, jnp.float32)
-    for number, (core, dp) in enumerate(parts):
-        span = slice(number * chunk, (number + 1) * chunk)
-        w_gate, w_up, w_down = weights(core, dp)
-        grad_inner = dot_nt(grad_ffn, w_down)
-        gate = gate_scr[:, span]
-        square = gate * gate
-        bent = jnp.tanh(GELU_A * (gate + 0.044715 * (square * gate)))
-        curve = 0.5 * gate * (1.0 + bent)
-        slope = 0.5 * (1.0 + bent) + 0.5 * gate * (1.0 - bent * bent) * (
-            GELU_A * (1.0 + 3.0 * 0.044715 * square)
+    gkv_scr[:head_width, :] = dot_tn(grad_kraw, normed_all_ref[...]).astype(BF)
+    gkv_scr[head_width:, :] = dot_tn(grad_value, normed_all_ref[...]).astype(BF)
+    grad_wq = dot_tn(gqraw_scr[...], normed_ref[...]).astype(BF)
+    held_q = dot_tn(order_q_ref[...], grad_wq).astype(BF)
+    held_kv = dot_tn(order_kv_ref[...], gkv_scr[...]).astype(BF)
+    places, _, width = own_ref.shape
+    rows_q = held_q.shape[0] // (2 * places)
+    rows_kv = held_kv.shape[0] // (2 * places)
+    for core, ref in enumerate((own_ref, other_ref)):
+        ref[:, :rows_q, :] = held_q[core * places * rows_q : (core + 1) * places * rows_q].reshape(
+            places, rows_q, width
         )
-        grad_up = (grad_inner * curve).astype(BF)
-        grad_gate = (grad_inner * up_scr[:, span] * slope).astype(BF)
-        grad_pre = grad_pre + dot_nn(grad_gate, w_gate) + dot_nn(grad_up, w_up)
-        piece_a, at_a = place_a(dp)
-        piece_b, at_b = place_b(dp)
-        shape = (chips, rows_f, width)
-        ga_refs[core][piece_a][at_a, :rows_f, :] = dot_tn(grad_gate, pre).astype(BF).reshape(shape)
-        gb_refs[core][piece_b][at_b, :rows_f, :] = dot_tn(grad_up, pre).astype(BF).reshape(shape)
-        gb_refs[core][piece_b][at_b, rows_f:, :] = (
-            dot_tn(inner_scr[:, span], grad_ffn).astype(BF).reshape(shape)
-        )
-    gspre_ref[...] = jnp.sum(grad_pre * unit_p, axis=0, keepdims=True)
-    grad_middle = grad_out + rms_back(unit_p, inverse_p, grad_pre * (1.0 + spre_ref[...]))
-    gresid_ref[...] = grad_middle
-    gsattn_ref[...] = jnp.sum(grad_middle * unit_a, axis=0, keepdims=True)
-    grad_proj = rms_back(unit_a, inverse_a, grad_middle * (1.0 + sattn_ref[...])).astype(BF)
-    grad_held = dot_nt(grad_proj, held_scr[...]).astype(BF)
-    gattn_ref[...] = dot_nt(grad_held, order_ref[...]).astype(BF)
-    for number, (core, dp) in enumerate(parts):
-        piece, at = place_a(dp)
-        span = slice(number * out_chunk, (number + 1) * out_chunk)
-        ga_refs[core][piece][at, rows_f:, :] = (
-            dot_tn(ahead_scr[:, span], grad_proj).astype(BF).reshape(chips, rows_o, width)
-        )
+        ref[:, rows_q : rows_q + rows_kv, :] = held_kv[
+            core * places * rows_kv : (core + 1) * places * rows_kv
+        ].reshape(places, rows_kv, width)
+        ref[:, rows_q + rows_kv :, :] = jnp.zeros((places, 16, width), BF)
 
 
 def shards_plain(
@@ -661,10 +709,15 @@
 
 def shards(*args):
     hidden_in, w_query, w_gate = args[0], args[2], args[6]
-    fits = hidden_in.shape[1] * lax.axis_size("ctx") <= 2048 and lax.axis_size("dp") == 4
-    if fits and w_query.shape[0] % 16 == 0 and w_gate.shape[0] % 16 == 0:
+    fits = hidden_in.shape[1] * lax.axis_size("ctx") <= 2048 and lax.axis_size("ctx") == 8
+    fits = fits and lax.axis_size("dp") == 4
+    if fits and w_query.shape[0] % 16 == 0 and w_gate.shape[0] % 16 == 0 and args[3].shape[0] == 8:
         return shards_kernels(*args)
     return shards_plain(*args)
+
+
+def swaps(block, swap):
+    return [swap(block, bits) for bits in range(1, 4)]
 
 
 def shards_kernels(
@@ -695,7 +748,9 @@
     head_width = w_key.shape[0] * owners
     heads = w_query.shape[0] * owners // head_width
     rows_q, rows_k, rows_f = w_query.shape[0], w_key.shape[0], w_gate.shape[0]
+    last = rows_q + 2 * rows_k
     scale_part = norm_scales.shape[0]
+    f32 = jnp.float32
     tie = lax.optimization_barrier
 
     far_core, far_dp, far_z = (
@@ -705,8 +760,14 @@
     )
     owner_of = (row ^ far_dp) * groups + (place ^ (2 * far_z + far_core))
     order_q = row_order(owner_of, rows_q)
-    order_k = row_order(owner_of, rows_k)
     order_s = row_order(owner_of, 1)
+    held_row = jnp.arange(2 * rows_k * owners, dtype=jnp.int32)
+    held_at = (
+        (held_row % (2 * rows_k)) // rows_k * head_width
+        + jnp.repeat(owner_of, 2 * rows_k) * rows_k
+        + held_row % rows_k
+    )
+    order_kv = (held_row[:, None] == held_at[None, :]).astype(BF)
     seq_core, seq_zed = (
         jnp.arange(groups, dtype=jnp.int32) // chips,
         jnp.arange(groups, dtype=jnp.int32) % chips,
@@ -714,112 +775,154 @@
     key_index = natural_rows(place ^ (2 * seq_zed + seq_core), block, groups).reshape(1, seq_len)
     row_index = natural_rows(place[None], block, groups).reshape(tokens, 1)
 
-    last_rows = jnp.zeros((8, width), BF).at[0, :scale_part].set(norm_scales)
+    last_rows = jnp.zeros((16, width), BF).at[0, :scale_part].set(norm_scales)
     last_rows = last_rows.at[1, :tokens].set((posit // 64).astype(BF))
     last_rows = last_rows.at[2, :tokens].set((posit % 64).astype(BF))
-    first = gather_over(
-        jnp.concatenate([w_query, w_key, w_value, last_rows], axis=0)[None], swap_z, chips
-    )
-    group_a = jnp.concatenate([w_gate, w_output], axis=0)[None]
-    group_b = jnp.concatenate([w_up, w_down], axis=0)[None]
+    first = jnp.concatenate([w_query, w_key, w_value, last_rows], axis=0)
+    feed = jnp.concatenate([w_gate, w_up, w_down], axis=0)
     inverse_in = lax.rsqrt(jnp.mean(resid * resid, axis=-1, keepdims=True) + EPS)
     unit_in = resid * inverse_in
-    first, group_a, group_b, unit_bf = tie((first, group_a, group_b, unit_in.astype(BF)[None]))
-    first = gather_over(first[None], swap_dp, count_dp)
-    group_a = gather_over(group_a, swap_z, chips)
-    group_b = gather_over(group_b, swap_z, chips)
-    first, group_a, group_b, unit_bf = tie((first, group_a, group_b, unit_bf))
-    first = first.reshape((owners // 2,) + first.shape[2:])
-    a_one = double(group_a, swap_dp, 1)
-    b_one = double(group_b, swap_dp, 2)
-    near = gather_over(unit_bf, swap_z, chips).reshape(chips * tokens, width)
-    first = jnp.concatenate([first, swap_ctx(first, 1)], axis=0)
-    full_query = reorder(order_q, first[:, :rows_q].reshape(-1, width))
-    full_key = reorder(order_k, first[:, rows_q : rows_q + rows_k].reshape(-1, width))
-    full_value = reorder(order_k, first[:, rows_q + rows_k : rows_q + 2 * rows_k].reshape(-1, width))
-    last = rows_q + 2 * rows_k
-    full_scales = reorder(order_s, first[:, last, :scale_part]).reshape(-1)
-    same_seq = first.reshape((2, count_dp, chips) + first.shape[1:])[:, 0, :, last:, :tokens]
-    pos_all = same_seq[:, :, 1].astype(jnp.float32) * 64.0 + same_seq[:, :, 2].astype(jnp.float32)
+    unit_bf = unit_in.astype(BF)
+    first = gather_over(first[None], swap_z, chips)
+    first, unit_bf, feed, w_output, order_q, order_kv = tie(
+        (first, unit_bf, feed, w_output, order_q, order_kv)
+    )
+    last_far = swap_ctx(first[:, last:], 1)
+    pos_all = jnp.stack([first[:, last:], last_far], axis=0)[:, :, :, :tokens].astype(f32)
+    pos_all = (pos_all[:, :, 1] * 64.0 + pos_all[:, :, 2]).reshape(seq_len)
     half = head_width // 2
     freq_table = 1000000.0 ** (-jnp.arange(half, dtype=jnp.float32) / half)
-    angle = pos_all.reshape(seq_len)[:, None] * freq_table[None, :]
+    angle = pos_all[:, None] * freq_table[None, :]
     cos_all, sine_all = jnp.cos(angle), jnp.sin(angle)
-    (a_one, b_one, near, full_query, full_key, full_value, full_scales, cos_all, sine_all) = tie(
-        (a_one, b_one, near, full_query, full_key, full_value, full_scales, cos_all, sine_all)
-    )
+    first = gather_over(first[None], swap_dp, count_dp).reshape((owners // 2,) + first.shape[1:])
+    near = gather_over(unit_bf[None], swap_z, chips).reshape(chips * tokens, width)
+    first, near, feed, w_output, cos_all, sine_all = tie(
+        (first, near, feed, w_output, cos_all, sine_all)
+    )
+    other = swap_ctx(first, 1)
     far = swap_ctx(near, 1)
-    a_two = swap_dp(a_one, 2)
-    b_two = swap_dp(b_one, 1)
-    a_one_far = swap_ctx(a_one, 1)
-    b_one_far = swap_ctx(b_one, 1)
+    out_own = gather_over(w_output[None], swap_z, chips)
+    scale_rows = jnp.concatenate([first[:, last, :scale_part], other[:, last, :scale_part]], axis=0)
+    full_scales = reorder(order_s, scale_rows).reshape(-1)
+    other, far, out_own, feed, full_scales = tie((other, far, out_own, feed, full_scales))
     scale_in, scale_attn, scale_pre, scale_post, scale_query, scale_key = [
         scale[None] for scale in split_scales(full_scales, width, head_width)
     ]
-    cos_own, sine_own = cos_all[:tokens], sine_all[:tokens]
-    f32 = jnp.float32
-    normed, normed_all, query_raw, key_raw, query_bf, key_bf, value_bf, attn_bf, lse = call_kernel(
-        attend_kernel,
+    feed_z2 = swap_z(feed, 2)
+    out_own = gather_over(out_own[None], swap_dp, count_dp).reshape((owners // 2, rows_q, width))
+    (w_q, w_kv, normed, normed_all, query_raw, key_raw, query_bf, key_bf, value_bf, attn_bf, lse) = (
+        call_kernel(
+            attend_kernel,
+            [
+                ((heads * head_width, width), BF),
+                ((2 * head_width, width), BF),
+                ((tokens, width), BF),
+                ((seq_len, width), BF),
+                ((tokens, heads * head_width), f32),
+                ((seq_len, head_width), f32),
+                ((tokens, heads * head_width), BF),
+                ((seq_len, head_width), BF),
+                ((seq_len, head_width), BF),
+                ((tokens, heads * head_width), BF),
+                ((tokens, heads), f32),
+            ],
+            [((heads * head_width, width), BF), ((2 * head_width, width), BF)],
+            12_000_000_000,
+            (
+                unit_in, near, far, first, other, order_q, order_kv, scale_in, scale_query, scale_key,
+                cos_all, sine_all, key_index, row_index,
+            ),
+        )
+    )
+    attn_bf, feed_z2, out_own, feed = tie((attn_bf, feed_z2, out_own, feed))
+    out_other = swap_ctx(out_own, 1)
+    feed_z1 = swap_z(feed, 1)
+    feed_z3 = swap_z(feed, 3)
+    feed_c0 = swap_ctx(feed, 1)
+    feed_c2 = swap_ctx(feed_z2, 1)
+    held_out, ahead, projected, middle, pre = call_kernel(
+        project_kernel,
         [
+            ((owners * rows_q, width), BF),
+            ((tokens, owners * rows_q), BF),
+            ((tokens, width), f32),
+            ((tokens, width), f32),
             ((tokens, width), BF),
-            ((seq_len, width), BF),
-            ((tokens, heads * head_width), f32),
-            ((seq_len, head_width), f32),
-            ((tokens, heads * head_width), BF),
-            ((seq_len, head_width), BF),
-            ((seq_len, head_width), BF),
-            ((tokens, heads * head_width), BF),
-            ((tokens, heads), f32),
         ],
         [],
-        20_000_000_000,
-        (
-            unit_in, near, far, full_query, full_key, full_value, scale_in, scale_query, scale_key,
-            cos_own, sine_own, cos_all, sine_all, key_index, row_index,
-        ),
-    )
-    a_one_far, b_one_far, a_two, b_two, attn_bf = tie((a_one_far, b_one_far, a_two, b_two, attn_bf))
-    a_two_far = swap_ctx(a_two, 1)
-    b_two_far = swap_ctx(b_two, 1)
-
-    pieces_a = (a_one, a_two, a_one_far, a_two_far)
-    pieces_b = (b_one, b_two, b_one_far, b_two_far)
-    held = owners * rows_q
-    hidden = owners * rows_f
+        2_000_000_000,
+        (attn_bf, order_q, out_own, out_other, resid, scale_attn, scale_pre),
+    )
+    pres = swaps(pre, swap_dp)
+    pre, pres, feed_z1, feed_z3, feed_c0, feed_c2 = tie((pre, pres, feed_z1, feed_z3, feed_c0, feed_c2))
+    feed_c1 = swap_ctx(feed_z1, 1)
+    feed_c3 = swap_ctx(feed_z3, 1)
+    part_shapes = [((tokens, width), f32)] + [((tokens, width), BF)] * 3
+    all_tokens = count_dp * tokens
+    hidden = groups * rows_f
     outs = call_kernel(
-        mid_kernel,
-        [((tokens, width), f32), ((tokens, width), f32), ((tokens, heads * head_width), BF)]
-        + [((1, width), f32)] * 3
-        + [(piece.shape, BF) for piece in pieces_a + pieces_b],
+        feed_kernel,
+        part_shapes
+        + [
+            ((all_tokens, hidden), f32),
+            ((all_tokens, hidden), f32),
+            ((all_tokens, hidden), BF),
+            ((all_tokens, width), BF),
+        ]
+        + [((hidden, width), BF)] * 3,
+        [],
+        3_000_000_000,
+        [pre] + pres + [feed, feed_z1, feed_z2, feed_z3, feed_c0, feed_c1, feed_c2, feed_c3],
+    )
+    parts, kept = outs[:4], outs[4:]
+    comes = [swap_dp(parts[bits], bits) for bits in range(1, 4)]
+    block_out, grad_ffn, grad_s_post = call_kernel(
+        turning_kernel,
+        [((tokens, width), f32), ((tokens, width), BF), ((1, width), f32)],
+        [],
+        100_000_000,
+        [parts[0]] + comes + [middle, grad_out[0], scale_post],
+    )
+    outs = call_kernel(
+        feed_back_kernel,
+        part_shapes + [((chips, 3 * rows_f, width), BF)] * 2,
+        [((all_tokens, width), BF), ((all_tokens, hidden), BF), ((all_tokens, hidden), BF)],
+        6_000_000_000,
+        [grad_ffn] + swaps(grad_ffn, swap_dp) + list(kept),
+    )
+    parts, (g_feed, g_feed_far) = outs[:4], outs[4:]
+    comes = [swap_dp(parts[bits], bits) for bits in range(1, 4)]
+    g_feed = add_bf16(g_feed, swap_ctx(g_feed_far, 1)).astype(BF)
+    g_feed, comes = tie((g_feed, comes))
+    feed_come1 = swap_z(g_feed[1], 1)
+    grad_resid_a, grad_attn, g_out, g_out_far, grad_s_attn, grad_s_pre = call_kernel(
+        project_back_kernel,
         [
-            ((held, width), BF),
-            ((tokens, held), BF),
-            ((tokens, hidden), f32),
-            ((tokens, hidden), f32),
-            ((tokens, hidden), BF),
+            ((tokens, width), f32),
+            ((tokens, heads * head_width), BF),
+            (out_own.shape, BF),
+            (out_own.shape, BF),
+            ((1, width), f32),
+            ((1, width), f32),
         ],
-        20_000_000_000,
-        (attn_bf, order_q, resid, grad_out[0], scale_attn, scale_pre, scale_post)
-        + pieces_a
-        + pieces_b,
-    )
-    block_out, grad_resid_a, grad_attn_bf, grad_s_attn, grad_s_pre, grad_s_post = outs[:6]
-    ga_one, ga_two, ga_one_far, ga_two_far, gb_one, gb_two, gb_one_far, gb_two_far = outs[6:]
-
-    ga_two = add_bf16(ga_two, swap_ctx(ga_two_far, 1)).astype(BF)
-    gb_two = add_bf16(gb_two, swap_ctx(gb_two_far, 1)).astype(BF)
-    ga_two, gb_two, grad_attn_bf = tie((ga_two, gb_two, grad_attn_bf))
-    ga_come = swap_dp(ga_two, 2)
-    gb_come = swap_dp(gb_two, 1)
-    ga_one = add_bf16(ga_one, swap_ctx(ga_one_far, 1))
-    gb_one = add_bf16(gb_one, swap_ctx(gb_one_far, 1))
-
-    (gwq, gwk, gwv, g_near, g_far, grad_normed_q, grad_s_in, grad_s_query, grad_s_key) = call_kernel(
+        [],
+        3_000_000_000,
+        [parts[0]]
+        + comes
+        + [grad_out[0], projected, middle, held_out, ahead, order_q, scale_attn, scale_pre],
+    )
+    grad_resid_a, grad_attn, g_out, g_out_far, grad_s_attn, grad_s_pre, feed_come1, g_feed = tie(
+        (grad_resid_a, grad_attn, g_out, g_out_far, grad_s_attn, grad_s_pre, feed_come1, g_feed)
+    )
+    g_out = add_bf16(g_out, swap_ctx(g_out_far, 1)).astype(BF).reshape(count_dp, chips, rows_q, width)
+    g_out, g_feed, grad_attn = tie((g_out, g_feed, grad_attn))
+    feed_come2 = swap_z(g_feed[2], 2)
+    out_comes = [swap_dp(g_out[bits], bits) for bits in range(1, 4)]
+    (packed, packed_far, g_near, g_far, grad_normed_q, grad_s_in, grad_s_query, grad_s_key) = call_kernel(
         attend_back_kernel,
         [
-            ((heads * head_width, width), BF),
-            ((head_width, width), BF),
-            ((head_width, width), BF),
+            (first.shape, BF),
+            (first.shape, BF),
             (near.shape, BF),
             (far.shape, BF),
             ((tokens, width), f32),
@@ -833,39 +936,38 @@
             ((heads * tokens, head_width), BF),
             ((heads * tokens, head_width), BF),
             ((tokens, heads * head_width), BF),
+            ((2 * head_width, width), BF),
         ],
-        20_000_000_000,
+        12_000_000_000,
         (
-            grad_attn_bf, attn_bf, query_bf, key_bf, value_bf, lse, query_raw, key_raw,
-            full_query, full_key, full_value, scale_query, scale_key, cos_own, sine_own, cos_all,
-            sine_all, key_index, row_index, normed, normed_all, unit_in, near, far,
+            grad_attn, attn_bf, query_bf, key_bf, value_bf, lse, query_raw, key_raw, w_q, w_kv,
+            scale_query, scale_key, cos_all, sine_all, key_index, row_index, normed, normed_all,
+            unit_in, near, far, order_q, order_kv,
         ),
     )
-    far_sum = add_bf16(g_near, swap_ctx(g_far, 1)).astype(BF).reshape(chips, tokens, width)
+    back = (packed, packed_far, g_near, g_far, grad_normed_q, grad_s_in, grad_s_query, grad_s_key)
+    back, feed_come2, out_comes, g_out, g_feed = tie((back, feed_come2, out_comes, g_out, g_feed))
+    packed, packed_far, g_near, g_far, grad_normed_q, grad_s_in, grad_s_query, grad_s_key = back
     grad_scales = jnp.concatenate(
         [grad_s_in, grad_s_attn, grad_s_pre, grad_s_post, grad_s_query, grad_s_key], axis=1
     ).reshape(owners, scale_part)
     scales_back = reorder_back(order_s, grad_scales)
-    packed = jnp.concatenate(
-        [
-            reorder_back(order_q, gwq).reshape(owners, rows_q, width),
-            reorder_back(order_k, gwk).reshape(owners, rows_k, width),
-            reorder_back(order_k, gwv).reshape(owners, rows_k, width),
-            jnp.zeros((owners, 8, width), BF).at[:, 0, :scale_part].set(scales_back),
-        ],
-        axis=1,
-    ).reshape(2, -1, width)
-    packed = add_bf16(packed[0], swap_ctx(packed[1], 1)).astype(BF)
-    grads_a = add_bf16(ga_one, ga_come).astype(BF)
-    grads_b = add_bf16(gb_one, gb_come).astype(BF)
-    grads_a, grads_b, packed, far_sum = tie((grads_a, grads_b, packed, far_sum))
-    grads_a = halve(grads_a, swap_dp, 1)
-    grads_b = halve(grads_b, swap_dp, 2)
+    scale_sum = add_bf16(scales_back[: owners // 2], swap_ctx(scales_back[owners // 2 :], 1))
+    scale_sum = jnp.pad(
+        scale_sum[:, None], ((0, 0), (last, packed.shape[1] - last - 1), (0, width - scale_part))
+    )
+    packed = (add_bf16(packed, swap_ctx(packed_far, 1)) + scale_sum).astype(BF)
+    feed_come3 = swap_z(g_feed[3, : 3 * rows_f // 2], 3)
+    far_sum = add_bf16(g_near, swap_ctx(g_far, 1)).astype(BF).reshape(chips, tokens, width)
+    out_sum = add_bf16(g_out[0], *out_comes).astype(BF)
+    packed, far_sum, out_sum, g_feed, feed_come3 = tie((packed, far_sum, out_sum, g_feed, feed_come3))
+    packed = scatter_over(packed.reshape((count_dp, chips) + packed.shape[1:]), swap_dp, count_dp)
     own_normed = scatter_over(far_sum, swap_z, chips) + grad_normed_q
-    grads_a, grads_b, packed, own_normed = tie((grads_a, grads_b, packed, own_normed))
-    own_first = scatter_chip(packed)
-    sum_a = scatter_over(grads_a, swap_z, chips)
-    sum_b = scatter_over(grads_b, swap_z, chips)
+    packed, own_normed, out_sum, g_feed = tie((packed.astype(BF), own_normed, out_sum, g_feed))
+    feed_come3 = jnp.concatenate([feed_come3, swap_z(g_feed[3, 3 * rows_f // 2 :], 3)], axis=0)
+    own_feed = add_bf16(g_feed[0], feed_come1, feed_come2, feed_come3)
+    own_output = scatter_over(out_sum, swap_z, chips)
+    own_first = scatter_over(packed, swap_z, chips)
     grad_resid = grad_resid_a + rms_back(unit_in, inverse_in, own_normed * (1.0 + scale_in))
     return (
         block_out[None],
@@ -873,10 +975,10 @@
         own_first[:rows_q],
         own_first[rows_q : rows_q + rows_k],
         own_first[rows_q + rows_k : last],
-        sum_a[rows_f:],
-        sum_a[:rows_f],
-        sum_b[:rows_f],
-        sum_b[rows_f:],
+        own_output,
+        own_feed[:rows_f],
+        own_feed[rows_f : 2 * rows_f],
+        own_feed[2 * rows_f :],
         own_first[last, :scale_part],
     )
 

time: 260 us -> 210 us (0.81)
  waiting for transfers between devices: 113 us -> 67 us
  Pallas kernels: 34.5 us -> 45.7 us
  other arithmetic: 29.1 us -> 18.4 us
  matrix products: 10.3 us -> 0.32 us
  starting transfers between devices: 61.7 us -> 67.6 us
    ppermute x14 -> x24, waiting for transfers between devices: 56.4 us -> 29.6 us  [swap_dp(): lax.ppermute(block, 'dp', [(place, place ^ bits) for place in range(count)])]
    ppermute x36 -> x38, waiting for transfers between devices: 56.8 us -> 37.4 us  [swap_ctx(): lax.ppermute(block, 'ctx', [(place, place ^ bits) for place in range(coun...]
    ppermute x14 -> x24, starting transfers between devices: 16.5 us -> 29.8 us  [swap_dp(): lax.ppermute(block, 'dp', [(place, place ^ bits) for place in range(count)])]
    pallas_call x3 -> x7, Pallas kernels: 34.5 us -> 45.7 us  [call_kernel(): pl.pallas_call(body, out_shape=[jax.ShapeDtypeStruct(shape, dtype) for sh...]
    concatenate x6 -> x1, other arithmetic: 8.19 us -> 0.02 us  [shards_kernels(): feed = jnp.concatenate([w_gate, w_up, w_down], axis=0)]
    ppermute x36 -> x38, starting transfers between devices: 45.2 us -> 37.8 us  [swap_ctx(): lax.ppermute(block, 'ctx', [(place, place ^ bits) for place in range(coun...]
    dot_general x4 -> x1, matrix products: 5.96 us -> 0.13 us  [reorder(): return jnp.dot(order, blocks, preferred_element_type=jnp.float32).astype(BF)]
    dot_general x4 -> x1, matrix products: 4.31 us -> 0.19 us  [outer_sum(): lax.dot_general(left, right, (((0,), (0,)), ((), ())), preferred_element_...]
  transfers between devices with their start and end apart: 50 -> 62, of which waited for: 27 -> 31; matrix products, arithmetic and copies ran while one was open for 11% -> 9% of each run, Pallas kernels for 7% -> 15%
where the time goes in v1:
time: 210 us
  starting transfers between devices  67.6 us (32%)
  waiting for transfers between devices  67 us (32%)
  Pallas kernels  45.7 us (22%)
  other arithmetic  18.4 us (9%)
  local copies, waits for them, and re-layouts  9.35 us (4%)
    pallas_call x7, Pallas kernels, call_kernel(): pl.pallas_call(body, out_shape=[jax.ShapeDtypeStruct(shape, dtype) for sh...  45.7 us
    ppermute x38, starting transfers between devices, swap_ctx(): lax.ppermute(block, 'ctx', [(place, place ^ bits) for place in range(coun...  37.8 us
    ppermute x38, waiting for transfers between devices, swap_ctx(): lax.ppermute(block, 'ctx', [(place, place ^ bits) for place in range(coun...  37.4 us
    ppermute x24, starting transfers between devices, swap_dp(): lax.ppermute(block, 'dp', [(place, place ^ bits) for place in range(count)])  29.8 us
    ppermute x24, waiting for transfers between devices, swap_dp(): lax.ppermute(block, 'dp', [(place, place ^ bits) for place in range(count)])  29.6 us
    unnamed x60, local copies, waits for them, and re-layouts  4.37 us
  transfers between devices with their start and end apart: 62, of which 31 were waited for; matrix products, arithmetic and copies ran while one was open for 9% of the time, Pallas kernels for 15%

profile of v1, /device:TPU:0, one launch (start us, length us, event | category | flops | bytes accessed | tf_op | source)
XLA Modules:
  0.0 209.5 jit_solution(11236013685916101446)
XLA Ops:
  3.1 5.1 %collective-permute-start.2 = (bf16[1,64,640]{2,1,0:T(8,128)(2,1)S(1)}, bf16[1,64,640]{2,1,0:T(8,128)(2,1)S(1)}, u32[]{:S(2)}, u32[]{:S(2)}) collective-permute-start(bf16[1,64,640]{2,1,0:T(8,128)(2,1)S(1)} %maximum_bitcast_fusion), channel_id=1, source_target_pairs={{0,6},{1,7},{2,4},{3,5},{4,2},{5,3},{6,0},{7,1},{8,14},{9,15},{10,... | collective-permute-start | bytes 245768 | tf_op jit(solution)/shard_map/ppermute | solution.py:75
  8.8 1.1 multiply_reduce_fusion.1
  10.2 1.1 fusion.47
  12.3 2.2 %fusion.order_q_ref.order_ref = bf16[1024,1024]{1,0:T(8,128)(2,1)} fusion(s32[1024]{0:T(1024)S(1)} %add.384), kind=kLoop, calls=%fused_computation.1 | loop fusion | flops 2097152 | bytes 2101248 | tf_op jit(solution)/shard_map/convert_element_type | solution.py:158
  15.2 3.3 %collective-permute-start.8 = (bf16[1,128,640]{2,1,0:T(8,128)(2,1)S(1)}, bf16[1,128,640]{2,1,0:T(8,128)(2,1)S(1)}, u32[]{:S(2)}, u32[]{:S(2)}) collective-permute-start(bf16[1,128,640]{2,1,0:T(8,128)(2,1)S(1)} %bitcast.113), channel_id=1, source_target_pairs={{0,6},{1,7},{2,4},{3,5},{4,2},{5,3},{6,0},{7,1},{8,14},{9,15},{10,... | collective-permute-start | bytes 491528 | tf_op jit(solution)/shard_map/ppermute | solution.py:75
  18.5 1.1 collective-permute-start.6
  19.6 2.4 %collective-permute-start.5 = (bf16[1,4,64,640]{3,2,1,0:T(8,128)(2,1)S(1)}, bf16[1,4,64,640]{3,2,1,0:T(8,128)(2,1)S(1)}, u32[]{:S(2)}, u32[]{:S(2)}) collective-permute-start(bf16[1,4,64,640]{3,2,1,0:T(8,128)(2,1)S(1)} %bitcast.97), channel_id=1, source_target_pairs={{0,24},{8,16},{16,8},{24,0},{1,25},{9,17},{17,9},{25,1},{2,26},{10... | collective-permute-start | bytes 983048 | tf_op jit(solution)/shard_map/ppermute | solution.py:70
  22.6 1.6 collective-permute-done.8
  24.2 1.5 collective-permute-start.3
  25.7 3.1 %multiply_sine_fusion = (f32[1024,128]{1,0:T(8,128)}, f32[1024,128]{1,0:T(8,128)}) fusion(f32[128]{0:T(128)S(1)} %multiply_power_fusion, f32[1024]{0:T(1024)S(1)} %bitcast.123), kind=kLoop, calls=%fused_computation.11 | loop fusion | flops 131072 | bytes 1053184 | tf_op jit(solution)/shard_map/sin | solution.py:796
  28.8 3.9 %collective-permute-done.7 = bf16[1,128,640]{2,1,0:T(8,128)(2,1)S(1)} collective-permute-done((bf16[1,128,640]{2,1,0:T(8,128)(2,1)S(1)}, bf16[1,128,640]{2,1,0:T(8,128)(2,1)S(1)}, u32[]{:S(2)}, u32[]{:S(2)}) %collective-permute-start.7) | collective-permute-done | bytes 163872 | tf_op jit(solution)/shard_map/ppermute | solution.py:75
  32.8 4.0 %collective-permute-done.4 = bf16[1,4,64,640]{3,2,1,0:T(8,128)(2,1)S(1)} collective-permute-done((bf16[1,4,64,640]{3,2,1,0:T(8,128)(2,1)S(1)}, bf16[1,4,64,640]{3,2,1,0:T(8,128)(2,1)S(1)}, u32[]{:S(2)}, u32[]{:S(2)}) %collective-permute-start.4) | collective-permute-done | bytes 327712 | tf_op jit(solution)/shard_map/ppermute | solution.py:70
  37.8 3.3 %collective-permute-start.14 = (bf16[1,32,640]{2,1,0:T(8,128)(2,1)S(1)}, bf16[1,32,640]{2,1,0:T(8,128)(2,1)S(1)}, u32[]{:S(2)}, u32[]{:S(2)}) collective-permute-start(bf16[1,32,640]{2,1,0:T(8,128)(2,1)S(1)} %bitcast.118), channel_id=1, source_target_pairs={{0,6},{1,7},{2,4},{3,5},{4,2},{5,3},{6,0},{7,1},{8,14},{9,15},{10,... | collective-permute-start | bytes 122888 | tf_op jit(solution)/shard_map/ppermute | solution.py:75
  42.3 1.4 collective-permute-done.14
  43.7 2.5 %collective-permute-done.13 = bf16[1,32,640]{2,1,0:T(8,128)(2,1)S(1)} collective-permute-done((bf16[1,32,640]{2,1,0:T(8,128)(2,1)S(1)}, bf16[1,32,640]{2,1,0:T(8,128)(2,1)S(1)}, u32[]{:S(2)}, u32[]{:S(2)}) %collective-permute-start.13) | collective-permute-done | bytes 40992 | tf_op jit(solution)/shard_map/ppermute | solution.py:75
  47.3 2.0 collective-permute-start.18
  50.8 1.8 collective-permute-start.15
  52.7 10.5 %shard_map.186 = (bf16[1024,640]{1,0:T(8,128)(2,1)}, bf16[512,640]{1,0:T(8,128)(2,1)}, bf16[128,640]{1,0:T(8,128)(2,1)S(1)}, bf16[1024,640]{1,0:T(8,128)(2,1)}, ...) custom-call(f32[128,640]{1,0:T(8,128)S(1)} %get-tuple-element.283.un, ...), custom_call_target="tpu_custom_call" | custom-call | flops 12000000000 | bytes 20000000 | tf_op jit(solution)/shard_map/pallas_call | solution.py:204
  67.3 3.5 %shard_map.187 = (bf16[1024,640]{1,0:T(8,128)(2,1)}, bf16[128,1024]{1,0:T(8,128)(2,1)S(1)}, f32[128,640]{1,0:T(8,128)S(1)}, f32[128,640]{1,0:T(8,128)S(1)}, bf16[128,640]{1,0:T(8,128)(2,1)S(1)}) custom-call(bf16[128,1024]{1,0:T(8,128)(2,1)S(1)} %get-tuple-element.181.attn_ref, bf16[1024,1024]{1,0:T(8,128)(2,1)} %fusion.order_q_ref.order_ref, ...), custom_call_target="tpu_custom_call" | custom-call | flops 2000000000 | bytes 20000000 | tf_op jit(solution)/shard_map/pallas_call | solution.py:204
  70.8 1.9 collective-permute-start.22
  75.4 3.5 %collective-permute-done.23.refs_5_ = bf16[192,640]{1,0:T(8,128)(2,1)S(1)} collective-permute-done((bf16[192,640]{1,0:T(8,128)(2,1)S(1)}, bf16[192,640]{1,0:T(8,128)(2,1)S(1)}, u32[]{:S(2)}, u32[]{:S(2)}) %collective-permute-start.23) | collective-permute-done | bytes 245792 | tf_op jit(solution)/shard_map/ppermute | solution.py:75
  78.9 2.4 %collective-permute-done.21.refs_2_ = bf16[128,640]{1,0:T(8,128)(2,1)S(1)} collective-permute-done((bf16[128,640]{1,0:T(8,128)(2,1)S(1)}, bf16[128,640]{1,0:T(8,128)(2,1)S(1)}, u32[]{:S(2)}, u32[]{:S(2)}) %collective-permute-start.21) | collective-permute-done | bytes 163872 | tf_op jit(solution)/shard_map/ppermute | solution.py:70
  84.2 5.9 %shard_map.188 = (f32[128,640]{1,0:T(8,128)}, bf16[128,640]{1,0:T(8,128)(2,1)S(1)}, bf16[128,640]{1,0:T(8,128)(2,1)S(1)}, bf16[128,640]{1,0:T(8,128)(2,1)S(1)}, ...) custom-call(bf16[128,640]{1,0:T(8,128)(2,1)S(1)} %get-tuple-element., ...), custom_call_target="tpu_custom_call" | custom-call | flops 3000000000 | bytes 20000000 | tf_op jit(solution)/shard_map/pallas_call | solution.py:204
  90.2 1.5 collective-permute-start.29
  92.5 1.2 collective-permute-start.31
  93.7 3.5 %collective-permute-done.29.come1_ref = bf16[128,640]{1,0:T(8,128)(2,1)S(1)} collective-permute-done((bf16[128,640]{1,0:T(8,128)(2,1)S(1)}, bf16[128,640]{1,0:T(8,128)(2,1)S(1)}, u32[]{:S(2)}, u32[]{:S(2)}) %collective-permute-start.29) | collective-permute-done | bytes 163872 | tf_op jit(solution)/shard_map/ppermute | solution.py:70
  97.2 3.9 %collective-permute-done.30.come2_ref = bf16[128,640]{1,0:T(8,128)(2,1)S(1)} collective-permute-done((bf16[128,640]{1,0:T(8,128)(2,1)S(1)}, bf16[128,640]{1,0:T(8,128)(2,1)S(1)}, u32[]{:S(2)}, u32[]{:S(2)}) %collective-permute-start.30) | collective-permute-done | bytes 163872 | tf_op jit(solution)/shard_map/ppermute | solution.py:70
  103.0 1.4 collective-permute-start.34
  105.0 1.5 collective-permute-start.32
  106.5 4.3 %collective-permute-done.34.refs_3_ = bf16[128,640]{1,0:T(8,128)(2,1)S(1)} collective-permute-done((bf16[128,640]{1,0:T(8,128)(2,1)S(1)}, bf16[128,640]{1,0:T(8,128)(2,1)S(1)}, u32[]{:S(2)}, u32[]{:S(2)}) %collective-permute-start.34) | collective-permute-done | bytes 163872 | tf_op jit(solution)/shard_map/ppermute | solution.py:70
  110.8 1.7 collective-permute-done.33.refs_2_
  112.6 7.3 %shard_map.190 = (f32[128,640]{1,0:T(8,128)S(1)}, bf16[128,640]{1,0:T(8,128)(2,1)S(1)}, bf16[128,640]{1,0:T(8,128)(2,1)S(1)}, bf16[128,640]{1,0:T(8,128)(2,1)S(1...) custom-call(bf16[128,640]{1,0:T(8,128)(2,1)S(1)} %get-tuple-element.200.refs_0_, ...), custom_call_target="tpu_custom_call" | custom-call | flops 6000000000 | bytes 20000000 | tf_op jit(solution)/shard_map/pallas_call | solution.py:204
  120.7 1.2 collective-permute-start.37
  121.9 1.4 collective-permute-start.38
  123.3 1.4 add_convert_fusion.1
  124.8 2.1 collective-permute-done.36.come1_ref
  126.8 3.7 %collective-permute-done.37.come2_ref = bf16[128,640]{1,0:T(8,128)(2,1)S(1)} collective-permute-done((bf16[128,640]{1,0:T(8,128)(2,1)S(1)}, bf16[128,640]{1,0:T(8,128)(2,1)S(1)}, u32[]{:S(2)}, u32[]{:S(2)}) %collective-permute-start.37) | collective-permute-done | bytes 163872 | tf_op jit(solution)/shard_map/ppermute | solution.py:70
  130.5 1.2 collective-permute-start.39
  131.8 5.0 %shard_map.191 = (f32[128,640]{1,0:T(8,128)S(1)}, bf16[128,1024]{1,0:T(8,128)(2,1)S(1)}, bf16[16,32,640]{2,1,0:T(8,128)(2,1)}, bf16[16,32,640]{2,1,0:T(8,128)(2,...) custom-call(f32[128,640]{1,0:T(8,128)S(1)} %get-tuple-element.208.own_ref, ...), custom_call_target="tpu_custom_call" | custom-call | flops 3000000000 | bytes 20000000 | tf_op jit(solution)/shard_map/pallas_call | solution.py:204
  137.7 2.3 %collective-permute-done.40 = bf16[16,32,640]{2,1,0:T(8,128)(2,1)S(1)} collective-permute-done((bf16[16,32,640]{2,1,0:T(8,128)(2,1)}, bf16[16,32,640]{2,1,0:T(8,128)(2,1)S(1)}, u32[]{:S(2)}, u32[]{:S(2)}) %collective-permute-start.40) | collective-permute-done | bytes 655392 | tf_op jit(solution)/shard_map/ppermute | solution.py:75
  140.0 1.2 add_convert_fusion.3
  141.3 2.7 %collective-permute-start.41 = (bf16[192,640]{1,0:T(8,128)(2,1)S(1)}, bf16[192,640]{1,0:T(8,128)(2,1)S(1)}, u32[]{:S(2)}, u32[]{:S(2)}) collective-permute-start(bf16[192,640]{1,0:T(8,128)(2,1)S(1)} %slice_bitcast_fusion), channel_id=1, source_target_pairs={{0,4},{1,5},{2,6},{3,7},{4,0},{5,1},{6,2},{7,3},{8,12},{9,13},{10,... | collective-permute-start | bytes 737288 | tf_op jit(solution)/shard_map/ppermute | solution.py:75
  144.1 1.7 collective-permute-start.44
  145.8 1.3 collective-permute-start.43
  147.6 12.5 %shard_map.192 = (bf16[16,64,640]{2,1,0:T(8,128)(2,1)}, bf16[16,64,640]{2,1,0:T(8,128)(2,1)}, bf16[512,640]{1,0:T(8,128)(2,1)}, bf16[512,640]{1,0:T(8,128)(2,1)}...) custom-call(bf16[128,1024]{1,0:T(8,128)(2,1)S(1)} %get-tuple-element.232.grad_attn, ...), custom_call_target="tpu_custom_call" | custom-call | flops 12000000000 | bytes 20000000 | tf_op jit(solution)/shard_map/pallas_call | solution.py:204
  161.9 1.1 collective-permute-start.48
  163.0 1.1 fusion.9
  164.7 1.6 add_convert_fusion
  166.3 2.8 %collective-permute-done.48 = bf16[96,640]{1,0:T(8,128)(2,1)S(1)} collective-permute-done((bf16[96,640]{1,0:T(8,128)(2,1)S(1)}, bf16[96,640]{1,0:T(8,128)(2,1)S(1)}, u32[]{:S(2)}, u32[]{:S(2)}) %collective-permute-start.48) | collective-permute-done | bytes 122912 | tf_op jit(solution)/shard_map/ppermute | solution.py:75
  170.2 1.5 collective-permute-start.54
  172.8 1.5 collective-permute-start.49
  174.4 1.4 collective-permute-start.51
  176.4 1.4 collective-permute-start.50
  177.8 2.1 %collective-permute-done.54 = bf16[128,640]{1,0:T(8,128)(2,1)S(1)} collective-permute-done((bf16[128,640]{1,0:T(8,128)(2,1)S(1)}, bf16[128,640]{1,0:T(8,128)(2,1)S(1)}, u32[]{:S(2)}, u32[]{:S(2)}) %collective-permute-start.54) | collective-permute-done | bytes 163872 | tf_op jit(solution)/shard_map/ppermute | solution.py:75
  179.9 6.3 %collective-permute-done.53 = bf16[128,640]{1,0:T(8,128)(2,1)S(1)} collective-permute-done((bf16[128,640]{1,0:T(8,128)(2,1)S(1)}, bf16[128,640]{1,0:T(8,128)(2,1)S(1)}, u32[]{:S(2)}, u32[]{:S(2)}) %collective-permute-start.53) | collective-permute-done | bytes 163872 | tf_op jit(solution)/shard_map/ppermute | solution.py:75
  186.3 2.5 %collective-permute-done.51 = bf16[4,64,640]{2,1,0:T(8,128)(2,1)S(1)} collective-permute-done((bf16[4,64,640]{2,1,0:T(8,128)(2,1)S(1)}, bf16[4,64,640]{2,1,0:T(8,128)(2,1)S(1)}, u32[]{:S(2)}, u32[]{:S(2)}) %collective-permute-start.51) | collective-permute-done | bytes 327712 | tf_op jit(solution)/shard_map/ppermute | solution.py:70
  188.8 1.4 collective-permute-done.50
  190.5 1.3 collective-permute-start.58
  191.8 1.3 collective-permute-start.60
  194.1 1.6 collective-permute-start.61
  197.6 2.5 %collective-permute-start.57 = (bf16[64,640]{1,0:T(8,128)(2,1)S(1)}, bf16[64,640]{1,0:T(8,128)(2,1)S(1)}, u32[]{:S(2)}, u32[]{:S(2)}) collective-permute-start(bf16[64,640]{1,0:T(8,128)(2,1)S(1)} %get-tuple-element.297), channel_id=1, source_target_pairs={{0,6},{1,7},{2,4},{3,5},{4,2},{5,3},{6,0},{7,1},{8,14},{9,15},{10,... | collective-permute-start | bytes 245768 | tf_op jit(solution)/shard_map/ppermute | solution.py:75
  200.1 1.4 collective-permute-done.59
  202.8 1.2 collective-permute-done.57
  204.0 2.8 %collective-permute-done.56 = bf16[64,640]{1,0:T(8,128)(2,1)S(1)} collective-permute-done((bf16[64,640]{1,0:T(8,128)(2,1)S(1)}, bf16[64,640]{1,0:T(8,128)(2,1)S(1)}, u32[]{:S(2)}, u32[]{:S(2)}) %collective-permute-start.56) | collective-permute-done | bytes 81952 | tf_op jit(solution)/shard_map/ppermute | solution.py:75
  (207 shorter events, 38.2 us)
Async XLA Ops:
  3.1 11.5 %collective-permute-start.2 = (bf16[1,64,640]{2,1,0:T(8,128)(2,1)S(1)}, bf16[1,64,640]{2,1,0:T(8,128)(2,1)S(1)}, u32[]{:S(2)}, u32[]{:S(2)}) collective-permute-start(bf16[1,64,640]{2,1,0:T(8,128)(2,1)S(1)} %maximum_bitcast_fusion), channel_id=1, source_target_pairs={{0,6},{1,7},{2,4},{3,5},{4,2},{5,3},{6,0},{7,1},{8,14},{9,15},{10,... | collective-permute-start | bytes 245768 | tf_op jit(solution)/shard_map/ppermute | solution.py:75
  8.2 6.9 %collective-permute-start.1 = (bf16[1,64,640]{2,1,0:T(8,128)(2,1)S(1)}, bf16[1,64,640]{2,1,0:T(8,128)(2,1)S(1)}, u32[]{:S(2)}, u32[]{:S(2)}) collective-permute-start(bf16[1,64,640]{2,1,0:T(8,128)(2,1)S(1)} %maximum_bitcast_fusion), channel_id=1, source_target_pairs={{0,4},{1,5},{2,6},{3,7},{4,0},{5,1},{6,2},{7,3},{8,12},{9,13},{10,... | collective-permute-start | bytes 245768 | tf_op jit(solution)/shard_map/ppermute | solution.py:75
  8.2 6.9 %collective-permute-start = (bf16[1,64,640]{2,1,0:T(8,128)(2,1)S(1)}, bf16[1,64,640]{2,1,0:T(8,128)(2,1)S(1)}, u32[]{:S(2)}, u32[]{:S(2)}) collective-permute-start(bf16[1,64,640]{2,1,0:T(8,128)(2,1)S(1)} %maximum_bitcast_fusion), channel_id=1, source_target_pairs={{0,2},{1,3},{2,0},{3,1},{4,6},{5,7},{6,4},{7,5},{8,10},{9,11},{10,... | collective-permute-start | bytes 245768 | tf_op jit(solution)/shard_map/ppermute | solution.py:75
  15.1 7.0 %collective-permute-start.9 = (bf16[4,16,640]{2,1,0:T(8,128)(2,1)S(1)}, bf16[4,16,640]{2,1,0:T(8,128)(2,1)S(1)}, u32[]{:S(2)}, u32[]{:S(2)}) collective-permute-start(bf16[4,16,640]{2,1,0:T(8,128)(2,1)S(1)} %get-tuple-element.300), channel_id=1, source_target_pairs={{0,1},{1,0},{2,3},{3,2},{4,5},{5,4},{6,7},{7,6},{8,9},{9,8},{10,11... | collective-permute-start | bytes 245768 | tf_op jit(solution)/shard_map/ppermute | solution.py:75
  15.2 9.0 %collective-permute-start.8 = (bf16[1,128,640]{2,1,0:T(8,128)(2,1)S(1)}, bf16[1,128,640]{2,1,0:T(8,128)(2,1)S(1)}, u32[]{:S(2)}, u32[]{:S(2)}) collective-permute-start(bf16[1,128,640]{2,1,0:T(8,128)(2,1)S(1)} %bitcast.113), channel_id=1, source_target_pairs={{0,6},{1,7},{2,4},{3,5},{4,2},{5,3},{6,0},{7,1},{8,14},{9,15},{10,... | collective-permute-start | bytes 491528 | tf_op jit(solution)/shard_map/ppermute | solution.py:75
  18.5 14.2 %collective-permute-start.7 = (bf16[1,128,640]{2,1,0:T(8,128)(2,1)S(1)}, bf16[1,128,640]{2,1,0:T(8,128)(2,1)S(1)}, u32[]{:S(2)}, u32[]{:S(2)}) collective-permute-start(bf16[1,128,640]{2,1,0:T(8,128)(2,1)S(1)} %bitcast.114), channel_id=1, source_target_pairs={{0,4},{1,5},{2,6},{3,7},{4,0},{5,1},{6,2},{7,3},{8,12},{9,13},{10,... | collective-permute-start | bytes 491528 | tf_op jit(solution)/shard_map/ppermute | solution.py:75
  18.5 14.1 %collective-permute-start.6 = (bf16[1,128,640]{2,1,0:T(8,128)(2,1)S(1)}, bf16[1,128,640]{2,1,0:T(8,128)(2,1)S(1)}, u32[]{:S(2)}, u32[]{:S(2)}) collective-permute-start(bf16[1,128,640]{2,1,0:T(8,128)(2,1)S(1)} %bitcast.115), channel_id=1, source_target_pairs={{0,2},{1,3},{2,0},{3,1},{4,6},{5,7},{6,4},{7,5},{8,10},{9,11},{10,... | collective-permute-start | bytes 491528 | tf_op jit(solution)/shard_map/ppermute | solution.py:75
  19.6 13.2 %collective-permute-start.5 = (bf16[1,4,64,640]{3,2,1,0:T(8,128)(2,1)S(1)}, bf16[1,4,64,640]{3,2,1,0:T(8,128)(2,1)S(1)}, u32[]{:S(2)}, u32[]{:S(2)}) collective-permute-start(bf16[1,4,64,640]{3,2,1,0:T(8,128)(2,1)S(1)} %bitcast.97), channel_id=1, source_target_pairs={{0,24},{8,16},{16,8},{24,0},{1,25},{9,17},{17,9},{25,1},{2,26},{10... | collective-permute-start | bytes 983048 | tf_op jit(solution)/shard_map/ppermute | solution.py:70
  22.1 14.7 %collective-permute-start.4 = (bf16[1,4,64,640]{3,2,1,0:T(8,128)(2,1)S(1)}, bf16[1,4,64,640]{3,2,1,0:T(8,128)(2,1)S(1)}, u32[]{:S(2)}, u32[]{:S(2)}) collective-permute-start(bf16[1,4,64,640]{3,2,1,0:T(8,128)(2,1)S(1)} %bitcast.98), channel_id=1, source_target_pairs={{0,16},{8,24},{16,0},{24,8},{1,17},{9,25},{17,1},{25,9},{2,18},{10... | collective-permute-start | bytes 983048 | tf_op jit(solution)/shard_map/ppermute | solution.py:70
  24.2 12.7 %collective-permute-start.3 = (bf16[1,4,64,640]{3,2,1,0:T(8,128)(2,1)S(1)}, bf16[1,4,64,640]{3,2,1,0:T(8,128)(2,1)S(1)}, u32[]{:S(2)}, u32[]{:S(2)}) collective-permute-start(bf16[1,4,64,640]{3,2,1,0:T(8,128)(2,1)S(1)} %bitcast.99), channel_id=1, source_target_pairs={{0,8},{8,0},{16,24},{24,16},{1,9},{9,1},{17,25},{25,17},{2,10},{10... | collective-permute-start | bytes 983048 | tf_op jit(solution)/shard_map/ppermute | solution.py:70
  37.1 9.2 %collective-permute-start.10 = (bf16[16,64,640]{2,1,0:T(8,128)(2,1)S(1)}, bf16[16,64,640]{2,1,0:T(8,128)(2,1)}, u32[]{:S(2)}, u32[]{:S(2)}) collective-permute-start(bf16[16,64,640]{2,1,0:T(8,128)(2,1)S(1)} %bitcast.101), channel_id=1, source_target_pairs={{0,1},{1,0},{2,3},{3,2},{4,5},{5,4},{6,7},{7,6},{8,9},{9,8},{10,11... | collective-permute-start | bytes 3932168 | tf_op jit(solution)/shard_map/ppermute | solution.py:75
  37.2 10.0 %collective-permute-start.11 = (bf16[512,640]{1,0:T(8,128)(2,1)S(1)}, bf16[512,640]{1,0:T(8,128)(2,1)S(1)}, u32[]{:S(2)}, u32[]{:S(2)}) collective-permute-start(bf16[512,640]{1,0:T(8,128)(2,1)S(1)} %bitcast.108), channel_id=1, source_target_pairs={{0,1},{1,0},{2,3},{3,2},{4,5},{5,4},{6,7},{7,6},{8,9},{9,8},{10,11... | collective-permute-start | bytes 1966088 | tf_op jit(solution)/shard_map/ppermute | solution.py:75
  37.8 5.8 %collective-permute-start.14 = (bf16[1,32,640]{2,1,0:T(8,128)(2,1)S(1)}, bf16[1,32,640]{2,1,0:T(8,128)(2,1)S(1)}, u32[]{:S(2)}, u32[]{:S(2)}) collective-permute-start(bf16[1,32,640]{2,1,0:T(8,128)(2,1)S(1)} %bitcast.118), channel_id=1, source_target_pairs={{0,6},{1,7},{2,4},{3,5},{4,2},{5,3},{6,0},{7,1},{8,14},{9,15},{10,... | collective-permute-start | bytes 122888 | tf_op jit(solution)/shard_map/ppermute | solution.py:75
  41.1 5.1 %collective-permute-start.13 = (bf16[1,32,640]{2,1,0:T(8,128)(2,1)S(1)}, bf16[1,32,640]{2,1,0:T(8,128)(2,1)S(1)}, u32[]{:S(2)}, u32[]{:S(2)}) collective-permute-start(bf16[1,32,640]{2,1,0:T(8,128)(2,1)S(1)} %bitcast.119), channel_id=1, source_target_pairs={{0,4},{1,5},{2,6},{3,7},{4,0},{5,1},{6,2},{7,3},{8,12},{9,13},{10,... | collective-permute-start | bytes 122888 | tf_op jit(solution)/shard_map/ppermute | solution.py:75
  41.4 4.8 %collective-permute-start.12 = (bf16[1,32,640]{2,1,0:T(8,128)(2,1)S(1)}, bf16[1,32,640]{2,1,0:T(8,128)(2,1)S(1)}, u32[]{:S(2)}, u32[]{:S(2)}) collective-permute-start(bf16[1,32,640]{2,1,0:T(8,128)(2,1)S(1)} %bitcast.120), channel_id=1, source_target_pairs={{0,2},{1,3},{2,0},{3,1},{4,6},{5,7},{6,4},{7,5},{8,10},{9,11},{10,... | collective-permute-start | bytes 122888 | tf_op jit(solution)/shard_map/ppermute | solution.py:75
  47.3 16.7 %collective-permute-start.18 = (bf16[1,4,32,640]{3,2,1,0:T(8,128)(2,1)S(1)}, bf16[1,4,32,640]{3,2,1,0:T(8,128)(2,1)S(1)}, u32[]{:S(2)}, u32[]{:S(2)}) collective-permute-start(bf16[1,4,32,640]{3,2,1,0:T(8,128)(2,1)S(1)} %bitcast.104), channel_id=1, source_target_pairs={{0,24},{8,16},{16,8},{24,0},{1,25},{9,17},{17,9},{25,1},{2,26},{10... | collective-permute-start | bytes 491528 | tf_op jit(solution)/shard_map/ppermute | solution.py:70
  49.2 14.7 %collective-permute-start.17 = (bf16[1,4,32,640]{3,2,1,0:T(8,128)(2,1)S(1)}, bf16[1,4,32,640]{3,2,1,0:T(8,128)(2,1)S(1)}, u32[]{:S(2)}, u32[]{:S(2)}) collective-permute-start(bf16[1,4,32,640]{3,2,1,0:T(8,128)(2,1)S(1)} %bitcast.105), channel_id=1, source_target_pairs={{0,16},{8,24},{16,0},{24,8},{1,17},{9,25},{17,1},{25,9},{2,18},{10... | collective-permute-start | bytes 491528 | tf_op jit(solution)/shard_map/ppermute | solution.py:70
  50.3 13.7 %collective-permute-start.16 = (bf16[1,4,32,640]{3,2,1,0:T(8,128)(2,1)S(1)}, bf16[1,4,32,640]{3,2,1,0:T(8,128)(2,1)S(1)}, u32[]{:S(2)}, u32[]{:S(2)}) collective-permute-start(bf16[1,4,32,640]{3,2,1,0:T(8,128)(2,1)S(1)} %bitcast.106), channel_id=1, source_target_pairs={{0,8},{8,0},{16,24},{24,16},{1,9},{9,1},{17,25},{25,17},{2,10},{10... | collective-permute-start | bytes 491528 | tf_op jit(solution)/shard_map/ppermute | solution.py:70
  50.8 13.2 %collective-permute-start.15 = (bf16[192,640]{1,0:T(8,128)(2,1)S(1)}, bf16[192,640]{1,0:T(8,128)(2,1)S(1)}, u32[]{:S(2)}, u32[]{:S(2)}) collective-permute-start(bf16[192,640]{1,0:T(8,128)(2,1)S(1)} %pad_maximum_fusion.4.refs_4_), channel_id=1, source_target_pairs={{0,4},{1,5},{2,6},{3,7},{4,0},{5,1},{6,2},{7,3},{8,12},{9,13},{10,... | collective-permute-start | bytes 737288 | tf_op jit(solution)/shard_map/ppermute | solution.py:75
  64.1 2.3 %collective-permute-start.19 = (bf16[16,32,640]{2,1,0:T(8,128)(2,1)S(1)}, bf16[16,32,640]{2,1,0:T(8,128)(2,1)S(1)}, u32[]{:S(2)}, u32[]{:S(2)}) collective-permute-start(bf16[16,32,640]{2,1,0:T(8,128)(2,1)S(1)} %bitcast.111), channel_id=1, source_target_pairs={{0,1},{1,0},{2,3},{3,2},{4,5},{5,4},{6,7},{7,6},{8,9},{9,8},{10,11... | collective-permute-start | bytes 1966088 | tf_op jit(solution)/shard_map/ppermute | solution.py:75
  64.2 8.6 %collective-permute-start.26 = (bf16[192,640]{1,0:T(8,128)(2,1)S(1)}, bf16[192,640]{1,0:T(8,128)(2,1)S(1)}, u32[]{:S(2)}, u32[]{:S(2)}) collective-permute-start(bf16[192,640]{1,0:T(8,128)(2,1)S(1)} %collective-permute-done.15.refs_6_), channel_id=1, source_target_pairs={{0,1},{1,0},{2,3},{3,2},{4,5},{5,4},{6,7},{7,6},{8,9},{9,8},{10,11... | collective-permute-start | bytes 737288 | tf_op jit(solution)/shard_map/ppermute | solution.py:75
  64.7 9.1 %collective-permute-start.25 = (bf16[192,640]{1,0:T(8,128)(2,1)S(1)}, bf16[192,640]{1,0:T(8,128)(2,1)S(1)}, u32[]{:S(2)}, u32[]{:S(2)}) collective-permute-start(bf16[192,640]{1,0:T(8,128)(2,1)S(1)} %pad_maximum_fusion.4.refs_4_), channel_id=1, source_target_pairs={{0,1},{1,0},{2,3},{3,2},{4,5},{5,4},{6,7},{7,6},{8,9},{9,8},{10,11... | collective-permute-start | bytes 737288 | tf_op jit(solution)/shard_map/ppermute | solution.py:75
  64.8 10.6 %collective-permute-start.24 = (bf16[192,640]{1,0:T(8,128)(2,1)S(1)}, bf16[192,640]{1,0:T(8,128)(2,1)S(1)}, u32[]{:S(2)}, u32[]{:S(2)}) collective-permute-start(bf16[192,640]{1,0:T(8,128)(2,1)S(1)} %pad_maximum_fusion.4.refs_4_), channel_id=1, source_target_pairs={{0,6},{1,7},{2,4},{3,5},{4,2},{5,3},{6,0},{7,1},{8,14},{9,15},{10,... | collective-permute-start | bytes 737288 | tf_op jit(solution)/shard_map/ppermute | solution.py:75
  65.6 13.3 %collective-permute-start.23 = (bf16[192,640]{1,0:T(8,128)(2,1)S(1)}, bf16[192,640]{1,0:T(8,128)(2,1)S(1)}, u32[]{:S(2)}, u32[]{:S(2)}) collective-permute-start(bf16[192,640]{1,0:T(8,128)(2,1)S(1)} %pad_maximum_fusion.4.refs_4_), channel_id=1, source_target_pairs={{0,2},{1,3},{2,0},{3,1},{4,6},{5,7},{6,4},{7,5},{8,10},{9,11},{10,... | collective-permute-start | bytes 737288 | tf_op jit(solution)/shard_map/ppermute | solution.py:75
  70.8 30.3 %copy-start.2 = (f32[128,640]{1,0:T(8,128)}, f32[128,640]{1,0:T(8,128)S(1)}, u32[]{:S(2)}) copy-start(f32[128,640]{1,0:T(8,128)S(1)} %get-tuple-element.198.middle_ref) | copy-start | bytes 983044
  70.8 30.3 %copy-start.1 = (f32[1,128,640]{2,1,0:T(8,128)S(1)}, f32[1,128,640]{2,1,0:T(8,128)}, u32[]{:S(2)}) copy-start(f32[1,128,640]{2,1,0:T(8,128)} %param.27) | copy-start | bytes 983044
  70.8 8.1 %collective-permute-start.22 = (bf16[128,640]{1,0:T(8,128)(2,1)S(1)}, bf16[128,640]{1,0:T(8,128)(2,1)S(1)}, u32[]{:S(2)}, u32[]{:S(2)}) collective-permute-start(bf16[128,640]{1,0:T(8,128)(2,1)S(1)} %get-tuple-element.186.refs_0_), channel_id=1, source_target_pairs={{0,24},{8,16},{16,8},{24,0},{1,25},{9,17},{17,9},{25,1},{2,26},{10... | collective-permute-start | bytes 491528 | tf_op jit(solution)/shard_map/ppermute | solution.py:70
  72.7 8.6 %collective-permute-start.21 = (bf16[128,640]{1,0:T(8,128)(2,1)S(1)}, bf16[128,640]{1,0:T(8,128)(2,1)S(1)}, u32[]{:S(2)}, u32[]{:S(2)}) collective-permute-start(bf16[128,640]{1,0:T(8,128)(2,1)S(1)} %get-tuple-element.186.refs_0_), channel_id=1, source_target_pairs={{0,16},{8,24},{16,0},{24,8},{1,17},{9,25},{17,1},{25,9},{2,18},{10... | collective-permute-start | bytes 491528 | tf_op jit(solution)/shard_map/ppermute | solution.py:70
  73.8 7.5 %collective-permute-start.20 = (bf16[128,640]{1,0:T(8,128)(2,1)S(1)}, bf16[128,640]{1,0:T(8,128)(2,1)S(1)}, u32[]{:S(2)}, u32[]{:S(2)}) collective-permute-start(bf16[128,640]{1,0:T(8,128)(2,1)S(1)} %get-tuple-element.186.refs_0_), channel_id=1, source_target_pairs={{0,8},{8,0},{16,24},{24,16},{1,9},{9,1},{17,25},{25,17},{2,10},{10... | collective-permute-start | bytes 491528 | tf_op jit(solution)/shard_map/ppermute | solution.py:70
  81.3 1.5 collective-permute-start.27
  81.3 1.9 collective-permute-start.28
  90.2 7.0 %collective-permute-start.29 = (bf16[128,640]{1,0:T(8,128)(2,1)S(1)}, bf16[128,640]{1,0:T(8,128)(2,1)S(1)}, u32[]{:S(2)}, u32[]{:S(2)}) collective-permute-start(bf16[128,640]{1,0:T(8,128)(2,1)S(1)} %get-tuple-element.195), channel_id=1, source_target_pairs={{0,8},{8,0},{16,24},{24,16},{1,9},{9,1},{17,25},{25,17},{2,10},{10... | collective-permute-start | bytes 491528 | tf_op jit(solution)/shard_map/ppermute | solution.py:70
  91.6 9.5 %collective-permute-start.30 = (bf16[128,640]{1,0:T(8,128)(2,1)S(1)}, bf16[128,640]{1,0:T(8,128)(2,1)S(1)}, u32[]{:S(2)}, u32[]{:S(2)}) collective-permute-start(bf16[128,640]{1,0:T(8,128)(2,1)S(1)} %get-tuple-element.196), channel_id=1, source_target_pairs={{0,16},{8,24},{16,0},{24,8},{1,17},{9,25},{17,1},{25,9},{2,18},{10... | collective-permute-start | bytes 491528 | tf_op jit(solution)/shard_map/ppermute | solution.py:70
  92.5 8.7 %collective-permute-start.31 = (bf16[128,640]{1,0:T(8,128)(2,1)S(1)}, bf16[128,640]{1,0:T(8,128)(2,1)S(1)}, u32[]{:S(2)}, u32[]{:S(2)}) collective-permute-start(bf16[128,640]{1,0:T(8,128)(2,1)S(1)} %get-tuple-element.197), channel_id=1, source_target_pairs={{0,24},{8,16},{16,8},{24,0},{1,25},{9,17},{17,9},{25,1},{2,26},{10... | collective-permute-start | bytes 491528 | tf_op jit(solution)/shard_map/ppermute | solution.py:70
  103.0 7.8 %collective-permute-start.34 = (bf16[128,640]{1,0:T(8,128)(2,1)S(1)}, bf16[128,640]{1,0:T(8,128)(2,1)S(1)}, u32[]{:S(2)}, u32[]{:S(2)}) collective-permute-start(bf16[128,640]{1,0:T(8,128)(2,1)S(1)} %get-tuple-element.200.refs_0_), channel_id=1, source_target_pairs={{0,24},{8,16},{16,8},{24,0},{1,25},{9,17},{17,9},{25,1},{2,26},{10... | collective-permute-start | bytes 491528 | tf_op jit(solution)/shard_map/ppermute | solution.py:70
  104.4 8.1 %collective-permute-start.33 = (bf16[128,640]{1,0:T(8,128)(2,1)S(1)}, bf16[128,640]{1,0:T(8,128)(2,1)S(1)}, u32[]{:S(2)}, u32[]{:S(2)}) collective-permute-start(bf16[128,640]{1,0:T(8,128)(2,1)S(1)} %get-tuple-element.200.refs_0_), channel_id=1, source_target_pairs={{0,16},{8,24},{16,0},{24,8},{1,17},{9,25},{17,1},{25,9},{2,18},{10... | collective-permute-start | bytes 491528 | tf_op jit(solution)/shard_map/ppermute | solution.py:70
  105.0 7.5 %collective-permute-start.32 = (bf16[128,640]{1,0:T(8,128)(2,1)S(1)}, bf16[128,640]{1,0:T(8,128)(2,1)S(1)}, u32[]{:S(2)}, u32[]{:S(2)}) collective-permute-start(bf16[128,640]{1,0:T(8,128)(2,1)S(1)} %get-tuple-element.200.refs_0_), channel_id=1, source_target_pairs={{0,8},{8,0},{16,24},{24,16},{1,9},{9,1},{17,25},{25,17},{2,10},{10... | collective-permute-start | bytes 491528 | tf_op jit(solution)/shard_map/ppermute | solution.py:70
  119.8 3.5 %collective-permute-start.35 = (bf16[4,192,640]{2,1,0:T(8,128)(2,1)}, bf16[4,192,640]{2,1,0:T(8,128)(2,1)S(1)}, u32[]{:S(2)}, u32[]{:S(2)}) collective-permute-start(bf16[4,192,640]{2,1,0:T(8,128)(2,1)} %get-tuple-element.210), channel_id=1, source_target_pairs={{0,1},{1,0},{2,3},{3,2},{4,5},{5,4},{6,7},{7,6},{8,9},{9,8},{10,11... | collective-permute-start | bytes 2949128 | tf_op jit(solution)/shard_map/ppermute | solution.py:75
  119.8 7.0 %collective-permute-start.36 = (bf16[128,640]{1,0:T(8,128)(2,1)S(1)}, bf16[128,640]{1,0:T(8,128)(2,1)S(1)}, u32[]{:S(2)}, u32[]{:S(2)}) collective-permute-start(bf16[128,640]{1,0:T(8,128)(2,1)S(1)} %get-tuple-element.211), channel_id=1, source_target_pairs={{0,8},{8,0},{16,24},{24,16},{1,9},{9,1},{17,25},{25,17},{2,10},{10... | collective-permute-start | bytes 491528 | tf_op jit(solution)/shard_map/ppermute | solution.py:70
  120.7 9.8 %collective-permute-start.37 = (bf16[128,640]{1,0:T(8,128)(2,1)S(1)}, bf16[128,640]{1,0:T(8,128)(2,1)S(1)}, u32[]{:S(2)}, u32[]{:S(2)}) collective-permute-start(bf16[128,640]{1,0:T(8,128)(2,1)S(1)} %get-tuple-element.212), channel_id=1, source_target_pairs={{0,16},{8,24},{16,0},{24,8},{1,17},{9,25},{17,1},{25,9},{2,18},{10... | collective-permute-start | bytes 491528 | tf_op jit(solution)/shard_map/ppermute | solution.py:70
  121.9 8.6 %collective-permute-start.38 = (bf16[128,640]{1,0:T(8,128)(2,1)S(1)}, bf16[128,640]{1,0:T(8,128)(2,1)S(1)}, u32[]{:S(2)}, u32[]{:S(2)}) collective-permute-start(bf16[128,640]{1,0:T(8,128)(2,1)S(1)} %get-tuple-element.213), channel_id=1, source_target_pairs={{0,24},{8,16},{16,8},{24,0},{1,25},{9,17},{17,9},{25,1},{2,26},{10... | collective-permute-start | bytes 491528 | tf_op jit(solution)/shard_map/ppermute | solution.py:70
  130.5 7.2 %collective-permute-start.39 = (bf16[192,640]{1,0:T(8,128)(2,1)S(1)}, bf16[192,640]{1,0:T(8,128)(2,1)S(1)}, u32[]{:S(2)}, u32[]{:S(2)}) collective-permute-start(bf16[192,640]{1,0:T(8,128)(2,1)S(1)} %slice_bitcast_fusion.1), channel_id=1, source_target_pairs={{0,2},{1,3},{2,0},{3,1},{4,6},{5,7},{6,4},{7,5},{8,10},{9,11},{10,... | collective-permute-start | bytes 737288 | tf_op jit(solution)/shard_map/ppermute | solution.py:75
  137.7 2.3 %collective-permute-start.40 = (bf16[16,32,640]{2,1,0:T(8,128)(2,1)}, bf16[16,32,640]{2,1,0:T(8,128)(2,1)S(1)}, u32[]{:S(2)}, u32[]{:S(2)}) collective-permute-start(bf16[16,32,640]{2,1,0:T(8,128)(2,1)} %get-tuple-element.229), channel_id=1, source_target_pairs={{0,1},{1,0},{2,3},{3,2},{4,5},{5,4},{6,7},{7,6},{8,9},{9,8},{10,11... | collective-permute-start | bytes 1966088 | tf_op jit(solution)/shard_map/ppermute | solution.py:75
  141.3 18.9 %collective-permute-start.41 = (bf16[192,640]{1,0:T(8,128)(2,1)S(1)}, bf16[192,640]{1,0:T(8,128)(2,1)S(1)}, u32[]{:S(2)}, u32[]{:S(2)}) collective-permute-start(bf16[192,640]{1,0:T(8,128)(2,1)S(1)} %slice_bitcast_fusion), channel_id=1, source_target_pairs={{0,4},{1,5},{2,6},{3,7},{4,0},{5,1},{6,2},{7,3},{8,12},{9,13},{10,... | collective-permute-start | bytes 737288 | tf_op jit(solution)/shard_map/ppermute | solution.py:75
  144.1 16.1 %collective-permute-start.44 = (bf16[4,32,640]{2,1,0:T(8,128)(2,1)S(1)}, bf16[4,32,640]{2,1,0:T(8,128)(2,1)S(1)}, u32[]{:S(2)}, u32[]{:S(2)}) collective-permute-start(bf16[4,32,640]{2,1,0:T(8,128)(2,1)S(1)} %get-tuple-element.290), channel_id=1, source_target_pairs={{0,24},{8,16},{16,8},{24,0},{1,25},{9,17},{17,9},{25,1},{2,26},{10... | collective-permute-start | bytes 491528 | tf_op jit(solution)/shard_map/ppermute | solution.py:70
  145.8 14.4 %collective-permute-start.43 = (bf16[4,32,640]{2,1,0:T(8,128)(2,1)S(1)}, bf16[4,32,640]{2,1,0:T(8,128)(2,1)S(1)}, u32[]{:S(2)}, u32[]{:S(2)}) collective-permute-start(bf16[4,32,640]{2,1,0:T(8,128)(2,1)S(1)} %get-tuple-element.291), channel_id=1, source_target_pairs={{0,16},{8,24},{16,0},{24,8},{1,17},{9,25},{17,1},{25,9},{2,18},{10... | collective-permute-start | bytes 491528 | tf_op jit(solution)/shard_map/ppermute | solution.py:70
  147.1 13.1 %collective-permute-start.42 = (bf16[4,32,640]{2,1,0:T(8,128)(2,1)S(1)}, bf16[4,32,640]{2,1,0:T(8,128)(2,1)S(1)}, u32[]{:S(2)}, u32[]{:S(2)}) collective-permute-start(bf16[4,32,640]{2,1,0:T(8,128)(2,1)S(1)} %get-tuple-element.292), channel_id=1, source_target_pairs={{0,8},{8,0},{16,24},{24,16},{1,9},{9,1},{17,25},{25,17},{2,10},{10... | collective-permute-start | bytes 491528 | tf_op jit(solution)/shard_map/ppermute | solution.py:70
  160.3 4.4 %collective-permute-start.45 = (bf16[16,64,640]{2,1,0:T(8,128)(2,1)}, bf16[16,64,640]{2,1,0:T(8,128)(2,1)}, u32[]{:S(2)}, u32[]{:S(2)}) collective-permute-start(bf16[16,64,640]{2,1,0:T(8,128)(2,1)} %get-tuple-element.254), channel_id=1, source_target_pairs={{0,1},{1,0},{2,3},{3,2},{4,5},{5,4},{6,7},{7,6},{8,9},{9,8},{10,11... | collective-permute-start | bytes 3932168 | tf_op jit(solution)/shard_map/ppermute | solution.py:75
  161.3 2.7 %collective-permute-start.46 = (bf16[16,96]{1,0:T(8,128)(2,1)S(1)}, bf16[16,96]{1,0:T(8,128)(2,1)S(1)}, u32[]{:S(2)}, u32[]{:S(2)}) collective-permute-start(bf16[16,96]{1,0:T(8,128)(2,1)S(1)} %slice.251), channel_id=1, source_target_pairs={{0,1},{1,0},{2,3},{3,2},{4,5},{5,4},{6,7},{7,6},{8,9},{9,8},{10,11... | collective-permute-start | bytes 9224 | tf_op jit(solution)/shard_map/ppermute | solution.py:75
  161.3 3.2 %collective-permute-start.47 = (bf16[512,640]{1,0:T(8,128)(2,1)}, bf16[512,640]{1,0:T(8,128)(2,1)S(1)}, u32[]{:S(2)}, u32[]{:S(2)}) collective-permute-start(bf16[512,640]{1,0:T(8,128)(2,1)} %get-tuple-element.262), channel_id=1, source_target_pairs={{0,1},{1,0},{2,3},{3,2},{4,5},{5,4},{6,7},{7,6},{8,9},{9,8},{10,11... | collective-permute-start | bytes 1966088 | tf_op jit(solution)/shard_map/ppermute | solution.py:75
  161.9 7.3 %collective-permute-start.48 = (bf16[96,640]{1,0:T(8,128)(2,1)S(1)}, bf16[96,640]{1,0:T(8,128)(2,1)S(1)}, u32[]{:S(2)}, u32[]{:S(2)}) collective-permute-start(bf16[96,640]{1,0:T(8,128)(2,1)S(1)} %slice_bitcast_fusion.9), channel_id=1, source_target_pairs={{0,6},{1,7},{2,4},{3,5},{4,2},{5,3},{6,0},{7,1},{8,14},{9,15},{10,... | collective-permute-start | bytes 368648 | tf_op jit(solution)/shard_map/ppermute | solution.py:75
  169.2 7.2 %collective-permute-start.52 = (bf16[128,640]{1,0:T(8,128)(2,1)S(1)}, bf16[128,640]{1,0:T(8,128)(2,1)S(1)}, u32[]{:S(2)}, u32[]{:S(2)}) collective-permute-start(bf16[128,640]{1,0:T(8,128)(2,1)S(1)} %get-tuple-element.287), channel_id=1, source_target_pairs={{0,2},{1,3},{2,0},{3,1},{4,6},{5,7},{6,4},{7,5},{8,10},{9,11},{10,... | collective-permute-start | bytes 491528 | tf_op jit(solution)/shard_map/ppermute | solution.py:75
  170.2 9.7 %collective-permute-start.54 = (bf16[128,640]{1,0:T(8,128)(2,1)S(1)}, bf16[128,640]{1,0:T(8,128)(2,1)S(1)}, u32[]{:S(2)}, u32[]{:S(2)}) collective-permute-start(bf16[128,640]{1,0:T(8,128)(2,1)S(1)} %get-tuple-element.288), channel_id=1, source_target_pairs={{0,6},{1,7},{2,4},{3,5},{4,2},{5,3},{6,0},{7,1},{8,14},{9,15},{10,... | collective-permute-start | bytes 491528 | tf_op jit(solution)/shard_map/ppermute | solution.py:75
  171.7 14.5 %collective-permute-start.53 = (bf16[128,640]{1,0:T(8,128)(2,1)S(1)}, bf16[128,640]{1,0:T(8,128)(2,1)S(1)}, u32[]{:S(2)}, u32[]{:S(2)}) collective-permute-start(bf16[128,640]{1,0:T(8,128)(2,1)S(1)} %get-tuple-element.289), channel_id=1, source_target_pairs={{0,4},{1,5},{2,6},{3,7},{4,0},{5,1},{6,2},{7,3},{8,12},{9,13},{10,... | collective-permute-start | bytes 491528 | tf_op jit(solution)/shard_map/ppermute | solution.py:75
  172.8 13.5 %collective-permute-start.49 = (bf16[4,64,640]{2,1,0:T(8,128)(2,1)S(1)}, bf16[4,64,640]{2,1,0:T(8,128)(2,1)S(1)}, u32[]{:S(2)}, u32[]{:S(2)}) collective-permute-start(bf16[4,64,640]{2,1,0:T(8,128)(2,1)S(1)} %get-tuple-element.284), channel_id=1, source_target_pairs={{0,8},{8,0},{16,24},{24,16},{1,9},{9,1},{17,25},{25,17},{2,10},{10... | collective-permute-start | bytes 983048 | tf_op jit(solution)/shard_map/ppermute | solution.py:70
  174.4 14.4 %collective-permute-start.51 = (bf16[4,64,640]{2,1,0:T(8,128)(2,1)S(1)}, bf16[4,64,640]{2,1,0:T(8,128)(2,1)S(1)}, u32[]{:S(2)}, u32[]{:S(2)}) collective-permute-start(bf16[4,64,640]{2,1,0:T(8,128)(2,1)S(1)} %get-tuple-element.285), channel_id=1, source_target_pairs={{0,24},{8,16},{16,8},{24,0},{1,25},{9,17},{17,9},{25,1},{2,26},{10... | collective-permute-start | bytes 983048 | tf_op jit(solution)/shard_map/ppermute | solution.py:70
  176.4 13.8 %collective-permute-start.50 = (bf16[4,64,640]{2,1,0:T(8,128)(2,1)S(1)}, bf16[4,64,640]{2,1,0:T(8,128)(2,1)S(1)}, u32[]{:S(2)}, u32[]{:S(2)}) collective-permute-start(bf16[4,64,640]{2,1,0:T(8,128)(2,1)S(1)} %get-tuple-element.286), channel_id=1, source_target_pairs={{0,16},{8,24},{16,0},{24,8},{1,17},{9,25},{17,1},{25,9},{2,18},{10... | collective-permute-start | bytes 983048 | tf_op jit(solution)/shard_map/ppermute | solution.py:70
  190.5 7.1 %collective-permute-start.58 = (bf16[32,640]{1,0:T(8,128)(2,1)S(1)}, bf16[32,640]{1,0:T(8,128)(2,1)S(1)}, u32[]{:S(2)}, u32[]{:S(2)}) collective-permute-start(bf16[32,640]{1,0:T(8,128)(2,1)S(1)} %get-tuple-element.301), channel_id=1, source_target_pairs={{0,2},{1,3},{2,0},{3,1},{4,6},{5,7},{6,4},{7,5},{8,10},{9,11},{10,... | collective-permute-start | bytes 122888 | tf_op jit(solution)/shard_map/ppermute | solution.py:75
  191.8 8.3 %collective-permute-start.60 = (bf16[32,640]{1,0:T(8,128)(2,1)S(1)}, bf16[32,640]{1,0:T(8,128)(2,1)S(1)}, u32[]{:S(2)}, u32[]{:S(2)}) collective-permute-start(bf16[32,640]{1,0:T(8,128)(2,1)S(1)} %get-tuple-element.302), channel_id=1, source_target_pairs={{0,6},{1,7},{2,4},{3,5},{4,2},{5,3},{6,0},{7,1},{8,14},{9,15},{10,... | collective-permute-start | bytes 122888 | tf_op jit(solution)/shard_map/ppermute | solution.py:75
  193.2 8.3 %collective-permute-start.59 = (bf16[32,640]{1,0:T(8,128)(2,1)S(1)}, bf16[32,640]{1,0:T(8,128)(2,1)S(1)}, u32[]{:S(2)}, u32[]{:S(2)}) collective-permute-start(bf16[32,640]{1,0:T(8,128)(2,1)S(1)} %get-tuple-element.303), channel_id=1, source_target_pairs={{0,4},{1,5},{2,6},{3,7},{4,0},{5,1},{6,2},{7,3},{8,12},{9,13},{10,... | collective-permute-start | bytes 122888 | tf_op jit(solution)/shard_map/ppermute | solution.py:75
  194.1 14.5 %collective-permute-start.61 = (bf16[96,640]{1,0:T(8,128)(2,1)S(1)}, bf16[96,640]{1,0:T(8,128)(2,1)S(1)}, u32[]{:S(2)}, u32[]{:S(2)}) collective-permute-start(bf16[96,640]{1,0:T(8,128)(2,1)S(1)} %slice_bitcast_fusion.8), channel_id=1, source_target_pairs={{0,6},{1,7},{2,4},{3,5},{4,2},{5,3},{6,0},{7,1},{8,14},{9,15},{10,... | collective-permute-start | bytes 368648 | tf_op jit(solution)/shard_map/ppermute | solution.py:75
  195.7 7.1 %collective-permute-start.55 = (bf16[64,640]{1,0:T(8,128)(2,1)S(1)}, bf16[64,640]{1,0:T(8,128)(2,1)S(1)}, u32[]{:S(2)}, u32[]{:S(2)}) collective-permute-start(bf16[64,640]{1,0:T(8,128)(2,1)S(1)} %get-tuple-element.296), channel_id=1, source_target_pairs={{0,2},{1,3},{2,0},{3,1},{4,6},{5,7},{6,4},{7,5},{8,10},{9,11},{10,... | collective-permute-start | bytes 245768 | tf_op jit(solution)/shard_map/ppermute | solution.py:75
  197.6 6.3 %collective-permute-start.57 = (bf16[64,640]{1,0:T(8,128)(2,1)S(1)}, bf16[64,640]{1,0:T(8,128)(2,1)S(1)}, u32[]{:S(2)}, u32[]{:S(2)}) collective-permute-start(bf16[64,640]{1,0:T(8,128)(2,1)S(1)} %get-tuple-element.297), channel_id=1, source_target_pairs={{0,6},{1,7},{2,4},{3,5},{4,2},{5,3},{6,0},{7,1},{8,14},{9,15},{10,... | collective-permute-start | bytes 245768 | tf_op jit(solution)/shard_map/ppermute | solution.py:75
  200.1 6.7 %collective-permute-start.56 = (bf16[64,640]{1,0:T(8,128)(2,1)S(1)}, bf16[64,640]{1,0:T(8,128)(2,1)S(1)}, u32[]{:S(2)}, u32[]{:S(2)}) collective-permute-start(bf16[64,640]{1,0:T(8,128)(2,1)S(1)} %get-tuple-element.298), channel_id=1, source_target_pairs={{0,4},{1,5},{2,6},{3,7},{4,0},{5,1},{6,2},{7,3},{8,12},{9,13},{10,... | collective-permute-start | bytes 245768 | tf_op jit(solution)/shard_map/ppermute | solution.py:75
  (27 other events, 153.7 us)

commit v2 on v1

--- a/solution.py
+++ b/solution.py
@@ -199,7 +199,7 @@
     return jnp.concatenate([first * cosine + second * sine, second * cosine - first * sine], axis=1)
 
 
-def call_kernel(body, out_shapes, scratch, flops, inputs):
+def call_kernel(body, out_shapes, scratch, flops, inputs, mebibytes=24):
     whole = pl.BlockSpec(memory_space=pltpu.VMEM)
     return pl.pallas_call(
         body,
@@ -207,7 +207,7 @@
         in_specs=[whole] * len(inputs),
         out_specs=[whole] * len(out_shapes),
         scratch_shapes=[pltpu.VMEM(shape, dtype) for shape, dtype in scratch],
-        compiler_params=pltpu.CompilerParams(vmem_limit_bytes=52 * 1024 * 1024),
+        compiler_params=pltpu.CompilerParams(vmem_limit_bytes=mebibytes * 1024 * 1024),
         cost_estimate=pl.CostEstimate(flops=flops, bytes_accessed=20_000_000, transcendentals=0),
     )(*inputs)
 
@@ -322,14 +322,13 @@
 
 def feed_back_kernel(*refs):
     grads = refs[:4]
-    gate_ref, up_ref, inner_ref, pre_ref, wg_ref, wu_ref, wd_ref = refs[4:11]
-    part_refs = refs[11:15]
-    own_ref, other_ref = refs[15:17]
-    gffn_scr, ggate_scr, gup_scr = refs[17:]
+    gate_ref, up_ref, wg_ref, wu_ref, wd_ref = refs[4:9]
+    part_refs = refs[9:13]
+    gffn_ref, ggate_ref, gup_ref = refs[13:]
     tokens = grads[0].shape[0]
     for number, ref in enumerate(grads):
         at = slice(number * tokens, (number + 1) * tokens)
-        gffn_scr[at, :] = ref[...]
+        gffn_ref[at, :] = ref[...]
         grad_inner = dot_nt(ref[...], wd_ref[...])
         gate = gate_ref[at, :]
         square = gate * gate
@@ -340,19 +339,22 @@
         )
         grad_up = (grad_inner * curve).astype(BF)
         grad_gate = (grad_inner * up_ref[at, :] * slope).astype(BF)
-        ggate_scr[at, :] = grad_gate
-        gup_scr[at, :] = grad_up
+        ggate_ref[at, :] = grad_gate
+        gup_ref[at, :] = grad_up
         part_refs[number][...] = (dot_nn(grad_gate, wg_ref[...]) + dot_nn(grad_up, wu_ref[...])).astype(
             part_refs[number].dtype
         )
+
+
+def feed_weights_kernel(inner_ref, pre_ref, gffn_ref, ggate_ref, gup_ref, own_ref, other_ref):
     places, rows, width = own_ref.shape
     rows = rows // 3
     shape = (places, rows, width)
     for core, ref in enumerate((own_ref, other_ref)):
         span = slice(core * places * rows, (core + 1) * places * rows)
-        ref[:, :rows, :] = dot_tn(ggate_scr[:, span], pre_ref[...]).astype(BF).reshape(shape)
-        ref[:, rows : 2 * rows, :] = dot_tn(gup_scr[:, span], pre_ref[...]).astype(BF).reshape(shape)
-        ref[:, 2 * rows :, :] = dot_tn(inner_ref[:, span], gffn_scr[...]).astype(BF).reshape(shape)
+        ref[:, :rows, :] = dot_tn(ggate_ref[:, span], pre_ref[...]).astype(BF).reshape(shape)
+        ref[:, rows : 2 * rows, :] = dot_tn(gup_ref[:, span], pre_ref[...]).astype(BF).reshape(shape)
+        ref[:, 2 * rows :, :] = dot_tn(inner_ref[:, span], gffn_ref[...]).astype(BF).reshape(shape)
 
 
 def project_back_kernel(
@@ -431,8 +433,10 @@
         + jnp.sum(grad_normed[half:] * far_ref[...].astype(jnp.float32), axis=0, keepdims=True)
         + jnp.sum(grad_q * unit_ref[...], axis=0, keepdims=True)
     )
-    gnear_ref[...] = grad_normed[:half].astype(BF)
-    gfar_ref[...] = grad_normed[half:].astype(BF)
+    gnear_ref[:, :head_width] = grad_kraw[:half]
+    gnear_ref[:, head_width:] = grad_value[:half]
+    gfar_ref[:, :head_width] = grad_kraw[half:]
+    gfar_ref[:, head_width:] = grad_value[half:]
     gkv_scr[:head_width, :] = dot_tn(grad_kraw, normed_all_ref[...]).astype(BF)
     gkv_scr[head_width:, :] = dot_tn(grad_value, normed_all_ref[...]).astype(BF)
     grad_wq = dot_tn(gqraw_scr[...], normed_ref[...]).astype(BF)
@@ -448,7 +452,6 @@
         ref[:, rows_q : rows_q + rows_kv, :] = held_kv[
             core * places * rows_kv : (core + 1) * places * rows_kv
         ].reshape(places, rows_kv, width)
-        ref[:, rows_q + rows_kv :, :] = jnp.zeros((places, 16, width), BF)
 
 
 def shards_plain(
@@ -775,7 +778,7 @@
     key_index = natural_rows(place ^ (2 * seq_zed + seq_core), block, groups).reshape(1, seq_len)
     row_index = natural_rows(place[None], block, groups).reshape(tokens, 1)
 
-    last_rows = jnp.zeros((16, width), BF).at[0, :scale_part].set(norm_scales)
+    last_rows = jnp.zeros((8, width), BF).at[0, :scale_part].set(norm_scales)
     last_rows = last_rows.at[1, :tokens].set((posit // 64).astype(BF))
     last_rows = last_rows.at[2, :tokens].set((posit % 64).astype(BF))
     first = jnp.concatenate([w_query, w_key, w_value, last_rows], axis=0)
@@ -802,13 +805,14 @@
     other = swap_ctx(first, 1)
     far = swap_ctx(near, 1)
     out_own = gather_over(w_output[None], swap_z, chips)
+    other, far, out_own, feed = tie((other, far, out_own, feed))
     scale_rows = jnp.concatenate([first[:, last, :scale_part], other[:, last, :scale_part]], axis=0)
     full_scales = reorder(order_s, scale_rows).reshape(-1)
-    other, far, out_own, feed, full_scales = tie((other, far, out_own, feed, full_scales))
     scale_in, scale_attn, scale_pre, scale_post, scale_query, scale_key = [
         scale[None] for scale in split_scales(full_scales, width, head_width)
     ]
     feed_z2 = swap_z(feed, 2)
+    feed_z1 = swap_z(feed, 1)
     out_own = gather_over(out_own[None], swap_dp, count_dp).reshape((owners // 2, rows_q, width))
     (w_q, w_kv, normed, normed_all, query_raw, key_raw, query_bf, key_bf, value_bf, attn_bf, lse) = (
         call_kernel(
@@ -832,13 +836,14 @@
                 unit_in, near, far, first, other, order_q, order_kv, scale_in, scale_query, scale_key,
                 cos_all, sine_all, key_index, row_index,
             ),
+            mebibytes=52,
         )
     )
-    attn_bf, feed_z2, out_own, feed = tie((attn_bf, feed_z2, out_own, feed))
+    attn_bf, feed_z1, feed_z2, out_own, feed = tie((attn_bf, feed_z1, feed_z2, out_own, feed))
     out_other = swap_ctx(out_own, 1)
-    feed_z1 = swap_z(feed, 1)
     feed_z3 = swap_z(feed, 3)
     feed_c0 = swap_ctx(feed, 1)
+    feed_c1 = swap_ctx(feed_z1, 1)
     feed_c2 = swap_ctx(feed_z2, 1)
     held_out, ahead, projected, middle, pre = call_kernel(
         project_kernel,
@@ -854,8 +859,7 @@
         (attn_bf, order_q, out_own, out_other, resid, scale_attn, scale_pre),
     )
     pres = swaps(pre, swap_dp)
-    pre, pres, feed_z1, feed_z3, feed_c0, feed_c2 = tie((pre, pres, feed_z1, feed_z3, feed_c0, feed_c2))
-    feed_c1 = swap_ctx(feed_z1, 1)
+    pre, pres, feed_z3, feed_c0, feed_c1, feed_c2 = tie((pre, pres, feed_z3, feed_c0, feed_c1, feed_c2))
     feed_c3 = swap_ctx(feed_z3, 1)
     part_shapes = [((tokens, width), f32)] + [((tokens, width), BF)] * 3
     all_tokens = count_dp * tokens
@@ -883,18 +887,25 @@
         100_000_000,
         [parts[0]] + comes + [middle, grad_out[0], scale_post],
     )
+    gate, up, inner, pre_all, w_g, w_u, w_d = kept
     outs = call_kernel(
         feed_back_kernel,
-        part_shapes + [((chips, 3 * rows_f, width), BF)] * 2,
-        [((all_tokens, width), BF), ((all_tokens, hidden), BF), ((all_tokens, hidden), BF)],
-        6_000_000_000,
-        [grad_ffn] + swaps(grad_ffn, swap_dp) + list(kept),
-    )
-    parts, (g_feed, g_feed_far) = outs[:4], outs[4:]
+        part_shapes + [((all_tokens, width), BF), ((all_tokens, hidden), BF), ((all_tokens, hidden), BF)],
+        [],
+        3_000_000_000,
+        [grad_ffn] + swaps(grad_ffn, swap_dp) + [gate, up, w_g, w_u, w_d],
+    )
+    parts, back = outs[:4], outs[4:]
     comes = [swap_dp(parts[bits], bits) for bits in range(1, 4)]
+    g_feed, g_feed_far = call_kernel(
+        feed_weights_kernel,
+        [((chips, 3 * rows_f, width), BF)] * 2,
+        [],
+        3_000_000_000,
+        [inner, pre_all] + list(back),
+    )
+    g_feed, g_feed_far, comes = tie((g_feed, g_feed_far, comes))
     g_feed = add_bf16(g_feed, swap_ctx(g_feed_far, 1)).astype(BF)
-    g_feed, comes = tie((g_feed, comes))
-    feed_come1 = swap_z(g_feed[1], 1)
     grad_resid_a, grad_attn, g_out, g_out_far, grad_s_attn, grad_s_pre = call_kernel(
         project_back_kernel,
         [
@@ -911,20 +922,18 @@
         + comes
         + [grad_out[0], projected, middle, held_out, ahead, order_q, scale_attn, scale_pre],
     )
-    grad_resid_a, grad_attn, g_out, g_out_far, grad_s_attn, grad_s_pre, feed_come1, g_feed = tie(
-        (grad_resid_a, grad_attn, g_out, g_out_far, grad_s_attn, grad_s_pre, feed_come1, g_feed)
-    )
     g_out = add_bf16(g_out, swap_ctx(g_out_far, 1)).astype(BF).reshape(count_dp, chips, rows_q, width)
     g_out, g_feed, grad_attn = tie((g_out, g_feed, grad_attn))
+    feed_come1 = swap_z(g_feed[1], 1)
     feed_come2 = swap_z(g_feed[2], 2)
     out_comes = [swap_dp(g_out[bits], bits) for bits in range(1, 4)]
     (packed, packed_far, g_near, g_far, grad_normed_q, grad_s_in, grad_s_query, grad_s_key) = call_kernel(
         attend_back_kernel,
         [
-            (first.shape, BF),
-            (first.shape, BF),
-            (near.shape, BF),
-            (far.shape, BF),
+            ((owners // 2, last, width), BF),
+            ((owners // 2, last, width), BF),
+            ((seq_len // 2, 2 * head_width), BF),
+            ((seq_len // 2, 2 * head_width), BF),
             ((tokens, width), f32),
             ((1, width), f32),
             ((1, head_width), f32),
@@ -944,26 +953,29 @@
             scale_query, scale_key, cos_all, sine_all, key_index, row_index, normed, normed_all,
             unit_in, near, far, order_q, order_kv,
         ),
+        mebibytes=24,
     )
     back = (packed, packed_far, g_near, g_far, grad_normed_q, grad_s_in, grad_s_query, grad_s_key)
-    back, feed_come2, out_comes, g_out, g_feed = tie((back, feed_come2, out_comes, g_out, g_feed))
+    back, feed_come1, feed_come2, out_comes, g_out, g_feed = tie(
+        (back, feed_come1, feed_come2, out_comes, g_out, g_feed)
+    )
     packed, packed_far, g_near, g_far, grad_normed_q, grad_s_in, grad_s_query, grad_s_key = back
     grad_scales = jnp.concatenate(
         [grad_s_in, grad_s_attn, grad_s_pre, grad_s_post, grad_s_query, grad_s_key], axis=1
     ).reshape(owners, scale_part)
     scales_back = reorder_back(order_s, grad_scales)
     scale_sum = add_bf16(scales_back[: owners // 2], swap_ctx(scales_back[owners // 2 :], 1))
-    scale_sum = jnp.pad(
-        scale_sum[:, None], ((0, 0), (last, packed.shape[1] - last - 1), (0, width - scale_part))
-    )
-    packed = (add_bf16(packed, swap_ctx(packed_far, 1)) + scale_sum).astype(BF)
+    scale_sum = jnp.pad(scale_sum[:, None], ((0, 0), (last, 7), (0, width - scale_part)))
+    packed = jnp.pad(add_bf16(packed, swap_ctx(packed_far, 1)), ((0, 0), (0, 8), (0, 0)))
+    packed = (packed + scale_sum).astype(BF)
     feed_come3 = swap_z(g_feed[3, : 3 * rows_f // 2], 3)
-    far_sum = add_bf16(g_near, swap_ctx(g_far, 1)).astype(BF).reshape(chips, tokens, width)
+    far_sum = add_bf16(g_near, swap_ctx(g_far, 1)).astype(BF).reshape(chips, tokens, 2 * head_width)
     out_sum = add_bf16(g_out[0], *out_comes).astype(BF)
     packed, far_sum, out_sum, g_feed, feed_come3 = tie((packed, far_sum, out_sum, g_feed, feed_come3))
     packed = scatter_over(packed.reshape((count_dp, chips) + packed.shape[1:]), swap_dp, count_dp)
-    own_normed = scatter_over(far_sum, swap_z, chips) + grad_normed_q
-    packed, own_normed, out_sum, g_feed = tie((packed.astype(BF), own_normed, out_sum, g_feed))
+    own_kv = scatter_over(far_sum, swap_z, chips).astype(BF)
+    packed, own_kv, out_sum, g_feed = tie((packed.astype(BF), own_kv, out_sum, g_feed))
+    own_normed = jnp.dot(own_kv, w_kv, preferred_element_type=jnp.float32) + grad_normed_q
     feed_come3 = jnp.concatenate([feed_come3, swap_z(g_feed[3, 3 * rows_f // 2 :], 3)], axis=0)
     own_feed = add_bf16(g_feed[0], feed_come1, feed_come2, feed_come3)
     own_output = scatter_over(out_sum, swap_z, chips)

time: 210 us -> 192 us (0.914)
  Pallas kernels: 45.7 us -> 28.5 us
  waiting for transfers between devices: 67 us -> 64.2 us
  other arithmetic: 18.4 us -> 15.7 us
  starting transfers between devices: 67.6 us -> 69.8 us
    pallas_call x7 -> x8, Pallas kernels: 45.7 us -> 28.5 us  [call_kernel(): pl.pallas_call(body, out_shape=[jax.ShapeDtypeStruct(shape, dtype) for sh...]
    ppermute x38, starting transfers between devices: 37.8 us -> 40.3 us  [swap_ctx(): lax.ppermute(block, 'ctx', [(place, place ^ bits) for place in range(coun...]
    unnamed x60 -> x70, local copies, waits for them, and re-layouts: 4.37 us -> 4.49 us
  transfers between devices with their start and end apart: 62 -> 62, of which waited for: 31 -> 29; matrix products, arithmetic and copies ran while one was open for 9% -> 8% of each run, Pallas kernels for 15% -> 12%
where the time goes in v2:
time: 192 us
  starting transfers between devices  69.8 us (36%)
  waiting for transfers between devices  64.2 us (33%)
  Pallas kernels  28.5 us (15%)
  other arithmetic  15.7 us (8%)
  local copies, waits for them, and re-layouts  11.2 us (6%)
    ppermute x38, starting transfers between devices, swap_ctx(): lax.ppermute(block, 'ctx', [(place, place ^ bits) for place in range(coun...  40.3 us
    ppermute x38, waiting for transfers between devices, swap_ctx(): lax.ppermute(block, 'ctx', [(place, place ^ bits) for place in range(coun...  36.6 us
    ppermute x24, starting transfers between devices, swap_dp(): lax.ppermute(block, 'dp', [(place, place ^ bits) for place in range(count)])  29.4 us
    pallas_call x8, Pallas kernels, call_kernel(): pl.pallas_call(body, out_shape=[jax.ShapeDtypeStruct(shape, dtype) for sh...  28.5 us
    ppermute x24, waiting for transfers between devices, swap_dp(): lax.ppermute(block, 'dp', [(place, place ^ bits) for place in range(count)])  27.6 us
    unnamed x70, local copies, waits for them, and re-layouts  4.49 us
  transfers between devices with their start and end apart: 62, of which 29 were waited for; matrix products, arithmetic and copies ran while one was open for 8% of the time, Pallas kernels for 12%

profile of v2, /device:TPU:0, one launch (start us, length us, event | category | flops | bytes accessed | tf_op | source)
XLA Modules:
  0.0 191.5 jit_solution(13158517713653194874)
XLA Ops:
  3.1 5.1 %collective-permute-start.2 = (bf16[1,56,640]{2,1,0:T(8,128)(2,1)S(1)}, bf16[1,56,640]{2,1,0:T(8,128)(2,1)S(1)}, u32[]{:S(2)}, u32[]{:S(2)}) collective-permute-start(bf16[1,56,640]{2,1,0:T(8,128)(2,1)S(1)} %maximum_bitcast_fusion), channel_id=1, source_target_pairs={{0,6},{1,7},{2,4},{3,5},{4,2},{5,3},{6,0},{7,1},{8,14},{9,15},{10,... | collective-permute-start | bytes 215048 | tf_op jit(solution)/shard_map/ppermute | solution.py:75
  12.3 2.2 %fusion.order_q_ref.order_ref = bf16[1024,1024]{1,0:T(8,128)(2,1)} fusion(s32[1024]{0:T(1024)S(1)} %add.386), kind=kLoop, calls=%fused_computation.1 | loop fusion | flops 2097152 | bytes 2101248 | tf_op jit(solution)/shard_map/convert_element_type | solution.py:158
  14.7 3.8 %collective-permute-start.8 = (bf16[1,128,640]{2,1,0:T(8,128)(2,1)S(1)}, bf16[1,128,640]{2,1,0:T(8,128)(2,1)S(1)}, u32[]{:S(2)}, u32[]{:S(2)}) collective-permute-start(bf16[1,128,640]{2,1,0:T(8,128)(2,1)S(1)} %bitcast.115), channel_id=1, source_target_pairs={{0,6},{1,7},{2,4},{3,5},{4,2},{5,3},{6,0},{7,1},{8,14},{9,15},{10,... | collective-permute-start | bytes 491528 | tf_op jit(solution)/shard_map/ppermute | solution.py:75
  19.2 2.5 %collective-permute-start.5 = (bf16[1,4,56,640]{3,2,1,0:T(8,128)(2,1)S(1)}, bf16[1,4,56,640]{3,2,1,0:T(8,128)(2,1)S(1)}, u32[]{:S(2)}, u32[]{:S(2)}) collective-permute-start(bf16[1,4,56,640]{3,2,1,0:T(8,128)(2,1)S(1)} %bitcast.104), channel_id=1, source_target_pairs={{0,24},{8,16},{16,8},{24,0},{1,25},{9,17},{17,9},{25,1},{2,26},{10... | collective-permute-start | bytes 860168 | tf_op jit(solution)/shard_map/ppermute | solution.py:70
  22.3 1.5 collective-permute-done.8
  23.7 1.5 collective-permute-start.3
  25.3 3.1 %multiply_sine_fusion = (f32[1024,128]{1,0:T(8,128)}, f32[1024,128]{1,0:T(8,128)}) fusion(f32[128]{0:T(128)S(1)} %multiply_power_fusion, f32[1024]{0:T(1024)S(1)} %bitcast.125), kind=kLoop, calls=%fused_computation.13 | loop fusion | flops 131072 | bytes 1053184 | tf_op jit(solution)/shard_map/sin | solution.py:799
  28.4 4.3 %collective-permute-done.7 = bf16[1,128,640]{2,1,0:T(8,128)(2,1)S(1)} collective-permute-done((bf16[1,128,640]{2,1,0:T(8,128)(2,1)S(1)}, bf16[1,128,640]{2,1,0:T(8,128)(2,1)S(1)}, u32[]{:S(2)}, u32[]{:S(2)}) %collective-permute-start.7) | collective-permute-done | bytes 163872 | tf_op jit(solution)/shard_map/ppermute | solution.py:75
  32.8 2.0 %collective-permute-done.4 = bf16[1,4,56,640]{3,2,1,0:T(8,128)(2,1)S(1)} collective-permute-done((bf16[1,4,56,640]{3,2,1,0:T(8,128)(2,1)S(1)}, bf16[1,4,56,640]{3,2,1,0:T(8,128)(2,1)S(1)}, u32[]{:S(2)}, u32[]{:S(2)}) %collective-permute-start.4) | collective-permute-done | bytes 286752 | tf_op jit(solution)/shard_map/ppermute | solution.py:70
  35.7 3.5 %collective-permute-start.14 = (bf16[1,32,640]{2,1,0:T(8,128)(2,1)S(1)}, bf16[1,32,640]{2,1,0:T(8,128)(2,1)S(1)}, u32[]{:S(2)}, u32[]{:S(2)}) collective-permute-start(bf16[1,32,640]{2,1,0:T(8,128)(2,1)S(1)} %bitcast.119), channel_id=1, source_target_pairs={{0,6},{1,7},{2,4},{3,5},{4,2},{5,3},{6,0},{7,1},{8,14},{9,15},{10,... | collective-permute-start | bytes 122888 | tf_op jit(solution)/shard_map/ppermute | solution.py:75
  39.2 1.2 collective-permute-start.13
  40.5 1.2 collective-permute-done.14
  41.7 2.5 %collective-permute-done.13 = bf16[1,32,640]{2,1,0:T(8,128)(2,1)S(1)} collective-permute-done((bf16[1,32,640]{2,1,0:T(8,128)(2,1)S(1)}, bf16[1,32,640]{2,1,0:T(8,128)(2,1)S(1)}, u32[]{:S(2)}, u32[]{:S(2)}) %collective-permute-start.13) | collective-permute-done | bytes 40992 | tf_op jit(solution)/shard_map/ppermute | solution.py:75
  45.7 2.4 %collective-permute-start.19 = (bf16[1,4,32,640]{3,2,1,0:T(8,128)(2,1)S(1)}, bf16[1,4,32,640]{3,2,1,0:T(8,128)(2,1)S(1)}, u32[]{:S(2)}, u32[]{:S(2)}) collective-permute-start(bf16[1,4,32,640]{3,2,1,0:T(8,128)(2,1)S(1)} %bitcast.111), channel_id=1, source_target_pairs={{0,24},{8,16},{16,8},{24,0},{1,25},{9,17},{17,9},{25,1},{2,26},{10... | collective-permute-start | bytes 491528 | tf_op jit(solution)/shard_map/ppermute | solution.py:70
  49.2 1.6 collective-permute-start.16
  50.8 1.7 collective-permute-start.15
  52.5 10.6 %shard_map.186 = (bf16[1024,640]{1,0:T(8,128)(2,1)}, bf16[512,640]{1,0:T(8,128)(2,1)}, bf16[128,640]{1,0:T(8,128)(2,1)S(1)}, bf16[1024,640]{1,0:T(8,128)(2,1)}, ...) custom-call(f32[128,640]{1,0:T(8,128)S(1)} %get-tuple-element.277.un, ...), custom_call_target="tpu_custom_call" | custom-call | flops 12000000000 | bytes 20000000 | tf_op jit(solution)/shard_map/pallas_call | solution.py:204
  65.8 1.1 collective-permute-start.24
  67.9 2.4 %collective-permute-start.23 = (bf16[128,640]{1,0:T(8,128)(2,1)S(1)}, bf16[128,640]{1,0:T(8,128)(2,1)S(1)}, u32[]{:S(2)}, u32[]{:S(2)}) collective-permute-start(bf16[128,640]{1,0:T(8,128)(2,1)S(1)} %get-tuple-element.183.refs_0_), channel_id=1, source_target_pairs={{0,24},{8,16},{16,8},{24,0},{1,25},{9,17},{17,9},{25,1},{2,26},{10... | collective-permute-start | bytes 491528 | tf_op jit(solution)/shard_map/ppermute | solution.py:70
  71.4 4.2 %collective-permute-done.24.refs_7_ = bf16[192,640]{1,0:T(8,128)(2,1)S(1)} collective-permute-done((bf16[192,640]{1,0:T(8,128)(2,1)S(1)}, bf16[192,640]{1,0:T(8,128)(2,1)S(1)}, u32[]{:S(2)}, u32[]{:S(2)}) %collective-permute-start.24) | collective-permute-done | bytes 245792 | tf_op jit(solution)/shard_map/ppermute | solution.py:75
  75.9 2.6 %collective-permute-done.22.refs_2_ = bf16[128,640]{1,0:T(8,128)(2,1)S(1)} collective-permute-done((bf16[128,640]{1,0:T(8,128)(2,1)S(1)}, bf16[128,640]{1,0:T(8,128)(2,1)S(1)}, u32[]{:S(2)}, u32[]{:S(2)}) %collective-permute-start.22) | collective-permute-done | bytes 163872 | tf_op jit(solution)/shard_map/ppermute | solution.py:70
  78.7 1.5 collective-permute-done.28.refs_11_
  80.2 2.7 %shard_map.188 = (f32[128,640]{1,0:T(8,128)S(1)}, bf16[128,640]{1,0:T(8,128)(2,1)S(1)}, bf16[128,640]{1,0:T(8,128)(2,1)S(1)}, bf16[128,640]{1,0:T(8,128)(2,1)S(1...) custom-call(bf16[128,640]{1,0:T(8,128)(2,1)S(1)} %get-tuple-element., ...), custom_call_target="tpu_custom_call" | custom-call | flops 3000000000 | bytes 20000000 | tf_op jit(solution)/shard_map/pallas_call | solution.py:204
  82.9 1.5 collective-permute-start.29
  85.1 1.3 collective-permute-start.31
  86.4 3.6 %collective-permute-done.29.come1_ref = bf16[128,640]{1,0:T(8,128)(2,1)S(1)} collective-permute-done((bf16[128,640]{1,0:T(8,128)(2,1)S(1)}, bf16[128,640]{1,0:T(8,128)(2,1)S(1)}, u32[]{:S(2)}, u32[]{:S(2)}) %collective-permute-start.29) | collective-permute-done | bytes 163872 | tf_op jit(solution)/shard_map/ppermute | solution.py:70
  90.0 3.8 %collective-permute-done.30.come2_ref = bf16[128,640]{1,0:T(8,128)(2,1)S(1)} collective-permute-done((bf16[128,640]{1,0:T(8,128)(2,1)S(1)}, bf16[128,640]{1,0:T(8,128)(2,1)S(1)}, u32[]{:S(2)}, u32[]{:S(2)}) %collective-permute-start.30) | collective-permute-done | bytes 163872 | tf_op jit(solution)/shard_map/ppermute | solution.py:70
  94.7 1.5 collective-permute-start.34
  96.9 1.4 collective-permute-start.32
  98.2 4.4 %collective-permute-done.34.refs_3_ = bf16[128,640]{1,0:T(8,128)(2,1)S(1)} collective-permute-done((bf16[128,640]{1,0:T(8,128)(2,1)S(1)}, bf16[128,640]{1,0:T(8,128)(2,1)S(1)}, u32[]{:S(2)}, u32[]{:S(2)}) %collective-permute-start.34) | collective-permute-done | bytes 163872 | tf_op jit(solution)/shard_map/ppermute | solution.py:70
  102.6 1.7 collective-permute-done.33.refs_2_
  104.4 2.8 %shard_map.190 = (f32[128,640]{1,0:T(8,128)S(1)}, bf16[128,640]{1,0:T(8,128)(2,1)S(1)}, bf16[128,640]{1,0:T(8,128)(2,1)S(1)}, bf16[128,640]{1,0:T(8,128)(2,1)S(1...) custom-call(bf16[128,640]{1,0:T(8,128)(2,1)S(1)} %get-tuple-element.197.refs_0_, ...), custom_call_target="tpu_custom_call" | custom-call | flops 3000000000 | bytes 20000000 | tf_op jit(solution)/shard_map/pallas_call | solution.py:204
  108.0 1.2 collective-permute-start.36
  109.2 1.5 collective-permute-start.37
  110.7 1.4 shard_map.191
  112.2 2.2 %collective-permute-done.35.come1_ref = bf16[128,640]{1,0:T(8,128)(2,1)S(1)} collective-permute-done((bf16[128,640]{1,0:T(8,128)(2,1)S(1)}, bf16[128,640]{1,0:T(8,128)(2,1)S(1)}, u32[]{:S(2)}, u32[]{:S(2)}) %collective-permute-start.35) | collective-permute-done | bytes 163872 | tf_op jit(solution)/shard_map/ppermute | solution.py:70
  114.4 2.7 %collective-permute-done.36.come2_ref = bf16[128,640]{1,0:T(8,128)(2,1)S(1)} collective-permute-done((bf16[128,640]{1,0:T(8,128)(2,1)S(1)}, bf16[128,640]{1,0:T(8,128)(2,1)S(1)}, u32[]{:S(2)}, u32[]{:S(2)}) %collective-permute-start.36) | collective-permute-done | bytes 163872 | tf_op jit(solution)/shard_map/ppermute | solution.py:70
  117.1 1.9 shard_map.192
  119.6 1.7 collective-permute-done.38
  122.3 1.3 collective-permute-start.44
  123.6 1.5 collective-permute-start.43
  126.0 1.7 collective-permute-start.41
  127.7 1.4 collective-permute-start.40
  129.2 7.2 %shard_map.193 = (bf16[16,48,640]{2,1,0:T(8,128)(2,1)S(1)}, bf16[16,48,640]{2,1,0:T(8,128)(2,1)S(1)}, bf16[512,512]{1,0:T(8,128)(2,1)S(1)}, bf16[512,512]{1,0:T(...) custom-call(bf16[128,1024]{1,0:T(8,128)(2,1)S(1)} %get-tuple-element, ...), custom_call_target="tpu_custom_call" | custom-call | flops 12000000000 | bytes 20000000 | tf_op jit(solution)/shard_map/pallas_call | solution.py:204
  138.2 1.4 collective-permute-done.41
  142.4 2.3 %collective-permute-start.48 = (bf16[96,640]{1,0:T(8,128)(2,1)S(1)}, bf16[96,640]{1,0:T(8,128)(2,1)S(1)}, u32[]{:S(2)}, u32[]{:S(2)}) collective-permute-start(bf16[96,640]{1,0:T(8,128)(2,1)S(1)} %slice_bitcast_fusion.9), channel_id=1, source_target_pairs={{0,6},{1,7},{2,4},{3,5},{4,2},{5,3},{6,0},{7,1},{8,14},{9,15},{10,... | collective-permute-start | bytes 368648 | tf_op jit(solution)/shard_map/ppermute | solution.py:75
  144.7 1.2 fusion.7
  146.5 3.5 %collective-permute-done.48 = bf16[96,640]{1,0:T(8,128)(2,1)S(1)} collective-permute-done((bf16[96,640]{1,0:T(8,128)(2,1)S(1)}, bf16[96,640]{1,0:T(8,128)(2,1)S(1)}, u32[]{:S(2)}, u32[]{:S(2)}) %collective-permute-start.48) | collective-permute-done | bytes 122912 | tf_op jit(solution)/shard_map/ppermute | solution.py:75
  150.0 1.4 collective-permute-start.52
  152.3 1.3 collective-permute-start.53
  154.7 1.3 collective-permute-start.51
  156.0 1.2 collective-permute-start.50
  157.2 2.5 %collective-permute-done.54 = bf16[128,512]{1,0:T(8,128)(2,1)S(1)} collective-permute-done((bf16[128,512]{1,0:T(8,128)(2,1)S(1)}, bf16[128,512]{1,0:T(8,128)(2,1)S(1)}, u32[]{:S(2)}, u32[]{:S(2)}) %collective-permute-start.54) | collective-permute-done | bytes 131104 | tf_op jit(solution)/shard_map/ppermute | solution.py:75
  159.7 5.2 %collective-permute-done.53 = bf16[128,512]{1,0:T(8,128)(2,1)S(1)} collective-permute-done((bf16[128,512]{1,0:T(8,128)(2,1)S(1)}, bf16[128,512]{1,0:T(8,128)(2,1)S(1)}, u32[]{:S(2)}, u32[]{:S(2)}) %collective-permute-start.53) | collective-permute-done | bytes 131104 | tf_op jit(solution)/shard_map/ppermute | solution.py:75
  165.1 2.8 %collective-permute-done.51 = bf16[4,56,640]{2,1,0:T(8,128)(2,1)S(1)} collective-permute-done((bf16[4,56,640]{2,1,0:T(8,128)(2,1)S(1)}, bf16[4,56,640]{2,1,0:T(8,128)(2,1)S(1)}, u32[]{:S(2)}, u32[]{:S(2)}) %collective-permute-start.51) | collective-permute-done | bytes 286752 | tf_op jit(solution)/shard_map/ppermute | solution.py:70
  167.8 1.4 collective-permute-done.50
  170.7 1.7 collective-permute-start.58
  172.4 2.5 %collective-permute-start.60 = (bf16[32,640]{1,0:T(8,128)(2,1)S(1)}, bf16[32,640]{1,0:T(8,128)(2,1)S(1)}, u32[]{:S(2)}, u32[]{:S(2)}) collective-permute-start(bf16[32,640]{1,0:T(8,128)(2,1)S(1)} %get-tuple-element.298), channel_id=1, source_target_pairs={{0,6},{1,7},{2,4},{3,5},{4,2},{5,3},{6,0},{7,1},{8,14},{9,15},{10,... | collective-permute-start | bytes 122888 | tf_op jit(solution)/shard_map/ppermute | solution.py:75
  174.8 1.5 collective-permute-start.61
  176.4 2.0 %collective-permute-start.55 = (bf16[56,640]{1,0:T(8,128)(2,1)S(1)}, bf16[56,640]{1,0:T(8,128)(2,1)S(1)}, u32[]{:S(2)}, u32[]{:S(2)}) collective-permute-start(bf16[56,640]{1,0:T(8,128)(2,1)S(1)} %get-tuple-element.292), channel_id=1, source_target_pairs={{0,2},{1,3},{2,0},{3,1},{4,6},{5,7},{6,4},{7,5},{8,10},{9,11},{10,... | collective-permute-start | bytes 215048 | tf_op jit(solution)/shard_map/ppermute | solution.py:75
  179.3 1.4 collective-permute-start.57
  180.9 1.8 collective-permute-done.59
  183.3 2.3 %collective-permute-done.57 = bf16[56,640]{1,0:T(8,128)(2,1)S(1)} collective-permute-done((bf16[56,640]{1,0:T(8,128)(2,1)S(1)}, bf16[56,640]{1,0:T(8,128)(2,1)S(1)}, u32[]{:S(2)}, u32[]{:S(2)}) %collective-permute-start.57) | collective-permute-done | bytes 71712 | tf_op jit(solution)/shard_map/ppermute | solution.py:75
  185.5 2.3 %collective-permute-done.56 = bf16[56,640]{1,0:T(8,128)(2,1)S(1)} collective-permute-done((bf16[56,640]{1,0:T(8,128)(2,1)S(1)}, bf16[56,640]{1,0:T(8,128)(2,1)S(1)}, u32[]{:S(2)}, u32[]{:S(2)}) %collective-permute-start.56) | collective-permute-done | bytes 71712 | tf_op jit(solution)/shard_map/ppermute | solution.py:75
  (216 shorter events, 36.3 us)
Async XLA Ops:
  3.1 11.4 %collective-permute-start.2 = (bf16[1,56,640]{2,1,0:T(8,128)(2,1)S(1)}, bf16[1,56,640]{2,1,0:T(8,128)(2,1)S(1)}, u32[]{:S(2)}, u32[]{:S(2)}) collective-permute-start(bf16[1,56,640]{2,1,0:T(8,128)(2,1)S(1)} %maximum_bitcast_fusion), channel_id=1, source_target_pairs={{0,6},{1,7},{2,4},{3,5},{4,2},{5,3},{6,0},{7,1},{8,14},{9,15},{10,... | collective-permute-start | bytes 215048 | tf_op jit(solution)/shard_map/ppermute | solution.py:75
  8.1 6.4 %collective-permute-start.1 = (bf16[1,56,640]{2,1,0:T(8,128)(2,1)S(1)}, bf16[1,56,640]{2,1,0:T(8,128)(2,1)S(1)}, u32[]{:S(2)}, u32[]{:S(2)}) collective-permute-start(bf16[1,56,640]{2,1,0:T(8,128)(2,1)S(1)} %maximum_bitcast_fusion), channel_id=1, source_target_pairs={{0,4},{1,5},{2,6},{3,7},{4,0},{5,1},{6,2},{7,3},{8,12},{9,13},{10,... | collective-permute-start | bytes 215048 | tf_op jit(solution)/shard_map/ppermute | solution.py:75
  8.1 6.4 %collective-permute-start = (bf16[1,56,640]{2,1,0:T(8,128)(2,1)S(1)}, bf16[1,56,640]{2,1,0:T(8,128)(2,1)S(1)}, u32[]{:S(2)}, u32[]{:S(2)}) collective-permute-start(bf16[1,56,640]{2,1,0:T(8,128)(2,1)S(1)} %maximum_bitcast_fusion), channel_id=1, source_target_pairs={{0,2},{1,3},{2,0},{3,1},{4,6},{5,7},{6,4},{7,5},{8,10},{9,11},{10,... | collective-permute-start | bytes 215048 | tf_op jit(solution)/shard_map/ppermute | solution.py:75
  14.6 7.1 %collective-permute-start.9 = (bf16[4,8,640]{2,1,0:T(8,128)(2,1)S(1)}, bf16[4,8,640]{2,1,0:T(8,128)(2,1)S(1)}, u32[]{:S(2)}, u32[]{:S(2)}) collective-permute-start(bf16[4,8,640]{2,1,0:T(8,128)(2,1)S(1)} %get-tuple-element.296), channel_id=1, source_target_pairs={{0,1},{1,0},{2,3},{3,2},{4,5},{5,4},{6,7},{7,6},{8,9},{9,8},{10,11... | collective-permute-start | bytes 122888 | tf_op jit(solution)/shard_map/ppermute | solution.py:75
  14.7 9.1 %collective-permute-start.8 = (bf16[1,128,640]{2,1,0:T(8,128)(2,1)S(1)}, bf16[1,128,640]{2,1,0:T(8,128)(2,1)S(1)}, u32[]{:S(2)}, u32[]{:S(2)}) collective-permute-start(bf16[1,128,640]{2,1,0:T(8,128)(2,1)S(1)} %bitcast.115), channel_id=1, source_target_pairs={{0,6},{1,7},{2,4},{3,5},{4,2},{5,3},{6,0},{7,1},{8,14},{9,15},{10,... | collective-permute-start | bytes 491528 | tf_op jit(solution)/shard_map/ppermute | solution.py:75
  18.5 14.2 %collective-permute-start.7 = (bf16[1,128,640]{2,1,0:T(8,128)(2,1)S(1)}, bf16[1,128,640]{2,1,0:T(8,128)(2,1)S(1)}, u32[]{:S(2)}, u32[]{:S(2)}) collective-permute-start(bf16[1,128,640]{2,1,0:T(8,128)(2,1)S(1)} %bitcast.116), channel_id=1, source_target_pairs={{0,4},{1,5},{2,6},{3,7},{4,0},{5,1},{6,2},{7,3},{8,12},{9,13},{10,... | collective-permute-start | bytes 491528 | tf_op jit(solution)/shard_map/ppermute | solution.py:75
  18.5 14.1 %collective-permute-start.6 = (bf16[1,128,640]{2,1,0:T(8,128)(2,1)S(1)}, bf16[1,128,640]{2,1,0:T(8,128)(2,1)S(1)}, u32[]{:S(2)}, u32[]{:S(2)}) collective-permute-start(bf16[1,128,640]{2,1,0:T(8,128)(2,1)S(1)} %bitcast.117), channel_id=1, source_target_pairs={{0,2},{1,3},{2,0},{3,1},{4,6},{5,7},{6,4},{7,5},{8,10},{9,11},{10,... | collective-permute-start | bytes 491528 | tf_op jit(solution)/shard_map/ppermute | solution.py:75
  19.2 13.6 %collective-permute-start.5 = (bf16[1,4,56,640]{3,2,1,0:T(8,128)(2,1)S(1)}, bf16[1,4,56,640]{3,2,1,0:T(8,128)(2,1)S(1)}, u32[]{:S(2)}, u32[]{:S(2)}) collective-permute-start(bf16[1,4,56,640]{3,2,1,0:T(8,128)(2,1)S(1)} %bitcast.104), channel_id=1, source_target_pairs={{0,24},{8,16},{16,8},{24,0},{1,25},{9,17},{17,9},{25,1},{2,26},{10... | collective-permute-start | bytes 860168 | tf_op jit(solution)/shard_map/ppermute | solution.py:70
  21.7 13.0 %collective-permute-start.4 = (bf16[1,4,56,640]{3,2,1,0:T(8,128)(2,1)S(1)}, bf16[1,4,56,640]{3,2,1,0:T(8,128)(2,1)S(1)}, u32[]{:S(2)}, u32[]{:S(2)}) collective-permute-start(bf16[1,4,56,640]{3,2,1,0:T(8,128)(2,1)S(1)} %bitcast.105), channel_id=1, source_target_pairs={{0,16},{8,24},{16,0},{24,8},{1,17},{9,25},{17,1},{25,9},{2,18},{10... | collective-permute-start | bytes 860168 | tf_op jit(solution)/shard_map/ppermute | solution.py:70
  23.7 11.1 %collective-permute-start.3 = (bf16[1,4,56,640]{3,2,1,0:T(8,128)(2,1)S(1)}, bf16[1,4,56,640]{3,2,1,0:T(8,128)(2,1)S(1)}, u32[]{:S(2)}, u32[]{:S(2)}) collective-permute-start(bf16[1,4,56,640]{3,2,1,0:T(8,128)(2,1)S(1)} %bitcast.106), channel_id=1, source_target_pairs={{0,8},{8,0},{16,24},{24,16},{1,9},{9,1},{17,25},{25,17},{2,10},{10... | collective-permute-start | bytes 860168 | tf_op jit(solution)/shard_map/ppermute | solution.py:70
  35.1 17.5 %copy-start.24 = (bf16[4,4,56,640]{3,2,1,0:T(8,128)(2,1)}, bf16[4,4,56,640]{3,2,1,0:T(8,128)(2,1)S(1)}, u32[]{:S(2)}) copy-start(bf16[4,4,56,640]{3,2,1,0:T(8,128)(2,1)S(1)} %pad_maximum_fusion) | copy-start | bytes 3440644
  35.1 9.6 %collective-permute-start.10 = (bf16[16,56,640]{2,1,0:T(8,128)(2,1)S(1)}, bf16[16,56,640]{2,1,0:T(8,128)(2,1)}, u32[]{:S(2)}, u32[]{:S(2)}) collective-permute-start(bf16[16,56,640]{2,1,0:T(8,128)(2,1)S(1)} %bitcast.108), channel_id=1, source_target_pairs={{0,1},{1,0},{2,3},{3,2},{4,5},{5,4},{6,7},{7,6},{8,9},{9,8},{10,11... | collective-permute-start | bytes 3440648 | tf_op jit(solution)/shard_map/ppermute | solution.py:75
  35.2 9.5 %collective-permute-start.11 = (bf16[512,640]{1,0:T(8,128)(2,1)S(1)}, bf16[512,640]{1,0:T(8,128)(2,1)S(1)}, u32[]{:S(2)}, u32[]{:S(2)}) collective-permute-start(bf16[512,640]{1,0:T(8,128)(2,1)S(1)} %bitcast.87), channel_id=1, source_target_pairs={{0,1},{1,0},{2,3},{3,2},{4,5},{5,4},{6,7},{7,6},{8,9},{9,8},{10,11... | collective-permute-start | bytes 1966088 | tf_op jit(solution)/shard_map/ppermute | solution.py:75
  35.7 5.9 %collective-permute-start.14 = (bf16[1,32,640]{2,1,0:T(8,128)(2,1)S(1)}, bf16[1,32,640]{2,1,0:T(8,128)(2,1)S(1)}, u32[]{:S(2)}, u32[]{:S(2)}) collective-permute-start(bf16[1,32,640]{2,1,0:T(8,128)(2,1)S(1)} %bitcast.119), channel_id=1, source_target_pairs={{0,6},{1,7},{2,4},{3,5},{4,2},{5,3},{6,0},{7,1},{8,14},{9,15},{10,... | collective-permute-start | bytes 122888 | tf_op jit(solution)/shard_map/ppermute | solution.py:75
  39.2 4.9 %collective-permute-start.13 = (bf16[1,32,640]{2,1,0:T(8,128)(2,1)S(1)}, bf16[1,32,640]{2,1,0:T(8,128)(2,1)S(1)}, u32[]{:S(2)}, u32[]{:S(2)}) collective-permute-start(bf16[1,32,640]{2,1,0:T(8,128)(2,1)S(1)} %bitcast.120), channel_id=1, source_target_pairs={{0,4},{1,5},{2,6},{3,7},{4,0},{5,1},{6,2},{7,3},{8,12},{9,13},{10,... | collective-permute-start | bytes 122888 | tf_op jit(solution)/shard_map/ppermute | solution.py:75
  40.4 4.2 %collective-permute-start.12 = (bf16[1,32,640]{2,1,0:T(8,128)(2,1)S(1)}, bf16[1,32,640]{2,1,0:T(8,128)(2,1)S(1)}, u32[]{:S(2)}, u32[]{:S(2)}) collective-permute-start(bf16[1,32,640]{2,1,0:T(8,128)(2,1)S(1)} %bitcast.121), channel_id=1, source_target_pairs={{0,2},{1,3},{2,0},{3,1},{4,6},{5,7},{6,4},{7,5},{8,10},{9,11},{10,... | collective-permute-start | bytes 122888 | tf_op jit(solution)/shard_map/ppermute | solution.py:75
  45.7 18.9 %collective-permute-start.19 = (bf16[1,4,32,640]{3,2,1,0:T(8,128)(2,1)S(1)}, bf16[1,4,32,640]{3,2,1,0:T(8,128)(2,1)S(1)}, u32[]{:S(2)}, u32[]{:S(2)}) collective-permute-start(bf16[1,4,32,640]{3,2,1,0:T(8,128)(2,1)S(1)} %bitcast.111), channel_id=1, source_target_pairs={{0,24},{8,16},{16,8},{24,0},{1,25},{9,17},{17,9},{25,1},{2,26},{10... | collective-permute-start | bytes 491528 | tf_op jit(solution)/shard_map/ppermute | solution.py:70
  48.0 16.6 %collective-permute-start.18 = (bf16[1,4,32,640]{3,2,1,0:T(8,128)(2,1)S(1)}, bf16[1,4,32,640]{3,2,1,0:T(8,128)(2,1)S(1)}, u32[]{:S(2)}, u32[]{:S(2)}) collective-permute-start(bf16[1,4,32,640]{3,2,1,0:T(8,128)(2,1)S(1)} %bitcast.112), channel_id=1, source_target_pairs={{0,16},{8,24},{16,0},{24,8},{1,17},{9,25},{17,1},{25,9},{2,18},{10... | collective-permute-start | bytes 491528 | tf_op jit(solution)/shard_map/ppermute | solution.py:70
  48.7 15.9 %collective-permute-start.17 = (bf16[1,4,32,640]{3,2,1,0:T(8,128)(2,1)S(1)}, bf16[1,4,32,640]{3,2,1,0:T(8,128)(2,1)S(1)}, u32[]{:S(2)}, u32[]{:S(2)}) collective-permute-start(bf16[1,4,32,640]{3,2,1,0:T(8,128)(2,1)S(1)} %bitcast.113), channel_id=1, source_target_pairs={{0,8},{8,0},{16,24},{24,16},{1,9},{9,1},{17,25},{25,17},{2,10},{10... | collective-permute-start | bytes 491528 | tf_op jit(solution)/shard_map/ppermute | solution.py:70
  49.2 15.5 %collective-permute-start.16 = (bf16[192,640]{1,0:T(8,128)(2,1)S(1)}, bf16[192,640]{1,0:T(8,128)(2,1)S(1)}, u32[]{:S(2)}, u32[]{:S(2)}) collective-permute-start(bf16[192,640]{1,0:T(8,128)(2,1)S(1)} %pad_maximum_fusion.4.refs_4_), channel_id=1, source_target_pairs={{0,4},{1,5},{2,6},{3,7},{4,0},{5,1},{6,2},{7,3},{8,12},{9,13},{10,... | collective-permute-start | bytes 737288 | tf_op jit(solution)/shard_map/ppermute | solution.py:75
  50.8 13.9 %collective-permute-start.15 = (bf16[192,640]{1,0:T(8,128)(2,1)S(1)}, bf16[192,640]{1,0:T(8,128)(2,1)S(1)}, u32[]{:S(2)}, u32[]{:S(2)}) collective-permute-start(bf16[192,640]{1,0:T(8,128)(2,1)S(1)} %pad_maximum_fusion.4.refs_4_), channel_id=1, source_target_pairs={{0,2},{1,3},{2,0},{3,1},{4,6},{5,7},{6,4},{7,5},{8,10},{9,11},{10,... | collective-permute-start | bytes 737288 | tf_op jit(solution)/shard_map/ppermute | solution.py:75
  64.7 2.2 %collective-permute-start.20 = (bf16[16,32,640]{2,1,0:T(8,128)(2,1)S(1)}, bf16[16,32,640]{2,1,0:T(8,128)(2,1)S(1)}, u32[]{:S(2)}, u32[]{:S(2)}) collective-permute-start(bf16[16,32,640]{2,1,0:T(8,128)(2,1)S(1)} %bitcast.90), channel_id=1, source_target_pairs={{0,1},{1,0},{2,3},{3,2},{4,5},{5,4},{6,7},{7,6},{8,9},{9,8},{10,11... | collective-permute-start | bytes 1966088 | tf_op jit(solution)/shard_map/ppermute | solution.py:75
  64.8 5.4 %collective-permute-start.26 = (bf16[192,640]{1,0:T(8,128)(2,1)S(1)}, bf16[192,640]{1,0:T(8,128)(2,1)S(1)}, u32[]{:S(2)}, u32[]{:S(2)}) collective-permute-start(bf16[192,640]{1,0:T(8,128)(2,1)S(1)} %collective-permute-done.15.refs_5_), channel_id=1, source_target_pairs={{0,1},{1,0},{2,3},{3,2},{4,5},{5,4},{6,7},{7,6},{8,9},{9,8},{10,11... | collective-permute-start | bytes 737288 | tf_op jit(solution)/shard_map/ppermute | solution.py:75
  65.3 5.6 %collective-permute-start.27 = (bf16[192,640]{1,0:T(8,128)(2,1)S(1)}, bf16[192,640]{1,0:T(8,128)(2,1)S(1)}, u32[]{:S(2)}, u32[]{:S(2)}) collective-permute-start(bf16[192,640]{1,0:T(8,128)(2,1)S(1)} %collective-permute-done.16.refs_6_), channel_id=1, source_target_pairs={{0,1},{1,0},{2,3},{3,2},{4,5},{5,4},{6,7},{7,6},{8,9},{9,8},{10,11... | collective-permute-start | bytes 737288 | tf_op jit(solution)/shard_map/ppermute | solution.py:75
  65.4 6.0 %collective-permute-start.25 = (bf16[192,640]{1,0:T(8,128)(2,1)S(1)}, bf16[192,640]{1,0:T(8,128)(2,1)S(1)}, u32[]{:S(2)}, u32[]{:S(2)}) collective-permute-start(bf16[192,640]{1,0:T(8,128)(2,1)S(1)} %pad_maximum_fusion.4.refs_4_), channel_id=1, source_target_pairs={{0,1},{1,0},{2,3},{3,2},{4,5},{5,4},{6,7},{7,6},{8,9},{9,8},{10,11... | collective-permute-start | bytes 737288 | tf_op jit(solution)/shard_map/ppermute | solution.py:75
  65.8 9.8 %collective-permute-start.24 = (bf16[192,640]{1,0:T(8,128)(2,1)S(1)}, bf16[192,640]{1,0:T(8,128)(2,1)S(1)}, u32[]{:S(2)}, u32[]{:S(2)}) collective-permute-start(bf16[192,640]{1,0:T(8,128)(2,1)S(1)} %pad_maximum_fusion.4.refs_4_), channel_id=1, source_target_pairs={{0,6},{1,7},{2,4},{3,5},{4,2},{5,3},{6,0},{7,1},{8,14},{9,15},{10,... | collective-permute-start | bytes 737288 | tf_op jit(solution)/shard_map/ppermute | solution.py:75
  67.9 25.9 %copy-start.8 = (f32[1,128,640]{2,1,0:T(8,128)S(1)}, f32[1,128,640]{2,1,0:T(8,128)}, u32[]{:S(2)}) copy-start(f32[1,128,640]{2,1,0:T(8,128)} %param.27) | copy-start | bytes 983044
  67.9 8.0 %collective-permute-start.23 = (bf16[128,640]{1,0:T(8,128)(2,1)S(1)}, bf16[128,640]{1,0:T(8,128)(2,1)S(1)}, u32[]{:S(2)}, u32[]{:S(2)}) collective-permute-start(bf16[128,640]{1,0:T(8,128)(2,1)S(1)} %get-tuple-element.183.refs_0_), channel_id=1, source_target_pairs={{0,24},{8,16},{16,8},{24,0},{1,25},{9,17},{17,9},{25,1},{2,26},{10... | collective-permute-start | bytes 491528 | tf_op jit(solution)/shard_map/ppermute | solution.py:70
  70.2 8.3 %collective-permute-start.22 = (bf16[128,640]{1,0:T(8,128)(2,1)S(1)}, bf16[128,640]{1,0:T(8,128)(2,1)S(1)}, u32[]{:S(2)}, u32[]{:S(2)}) collective-permute-start(bf16[128,640]{1,0:T(8,128)(2,1)S(1)} %get-tuple-element.183.refs_0_), channel_id=1, source_target_pairs={{0,16},{8,24},{16,0},{24,8},{1,17},{9,25},{17,1},{25,9},{2,18},{10... | collective-permute-start | bytes 491528 | tf_op jit(solution)/shard_map/ppermute | solution.py:70
  70.9 7.8 %collective-permute-start.21 = (bf16[128,640]{1,0:T(8,128)(2,1)S(1)}, bf16[128,640]{1,0:T(8,128)(2,1)S(1)}, u32[]{:S(2)}, u32[]{:S(2)}) collective-permute-start(bf16[128,640]{1,0:T(8,128)(2,1)S(1)} %get-tuple-element.183.refs_0_), channel_id=1, source_target_pairs={{0,8},{8,0},{16,24},{24,16},{1,9},{9,1},{17,25},{25,17},{2,10},{10... | collective-permute-start | bytes 491528 | tf_op jit(solution)/shard_map/ppermute | solution.py:70
  78.7 1.5 collective-permute-start.28
  82.9 7.1 %collective-permute-start.29 = (bf16[128,640]{1,0:T(8,128)(2,1)S(1)}, bf16[128,640]{1,0:T(8,128)(2,1)S(1)}, u32[]{:S(2)}, u32[]{:S(2)}) collective-permute-start(bf16[128,640]{1,0:T(8,128)(2,1)S(1)} %get-tuple-element.192), channel_id=1, source_target_pairs={{0,8},{8,0},{16,24},{24,16},{1,9},{9,1},{17,25},{25,17},{2,10},{10... | collective-permute-start | bytes 491528 | tf_op jit(solution)/shard_map/ppermute | solution.py:70
  84.3 9.4 %collective-permute-start.30 = (bf16[128,640]{1,0:T(8,128)(2,1)S(1)}, bf16[128,640]{1,0:T(8,128)(2,1)S(1)}, u32[]{:S(2)}, u32[]{:S(2)}) collective-permute-start(bf16[128,640]{1,0:T(8,128)(2,1)S(1)} %get-tuple-element.193), channel_id=1, source_target_pairs={{0,16},{8,24},{16,0},{24,8},{1,17},{9,25},{17,1},{25,9},{2,18},{10... | collective-permute-start | bytes 491528 | tf_op jit(solution)/shard_map/ppermute | solution.py:70
  85.1 8.7 %collective-permute-start.31 = (bf16[128,640]{1,0:T(8,128)(2,1)S(1)}, bf16[128,640]{1,0:T(8,128)(2,1)S(1)}, u32[]{:S(2)}, u32[]{:S(2)}) collective-permute-start(bf16[128,640]{1,0:T(8,128)(2,1)S(1)} %get-tuple-element.194), channel_id=1, source_target_pairs={{0,24},{8,16},{16,8},{24,0},{1,25},{9,17},{17,9},{25,1},{2,26},{10... | collective-permute-start | bytes 491528 | tf_op jit(solution)/shard_map/ppermute | solution.py:70
  94.7 7.9 %collective-permute-start.34 = (bf16[128,640]{1,0:T(8,128)(2,1)S(1)}, bf16[128,640]{1,0:T(8,128)(2,1)S(1)}, u32[]{:S(2)}, u32[]{:S(2)}) collective-permute-start(bf16[128,640]{1,0:T(8,128)(2,1)S(1)} %get-tuple-element.197.refs_0_), channel_id=1, source_target_pairs={{0,24},{8,16},{16,8},{24,0},{1,25},{9,17},{17,9},{25,1},{2,26},{10... | collective-permute-start | bytes 491528 | tf_op jit(solution)/shard_map/ppermute | solution.py:70
  96.2 8.1 %collective-permute-start.33 = (bf16[128,640]{1,0:T(8,128)(2,1)S(1)}, bf16[128,640]{1,0:T(8,128)(2,1)S(1)}, u32[]{:S(2)}, u32[]{:S(2)}) collective-permute-start(bf16[128,640]{1,0:T(8,128)(2,1)S(1)} %get-tuple-element.197.refs_0_), channel_id=1, source_target_pairs={{0,16},{8,24},{16,0},{24,8},{1,17},{9,25},{17,1},{25,9},{2,18},{10... | collective-permute-start | bytes 491528 | tf_op jit(solution)/shard_map/ppermute | solution.py:70
  96.9 7.5 %collective-permute-start.32 = (bf16[128,640]{1,0:T(8,128)(2,1)S(1)}, bf16[128,640]{1,0:T(8,128)(2,1)S(1)}, u32[]{:S(2)}, u32[]{:S(2)}) collective-permute-start(bf16[128,640]{1,0:T(8,128)(2,1)S(1)} %get-tuple-element.197.refs_0_), channel_id=1, source_target_pairs={{0,8},{8,0},{16,24},{24,16},{1,9},{9,1},{17,25},{25,17},{2,10},{10... | collective-permute-start | bytes 491528 | tf_op jit(solution)/shard_map/ppermute | solution.py:70
  107.2 7.2 %collective-permute-start.35 = (bf16[128,640]{1,0:T(8,128)(2,1)S(1)}, bf16[128,640]{1,0:T(8,128)(2,1)S(1)}, u32[]{:S(2)}, u32[]{:S(2)}) collective-permute-start(bf16[128,640]{1,0:T(8,128)(2,1)S(1)} %get-tuple-element.211), channel_id=1, source_target_pairs={{0,8},{8,0},{16,24},{24,16},{1,9},{9,1},{17,25},{25,17},{2,10},{10... | collective-permute-start | bytes 491528 | tf_op jit(solution)/shard_map/ppermute | solution.py:70
  108.0 9.0 %collective-permute-start.36 = (bf16[128,640]{1,0:T(8,128)(2,1)S(1)}, bf16[128,640]{1,0:T(8,128)(2,1)S(1)}, u32[]{:S(2)}, u32[]{:S(2)}) collective-permute-start(bf16[128,640]{1,0:T(8,128)(2,1)S(1)} %get-tuple-element.212), channel_id=1, source_target_pairs={{0,16},{8,24},{16,0},{24,8},{1,17},{9,25},{17,1},{25,9},{2,18},{10... | collective-permute-start | bytes 491528 | tf_op jit(solution)/shard_map/ppermute | solution.py:70
  109.2 7.8 %collective-permute-start.37 = (bf16[128,640]{1,0:T(8,128)(2,1)S(1)}, bf16[128,640]{1,0:T(8,128)(2,1)S(1)}, u32[]{:S(2)}, u32[]{:S(2)}) collective-permute-start(bf16[128,640]{1,0:T(8,128)(2,1)S(1)} %get-tuple-element.213), channel_id=1, source_target_pairs={{0,24},{8,16},{16,8},{24,0},{1,25},{9,17},{17,9},{25,1},{2,26},{10... | collective-permute-start | bytes 491528 | tf_op jit(solution)/shard_map/ppermute | solution.py:70
  117.0 4.4 %collective-permute-start.39 = (bf16[4,192,640]{2,1,0:T(8,128)(2,1)S(1)}, bf16[4,192,640]{2,1,0:T(8,128)(2,1)S(1)}, u32[]{:S(2)}, u32[]{:S(2)}) collective-permute-start(bf16[4,192,640]{2,1,0:T(8,128)(2,1)S(1)} %get-tuple-element.224), channel_id=1, source_target_pairs={{0,1},{1,0},{2,3},{3,2},{4,5},{5,4},{6,7},{7,6},{8,9},{9,8},{10,11... | collective-permute-start | bytes 2949128 | tf_op jit(solution)/shard_map/ppermute | solution.py:75
  119.0 2.3 %collective-permute-start.38 = (bf16[16,32,640]{2,1,0:T(8,128)(2,1)S(1)}, bf16[16,32,640]{2,1,0:T(8,128)(2,1)S(1)}, u32[]{:S(2)}, u32[]{:S(2)}) collective-permute-start(bf16[16,32,640]{2,1,0:T(8,128)(2,1)S(1)} %get-tuple-element.222), channel_id=1, source_target_pairs={{0,1},{1,0},{2,3},{3,2},{4,5},{5,4},{6,7},{7,6},{8,9},{9,8},{10,11... | collective-permute-start | bytes 1966088 | tf_op jit(solution)/shard_map/ppermute | solution.py:75
  122.3 15.8 %collective-permute-start.44 = (bf16[4,32,640]{2,1,0:T(8,128)(2,1)S(1)}, bf16[4,32,640]{2,1,0:T(8,128)(2,1)S(1)}, u32[]{:S(2)}, u32[]{:S(2)}) collective-permute-start(bf16[4,32,640]{2,1,0:T(8,128)(2,1)S(1)} %get-tuple-element.283), channel_id=1, source_target_pairs={{0,24},{8,16},{16,8},{24,0},{1,25},{9,17},{17,9},{25,1},{2,26},{10... | collective-permute-start | bytes 491528 | tf_op jit(solution)/shard_map/ppermute | solution.py:70
  123.6 14.6 %collective-permute-start.43 = (bf16[4,32,640]{2,1,0:T(8,128)(2,1)S(1)}, bf16[4,32,640]{2,1,0:T(8,128)(2,1)S(1)}, u32[]{:S(2)}, u32[]{:S(2)}) collective-permute-start(bf16[4,32,640]{2,1,0:T(8,128)(2,1)S(1)} %get-tuple-element.284), channel_id=1, source_target_pairs={{0,16},{8,24},{16,0},{24,8},{1,17},{9,25},{17,1},{25,9},{2,18},{10... | collective-permute-start | bytes 491528 | tf_op jit(solution)/shard_map/ppermute | solution.py:70
  125.1 13.1 %collective-permute-start.42 = (bf16[4,32,640]{2,1,0:T(8,128)(2,1)S(1)}, bf16[4,32,640]{2,1,0:T(8,128)(2,1)S(1)}, u32[]{:S(2)}, u32[]{:S(2)}) collective-permute-start(bf16[4,32,640]{2,1,0:T(8,128)(2,1)S(1)} %get-tuple-element.285), channel_id=1, source_target_pairs={{0,8},{8,0},{16,24},{24,16},{1,9},{9,1},{17,25},{25,17},{2,10},{10... | collective-permute-start | bytes 491528 | tf_op jit(solution)/shard_map/ppermute | solution.py:70
  126.0 13.7 %collective-permute-start.41 = (bf16[192,640]{1,0:T(8,128)(2,1)S(1)}, bf16[192,640]{1,0:T(8,128)(2,1)S(1)}, u32[]{:S(2)}, u32[]{:S(2)}) collective-permute-start(bf16[192,640]{1,0:T(8,128)(2,1)S(1)} %get-tuple-element.281), channel_id=1, source_target_pairs={{0,4},{1,5},{2,6},{3,7},{4,0},{5,1},{6,2},{7,3},{8,12},{9,13},{10,... | collective-permute-start | bytes 737288 | tf_op jit(solution)/shard_map/ppermute | solution.py:75
  127.7 12.1 %collective-permute-start.40 = (bf16[192,640]{1,0:T(8,128)(2,1)S(1)}, bf16[192,640]{1,0:T(8,128)(2,1)S(1)}, u32[]{:S(2)}, u32[]{:S(2)}) collective-permute-start(bf16[192,640]{1,0:T(8,128)(2,1)S(1)} %get-tuple-element.282), channel_id=1, source_target_pairs={{0,2},{1,3},{2,0},{3,1},{4,6},{5,7},{6,4},{7,5},{8,10},{9,11},{10,... | collective-permute-start | bytes 737288 | tf_op jit(solution)/shard_map/ppermute | solution.py:75
  140.7 5.4 %collective-permute-start.45 = (bf16[16,48,640]{2,1,0:T(8,128)(2,1)}, bf16[16,48,640]{2,1,0:T(8,128)(2,1)S(1)}, u32[]{:S(2)}, u32[]{:S(2)}) collective-permute-start(bf16[16,48,640]{2,1,0:T(8,128)(2,1)} %copy-done.9), channel_id=1, source_target_pairs={{0,1},{1,0},{2,3},{3,2},{4,5},{5,4},{6,7},{7,6},{8,9},{9,8},{10,11... | collective-permute-start | bytes 2949128 | tf_op jit(solution)/shard_map/ppermute | solution.py:75
  140.9 5.0 %collective-permute-start.46 = (bf16[16,96]{1,0:T(8,128)(2,1)S(1)}, bf16[16,96]{1,0:T(8,128)(2,1)S(1)}, u32[]{:S(2)}, u32[]{:S(2)}) collective-permute-start(bf16[16,96]{1,0:T(8,128)(2,1)S(1)} %slice.250), channel_id=1, source_target_pairs={{0,1},{1,0},{2,3},{3,2},{4,5},{5,4},{6,7},{7,6},{8,9},{9,8},{10,11... | collective-permute-start | bytes 9224 | tf_op jit(solution)/shard_map/ppermute | solution.py:75
  141.4 4.5 %collective-permute-start.47 = (bf16[512,512]{1,0:T(8,128)(2,1)}, bf16[512,512]{1,0:T(8,128)(2,1)S(1)}, u32[]{:S(2)}, u32[]{:S(2)}) collective-permute-start(bf16[512,512]{1,0:T(8,128)(2,1)} %copy-done.12), channel_id=1, source_target_pairs={{0,1},{1,0},{2,3},{3,2},{4,5},{5,4},{6,7},{7,6},{8,9},{9,8},{10,11... | collective-permute-start | bytes 1572872 | tf_op jit(solution)/shard_map/ppermute | solution.py:75
  142.4 7.6 %collective-permute-start.48 = (bf16[96,640]{1,0:T(8,128)(2,1)S(1)}, bf16[96,640]{1,0:T(8,128)(2,1)S(1)}, u32[]{:S(2)}, u32[]{:S(2)}) collective-permute-start(bf16[96,640]{1,0:T(8,128)(2,1)S(1)} %slice_bitcast_fusion.9), channel_id=1, source_target_pairs={{0,6},{1,7},{2,4},{3,5},{4,2},{5,3},{6,0},{7,1},{8,14},{9,15},{10,... | collective-permute-start | bytes 368648 | tf_op jit(solution)/shard_map/ppermute | solution.py:75
  150.0 6.0 %collective-permute-start.52 = (bf16[128,512]{1,0:T(8,128)(2,1)S(1)}, bf16[128,512]{1,0:T(8,128)(2,1)S(1)}, u32[]{:S(2)}, u32[]{:S(2)}) collective-permute-start(bf16[128,512]{1,0:T(8,128)(2,1)S(1)} %get-tuple-element.286), channel_id=1, source_target_pairs={{0,2},{1,3},{2,0},{3,1},{4,6},{5,7},{6,4},{7,5},{8,10},{9,11},{10,... | collective-permute-start | bytes 393224 | tf_op jit(solution)/shard_map/ppermute | solution.py:75
  151.4 8.3 %collective-permute-start.54 = (bf16[128,512]{1,0:T(8,128)(2,1)S(1)}, bf16[128,512]{1,0:T(8,128)(2,1)S(1)}, u32[]{:S(2)}, u32[]{:S(2)}) collective-permute-start(bf16[128,512]{1,0:T(8,128)(2,1)S(1)} %get-tuple-element.287), channel_id=1, source_target_pairs={{0,6},{1,7},{2,4},{3,5},{4,2},{5,3},{6,0},{7,1},{8,14},{9,15},{10,... | collective-permute-start | bytes 393224 | tf_op jit(solution)/shard_map/ppermute | solution.py:75
  152.3 12.7 %collective-permute-start.53 = (bf16[128,512]{1,0:T(8,128)(2,1)S(1)}, bf16[128,512]{1,0:T(8,128)(2,1)S(1)}, u32[]{:S(2)}, u32[]{:S(2)}) collective-permute-start(bf16[128,512]{1,0:T(8,128)(2,1)S(1)} %get-tuple-element.288), channel_id=1, source_target_pairs={{0,4},{1,5},{2,6},{3,7},{4,0},{5,1},{6,2},{7,3},{8,12},{9,13},{10,... | collective-permute-start | bytes 393224 | tf_op jit(solution)/shard_map/ppermute | solution.py:75
  153.7 11.4 %collective-permute-start.49 = (bf16[4,56,640]{2,1,0:T(8,128)(2,1)S(1)}, bf16[4,56,640]{2,1,0:T(8,128)(2,1)S(1)}, u32[]{:S(2)}, u32[]{:S(2)}) collective-permute-start(bf16[4,56,640]{2,1,0:T(8,128)(2,1)S(1)} %get-tuple-element.278), channel_id=1, source_target_pairs={{0,8},{8,0},{16,24},{24,16},{1,9},{9,1},{17,25},{25,17},{2,10},{10... | collective-permute-start | bytes 860168 | tf_op jit(solution)/shard_map/ppermute | solution.py:70
  154.7 13.2 %collective-permute-start.51 = (bf16[4,56,640]{2,1,0:T(8,128)(2,1)S(1)}, bf16[4,56,640]{2,1,0:T(8,128)(2,1)S(1)}, u32[]{:S(2)}, u32[]{:S(2)}) collective-permute-start(bf16[4,56,640]{2,1,0:T(8,128)(2,1)S(1)} %get-tuple-element.279), channel_id=1, source_target_pairs={{0,24},{8,16},{16,8},{24,0},{1,25},{9,17},{17,9},{25,1},{2,26},{10... | collective-permute-start | bytes 860168 | tf_op jit(solution)/shard_map/ppermute | solution.py:70
  156.0 13.2 %collective-permute-start.50 = (bf16[4,56,640]{2,1,0:T(8,128)(2,1)S(1)}, bf16[4,56,640]{2,1,0:T(8,128)(2,1)S(1)}, u32[]{:S(2)}, u32[]{:S(2)}) collective-permute-start(bf16[4,56,640]{2,1,0:T(8,128)(2,1)S(1)} %get-tuple-element.280), channel_id=1, source_target_pairs={{0,16},{8,24},{16,0},{24,8},{1,17},{9,25},{17,1},{25,9},{2,18},{10... | collective-permute-start | bytes 860168 | tf_op jit(solution)/shard_map/ppermute | solution.py:70
  170.7 8.6 %collective-permute-start.58 = (bf16[32,640]{1,0:T(8,128)(2,1)S(1)}, bf16[32,640]{1,0:T(8,128)(2,1)S(1)}, u32[]{:S(2)}, u32[]{:S(2)}) collective-permute-start(bf16[32,640]{1,0:T(8,128)(2,1)S(1)} %get-tuple-element.297), channel_id=1, source_target_pairs={{0,2},{1,3},{2,0},{3,1},{4,6},{5,7},{6,4},{7,5},{8,10},{9,11},{10,... | collective-permute-start | bytes 122888 | tf_op jit(solution)/shard_map/ppermute | solution.py:75
  172.4 8.3 %collective-permute-start.60 = (bf16[32,640]{1,0:T(8,128)(2,1)S(1)}, bf16[32,640]{1,0:T(8,128)(2,1)S(1)}, u32[]{:S(2)}, u32[]{:S(2)}) collective-permute-start(bf16[32,640]{1,0:T(8,128)(2,1)S(1)} %get-tuple-element.298), channel_id=1, source_target_pairs={{0,6},{1,7},{2,4},{3,5},{4,2},{5,3},{6,0},{7,1},{8,14},{9,15},{10,... | collective-permute-start | bytes 122888 | tf_op jit(solution)/shard_map/ppermute | solution.py:75
  174.8 7.8 %collective-permute-start.59 = (bf16[32,640]{1,0:T(8,128)(2,1)S(1)}, bf16[32,640]{1,0:T(8,128)(2,1)S(1)}, u32[]{:S(2)}, u32[]{:S(2)}) collective-permute-start(bf16[32,640]{1,0:T(8,128)(2,1)S(1)} %get-tuple-element.299), channel_id=1, source_target_pairs={{0,4},{1,5},{2,6},{3,7},{4,0},{5,1},{6,2},{7,3},{8,12},{9,13},{10,... | collective-permute-start | bytes 122888 | tf_op jit(solution)/shard_map/ppermute | solution.py:75
  174.8 14.8 %collective-permute-start.61 = (bf16[96,640]{1,0:T(8,128)(2,1)S(1)}, bf16[96,640]{1,0:T(8,128)(2,1)S(1)}, u32[]{:S(2)}, u32[]{:S(2)}) collective-permute-start(bf16[96,640]{1,0:T(8,128)(2,1)S(1)} %slice_bitcast_fusion.8), channel_id=1, source_target_pairs={{0,6},{1,7},{2,4},{3,5},{4,2},{5,3},{6,0},{7,1},{8,14},{9,15},{10,... | collective-permute-start | bytes 368648 | tf_op jit(solution)/shard_map/ppermute | solution.py:75
  176.4 6.9 %collective-permute-start.55 = (bf16[56,640]{1,0:T(8,128)(2,1)S(1)}, bf16[56,640]{1,0:T(8,128)(2,1)S(1)}, u32[]{:S(2)}, u32[]{:S(2)}) collective-permute-start(bf16[56,640]{1,0:T(8,128)(2,1)S(1)} %get-tuple-element.292), channel_id=1, source_target_pairs={{0,2},{1,3},{2,0},{3,1},{4,6},{5,7},{6,4},{7,5},{8,10},{9,11},{10,... | collective-permute-start | bytes 215048 | tf_op jit(solution)/shard_map/ppermute | solution.py:75
  179.3 6.2 %collective-permute-start.57 = (bf16[56,640]{1,0:T(8,128)(2,1)S(1)}, bf16[56,640]{1,0:T(8,128)(2,1)S(1)}, u32[]{:S(2)}, u32[]{:S(2)}) collective-permute-start(bf16[56,640]{1,0:T(8,128)(2,1)S(1)} %get-tuple-element.293), channel_id=1, source_target_pairs={{0,6},{1,7},{2,4},{3,5},{4,2},{5,3},{6,0},{7,1},{8,14},{9,15},{10,... | collective-permute-start | bytes 215048 | tf_op jit(solution)/shard_map/ppermute | solution.py:75
  180.7 7.2 %collective-permute-start.56 = (bf16[56,640]{1,0:T(8,128)(2,1)S(1)}, bf16[56,640]{1,0:T(8,128)(2,1)S(1)}, u32[]{:S(2)}, u32[]{:S(2)}) collective-permute-start(bf16[56,640]{1,0:T(8,128)(2,1)S(1)} %get-tuple-element.294), channel_id=1, source_target_pairs={{0,4},{1,5},{2,6},{3,7},{4,0},{5,1},{6,2},{7,3},{8,12},{9,13},{10,... | collective-permute-start | bytes 215048 | tf_op jit(solution)/shard_map/ppermute | solution.py:75
  (32 other events, 196.0 us)

commit v3 on v2

--- a/solution.py
+++ b/solution.py
@@ -204,7 +204,9 @@
     return pl.pallas_call(
         body,
         out_shape=[jax.ShapeDtypeStruct(shape, dtype) for shape, dtype in out_shapes],
-        in_specs=[whole] * len(inputs),
+        in_specs=[
+            pl.BlockSpec(memory_space=pltpu.SMEM) if entry.ndim == 1 else whole for entry in inputs
+        ],
         out_specs=[whole] * len(out_shapes),
         scratch_shapes=[pltpu.VMEM(shape, dtype) for shape, dtype in scratch],
         compiler_params=pltpu.CompilerParams(vmem_limit_bytes=mebibytes * 1024 * 1024),
@@ -212,23 +214,25 @@
     )(*inputs)
 
 
+def owner_rows(owner_ref, entry, rows):
+    return pl.ds(pl.multiple_of(owner_ref[entry] * rows, rows), rows)
+
+
 def attend_kernel(
-    unit_ref, near_ref, far_ref, own_ref, other_ref, order_q_ref, order_kv_ref, sin_scale_ref, sq_ref,
+    unit_ref, near_ref, far_ref, own_ref, other_ref, owner_ref, order_kv_ref, sin_scale_ref, sq_ref,
     sk_ref, cos_all_ref, sine_all_ref, key_index_ref, row_index_ref,
     wq_ref, wkv_ref, normed_ref, normed_all_ref, qraw_ref, kraw_ref, q_ref, k_ref, v_ref, attn_ref, lse_ref,
-    held_q, held_kv,
+    held_kv,
 ):
     places, _, width = own_ref.shape
-    rows_q = held_q.shape[0] // (2 * places)
+    rows_q = wq_ref.shape[0] // (2 * places)
     rows_kv = held_kv.shape[0] // (2 * places)
     for core, ref in enumerate((own_ref, other_ref)):
-        held_q[core * places * rows_q : (core + 1) * places * rows_q, :] = ref[:, :rows_q, :].reshape(
-            places * rows_q, width
-        )
+        for at in range(places):
+            wq_ref[owner_rows(owner_ref, core * places + at, rows_q), :] = ref[at, :rows_q, :]
         held_kv[core * places * rows_kv : (core + 1) * places * rows_kv, :] = ref[
             :, rows_q : rows_q + rows_kv, :
         ].reshape(places * rows_kv, width)
-    wq_ref[...] = dot_nn(order_q_ref[...], held_q[...]).astype(BF)
     wkv_ref[...] = dot_nn(order_kv_ref[...], held_kv[...]).astype(BF)
     tokens = unit_ref.shape[0]
     scale_in = 1.0 + sin_scale_ref[...]
@@ -262,14 +266,14 @@
 
 
 def project_kernel(
-    attn_ref, order_ref, own_ref, other_ref, resid_ref, sattn_ref, spre_ref,
-    held_ref, ahead_ref, projected_ref, middle_ref, pre_ref,
+    attn_ref, owner_ref, own_ref, other_ref, resid_ref, sattn_ref, spre_ref,
+    wo_ref, projected_ref, middle_ref, pre_ref,
 ):
-    places, rows, width = own_ref.shape
-    held_ref[: places * rows, :] = own_ref[...].reshape(places * rows, width)
-    held_ref[places * rows :, :] = other_ref[...].reshape(places * rows, width)
-    ahead_ref[...] = dot_nn(attn_ref[...], order_ref[...]).astype(BF)
-    projected = dot_nn(ahead_ref[...], held_ref[...])
+    places, rows, _ = own_ref.shape
+    for core, ref in enumerate((own_ref, other_ref)):
+        for at in range(places):
+            wo_ref[owner_rows(owner_ref, core * places + at, rows), :] = ref[at]
+    projected = dot_nn(attn_ref[...], wo_ref[...])
     projected_ref[...] = projected
     unit, _ = unit_of(projected)
     middle = resid_ref[...] + unit * (1.0 + sattn_ref[...])
@@ -358,9 +362,10 @@
 
 
 def project_back_kernel(
-    own_ref, come1_ref, come2_ref, come3_ref, gout_ref, projected_ref, middle_ref, held_ref, ahead_ref,
-    order_ref, sattn_ref, spre_ref,
+    own_ref, come1_ref, come2_ref, come3_ref, gout_ref, projected_ref, middle_ref, wo_ref, attn_ref,
+    owner_ref, sattn_ref, spre_ref,
     gresid_ref, gattn_ref, gown_ref, gother_ref, gsattn_ref, gspre_ref,
+    gwo_scr,
 ):
     grad_pre = own_ref[...]
     for ref in (come1_ref, come2_ref, come3_ref):
@@ -372,19 +377,20 @@
     gresid_ref[...] = grad_middle
     gsattn_ref[...] = jnp.sum(grad_middle * unit_a, axis=0, keepdims=True)
     grad_proj = rms_back(unit_a, inverse_a, grad_middle * (1.0 + sattn_ref[...])).astype(BF)
-    grad_held = dot_nt(grad_proj, held_ref[...]).astype(BF)
-    gattn_ref[...] = dot_nt(grad_held, order_ref[...]).astype(BF)
-    half = held_ref.shape[0] // 2
-    gown_ref[...] = dot_tn(ahead_ref[:, :half], grad_proj).astype(BF).reshape(gown_ref.shape)
-    gother_ref[...] = dot_tn(ahead_ref[:, half:], grad_proj).astype(BF).reshape(gother_ref.shape)
+    gattn_ref[...] = dot_nt(grad_proj, wo_ref[...]).astype(BF)
+    gwo_scr[...] = dot_tn(attn_ref[...], grad_proj).astype(BF)
+    places, rows, _ = gown_ref.shape
+    for core, ref in enumerate((gown_ref, gother_ref)):
+        for at in range(places):
+            ref[at] = gwo_scr[owner_rows(owner_ref, core * places + at, rows), :]
 
 
 def attend_back_kernel(
     grad_attn_ref, attn_ref, q_ref, k_ref, v_ref, lse_ref, qraw_ref, kraw_ref, wq_ref, wkv_ref,
     sq_ref, sk_ref, cos_all_ref, sine_all_ref, key_index_ref, row_index_ref,
-    normed_ref, normed_all_ref, unit_ref, near_ref, far_ref, order_q_ref, order_kv_ref,
+    normed_ref, normed_all_ref, unit_ref, near_ref, far_ref, owner_ref, order_kv_ref,
     own_ref, other_ref, gnear_ref, gfar_ref, gq_ref, gsin_ref, gsq_ref, gsk_ref,
-    probs_scr, gscores_scr, grows_scr, qrows_scr, gqraw_scr, gkv_scr,
+    probs_scr, gscores_scr, grows_scr, qrows_scr, gqraw_scr, gkv_scr, gwq_scr,
 ):
     head_width = sq_ref.shape[1]
     heads = wq_ref.shape[0] // head_width
@@ -439,19 +445,34 @@
     gfar_ref[:, head_width:] = grad_value[half:]
     gkv_scr[:head_width, :] = dot_tn(grad_kraw, normed_all_ref[...]).astype(BF)
     gkv_scr[head_width:, :] = dot_tn(grad_value, normed_all_ref[...]).astype(BF)
-    grad_wq = dot_tn(gqraw_scr[...], normed_ref[...]).astype(BF)
-    held_q = dot_tn(order_q_ref[...], grad_wq).astype(BF)
+    gwq_scr[...] = dot_tn(gqraw_scr[...], normed_ref[...]).astype(BF)
     held_kv = dot_tn(order_kv_ref[...], gkv_scr[...]).astype(BF)
     places, _, width = own_ref.shape
-    rows_q = held_q.shape[0] // (2 * places)
+    rows_q = gwq_scr.shape[0] // (2 * places)
     rows_kv = held_kv.shape[0] // (2 * places)
     for core, ref in enumerate((own_ref, other_ref)):
-        ref[:, :rows_q, :] = held_q[core * places * rows_q : (core + 1) * places * rows_q].reshape(
-            places, rows_q, width
-        )
+        for at in range(places):
+            ref[at, :rows_q, :] = gwq_scr[owner_rows(owner_ref, core * places + at, rows_q), :]
         ref[:, rows_q : rows_q + rows_kv, :] = held_kv[
             core * places * rows_kv : (core + 1) * places * rows_kv
         ].reshape(places, rows_kv, width)
+
+
+def ending_kernel(*refs):
+    firsts, outs, feeds, results = refs[:4], refs[4:8], refs[8:13], refs[13:]
+    total = add_bf16(*[ref[...] for ref in firsts])
+    row = 0
+    for ref in results[:4]:
+        ref[...] = total[row : row + ref.shape[0]]
+        row = row + ref.shape[0]
+    results[4][...] = add_bf16(*[ref[...] for ref in outs])
+    total = add_bf16(*[ref[...] for ref in feeds[:3]]) + jnp.concatenate(
+        [ref[...].astype(jnp.float32) for ref in feeds[3:]], axis=0
+    )
+    row = 0
+    for ref in results[5:]:
+        ref[...] = total[row : row + ref.shape[0]]
+        row = row + ref.shape[0]
 
 
 def shards_plain(
@@ -762,7 +783,6 @@
         jnp.arange(owners, dtype=jnp.int32) % chips,
     )
     owner_of = (row ^ far_dp) * groups + (place ^ (2 * far_z + far_core))
-    order_q = row_order(owner_of, rows_q)
     order_s = row_order(owner_of, 1)
     held_row = jnp.arange(2 * rows_k * owners, dtype=jnp.int32)
     held_at = (
@@ -778,18 +798,21 @@
     key_index = natural_rows(place ^ (2 * seq_zed + seq_core), block, groups).reshape(1, seq_len)
     row_index = natural_rows(place[None], block, groups).reshape(tokens, 1)
 
-    last_rows = jnp.zeros((8, width), BF).at[0, :scale_part].set(norm_scales)
-    last_rows = last_rows.at[1, :tokens].set((posit // 64).astype(BF))
-    last_rows = last_rows.at[2, :tokens].set((posit % 64).astype(BF))
+    last_rows = jnp.concatenate(
+        [
+            jnp.pad(values[None], ((0, 0), (0, width - values.shape[0])))
+            for values in (norm_scales, (posit // 64).astype(BF), (posit % 64).astype(BF))
+        ]
+        + [jnp.zeros((5, width), BF)],
+        axis=0,
+    )
     first = jnp.concatenate([w_query, w_key, w_value, last_rows], axis=0)
     feed = jnp.concatenate([w_gate, w_up, w_down], axis=0)
     inverse_in = lax.rsqrt(jnp.mean(resid * resid, axis=-1, keepdims=True) + EPS)
     unit_in = resid * inverse_in
     unit_bf = unit_in.astype(BF)
     first = gather_over(first[None], swap_z, chips)
-    first, unit_bf, feed, w_output, order_q, order_kv = tie(
-        (first, unit_bf, feed, w_output, order_q, order_kv)
-    )
+    first, unit_bf, feed, w_output, order_kv = tie((first, unit_bf, feed, w_output, order_kv))
     last_far = swap_ctx(first[:, last:], 1)
     pos_all = jnp.stack([first[:, last:], last_far], axis=0)[:, :, :, :tokens].astype(f32)
     pos_all = (pos_all[:, :, 1] * 64.0 + pos_all[:, :, 2]).reshape(seq_len)
@@ -830,10 +853,10 @@
                 ((tokens, heads * head_width), BF),
                 ((tokens, heads), f32),
             ],
-            [((heads * head_width, width), BF), ((2 * head_width, width), BF)],
+            [((2 * head_width, width), BF)],
             12_000_000_000,
             (
-                unit_in, near, far, first, other, order_q, order_kv, scale_in, scale_query, scale_key,
+                unit_in, near, far, first, other, owner_of, order_kv, scale_in, scale_query, scale_key,
                 cos_all, sine_all, key_index, row_index,
             ),
             mebibytes=52,
@@ -845,18 +868,17 @@
     feed_c0 = swap_ctx(feed, 1)
     feed_c1 = swap_ctx(feed_z1, 1)
     feed_c2 = swap_ctx(feed_z2, 1)
-    held_out, ahead, projected, middle, pre = call_kernel(
+    full_output, projected, middle, pre = call_kernel(
         project_kernel,
         [
             ((owners * rows_q, width), BF),
-            ((tokens, owners * rows_q), BF),
             ((tokens, width), f32),
             ((tokens, width), f32),
             ((tokens, width), BF),
         ],
         [],
         2_000_000_000,
-        (attn_bf, order_q, out_own, out_other, resid, scale_attn, scale_pre),
+        (attn_bf, owner_of, out_own, out_other, resid, scale_attn, scale_pre),
     )
     pres = swaps(pre, swap_dp)
     pre, pres, feed_z3, feed_c0, feed_c1, feed_c2 = tie((pre, pres, feed_z3, feed_c0, feed_c1, feed_c2))
@@ -916,11 +938,11 @@
             ((1, width), f32),
             ((1, width), f32),
         ],
-        [],
+        [((owners * rows_q, width), BF)],
         3_000_000_000,
         [parts[0]]
         + comes
-        + [grad_out[0], projected, middle, held_out, ahead, order_q, scale_attn, scale_pre],
+        + [grad_out[0], projected, middle, full_output, attn_bf, owner_of, scale_attn, scale_pre],
     )
     g_out = add_bf16(g_out, swap_ctx(g_out_far, 1)).astype(BF).reshape(count_dp, chips, rows_q, width)
     g_out, g_feed, grad_attn = tie((g_out, g_feed, grad_attn))
@@ -946,14 +968,15 @@
             ((heads * tokens, head_width), BF),
             ((tokens, heads * head_width), BF),
             ((2 * head_width, width), BF),
+            ((heads * head_width, width), BF),
         ],
         12_000_000_000,
         (
             grad_attn, attn_bf, query_bf, key_bf, value_bf, lse, query_raw, key_raw, w_q, w_kv,
             scale_query, scale_key, cos_all, sine_all, key_index, row_index, normed, normed_all,
-            unit_in, near, far, order_q, order_kv,
+            unit_in, near, far, owner_of, order_kv,
         ),
-        mebibytes=24,
+        mebibytes=36,
     )
     back = (packed, packed_far, g_near, g_far, grad_normed_q, grad_s_in, grad_s_query, grad_s_key)
     back, feed_come1, feed_come2, out_comes, g_out, g_feed = tie(
@@ -976,22 +999,42 @@
     own_kv = scatter_over(far_sum, swap_z, chips).astype(BF)
     packed, own_kv, out_sum, g_feed = tie((packed.astype(BF), own_kv, out_sum, g_feed))
     own_normed = jnp.dot(own_kv, w_kv, preferred_element_type=jnp.float32) + grad_normed_q
-    feed_come3 = jnp.concatenate([feed_come3, swap_z(g_feed[3, 3 * rows_f // 2 :], 3)], axis=0)
-    own_feed = add_bf16(g_feed[0], feed_come1, feed_come2, feed_come3)
-    own_output = scatter_over(out_sum, swap_z, chips)
-    own_first = scatter_over(packed, swap_z, chips)
+    half_rows = 3 * rows_f // 2
+    feed_end3 = swap_z(g_feed[3, half_rows:], 3)
+    out_comes = [swap_z(out_sum[bits], bits) for bits in range(1, 4)]
+    first_comes = [swap_z(packed[bits], bits) for bits in range(1, 4)]
+    own_query, own_key, own_value, own_last, own_output, own_gate, own_up, own_down = call_kernel(
+        ending_kernel,
+        [
+            ((rows_q, width), f32),
+            ((rows_k, width), f32),
+            ((rows_k, width), f32),
+            ((8, width), f32),
+            ((rows_q, width), f32),
+            ((rows_f, width), f32),
+            ((rows_f, width), f32),
+            ((rows_f, width), f32),
+        ],
+        [],
+        10_000_000,
+        [packed[0]]
+        + first_comes
+        + [out_sum[0]]
+        + out_comes
+        + [g_feed[0], feed_come1, feed_come2, feed_come3, feed_end3],
+    )
     grad_resid = grad_resid_a + rms_back(unit_in, inverse_in, own_normed * (1.0 + scale_in))
     return (
         block_out[None],
         grad_resid[None],
-        own_first[:rows_q],
-        own_first[rows_q : rows_q + rows_k],
-        own_first[rows_q + rows_k : last],
+        own_query,
+        own_key,
+        own_value,
         own_output,
-        own_feed[:rows_f],
-        own_feed[rows_f : 2 * rows_f],
-        own_feed[2 * rows_f :],
-        own_first[last, :scale_part],
+        own_gate,
+        own_up,
+        own_down,
+        own_last[0, :scale_part],
     )
 
 

time: 192 us -> 186 us (0.969)
  other arithmetic: 15.7 us -> 10.9 us
  Pallas kernels: 28.5 us -> 26.3 us
    concatenate x0 -> x1, local copies, waits for them, and re-layouts: none -> 2.24 us  [shards_kernels(): first = jnp.concatenate([w_query, w_key, w_value, last_rows], axis=0)]
    pallas_call x8 -> x9, Pallas kernels: 28.5 us -> 26.3 us  [call_kernel(): pl.pallas_call(body, out_shape=[jax.ShapeDtypeStruct(shape, dtype) for sh...]
    convert_element_type x2 -> x1, other arithmetic: 2.87 us -> 0.71 us  [shards_kernels(): (posit % 64).astype(BF)]
    slice x3 -> x0, local copies, waits for them, and re-layouts: 2.04 us -> none  [the longest x1 0.79 us: shards_kernels(): own_feed[2 * rows_f:]]
    unnamed x70 -> x60, local copies, waits for them, and re-layouts: 4.49 us -> 2.58 us
  transfers between devices with their start and end apart: 62 -> 62, of which waited for: 29 -> 29; matrix products, arithmetic and copies ran while one was open for 8% -> 6% of each run, Pallas kernels for 12% -> 10%
where the time goes in v3:
time: 186 us; the launch traced here: 185 us
  starting transfers between devices  70.4 us (38%)
  waiting for transfers between devices  65.4 us (35%)
  Pallas kernels  26.3 us (14%)
  other arithmetic  10.9 us (6%)
  local copies, waits for them, and re-layouts  10.2 us (5%)
    ppermute x38, starting transfers between devices, swap_ctx(): lax.ppermute(block, 'ctx', [(place, place ^ bits) for place in range(coun...  41 us
    ppermute x38, waiting for transfers between devices, swap_ctx(): lax.ppermute(block, 'ctx', [(place, place ^ bits) for place in range(coun...  36.7 us
    ppermute x24, starting transfers between devices, swap_dp(): lax.ppermute(block, 'dp', [(place, place ^ bits) for place in range(count)])  29.4 us
    ppermute x24, waiting for transfers between devices, swap_dp(): lax.ppermute(block, 'dp', [(place, place ^ bits) for place in range(count)])  28.7 us
    pallas_call x9, Pallas kernels, call_kernel(): pl.pallas_call(body, out_shape=[jax.ShapeDtypeStruct(shape, dtype) for sh...  26.3 us
  transfers between devices with their start and end apart: 62, of which 29 were waited for; matrix products, arithmetic and copies ran while one was open for 6% of the time, Pallas kernels for 10%

profile of v3, /device:TPU:0, one launch (start us, length us, event | category | flops | bytes accessed | tf_op | source)
XLA Modules:
  0.0 185.2 jit_solution(5829512806353609833)
XLA Ops:
  2.1 2.2 %concatenate.28 = bf16[56,640]{1,0:T(8,128)(2,1)S(1)} concatenate(bf16[32,640]{1,0:T(8,128)(2,1)} %param.13, bf16[8,640]{1,0:T(8,128)(2,1)} %param.14, bf16[8,640]{1,0:T(8,128)(2,1)} %param.15, bf16[1,640]{1,0:T(2,128)(2,1)S(1)} %pad.19, bf16[1,640]{1,0:T(2,128)(2,1)S(1)} %pad.20, bf16[1,640]{1,0:T(2,128)(2,1)S(1)} %pad.21, bf16[5,640]{1,0:T(8,128)(2,1)S(1)} %broadcast_in_dim.72), dimensions={0} | concatenate | bytes 143360 | tf_op jit(solution)/shard_map/concatenate | solution.py:809
  4.3 5.1 %collective-permute-start.2 = (bf16[1,56,640]{2,1,0:T(8,128)(2,1)S(1)}, bf16[1,56,640]{2,1,0:T(8,128)(2,1)S(1)}, u32[]{:S(2)}, u32[]{:S(2)}) collective-permute-start(bf16[1,56,640]{2,1,0:T(8,128)(2,1)S(1)} %bitcast.115), channel_id=1, source_target_pairs={{0,6},{1,7},{2,4},{3,5},{4,2},{5,3},{6,0},{7,1},{8,14},{9,15},{10,... | collective-permute-start | bytes 215048 | tf_op jit(solution)/shard_map/ppermute | solution.py:75
  13.4 2.1 %collective-permute-done.1 = bf16[1,56,640]{2,1,0:T(8,128)(2,1)S(1)} collective-permute-done((bf16[1,56,640]{2,1,0:T(8,128)(2,1)S(1)}, bf16[1,56,640]{2,1,0:T(8,128)(2,1)S(1)}, u32[]{:S(2)}, u32[]{:S(2)}) %collective-permute-start.1) | collective-permute-done | bytes 71712 | tf_op jit(solution)/shard_map/ppermute | solution.py:75
  15.6 2.8 %collective-permute-start.8 = (bf16[1,128,640]{2,1,0:T(8,128)(2,1)S(1)}, bf16[1,128,640]{2,1,0:T(8,128)(2,1)S(1)}, u32[]{:S(2)}, u32[]{:S(2)}) collective-permute-start(bf16[1,128,640]{2,1,0:T(8,128)(2,1)S(1)} %bitcast.111), channel_id=1, source_target_pairs={{0,6},{1,7},{2,4},{3,5},{4,2},{5,3},{6,0},{7,1},{8,14},{9,15},{10,... | collective-permute-start | bytes 491528 | tf_op jit(solution)/shard_map/ppermute | solution.py:75
  18.4 1.7 collective-permute-start.6
  20.1 2.4 %collective-permute-start.5 = (bf16[1,4,56,640]{3,2,1,0:T(8,128)(2,1)S(1)}, bf16[1,4,56,640]{3,2,1,0:T(8,128)(2,1)S(1)}, u32[]{:S(2)}, u32[]{:S(2)}) collective-permute-start(bf16[1,4,56,640]{3,2,1,0:T(8,128)(2,1)S(1)} %bitcast.100), channel_id=1, source_target_pairs={{0,24},{8,16},{16,8},{24,0},{1,25},{9,17},{17,9},{25,1},{2,26},{10... | collective-permute-start | bytes 860168 | tf_op jit(solution)/shard_map/ppermute | solution.py:70
  23.1 1.6 collective-permute-done.8
  24.6 1.5 collective-permute-start.3
  26.1 3.1 %multiply_sine_fusion = (f32[1024,128]{1,0:T(8,128)}, f32[1024,128]{1,0:T(8,128)}) fusion(f32[128]{0:T(128)S(1)} %multiply_power_fusion, f32[1024]{0:T(1024)S(1)} %bitcast.125), kind=kLoop, calls=%fused_computation.11 | loop fusion | flops 131072 | bytes 1053184 | tf_op jit(solution)/shard_map/sin | solution.py:822
  29.2 4.0 %collective-permute-done.7 = bf16[1,128,640]{2,1,0:T(8,128)(2,1)S(1)} collective-permute-done((bf16[1,128,640]{2,1,0:T(8,128)(2,1)S(1)}, bf16[1,128,640]{2,1,0:T(8,128)(2,1)S(1)}, u32[]{:S(2)}, u32[]{:S(2)}) %collective-permute-start.7) | collective-permute-done | bytes 163872 | tf_op jit(solution)/shard_map/ppermute | solution.py:75
  33.4 2.1 %collective-permute-done.4 = bf16[1,4,56,640]{3,2,1,0:T(8,128)(2,1)S(1)} collective-permute-done((bf16[1,4,56,640]{3,2,1,0:T(8,128)(2,1)S(1)}, bf16[1,4,56,640]{3,2,1,0:T(8,128)(2,1)S(1)}, u32[]{:S(2)}, u32[]{:S(2)}) %collective-permute-start.4) | collective-permute-done | bytes 286752 | tf_op jit(solution)/shard_map/ppermute | solution.py:70
  36.4 2.7 %collective-permute-start.14 = (bf16[1,32,640]{2,1,0:T(8,128)(2,1)S(1)}, bf16[1,32,640]{2,1,0:T(8,128)(2,1)S(1)}, u32[]{:S(2)}, u32[]{:S(2)}) collective-permute-start(bf16[1,32,640]{2,1,0:T(8,128)(2,1)S(1)} %bitcast.119), channel_id=1, source_target_pairs={{0,6},{1,7},{2,4},{3,5},{4,2},{5,3},{6,0},{7,1},{8,14},{9,15},{10,... | collective-permute-start | bytes 122888 | tf_op jit(solution)/shard_map/ppermute | solution.py:75
  39.2 1.8 collective-permute-start.13
  41.1 1.3 collective-permute-done.14
  42.4 2.4 %collective-permute-done.13 = bf16[1,32,640]{2,1,0:T(8,128)(2,1)S(1)} collective-permute-done((bf16[1,32,640]{2,1,0:T(8,128)(2,1)S(1)}, bf16[1,32,640]{2,1,0:T(8,128)(2,1)S(1)}, u32[]{:S(2)}, u32[]{:S(2)}) %collective-permute-start.13) | collective-permute-done | bytes 40992 | tf_op jit(solution)/shard_map/ppermute | solution.py:75
  46.1 2.5 %collective-permute-start.19 = (bf16[1,4,32,640]{3,2,1,0:T(8,128)(2,1)S(1)}, bf16[1,4,32,640]{3,2,1,0:T(8,128)(2,1)S(1)}, u32[]{:S(2)}, u32[]{:S(2)}) collective-permute-start(bf16[1,4,32,640]{3,2,1,0:T(8,128)(2,1)S(1)} %bitcast.107), channel_id=1, source_target_pairs={{0,24},{8,16},{16,8},{24,0},{1,25},{9,17},{17,9},{25,1},{2,26},{10... | collective-permute-start | bytes 491528 | tf_op jit(solution)/shard_map/ppermute | solution.py:70
  50.7 1.3 collective-permute-start.15
  52.0 8.2 %shard_map.186 = (bf16[1024,640]{1,0:T(8,128)(2,1)}, bf16[512,640]{1,0:T(8,128)(2,1)}, bf16[128,640]{1,0:T(8,128)(2,1)S(1)}, bf16[1024,640]{1,0:T(8,128)(2,1)}, ...) custom-call(f32[128,640]{1,0:T(8,128)S(1)} %get-tuple-element.253.un, ...), custom_call_target="tpu_custom_call" | custom-call | flops 12000000000 | bytes 20000000 | tf_op jit(solution)/shard_map/pallas_call | solution.py:204
  60.4 1.4 collective-permute-done.16.refs_6_
  62.8 1.7 collective-permute-start.24
  64.5 1.2 shard_map.187
  65.8 2.4 %collective-permute-start.23 = (bf16[128,640]{1,0:T(8,128)(2,1)S(1)}, bf16[128,640]{1,0:T(8,128)(2,1)S(1)}, u32[]{:S(2)}, u32[]{:S(2)}) collective-permute-start(bf16[128,640]{1,0:T(8,128)(2,1)S(1)} %get-tuple-element.152.refs_0_), channel_id=1, source_target_pairs={{0,24},{8,16},{16,8},{24,0},{1,25},{9,17},{17,9},{25,1},{2,26},{10... | collective-permute-start | bytes 491528 | tf_op jit(solution)/shard_map/ppermute | solution.py:70
  69.4 3.3 %collective-permute-done.24.refs_7_ = bf16[192,640]{1,0:T(8,128)(2,1)S(1)} collective-permute-done((bf16[192,640]{1,0:T(8,128)(2,1)S(1)}, bf16[192,640]{1,0:T(8,128)(2,1)S(1)}, u32[]{:S(2)}, u32[]{:S(2)}) %collective-permute-start.24) | collective-permute-done | bytes 245792 | tf_op jit(solution)/shard_map/ppermute | solution.py:75
  73.8 2.4 %collective-permute-done.22.refs_2_ = bf16[128,640]{1,0:T(8,128)(2,1)S(1)} collective-permute-done((bf16[128,640]{1,0:T(8,128)(2,1)S(1)}, bf16[128,640]{1,0:T(8,128)(2,1)S(1)}, u32[]{:S(2)}, u32[]{:S(2)}) %collective-permute-start.22) | collective-permute-done | bytes 163872 | tf_op jit(solution)/shard_map/ppermute | solution.py:70
  76.2 1.5 collective-permute-done.28.refs_11_
  77.7 2.7 %shard_map.188 = (f32[128,640]{1,0:T(8,128)S(1)}, bf16[128,640]{1,0:T(8,128)(2,1)S(1)}, bf16[128,640]{1,0:T(8,128)(2,1)S(1)}, bf16[128,640]{1,0:T(8,128)(2,1)S(1...) custom-call(bf16[128,640]{1,0:T(8,128)(2,1)S(1)} %get-tuple-element., ...), custom_call_target="tpu_custom_call" | custom-call | flops 3000000000 | bytes 20000000 | tf_op jit(solution)/shard_map/pallas_call | solution.py:204
  80.4 1.6 collective-permute-start.29
  82.8 1.2 collective-permute-start.31
  83.9 3.5 %collective-permute-done.29.come1_ref = bf16[128,640]{1,0:T(8,128)(2,1)S(1)} collective-permute-done((bf16[128,640]{1,0:T(8,128)(2,1)S(1)}, bf16[128,640]{1,0:T(8,128)(2,1)S(1)}, u32[]{:S(2)}, u32[]{:S(2)}) %collective-permute-start.29) | collective-permute-done | bytes 163872 | tf_op jit(solution)/shard_map/ppermute | solution.py:70
  87.5 3.9 %collective-permute-done.30.come2_ref = bf16[128,640]{1,0:T(8,128)(2,1)S(1)} collective-permute-done((bf16[128,640]{1,0:T(8,128)(2,1)S(1)}, bf16[128,640]{1,0:T(8,128)(2,1)S(1)}, u32[]{:S(2)}, u32[]{:S(2)}) %collective-permute-start.30) | collective-permute-done | bytes 163872 | tf_op jit(solution)/shard_map/ppermute | solution.py:70
  92.4 1.4 collective-permute-start.34
  94.4 1.5 collective-permute-start.32
  95.9 4.3 %collective-permute-done.34.refs_3_ = bf16[128,640]{1,0:T(8,128)(2,1)S(1)} collective-permute-done((bf16[128,640]{1,0:T(8,128)(2,1)S(1)}, bf16[128,640]{1,0:T(8,128)(2,1)S(1)}, u32[]{:S(2)}, u32[]{:S(2)}) %collective-permute-start.34) | collective-permute-done | bytes 163872 | tf_op jit(solution)/shard_map/ppermute | solution.py:70
  100.2 1.7 collective-permute-done.33.refs_2_
  101.9 2.6 %shard_map.190 = (f32[128,640]{1,0:T(8,128)S(1)}, bf16[128,640]{1,0:T(8,128)(2,1)S(1)}, bf16[128,640]{1,0:T(8,128)(2,1)S(1)}, bf16[128,640]{1,0:T(8,128)(2,1)S(1...) custom-call(bf16[128,640]{1,0:T(8,128)(2,1)S(1)} %get-tuple-element.166.refs_0_, ...), custom_call_target="tpu_custom_call" | custom-call | flops 3000000000 | bytes 20000000 | tf_op jit(solution)/shard_map/pallas_call | solution.py:204
  105.4 1.3 collective-permute-start.36
  106.7 1.4 collective-permute-start.37
  108.1 1.6 shard_map.191
  109.7 2.0 %collective-permute-done.35.come1_ref = bf16[128,640]{1,0:T(8,128)(2,1)S(1)} collective-permute-done((bf16[128,640]{1,0:T(8,128)(2,1)S(1)}, bf16[128,640]{1,0:T(8,128)(2,1)S(1)}, u32[]{:S(2)}, u32[]{:S(2)}) %collective-permute-start.35) | collective-permute-done | bytes 163872 | tf_op jit(solution)/shard_map/ppermute | solution.py:70
  111.7 2.7 %collective-permute-done.36.come2_ref = bf16[128,640]{1,0:T(8,128)(2,1)S(1)} collective-permute-done((bf16[128,640]{1,0:T(8,128)(2,1)S(1)}, bf16[128,640]{1,0:T(8,128)(2,1)S(1)}, u32[]{:S(2)}, u32[]{:S(2)}) %collective-permute-start.36) | collective-permute-done | bytes 163872 | tf_op jit(solution)/shard_map/ppermute | solution.py:70
  114.4 1.8 shard_map.192
  116.8 1.7 collective-permute-done.38
  119.2 1.3 collective-permute-start.44
  120.4 1.4 collective-permute-start.43
  123.1 2.4 %collective-permute-start.40 = (bf16[192,640]{1,0:T(8,128)(2,1)S(1)}, bf16[192,640]{1,0:T(8,128)(2,1)S(1)}, u32[]{:S(2)}, u32[]{:S(2)}) collective-permute-start(bf16[192,640]{1,0:T(8,128)(2,1)S(1)} %get-tuple-element.258), channel_id=1, source_target_pairs={{0,2},{1,3},{2,0},{3,1},{4,6},{5,7},{6,4},{7,5},{8,10},{9,11},{10,... | collective-permute-start | bytes 737288 | tf_op jit(solution)/shard_map/ppermute | solution.py:75
  125.6 6.3 %shard_map.193 = (bf16[16,48,640]{2,1,0:T(8,128)(2,1)S(1)}, bf16[16,48,640]{2,1,0:T(8,128)(2,1)S(1)}, bf16[512,512]{1,0:T(8,128)(2,1)S(1)}, bf16[512,512]{1,0:T(...) custom-call(bf16[128,1024]{1,0:T(8,128)(2,1)S(1)} %get-tuple-element, ...), custom_call_target="tpu_custom_call" | custom-call | flops 12000000000 | bytes 20000000 | tf_op jit(solution)/shard_map/pallas_call | solution.py:204
  133.7 2.2 %collective-permute-done.41.refs_10_ = bf16[192,640]{1,0:T(8,128)(2,1)S(1)} collective-permute-done((bf16[192,640]{1,0:T(8,128)(2,1)S(1)}, bf16[192,640]{1,0:T(8,128)(2,1)S(1)}, u32[]{:S(2)}, u32[]{:S(2)}) %collective-permute-start.41) | collective-permute-done | bytes 245792 | tf_op jit(solution)/shard_map/ppermute | solution.py:75
  138.7 1.8 collective-permute-start.48
  140.5 1.2 fusion.4
  142.3 3.9 %collective-permute-done.48.refs_11_ = bf16[96,640]{1,0:T(8,128)(2,1)S(1)} collective-permute-done((bf16[96,640]{1,0:T(8,128)(2,1)S(1)}, bf16[96,640]{1,0:T(8,128)(2,1)S(1)}, u32[]{:S(2)}, u32[]{:S(2)}) %collective-permute-start.48) | collective-permute-done | bytes 122912 | tf_op jit(solution)/shard_map/ppermute | solution.py:75
  146.4 2.6 %collective-permute-start.54 = (bf16[128,512]{1,0:T(8,128)(2,1)S(1)}, bf16[128,512]{1,0:T(8,128)(2,1)S(1)}, u32[]{:S(2)}, u32[]{:S(2)}) collective-permute-start(bf16[128,512]{1,0:T(8,128)(2,1)S(1)} %get-tuple-element.263), channel_id=1, source_target_pairs={{0,6},{1,7},{2,4},{3,5},{4,2},{5,3},{6,0},{7,1},{8,14},{9,15},{10,... | collective-permute-start | bytes 393224 | tf_op jit(solution)/shard_map/ppermute | solution.py:75
  149.9 1.3 collective-permute-start.49
  151.3 1.4 collective-permute-start.51
  153.6 2.5 %collective-permute-done.54 = bf16[128,512]{1,0:T(8,128)(2,1)S(1)} collective-permute-done((bf16[128,512]{1,0:T(8,128)(2,1)S(1)}, bf16[128,512]{1,0:T(8,128)(2,1)S(1)}, u32[]{:S(2)}, u32[]{:S(2)}) %collective-permute-start.54) | collective-permute-done | bytes 131104 | tf_op jit(solution)/shard_map/ppermute | solution.py:75
  156.1 4.9 %collective-permute-done.53 = bf16[128,512]{1,0:T(8,128)(2,1)S(1)} collective-permute-done((bf16[128,512]{1,0:T(8,128)(2,1)S(1)}, bf16[128,512]{1,0:T(8,128)(2,1)S(1)}, u32[]{:S(2)}, u32[]{:S(2)}) %collective-permute-start.53) | collective-permute-done | bytes 131104 | tf_op jit(solution)/shard_map/ppermute | solution.py:75
  161.1 3.3 %collective-permute-done.51 = bf16[4,56,640]{2,1,0:T(8,128)(2,1)S(1)} collective-permute-done((bf16[4,56,640]{2,1,0:T(8,128)(2,1)S(1)}, bf16[4,56,640]{2,1,0:T(8,128)(2,1)S(1)}, u32[]{:S(2)}, u32[]{:S(2)}) %collective-permute-start.51) | collective-permute-done | bytes 286752 | tf_op jit(solution)/shard_map/ppermute | solution.py:70
  164.4 1.4 collective-permute-done.50
  167.2 1.9 %collective-permute-start.61 = (bf16[96,640]{1,0:T(8,128)(2,1)S(1)}, bf16[96,640]{1,0:T(8,128)(2,1)S(1)}, u32[]{:S(2)}, u32[]{:S(2)}) collective-permute-start(bf16[96,640]{1,0:T(8,128)(2,1)S(1)} %slice_bitcast_fusion.9), channel_id=1, source_target_pairs={{0,6},{1,7},{2,4},{3,5},{4,2},{5,3},{6,0},{7,1},{8,14},{9,15},{10,... | collective-permute-start | bytes 368648 | tf_op jit(solution)/shard_map/ppermute | solution.py:75
  169.1 2.1 %collective-permute-start.60 = (bf16[32,640]{1,0:T(8,128)(2,1)S(1)}, bf16[32,640]{1,0:T(8,128)(2,1)S(1)}, u32[]{:S(2)}, u32[]{:S(2)}) collective-permute-start(bf16[32,640]{1,0:T(8,128)(2,1)S(1)} %get-tuple-element.271), channel_id=1, source_target_pairs={{0,6},{1,7},{2,4},{3,5},{4,2},{5,3},{6,0},{7,1},{8,14},{9,15},{10,... | collective-permute-start | bytes 122888 | tf_op jit(solution)/shard_map/ppermute | solution.py:75
  171.2 2.4 %collective-permute-start.58 = (bf16[32,640]{1,0:T(8,128)(2,1)S(1)}, bf16[32,640]{1,0:T(8,128)(2,1)S(1)}, u32[]{:S(2)}, u32[]{:S(2)}) collective-permute-start(bf16[32,640]{1,0:T(8,128)(2,1)S(1)} %get-tuple-element.273), channel_id=1, source_target_pairs={{0,2},{1,3},{2,0},{3,1},{4,6},{5,7},{6,4},{7,5},{8,10},{9,11},{10,... | collective-permute-start | bytes 122888 | tf_op jit(solution)/shard_map/ppermute | solution.py:75
  173.6 2.1 %collective-permute-start.57 = (bf16[56,640]{1,0:T(8,128)(2,1)S(1)}, bf16[56,640]{1,0:T(8,128)(2,1)S(1)}, u32[]{:S(2)}, u32[]{:S(2)}) collective-permute-start(bf16[56,640]{1,0:T(8,128)(2,1)S(1)} %get-tuple-element.265), channel_id=1, source_target_pairs={{0,6},{1,7},{2,4},{3,5},{4,2},{5,3},{6,0},{7,1},{8,14},{9,15},{10,... | collective-permute-start | bytes 215048 | tf_op jit(solution)/shard_map/ppermute | solution.py:75
  176.5 2.9 %collective-permute-start.56 = (bf16[56,640]{1,0:T(8,128)(2,1)S(1)}, bf16[56,640]{1,0:T(8,128)(2,1)S(1)}, u32[]{:S(2)}, u32[]{:S(2)}) collective-permute-start(bf16[56,640]{1,0:T(8,128)(2,1)S(1)} %get-tuple-element.266), channel_id=1, source_target_pairs={{0,4},{1,5},{2,6},{3,7},{4,0},{5,1},{6,2},{7,3},{8,12},{9,13},{10,... | collective-permute-start | bytes 215048 | tf_op jit(solution)/shard_map/ppermute | solution.py:75
  180.4 1.4 collective-permute-done.56.refs_2_
  181.8 2.0 %collective-permute-done.55.refs_1_ = bf16[56,640]{1,0:T(8,128)(2,1)S(1)} collective-permute-done((bf16[56,640]{1,0:T(8,128)(2,1)S(1)}, bf16[56,640]{1,0:T(8,128)(2,1)S(1)}, u32[]{:S(2)}, u32[]{:S(2)}) %collective-permute-start.55) | collective-permute-done | bytes 71712 | tf_op jit(solution)/shard_map/ppermute | solution.py:75
  (199 shorter events, 31.3 us)
Async XLA Ops:
  4.3 9.1 %collective-permute-start.2 = (bf16[1,56,640]{2,1,0:T(8,128)(2,1)S(1)}, bf16[1,56,640]{2,1,0:T(8,128)(2,1)S(1)}, u32[]{:S(2)}, u32[]{:S(2)}) collective-permute-start(bf16[1,56,640]{2,1,0:T(8,128)(2,1)S(1)} %bitcast.115), channel_id=1, source_target_pairs={{0,6},{1,7},{2,4},{3,5},{4,2},{5,3},{6,0},{7,1},{8,14},{9,15},{10,... | collective-permute-start | bytes 215048 | tf_op jit(solution)/shard_map/ppermute | solution.py:75
  9.4 6.1 %collective-permute-start.1 = (bf16[1,56,640]{2,1,0:T(8,128)(2,1)S(1)}, bf16[1,56,640]{2,1,0:T(8,128)(2,1)S(1)}, u32[]{:S(2)}, u32[]{:S(2)}) collective-permute-start(bf16[1,56,640]{2,1,0:T(8,128)(2,1)S(1)} %bitcast.116), channel_id=1, source_target_pairs={{0,4},{1,5},{2,6},{3,7},{4,0},{5,1},{6,2},{7,3},{8,12},{9,13},{10,... | collective-permute-start | bytes 215048 | tf_op jit(solution)/shard_map/ppermute | solution.py:75
  9.4 6.1 %collective-permute-start = (bf16[1,56,640]{2,1,0:T(8,128)(2,1)S(1)}, bf16[1,56,640]{2,1,0:T(8,128)(2,1)S(1)}, u32[]{:S(2)}, u32[]{:S(2)}) collective-permute-start(bf16[1,56,640]{2,1,0:T(8,128)(2,1)S(1)} %bitcast.117), channel_id=1, source_target_pairs={{0,2},{1,3},{2,0},{3,1},{4,6},{5,7},{6,4},{7,5},{8,10},{9,11},{10,... | collective-permute-start | bytes 215048 | tf_op jit(solution)/shard_map/ppermute | solution.py:75
  15.6 7.0 %collective-permute-start.9 = (bf16[4,8,640]{2,1,0:T(8,128)(2,1)S(1)}, bf16[4,8,640]{2,1,0:T(8,128)(2,1)S(1)}, u32[]{:S(2)}, u32[]{:S(2)}) collective-permute-start(bf16[4,8,640]{2,1,0:T(8,128)(2,1)S(1)} %get-tuple-element.270), channel_id=1, source_target_pairs={{0,1},{1,0},{2,3},{3,2},{4,5},{5,4},{6,7},{7,6},{8,9},{9,8},{10,11... | collective-permute-start | bytes 122888 | tf_op jit(solution)/shard_map/ppermute | solution.py:75
  15.6 9.0 %collective-permute-start.8 = (bf16[1,128,640]{2,1,0:T(8,128)(2,1)S(1)}, bf16[1,128,640]{2,1,0:T(8,128)(2,1)S(1)}, u32[]{:S(2)}, u32[]{:S(2)}) collective-permute-start(bf16[1,128,640]{2,1,0:T(8,128)(2,1)S(1)} %bitcast.111), channel_id=1, source_target_pairs={{0,6},{1,7},{2,4},{3,5},{4,2},{5,3},{6,0},{7,1},{8,14},{9,15},{10,... | collective-permute-start | bytes 491528 | tf_op jit(solution)/shard_map/ppermute | solution.py:75
  18.4 14.8 %collective-permute-start.7 = (bf16[1,128,640]{2,1,0:T(8,128)(2,1)S(1)}, bf16[1,128,640]{2,1,0:T(8,128)(2,1)S(1)}, u32[]{:S(2)}, u32[]{:S(2)}) collective-permute-start(bf16[1,128,640]{2,1,0:T(8,128)(2,1)S(1)} %bitcast.112), channel_id=1, source_target_pairs={{0,4},{1,5},{2,6},{3,7},{4,0},{5,1},{6,2},{7,3},{8,12},{9,13},{10,... | collective-permute-start | bytes 491528 | tf_op jit(solution)/shard_map/ppermute | solution.py:75
  18.4 14.8 %collective-permute-start.6 = (bf16[1,128,640]{2,1,0:T(8,128)(2,1)S(1)}, bf16[1,128,640]{2,1,0:T(8,128)(2,1)S(1)}, u32[]{:S(2)}, u32[]{:S(2)}) collective-permute-start(bf16[1,128,640]{2,1,0:T(8,128)(2,1)S(1)} %bitcast.113), channel_id=1, source_target_pairs={{0,2},{1,3},{2,0},{3,1},{4,6},{5,7},{6,4},{7,5},{8,10},{9,11},{10,... | collective-permute-start | bytes 491528 | tf_op jit(solution)/shard_map/ppermute | solution.py:75
  20.1 13.3 %collective-permute-start.5 = (bf16[1,4,56,640]{3,2,1,0:T(8,128)(2,1)S(1)}, bf16[1,4,56,640]{3,2,1,0:T(8,128)(2,1)S(1)}, u32[]{:S(2)}, u32[]{:S(2)}) collective-permute-start(bf16[1,4,56,640]{3,2,1,0:T(8,128)(2,1)S(1)} %bitcast.100), channel_id=1, source_target_pairs={{0,24},{8,16},{16,8},{24,0},{1,25},{9,17},{17,9},{25,1},{2,26},{10... | collective-permute-start | bytes 860168 | tf_op jit(solution)/shard_map/ppermute | solution.py:70
  22.6 12.9 %collective-permute-start.4 = (bf16[1,4,56,640]{3,2,1,0:T(8,128)(2,1)S(1)}, bf16[1,4,56,640]{3,2,1,0:T(8,128)(2,1)S(1)}, u32[]{:S(2)}, u32[]{:S(2)}) collective-permute-start(bf16[1,4,56,640]{3,2,1,0:T(8,128)(2,1)S(1)} %bitcast.101), channel_id=1, source_target_pairs={{0,16},{8,24},{16,0},{24,8},{1,17},{9,25},{17,1},{25,9},{2,18},{10... | collective-permute-start | bytes 860168 | tf_op jit(solution)/shard_map/ppermute | solution.py:70
  24.6 10.9 %collective-permute-start.3 = (bf16[1,4,56,640]{3,2,1,0:T(8,128)(2,1)S(1)}, bf16[1,4,56,640]{3,2,1,0:T(8,128)(2,1)S(1)}, u32[]{:S(2)}, u32[]{:S(2)}) collective-permute-start(bf16[1,4,56,640]{3,2,1,0:T(8,128)(2,1)S(1)} %bitcast.102), channel_id=1, source_target_pairs={{0,8},{8,0},{16,24},{24,16},{1,9},{9,1},{17,25},{25,17},{2,10},{10... | collective-permute-start | bytes 860168 | tf_op jit(solution)/shard_map/ppermute | solution.py:70
  35.8 16.3 %copy-start.21 = (bf16[4,4,56,640]{3,2,1,0:T(8,128)(2,1)}, bf16[4,4,56,640]{3,2,1,0:T(8,128)(2,1)S(1)}, u32[]{:S(2)}) copy-start(bf16[4,4,56,640]{3,2,1,0:T(8,128)(2,1)S(1)} %pad_maximum_fusion) | copy-start | bytes 3440644
  35.8 9.3 %collective-permute-start.10 = (bf16[16,56,640]{2,1,0:T(8,128)(2,1)S(1)}, bf16[16,56,640]{2,1,0:T(8,128)(2,1)}, u32[]{:S(2)}, u32[]{:S(2)}) collective-permute-start(bf16[16,56,640]{2,1,0:T(8,128)(2,1)S(1)} %bitcast.104), channel_id=1, source_target_pairs={{0,1},{1,0},{2,3},{3,2},{4,5},{5,4},{6,7},{7,6},{8,9},{9,8},{10,11... | collective-permute-start | bytes 3440648 | tf_op jit(solution)/shard_map/ppermute | solution.py:75
  35.9 9.2 %collective-permute-start.11 = (bf16[512,640]{1,0:T(8,128)(2,1)S(1)}, bf16[512,640]{1,0:T(8,128)(2,1)S(1)}, u32[]{:S(2)}, u32[]{:S(2)}) collective-permute-start(bf16[512,640]{1,0:T(8,128)(2,1)S(1)} %bitcast.83), channel_id=1, source_target_pairs={{0,1},{1,0},{2,3},{3,2},{4,5},{5,4},{6,7},{7,6},{8,9},{9,8},{10,11... | collective-permute-start | bytes 1966088 | tf_op jit(solution)/shard_map/ppermute | solution.py:75
  36.4 5.9 %collective-permute-start.14 = (bf16[1,32,640]{2,1,0:T(8,128)(2,1)S(1)}, bf16[1,32,640]{2,1,0:T(8,128)(2,1)S(1)}, u32[]{:S(2)}, u32[]{:S(2)}) collective-permute-start(bf16[1,32,640]{2,1,0:T(8,128)(2,1)S(1)} %bitcast.119), channel_id=1, source_target_pairs={{0,6},{1,7},{2,4},{3,5},{4,2},{5,3},{6,0},{7,1},{8,14},{9,15},{10,... | collective-permute-start | bytes 122888 | tf_op jit(solution)/shard_map/ppermute | solution.py:75
  39.2 5.6 %collective-permute-start.13 = (bf16[1,32,640]{2,1,0:T(8,128)(2,1)S(1)}, bf16[1,32,640]{2,1,0:T(8,128)(2,1)S(1)}, u32[]{:S(2)}, u32[]{:S(2)}) collective-permute-start(bf16[1,32,640]{2,1,0:T(8,128)(2,1)S(1)} %bitcast.120), channel_id=1, source_target_pairs={{0,4},{1,5},{2,6},{3,7},{4,0},{5,1},{6,2},{7,3},{8,12},{9,13},{10,... | collective-permute-start | bytes 122888 | tf_op jit(solution)/shard_map/ppermute | solution.py:75
  41.0 4.0 %collective-permute-start.12 = (bf16[1,32,640]{2,1,0:T(8,128)(2,1)S(1)}, bf16[1,32,640]{2,1,0:T(8,128)(2,1)S(1)}, u32[]{:S(2)}, u32[]{:S(2)}) collective-permute-start(bf16[1,32,640]{2,1,0:T(8,128)(2,1)S(1)} %bitcast.121), channel_id=1, source_target_pairs={{0,2},{1,3},{2,0},{3,1},{4,6},{5,7},{6,4},{7,5},{8,10},{9,11},{10,... | collective-permute-start | bytes 122888 | tf_op jit(solution)/shard_map/ppermute | solution.py:75
  46.1 14.1 %collective-permute-start.19 = (bf16[1,4,32,640]{3,2,1,0:T(8,128)(2,1)S(1)}, bf16[1,4,32,640]{3,2,1,0:T(8,128)(2,1)S(1)}, u32[]{:S(2)}, u32[]{:S(2)}) collective-permute-start(bf16[1,4,32,640]{3,2,1,0:T(8,128)(2,1)S(1)} %bitcast.107), channel_id=1, source_target_pairs={{0,24},{8,16},{16,8},{24,0},{1,25},{9,17},{17,9},{25,1},{2,26},{10... | collective-permute-start | bytes 491528 | tf_op jit(solution)/shard_map/ppermute | solution.py:70
  48.6 11.6 %collective-permute-start.18 = (bf16[1,4,32,640]{3,2,1,0:T(8,128)(2,1)S(1)}, bf16[1,4,32,640]{3,2,1,0:T(8,128)(2,1)S(1)}, u32[]{:S(2)}, u32[]{:S(2)}) collective-permute-start(bf16[1,4,32,640]{3,2,1,0:T(8,128)(2,1)S(1)} %bitcast.108), channel_id=1, source_target_pairs={{0,16},{8,24},{16,0},{24,8},{1,17},{9,25},{17,1},{25,9},{2,18},{10... | collective-permute-start | bytes 491528 | tf_op jit(solution)/shard_map/ppermute | solution.py:70
  49.1 11.1 %collective-permute-start.17 = (bf16[1,4,32,640]{3,2,1,0:T(8,128)(2,1)S(1)}, bf16[1,4,32,640]{3,2,1,0:T(8,128)(2,1)S(1)}, u32[]{:S(2)}, u32[]{:S(2)}) collective-permute-start(bf16[1,4,32,640]{3,2,1,0:T(8,128)(2,1)S(1)} %bitcast.109), channel_id=1, source_target_pairs={{0,8},{8,0},{16,24},{24,16},{1,9},{9,1},{17,25},{25,17},{2,10},{10... | collective-permute-start | bytes 491528 | tf_op jit(solution)/shard_map/ppermute | solution.py:70
  49.7 12.1 %collective-permute-start.16 = (bf16[192,640]{1,0:T(8,128)(2,1)S(1)}, bf16[192,640]{1,0:T(8,128)(2,1)S(1)}, u32[]{:S(2)}, u32[]{:S(2)}) collective-permute-start(bf16[192,640]{1,0:T(8,128)(2,1)S(1)} %pad_maximum_fusion.4.refs_4_), channel_id=1, source_target_pairs={{0,4},{1,5},{2,6},{3,7},{4,0},{5,1},{6,2},{7,3},{8,12},{9,13},{10,... | collective-permute-start | bytes 737288 | tf_op jit(solution)/shard_map/ppermute | solution.py:75
  50.7 11.0 %collective-permute-start.15 = (bf16[192,640]{1,0:T(8,128)(2,1)S(1)}, bf16[192,640]{1,0:T(8,128)(2,1)S(1)}, u32[]{:S(2)}, u32[]{:S(2)}) collective-permute-start(bf16[192,640]{1,0:T(8,128)(2,1)S(1)} %pad_maximum_fusion.4.refs_4_), channel_id=1, source_target_pairs={{0,2},{1,3},{2,0},{3,1},{4,6},{5,7},{6,4},{7,5},{8,10},{9,11},{10,... | collective-permute-start | bytes 737288 | tf_op jit(solution)/shard_map/ppermute | solution.py:75
  61.8 2.7 %collective-permute-start.20 = (bf16[16,32,640]{2,1,0:T(8,128)(2,1)S(1)}, bf16[16,32,640]{2,1,0:T(8,128)(2,1)S(1)}, u32[]{:S(2)}, u32[]{:S(2)}) collective-permute-start(bf16[16,32,640]{2,1,0:T(8,128)(2,1)S(1)} %bitcast.86), channel_id=1, source_target_pairs={{0,1},{1,0},{2,3},{3,2},{4,5},{5,4},{6,7},{7,6},{8,9},{9,8},{10,11... | collective-permute-start | bytes 1966088 | tf_op jit(solution)/shard_map/ppermute | solution.py:75
  61.8 6.4 %collective-permute-start.26 = (bf16[192,640]{1,0:T(8,128)(2,1)S(1)}, bf16[192,640]{1,0:T(8,128)(2,1)S(1)}, u32[]{:S(2)}, u32[]{:S(2)}) collective-permute-start(bf16[192,640]{1,0:T(8,128)(2,1)S(1)} %collective-permute-done.15.refs_5_), channel_id=1, source_target_pairs={{0,1},{1,0},{2,3},{3,2},{4,5},{5,4},{6,7},{7,6},{8,9},{9,8},{10,11... | collective-permute-start | bytes 737288 | tf_op jit(solution)/shard_map/ppermute | solution.py:75
  62.3 6.5 %collective-permute-start.27 = (bf16[192,640]{1,0:T(8,128)(2,1)S(1)}, bf16[192,640]{1,0:T(8,128)(2,1)S(1)}, u32[]{:S(2)}, u32[]{:S(2)}) collective-permute-start(bf16[192,640]{1,0:T(8,128)(2,1)S(1)} %collective-permute-done.16.refs_6_), channel_id=1, source_target_pairs={{0,1},{1,0},{2,3},{3,2},{4,5},{5,4},{6,7},{7,6},{8,9},{9,8},{10,11... | collective-permute-start | bytes 737288 | tf_op jit(solution)/shard_map/ppermute | solution.py:75
  62.3 7.0 %collective-permute-start.25 = (bf16[192,640]{1,0:T(8,128)(2,1)S(1)}, bf16[192,640]{1,0:T(8,128)(2,1)S(1)}, u32[]{:S(2)}, u32[]{:S(2)}) collective-permute-start(bf16[192,640]{1,0:T(8,128)(2,1)S(1)} %pad_maximum_fusion.4.refs_4_), channel_id=1, source_target_pairs={{0,1},{1,0},{2,3},{3,2},{4,5},{5,4},{6,7},{7,6},{8,9},{9,8},{10,11... | collective-permute-start | bytes 737288 | tf_op jit(solution)/shard_map/ppermute | solution.py:75
  62.8 9.8 %collective-permute-start.24 = (bf16[192,640]{1,0:T(8,128)(2,1)S(1)}, bf16[192,640]{1,0:T(8,128)(2,1)S(1)}, u32[]{:S(2)}, u32[]{:S(2)}) collective-permute-start(bf16[192,640]{1,0:T(8,128)(2,1)S(1)} %pad_maximum_fusion.4.refs_4_), channel_id=1, source_target_pairs={{0,6},{1,7},{2,4},{3,5},{4,2},{5,3},{6,0},{7,1},{8,14},{9,15},{10,... | collective-permute-start | bytes 737288 | tf_op jit(solution)/shard_map/ppermute | solution.py:75
  65.8 25.7 %copy-start.7 = (f32[1,128,640]{2,1,0:T(8,128)S(1)}, f32[1,128,640]{2,1,0:T(8,128)}, u32[]{:S(2)}) copy-start(f32[1,128,640]{2,1,0:T(8,128)} %param.21) | copy-start | bytes 983044
  65.8 8.0 %collective-permute-start.23 = (bf16[128,640]{1,0:T(8,128)(2,1)S(1)}, bf16[128,640]{1,0:T(8,128)(2,1)S(1)}, u32[]{:S(2)}, u32[]{:S(2)}) collective-permute-start(bf16[128,640]{1,0:T(8,128)(2,1)S(1)} %get-tuple-element.152.refs_0_), channel_id=1, source_target_pairs={{0,24},{8,16},{16,8},{24,0},{1,25},{9,17},{17,9},{25,1},{2,26},{10... | collective-permute-start | bytes 491528 | tf_op jit(solution)/shard_map/ppermute | solution.py:70
  68.2 7.9 %collective-permute-start.22 = (bf16[128,640]{1,0:T(8,128)(2,1)S(1)}, bf16[128,640]{1,0:T(8,128)(2,1)S(1)}, u32[]{:S(2)}, u32[]{:S(2)}) collective-permute-start(bf16[128,640]{1,0:T(8,128)(2,1)S(1)} %get-tuple-element.152.refs_0_), channel_id=1, source_target_pairs={{0,16},{8,24},{16,0},{24,8},{1,17},{9,25},{17,1},{25,9},{2,18},{10... | collective-permute-start | bytes 491528 | tf_op jit(solution)/shard_map/ppermute | solution.py:70
  68.8 7.4 %collective-permute-start.21 = (bf16[128,640]{1,0:T(8,128)(2,1)S(1)}, bf16[128,640]{1,0:T(8,128)(2,1)S(1)}, u32[]{:S(2)}, u32[]{:S(2)}) collective-permute-start(bf16[128,640]{1,0:T(8,128)(2,1)S(1)} %get-tuple-element.152.refs_0_), channel_id=1, source_target_pairs={{0,8},{8,0},{16,24},{24,16},{1,9},{9,1},{17,25},{25,17},{2,10},{10... | collective-permute-start | bytes 491528 | tf_op jit(solution)/shard_map/ppermute | solution.py:70
  76.2 1.5 collective-permute-start.28
  80.4 7.1 %collective-permute-start.29 = (bf16[128,640]{1,0:T(8,128)(2,1)S(1)}, bf16[128,640]{1,0:T(8,128)(2,1)S(1)}, u32[]{:S(2)}, u32[]{:S(2)}) collective-permute-start(bf16[128,640]{1,0:T(8,128)(2,1)S(1)} %get-tuple-element.161), channel_id=1, source_target_pairs={{0,8},{8,0},{16,24},{24,16},{1,9},{9,1},{17,25},{25,17},{2,10},{10... | collective-permute-start | bytes 491528 | tf_op jit(solution)/shard_map/ppermute | solution.py:70
  82.0 9.5 %collective-permute-start.30 = (bf16[128,640]{1,0:T(8,128)(2,1)S(1)}, bf16[128,640]{1,0:T(8,128)(2,1)S(1)}, u32[]{:S(2)}, u32[]{:S(2)}) collective-permute-start(bf16[128,640]{1,0:T(8,128)(2,1)S(1)} %get-tuple-element.162), channel_id=1, source_target_pairs={{0,16},{8,24},{16,0},{24,8},{1,17},{9,25},{17,1},{25,9},{2,18},{10... | collective-permute-start | bytes 491528 | tf_op jit(solution)/shard_map/ppermute | solution.py:70
  82.8 8.7 %collective-permute-start.31 = (bf16[128,640]{1,0:T(8,128)(2,1)S(1)}, bf16[128,640]{1,0:T(8,128)(2,1)S(1)}, u32[]{:S(2)}, u32[]{:S(2)}) collective-permute-start(bf16[128,640]{1,0:T(8,128)(2,1)S(1)} %get-tuple-element.163), channel_id=1, source_target_pairs={{0,24},{8,16},{16,8},{24,0},{1,25},{9,17},{17,9},{25,1},{2,26},{10... | collective-permute-start | bytes 491528 | tf_op jit(solution)/shard_map/ppermute | solution.py:70
  92.4 7.8 %collective-permute-start.34 = (bf16[128,640]{1,0:T(8,128)(2,1)S(1)}, bf16[128,640]{1,0:T(8,128)(2,1)S(1)}, u32[]{:S(2)}, u32[]{:S(2)}) collective-permute-start(bf16[128,640]{1,0:T(8,128)(2,1)S(1)} %get-tuple-element.166.refs_0_), channel_id=1, source_target_pairs={{0,24},{8,16},{16,8},{24,0},{1,25},{9,17},{17,9},{25,1},{2,26},{10... | collective-permute-start | bytes 491528 | tf_op jit(solution)/shard_map/ppermute | solution.py:70
  93.8 8.1 %collective-permute-start.33 = (bf16[128,640]{1,0:T(8,128)(2,1)S(1)}, bf16[128,640]{1,0:T(8,128)(2,1)S(1)}, u32[]{:S(2)}, u32[]{:S(2)}) collective-permute-start(bf16[128,640]{1,0:T(8,128)(2,1)S(1)} %get-tuple-element.166.refs_0_), channel_id=1, source_target_pairs={{0,16},{8,24},{16,0},{24,8},{1,17},{9,25},{17,1},{25,9},{2,18},{10... | collective-permute-start | bytes 491528 | tf_op jit(solution)/shard_map/ppermute | solution.py:70
  94.4 7.5 %collective-permute-start.32 = (bf16[128,640]{1,0:T(8,128)(2,1)S(1)}, bf16[128,640]{1,0:T(8,128)(2,1)S(1)}, u32[]{:S(2)}, u32[]{:S(2)}) collective-permute-start(bf16[128,640]{1,0:T(8,128)(2,1)S(1)} %get-tuple-element.166.refs_0_), channel_id=1, source_target_pairs={{0,8},{8,0},{16,24},{24,16},{1,9},{9,1},{17,25},{25,17},{2,10},{10... | collective-permute-start | bytes 491528 | tf_op jit(solution)/shard_map/ppermute | solution.py:70
  104.5 7.2 %collective-permute-start.35 = (bf16[128,640]{1,0:T(8,128)(2,1)S(1)}, bf16[128,640]{1,0:T(8,128)(2,1)S(1)}, u32[]{:S(2)}, u32[]{:S(2)}) collective-permute-start(bf16[128,640]{1,0:T(8,128)(2,1)S(1)} %get-tuple-element.180), channel_id=1, source_target_pairs={{0,8},{8,0},{16,24},{24,16},{1,9},{9,1},{17,25},{25,17},{2,10},{10... | collective-permute-start | bytes 491528 | tf_op jit(solution)/shard_map/ppermute | solution.py:70
  105.4 9.0 %collective-permute-start.36 = (bf16[128,640]{1,0:T(8,128)(2,1)S(1)}, bf16[128,640]{1,0:T(8,128)(2,1)S(1)}, u32[]{:S(2)}, u32[]{:S(2)}) collective-permute-start(bf16[128,640]{1,0:T(8,128)(2,1)S(1)} %get-tuple-element.181), channel_id=1, source_target_pairs={{0,16},{8,24},{16,0},{24,8},{1,17},{9,25},{17,1},{25,9},{2,18},{10... | collective-permute-start | bytes 491528 | tf_op jit(solution)/shard_map/ppermute | solution.py:70
  106.7 7.7 %collective-permute-start.37 = (bf16[128,640]{1,0:T(8,128)(2,1)S(1)}, bf16[128,640]{1,0:T(8,128)(2,1)S(1)}, u32[]{:S(2)}, u32[]{:S(2)}) collective-permute-start(bf16[128,640]{1,0:T(8,128)(2,1)S(1)} %get-tuple-element.182), channel_id=1, source_target_pairs={{0,24},{8,16},{16,8},{24,0},{1,25},{9,17},{17,9},{25,1},{2,26},{10... | collective-permute-start | bytes 491528 | tf_op jit(solution)/shard_map/ppermute | solution.py:70
  114.4 4.3 %collective-permute-start.39 = (bf16[4,192,640]{2,1,0:T(8,128)(2,1)S(1)}, bf16[4,192,640]{2,1,0:T(8,128)(2,1)S(1)}, u32[]{:S(2)}, u32[]{:S(2)}) collective-permute-start(bf16[4,192,640]{2,1,0:T(8,128)(2,1)S(1)} %get-tuple-element.192), channel_id=1, source_target_pairs={{0,1},{1,0},{2,3},{3,2},{4,5},{5,4},{6,7},{7,6},{8,9},{9,8},{10,11... | collective-permute-start | bytes 2949128 | tf_op jit(solution)/shard_map/ppermute | solution.py:75
  116.3 2.3 %collective-permute-start.38 = (bf16[16,32,640]{2,1,0:T(8,128)(2,1)S(1)}, bf16[16,32,640]{2,1,0:T(8,128)(2,1)S(1)}, u32[]{:S(2)}, u32[]{:S(2)}) collective-permute-start(bf16[16,32,640]{2,1,0:T(8,128)(2,1)S(1)} %get-tuple-element.190), channel_id=1, source_target_pairs={{0,1},{1,0},{2,3},{3,2},{4,5},{5,4},{6,7},{7,6},{8,9},{9,8},{10,11... | collective-permute-start | bytes 1966088 | tf_op jit(solution)/shard_map/ppermute | solution.py:75
  119.2 14.5 %collective-permute-start.44 = (bf16[4,32,640]{2,1,0:T(8,128)(2,1)S(1)}, bf16[4,32,640]{2,1,0:T(8,128)(2,1)S(1)}, u32[]{:S(2)}, u32[]{:S(2)}) collective-permute-start(bf16[4,32,640]{2,1,0:T(8,128)(2,1)S(1)} %get-tuple-element.259), channel_id=1, source_target_pairs={{0,24},{8,16},{16,8},{24,0},{1,25},{9,17},{17,9},{25,1},{2,26},{10... | collective-permute-start | bytes 491528 | tf_op jit(solution)/shard_map/ppermute | solution.py:70
  120.4 13.3 %collective-permute-start.43 = (bf16[4,32,640]{2,1,0:T(8,128)(2,1)S(1)}, bf16[4,32,640]{2,1,0:T(8,128)(2,1)S(1)}, u32[]{:S(2)}, u32[]{:S(2)}) collective-permute-start(bf16[4,32,640]{2,1,0:T(8,128)(2,1)S(1)} %get-tuple-element.260), channel_id=1, source_target_pairs={{0,16},{8,24},{16,0},{24,8},{1,17},{9,25},{17,1},{25,9},{2,18},{10... | collective-permute-start | bytes 491528 | tf_op jit(solution)/shard_map/ppermute | solution.py:70
  121.8 11.9 %collective-permute-start.42 = (bf16[4,32,640]{2,1,0:T(8,128)(2,1)S(1)}, bf16[4,32,640]{2,1,0:T(8,128)(2,1)S(1)}, u32[]{:S(2)}, u32[]{:S(2)}) collective-permute-start(bf16[4,32,640]{2,1,0:T(8,128)(2,1)S(1)} %get-tuple-element.261), channel_id=1, source_target_pairs={{0,8},{8,0},{16,24},{24,16},{1,9},{9,1},{17,25},{25,17},{2,10},{10... | collective-permute-start | bytes 491528 | tf_op jit(solution)/shard_map/ppermute | solution.py:70
  122.8 13.2 %collective-permute-start.41 = (bf16[192,640]{1,0:T(8,128)(2,1)S(1)}, bf16[192,640]{1,0:T(8,128)(2,1)S(1)}, u32[]{:S(2)}, u32[]{:S(2)}) collective-permute-start(bf16[192,640]{1,0:T(8,128)(2,1)S(1)} %get-tuple-element.257), channel_id=1, source_target_pairs={{0,4},{1,5},{2,6},{3,7},{4,0},{5,1},{6,2},{7,3},{8,12},{9,13},{10,... | collective-permute-start | bytes 737288 | tf_op jit(solution)/shard_map/ppermute | solution.py:75
  123.1 13.0 %collective-permute-start.40 = (bf16[192,640]{1,0:T(8,128)(2,1)S(1)}, bf16[192,640]{1,0:T(8,128)(2,1)S(1)}, u32[]{:S(2)}, u32[]{:S(2)}) collective-permute-start(bf16[192,640]{1,0:T(8,128)(2,1)S(1)} %get-tuple-element.258), channel_id=1, source_target_pairs={{0,2},{1,3},{2,0},{3,1},{4,6},{5,7},{6,4},{7,5},{8,10},{9,11},{10,... | collective-permute-start | bytes 737288 | tf_op jit(solution)/shard_map/ppermute | solution.py:75
  137.0 4.9 %collective-permute-start.45 = (bf16[16,48,640]{2,1,0:T(8,128)(2,1)}, bf16[16,48,640]{2,1,0:T(8,128)(2,1)S(1)}, u32[]{:S(2)}, u32[]{:S(2)}) collective-permute-start(bf16[16,48,640]{2,1,0:T(8,128)(2,1)} %copy-done.10), channel_id=1, source_target_pairs={{0,1},{1,0},{2,3},{3,2},{4,5},{5,4},{6,7},{7,6},{8,9},{9,8},{10,11... | collective-permute-start | bytes 2949128 | tf_op jit(solution)/shard_map/ppermute | solution.py:75
  137.2 4.5 %collective-permute-start.46 = (bf16[16,96]{1,0:T(8,128)(2,1)S(1)}, bf16[16,96]{1,0:T(8,128)(2,1)S(1)}, u32[]{:S(2)}, u32[]{:S(2)}) collective-permute-start(bf16[16,96]{1,0:T(8,128)(2,1)S(1)} %slice.172), channel_id=1, source_target_pairs={{0,1},{1,0},{2,3},{3,2},{4,5},{5,4},{6,7},{7,6},{8,9},{9,8},{10,11... | collective-permute-start | bytes 9224 | tf_op jit(solution)/shard_map/ppermute | solution.py:75
  137.7 4.0 %collective-permute-start.47 = (bf16[512,512]{1,0:T(8,128)(2,1)}, bf16[512,512]{1,0:T(8,128)(2,1)S(1)}, u32[]{:S(2)}, u32[]{:S(2)}) collective-permute-start(bf16[512,512]{1,0:T(8,128)(2,1)} %copy-done.13), channel_id=1, source_target_pairs={{0,1},{1,0},{2,3},{3,2},{4,5},{5,4},{6,7},{7,6},{8,9},{9,8},{10,11... | collective-permute-start | bytes 1572872 | tf_op jit(solution)/shard_map/ppermute | solution.py:75
  138.7 7.5 %collective-permute-start.48 = (bf16[96,640]{1,0:T(8,128)(2,1)S(1)}, bf16[96,640]{1,0:T(8,128)(2,1)S(1)}, u32[]{:S(2)}, u32[]{:S(2)}) collective-permute-start(bf16[96,640]{1,0:T(8,128)(2,1)S(1)} %slice_bitcast_fusion.10), channel_id=1, source_target_pairs={{0,6},{1,7},{2,4},{3,5},{4,2},{5,3},{6,0},{7,1},{8,14},{9,15},{10,... | collective-permute-start | bytes 368648 | tf_op jit(solution)/shard_map/ppermute | solution.py:75
  146.3 6.4 %collective-permute-start.52 = (bf16[128,512]{1,0:T(8,128)(2,1)S(1)}, bf16[128,512]{1,0:T(8,128)(2,1)S(1)}, u32[]{:S(2)}, u32[]{:S(2)}) collective-permute-start(bf16[128,512]{1,0:T(8,128)(2,1)S(1)} %get-tuple-element.262), channel_id=1, source_target_pairs={{0,2},{1,3},{2,0},{3,1},{4,6},{5,7},{6,4},{7,5},{8,10},{9,11},{10,... | collective-permute-start | bytes 393224 | tf_op jit(solution)/shard_map/ppermute | solution.py:75
  146.4 9.7 %collective-permute-start.54 = (bf16[128,512]{1,0:T(8,128)(2,1)S(1)}, bf16[128,512]{1,0:T(8,128)(2,1)S(1)}, u32[]{:S(2)}, u32[]{:S(2)}) collective-permute-start(bf16[128,512]{1,0:T(8,128)(2,1)S(1)} %get-tuple-element.263), channel_id=1, source_target_pairs={{0,6},{1,7},{2,4},{3,5},{4,2},{5,3},{6,0},{7,1},{8,14},{9,15},{10,... | collective-permute-start | bytes 393224 | tf_op jit(solution)/shard_map/ppermute | solution.py:75
  149.0 12.0 %collective-permute-start.53 = (bf16[128,512]{1,0:T(8,128)(2,1)S(1)}, bf16[128,512]{1,0:T(8,128)(2,1)S(1)}, u32[]{:S(2)}, u32[]{:S(2)}) collective-permute-start(bf16[128,512]{1,0:T(8,128)(2,1)S(1)} %get-tuple-element.264), channel_id=1, source_target_pairs={{0,4},{1,5},{2,6},{3,7},{4,0},{5,1},{6,2},{7,3},{8,12},{9,13},{10,... | collective-permute-start | bytes 393224 | tf_op jit(solution)/shard_map/ppermute | solution.py:75
  149.9 11.2 %collective-permute-start.49 = (bf16[4,56,640]{2,1,0:T(8,128)(2,1)S(1)}, bf16[4,56,640]{2,1,0:T(8,128)(2,1)S(1)}, u32[]{:S(2)}, u32[]{:S(2)}) collective-permute-start(bf16[4,56,640]{2,1,0:T(8,128)(2,1)S(1)} %get-tuple-element.254), channel_id=1, source_target_pairs={{0,8},{8,0},{16,24},{24,16},{1,9},{9,1},{17,25},{25,17},{2,10},{10... | collective-permute-start | bytes 860168 | tf_op jit(solution)/shard_map/ppermute | solution.py:70
  151.3 13.2 %collective-permute-start.51 = (bf16[4,56,640]{2,1,0:T(8,128)(2,1)S(1)}, bf16[4,56,640]{2,1,0:T(8,128)(2,1)S(1)}, u32[]{:S(2)}, u32[]{:S(2)}) collective-permute-start(bf16[4,56,640]{2,1,0:T(8,128)(2,1)S(1)} %get-tuple-element.255), channel_id=1, source_target_pairs={{0,24},{8,16},{16,8},{24,0},{1,25},{9,17},{17,9},{25,1},{2,26},{10... | collective-permute-start | bytes 860168 | tf_op jit(solution)/shard_map/ppermute | solution.py:70
  152.7 13.1 %collective-permute-start.50 = (bf16[4,56,640]{2,1,0:T(8,128)(2,1)S(1)}, bf16[4,56,640]{2,1,0:T(8,128)(2,1)S(1)}, u32[]{:S(2)}, u32[]{:S(2)}) collective-permute-start(bf16[4,56,640]{2,1,0:T(8,128)(2,1)S(1)} %get-tuple-element.256), channel_id=1, source_target_pairs={{0,16},{8,24},{16,0},{24,8},{1,17},{9,25},{17,1},{25,9},{2,18},{10... | collective-permute-start | bytes 860168 | tf_op jit(solution)/shard_map/ppermute | solution.py:70
  167.2 16.5 %collective-permute-start.61 = (bf16[96,640]{1,0:T(8,128)(2,1)S(1)}, bf16[96,640]{1,0:T(8,128)(2,1)S(1)}, u32[]{:S(2)}, u32[]{:S(2)}) collective-permute-start(bf16[96,640]{1,0:T(8,128)(2,1)S(1)} %slice_bitcast_fusion.9), channel_id=1, source_target_pairs={{0,6},{1,7},{2,4},{3,5},{4,2},{5,3},{6,0},{7,1},{8,14},{9,15},{10,... | collective-permute-start | bytes 368648 | tf_op jit(solution)/shard_map/ppermute | solution.py:75
  169.1 7.4 %collective-permute-start.60 = (bf16[32,640]{1,0:T(8,128)(2,1)S(1)}, bf16[32,640]{1,0:T(8,128)(2,1)S(1)}, u32[]{:S(2)}, u32[]{:S(2)}) collective-permute-start(bf16[32,640]{1,0:T(8,128)(2,1)S(1)} %get-tuple-element.271), channel_id=1, source_target_pairs={{0,6},{1,7},{2,4},{3,5},{4,2},{5,3},{6,0},{7,1},{8,14},{9,15},{10,... | collective-permute-start | bytes 122888 | tf_op jit(solution)/shard_map/ppermute | solution.py:75
  171.2 8.2 %collective-permute-start.59 = (bf16[32,640]{1,0:T(8,128)(2,1)S(1)}, bf16[32,640]{1,0:T(8,128)(2,1)S(1)}, u32[]{:S(2)}, u32[]{:S(2)}) collective-permute-start(bf16[32,640]{1,0:T(8,128)(2,1)S(1)} %get-tuple-element.272), channel_id=1, source_target_pairs={{0,4},{1,5},{2,6},{3,7},{4,0},{5,1},{6,2},{7,3},{8,12},{9,13},{10,... | collective-permute-start | bytes 122888 | tf_op jit(solution)/shard_map/ppermute | solution.py:75
  171.2 9.2 %collective-permute-start.58 = (bf16[32,640]{1,0:T(8,128)(2,1)S(1)}, bf16[32,640]{1,0:T(8,128)(2,1)S(1)}, u32[]{:S(2)}, u32[]{:S(2)}) collective-permute-start(bf16[32,640]{1,0:T(8,128)(2,1)S(1)} %get-tuple-element.273), channel_id=1, source_target_pairs={{0,2},{1,3},{2,0},{3,1},{4,6},{5,7},{6,4},{7,5},{8,10},{9,11},{10,... | collective-permute-start | bytes 122888 | tf_op jit(solution)/shard_map/ppermute | solution.py:75
  173.6 6.8 %collective-permute-start.57 = (bf16[56,640]{1,0:T(8,128)(2,1)S(1)}, bf16[56,640]{1,0:T(8,128)(2,1)S(1)}, u32[]{:S(2)}, u32[]{:S(2)}) collective-permute-start(bf16[56,640]{1,0:T(8,128)(2,1)S(1)} %get-tuple-element.265), channel_id=1, source_target_pairs={{0,6},{1,7},{2,4},{3,5},{4,2},{5,3},{6,0},{7,1},{8,14},{9,15},{10,... | collective-permute-start | bytes 215048 | tf_op jit(solution)/shard_map/ppermute | solution.py:75
  176.5 5.2 %collective-permute-start.56 = (bf16[56,640]{1,0:T(8,128)(2,1)S(1)}, bf16[56,640]{1,0:T(8,128)(2,1)S(1)}, u32[]{:S(2)}, u32[]{:S(2)}) collective-permute-start(bf16[56,640]{1,0:T(8,128)(2,1)S(1)} %get-tuple-element.266), channel_id=1, source_target_pairs={{0,4},{1,5},{2,6},{3,7},{4,0},{5,1},{6,2},{7,3},{8,12},{9,13},{10,... | collective-permute-start | bytes 215048 | tf_op jit(solution)/shard_map/ppermute | solution.py:75
  179.4 4.3 %collective-permute-start.55 = (bf16[56,640]{1,0:T(8,128)(2,1)S(1)}, bf16[56,640]{1,0:T(8,128)(2,1)S(1)}, u32[]{:S(2)}, u32[]{:S(2)}) collective-permute-start(bf16[56,640]{1,0:T(8,128)(2,1)S(1)} %get-tuple-element.267), channel_id=1, source_target_pairs={{0,2},{1,3},{2,0},{3,1},{4,6},{5,7},{6,4},{7,5},{8,10},{9,11},{10,... | collective-permute-start | bytes 215048 | tf_op jit(solution)/shard_map/ppermute | solution.py:75
  (27 other events, 190.8 us)

commit v4 on v3

--- a/solution.py
+++ b/solution.py
@@ -459,15 +459,24 @@
 
 
 def ending_kernel(*refs):
-    firsts, outs, feeds, results = refs[:4], refs[4:8], refs[8:13], refs[13:]
-    total = add_bf16(*[ref[...] for ref in firsts])
+    first_ref, out_ref = refs[:2]
+    comes = [ref[...].astype(jnp.float32) for ref in refs[2:5]]
+    feeds, results = refs[5:9], refs[9:]
+    rows_q = out_ref.shape[0]
+    rows = rows_q + first_ref.shape[0]
+    total = first_ref[...].astype(jnp.float32)
+    for come in comes:
+        total = total + come[rows_q:rows]
     row = 0
     for ref in results[:4]:
         ref[...] = total[row : row + ref.shape[0]]
         row = row + ref.shape[0]
-    results[4][...] = add_bf16(*[ref[...] for ref in outs])
+    total = out_ref[...].astype(jnp.float32)
+    for come in comes:
+        total = total + come[:rows_q]
+    results[4][...] = total
     total = add_bf16(*[ref[...] for ref in feeds[:3]]) + jnp.concatenate(
-        [ref[...].astype(jnp.float32) for ref in feeds[3:]], axis=0
+        [feeds[3][...].astype(jnp.float32), comes[2][rows:]], axis=0
     )
     row = 0
     for ref in results[5:]:
@@ -1000,9 +1009,10 @@
     packed, own_kv, out_sum, g_feed = tie((packed.astype(BF), own_kv, out_sum, g_feed))
     own_normed = jnp.dot(own_kv, w_kv, preferred_element_type=jnp.float32) + grad_normed_q
     half_rows = 3 * rows_f // 2
-    feed_end3 = swap_z(g_feed[3, half_rows:], 3)
-    out_comes = [swap_z(out_sum[bits], bits) for bits in range(1, 4)]
-    first_comes = [swap_z(packed[bits], bits) for bits in range(1, 4)]
+    last_comes = []
+    for bits in range(1, 4):
+        blocks = [out_sum[bits], packed[bits]] + ([g_feed[3, half_rows:]] if bits == 3 else [])
+        last_comes.append(swap_z(jnp.concatenate(blocks, axis=0), bits))
     own_query, own_key, own_value, own_last, own_output, own_gate, own_up, own_down = call_kernel(
         ending_kernel,
         [
@@ -1017,11 +1027,9 @@
         ],
         [],
         10_000_000,
-        [packed[0]]
-        + first_comes
-        + [out_sum[0]]
-        + out_comes
-        + [g_feed[0], feed_come1, feed_come2, feed_come3, feed_end3],
+        [packed[0], out_sum[0]]
+        + last_comes
+        + [g_feed[0], feed_come1, feed_come2, feed_come3],
     )
     grad_resid = grad_resid_a + rms_back(unit_in, inverse_in, own_normed * (1.0 + scale_in))
     return (

time: 186 us -> 184 us (0.989)
  starting transfers between devices: 70.4 us -> 62.7 us
  waiting for transfers between devices: 65.4 us -> 68.5 us
    ppermute x38 -> x34, starting transfers between devices: 41 us -> 34.3 us  [swap_ctx(): lax.ppermute(block, 'ctx', [(place, place ^ bits) for place in range(coun...]
    ppermute x38 -> x34, waiting for transfers between devices: 36.7 us -> 39.9 us  [swap_ctx(): lax.ppermute(block, 'ctx', [(place, place ^ bits) for place in range(coun...]
    unnamed x60 -> x72, local copies, waits for them, and re-layouts: 2.58 us -> 3.91 us
  transfers between devices with their start and end apart: 62 -> 58, of which waited for: 29 -> 31; matrix products, arithmetic and copies ran while one was open for 6% -> 6% of each run, Pallas kernels for 10% -> 11%
where the time goes in v4:
time: 184 us; the launch traced here: 182 us
  waiting for transfers between devices  68.5 us (37%)
  starting transfers between devices  62.7 us (34%)
  Pallas kernels  26.4 us (14%)
  local copies, waits for them, and re-layouts  11.5 us (6%)
  other arithmetic  10.9 us (6%)
    ppermute x34, waiting for transfers between devices, swap_ctx(): lax.ppermute(block, 'ctx', [(place, place ^ bits) for place in range(coun...  39.9 us
    ppermute x34, starting transfers between devices, swap_ctx(): lax.ppermute(block, 'ctx', [(place, place ^ bits) for place in range(coun...  34.3 us
    ppermute x24, waiting for transfers between devices, swap_dp(): lax.ppermute(block, 'dp', [(place, place ^ bits) for place in range(count)])  28.5 us
    ppermute x24, starting transfers between devices, swap_dp(): lax.ppermute(block, 'dp', [(place, place ^ bits) for place in range(count)])  28.4 us
    pallas_call x9, Pallas kernels, call_kernel(): pl.pallas_call(body, out_shape=[jax.ShapeDtypeStruct(shape, dtype) for sh...  26.4 us
    unnamed x72, local copies, waits for them, and re-layouts  3.91 us
  transfers between devices with their start and end apart: 58, of which 31 were waited for; matrix products, arithmetic and copies ran while one was open for 6% of the time, Pallas kernels for 11%

profile of v4, /device:TPU:0, one launch (start us, length us, event | category | flops | bytes accessed | tf_op | source)
XLA Modules:
  0.0 182.0 jit_solution(7491848837177162936)
XLA Ops:
  2.1 2.2 %concatenate.37 = bf16[56,640]{1,0:T(8,128)(2,1)S(1)} concatenate(bf16[32,640]{1,0:T(8,128)(2,1)} %param.13, bf16[8,640]{1,0:T(8,128)(2,1)} %param.14, bf16[8,640]{1,0:T(8,128)(2,1)} %param.15, bf16[1,640]{1,0:T(2,128)(2,1)S(1)} %pad.19, bf16[1,640]{1,0:T(2,128)(2,1)S(1)} %pad.20, bf16[1,640]{1,0:T(2,128)(2,1)S(1)} %pad.21, bf16[5,640]{1,0:T(8,128)(2,1)S(1)} %broadcast_in_dim.72), dimensions={0} | concatenate | bytes 143360 | tf_op jit(solution)/shard_map/concatenate | solution.py:818
  4.3 5.1 %collective-permute-start.2 = (bf16[1,56,640]{2,1,0:T(8,128)(2,1)S(1)}, bf16[1,56,640]{2,1,0:T(8,128)(2,1)S(1)}, u32[]{:S(2)}, u32[]{:S(2)}) collective-permute-start(bf16[1,56,640]{2,1,0:T(8,128)(2,1)S(1)} %bitcast.115), channel_id=1, source_target_pairs={{0,6},{1,7},{2,4},{3,5},{4,2},{5,3},{6,0},{7,1},{8,14},{9,15},{10,... | collective-permute-start | bytes 215048 | tf_op jit(solution)/shard_map/ppermute | solution.py:75
  10.1 1.1 multiply_reduce_fusion.1
  13.4 2.1 %collective-permute-done.1 = bf16[1,56,640]{2,1,0:T(8,128)(2,1)S(1)} collective-permute-done((bf16[1,56,640]{2,1,0:T(8,128)(2,1)S(1)}, bf16[1,56,640]{2,1,0:T(8,128)(2,1)S(1)}, u32[]{:S(2)}, u32[]{:S(2)}) %collective-permute-start.1) | collective-permute-done | bytes 71712 | tf_op jit(solution)/shard_map/ppermute | solution.py:75
  15.6 2.8 %collective-permute-start.8 = (bf16[1,128,640]{2,1,0:T(8,128)(2,1)S(1)}, bf16[1,128,640]{2,1,0:T(8,128)(2,1)S(1)}, u32[]{:S(2)}, u32[]{:S(2)}) collective-permute-start(bf16[1,128,640]{2,1,0:T(8,128)(2,1)S(1)} %bitcast.111), channel_id=1, source_target_pairs={{0,6},{1,7},{2,4},{3,5},{4,2},{5,3},{6,0},{7,1},{8,14},{9,15},{10,... | collective-permute-start | bytes 491528 | tf_op jit(solution)/shard_map/ppermute | solution.py:75
  18.4 1.7 collective-permute-start.6
  20.1 2.4 %collective-permute-start.5 = (bf16[1,4,56,640]{3,2,1,0:T(8,128)(2,1)S(1)}, bf16[1,4,56,640]{3,2,1,0:T(8,128)(2,1)S(1)}, u32[]{:S(2)}, u32[]{:S(2)}) collective-permute-start(bf16[1,4,56,640]{3,2,1,0:T(8,128)(2,1)S(1)} %bitcast.100), channel_id=1, source_target_pairs={{0,24},{8,16},{16,8},{24,0},{1,25},{9,17},{17,9},{25,1},{2,26},{10... | collective-permute-start | bytes 860168 | tf_op jit(solution)/shard_map/ppermute | solution.py:70
  23.1 1.6 collective-permute-done.8
  24.6 1.5 collective-permute-start.3
  26.1 3.1 %multiply_sine_fusion = (f32[1024,128]{1,0:T(8,128)}, f32[1024,128]{1,0:T(8,128)}) fusion(f32[128]{0:T(128)S(1)} %multiply_power_fusion, f32[1024]{0:T(1024)S(1)} %bitcast.125), kind=kLoop, calls=%fused_computation.11 | loop fusion | flops 131072 | bytes 1053184 | tf_op jit(solution)/shard_map/sin | solution.py:831
  29.2 4.0 %collective-permute-done.7 = bf16[1,128,640]{2,1,0:T(8,128)(2,1)S(1)} collective-permute-done((bf16[1,128,640]{2,1,0:T(8,128)(2,1)S(1)}, bf16[1,128,640]{2,1,0:T(8,128)(2,1)S(1)}, u32[]{:S(2)}, u32[]{:S(2)}) %collective-permute-start.7) | collective-permute-done | bytes 163872 | tf_op jit(solution)/shard_map/ppermute | solution.py:75
  33.4 2.1 %collective-permute-done.4 = bf16[1,4,56,640]{3,2,1,0:T(8,128)(2,1)S(1)} collective-permute-done((bf16[1,4,56,640]{3,2,1,0:T(8,128)(2,1)S(1)}, bf16[1,4,56,640]{3,2,1,0:T(8,128)(2,1)S(1)}, u32[]{:S(2)}, u32[]{:S(2)}) %collective-permute-start.4) | collective-permute-done | bytes 286752 | tf_op jit(solution)/shard_map/ppermute | solution.py:70
  36.4 2.7 %collective-permute-start.14 = (bf16[1,32,640]{2,1,0:T(8,128)(2,1)S(1)}, bf16[1,32,640]{2,1,0:T(8,128)(2,1)S(1)}, u32[]{:S(2)}, u32[]{:S(2)}) collective-permute-start(bf16[1,32,640]{2,1,0:T(8,128)(2,1)S(1)} %bitcast.119), channel_id=1, source_target_pairs={{0,6},{1,7},{2,4},{3,5},{4,2},{5,3},{6,0},{7,1},{8,14},{9,15},{10,... | collective-permute-start | bytes 122888 | tf_op jit(solution)/shard_map/ppermute | solution.py:75
  39.2 1.8 %collective-permute-start.13 = (bf16[1,32,640]{2,1,0:T(8,128)(2,1)S(1)}, bf16[1,32,640]{2,1,0:T(8,128)(2,1)S(1)}, u32[]{:S(2)}, u32[]{:S(2)}) collective-permute-start(bf16[1,32,640]{2,1,0:T(8,128)(2,1)S(1)} %bitcast.120), channel_id=1, source_target_pairs={{0,4},{1,5},{2,6},{3,7},{4,0},{5,1},{6,2},{7,3},{8,12},{9,13},{10,... | collective-permute-start | bytes 122888 | tf_op jit(solution)/shard_map/ppermute | solution.py:75
  41.1 1.3 collective-permute-done.14
  42.4 2.4 %collective-permute-done.13 = bf16[1,32,640]{2,1,0:T(8,128)(2,1)S(1)} collective-permute-done((bf16[1,32,640]{2,1,0:T(8,128)(2,1)S(1)}, bf16[1,32,640]{2,1,0:T(8,128)(2,1)S(1)}, u32[]{:S(2)}, u32[]{:S(2)}) %collective-permute-start.13) | collective-permute-done | bytes 40992 | tf_op jit(solution)/shard_map/ppermute | solution.py:75
  46.1 2.5 %collective-permute-start.19 = (bf16[1,4,32,640]{3,2,1,0:T(8,128)(2,1)S(1)}, bf16[1,4,32,640]{3,2,1,0:T(8,128)(2,1)S(1)}, u32[]{:S(2)}, u32[]{:S(2)}) collective-permute-start(bf16[1,4,32,640]{3,2,1,0:T(8,128)(2,1)S(1)} %bitcast.107), channel_id=1, source_target_pairs={{0,24},{8,16},{16,8},{24,0},{1,25},{9,17},{17,9},{25,1},{2,26},{10... | collective-permute-start | bytes 491528 | tf_op jit(solution)/shard_map/ppermute | solution.py:70
  49.7 1.1 collective-permute-start.16
  50.7 1.3 collective-permute-start.15
  52.0 8.2 %shard_map.186 = (bf16[1024,640]{1,0:T(8,128)(2,1)}, bf16[512,640]{1,0:T(8,128)(2,1)}, bf16[128,640]{1,0:T(8,128)(2,1)S(1)}, bf16[1024,640]{1,0:T(8,128)(2,1)}, ...) custom-call(f32[128,640]{1,0:T(8,128)S(1)} %get-tuple-element.253.un, ...), custom_call_target="tpu_custom_call" | custom-call | flops 12000000000 | bytes 20000000 | tf_op jit(solution)/shard_map/pallas_call | solution.py:204
  62.8 1.9 %collective-permute-start.24 = (bf16[192,640]{1,0:T(8,128)(2,1)S(1)}, bf16[192,640]{1,0:T(8,128)(2,1)S(1)}, u32[]{:S(2)}, u32[]{:S(2)}) collective-permute-start(bf16[192,640]{1,0:T(8,128)(2,1)S(1)} %pad_maximum_fusion.4.refs_4_), channel_id=1, source_target_pairs={{0,6},{1,7},{2,4},{3,5},{4,2},{5,3},{6,0},{7,1},{8,14},{9,15},{10,... | collective-permute-start | bytes 737288 | tf_op jit(solution)/shard_map/ppermute | solution.py:75
  64.7 1.2 shard_map.187
  66.0 2.5 %collective-permute-start.23 = (bf16[128,640]{1,0:T(8,128)(2,1)S(1)}, bf16[128,640]{1,0:T(8,128)(2,1)S(1)}, u32[]{:S(2)}, u32[]{:S(2)}) collective-permute-start(bf16[128,640]{1,0:T(8,128)(2,1)S(1)} %get-tuple-element.152.refs_0_), channel_id=1, source_target_pairs={{0,24},{8,16},{16,8},{24,0},{1,25},{9,17},{17,9},{25,1},{2,26},{10... | collective-permute-start | bytes 491528 | tf_op jit(solution)/shard_map/ppermute | solution.py:70
  69.6 3.1 %collective-permute-done.24.refs_7_ = bf16[192,640]{1,0:T(8,128)(2,1)S(1)} collective-permute-done((bf16[192,640]{1,0:T(8,128)(2,1)S(1)}, bf16[192,640]{1,0:T(8,128)(2,1)S(1)}, u32[]{:S(2)}, u32[]{:S(2)}) %collective-permute-start.24) | collective-permute-done | bytes 245792 | tf_op jit(solution)/shard_map/ppermute | solution.py:75
  72.7 1.2 collective-permute-done.23.refs_3_
  73.9 2.5 %collective-permute-done.22.refs_2_ = bf16[128,640]{1,0:T(8,128)(2,1)S(1)} collective-permute-done((bf16[128,640]{1,0:T(8,128)(2,1)S(1)}, bf16[128,640]{1,0:T(8,128)(2,1)S(1)}, u32[]{:S(2)}, u32[]{:S(2)}) %collective-permute-start.22) | collective-permute-done | bytes 163872 | tf_op jit(solution)/shard_map/ppermute | solution.py:70
  76.5 1.5 collective-permute-done.28.refs_11_
  78.0 2.7 %shard_map.188 = (f32[128,640]{1,0:T(8,128)S(1)}, bf16[128,640]{1,0:T(8,128)(2,1)S(1)}, bf16[128,640]{1,0:T(8,128)(2,1)S(1)}, bf16[128,640]{1,0:T(8,128)(2,1)S(1...) custom-call(bf16[128,640]{1,0:T(8,128)(2,1)S(1)} %get-tuple-element., ...), custom_call_target="tpu_custom_call" | custom-call | flops 3000000000 | bytes 20000000 | tf_op jit(solution)/shard_map/pallas_call | solution.py:204
  80.7 1.5 collective-permute-start.29
  83.0 1.3 collective-permute-start.31
  84.3 3.6 %collective-permute-done.29.come1_ref = bf16[128,640]{1,0:T(8,128)(2,1)S(1)} collective-permute-done((bf16[128,640]{1,0:T(8,128)(2,1)S(1)}, bf16[128,640]{1,0:T(8,128)(2,1)S(1)}, u32[]{:S(2)}, u32[]{:S(2)}) %collective-permute-start.29) | collective-permute-done | bytes 163872 | tf_op jit(solution)/shard_map/ppermute | solution.py:70
  87.8 3.9 %collective-permute-done.30.come2_ref = bf16[128,640]{1,0:T(8,128)(2,1)S(1)} collective-permute-done((bf16[128,640]{1,0:T(8,128)(2,1)S(1)}, bf16[128,640]{1,0:T(8,128)(2,1)S(1)}, u32[]{:S(2)}, u32[]{:S(2)}) %collective-permute-start.30) | collective-permute-done | bytes 163872 | tf_op jit(solution)/shard_map/ppermute | solution.py:70
  92.7 1.4 collective-permute-start.34
  94.7 1.5 collective-permute-start.32
  96.2 4.3 %collective-permute-done.34.refs_3_ = bf16[128,640]{1,0:T(8,128)(2,1)S(1)} collective-permute-done((bf16[128,640]{1,0:T(8,128)(2,1)S(1)}, bf16[128,640]{1,0:T(8,128)(2,1)S(1)}, u32[]{:S(2)}, u32[]{:S(2)}) %collective-permute-start.34) | collective-permute-done | bytes 163872 | tf_op jit(solution)/shard_map/ppermute | solution.py:70
  100.5 1.7 collective-permute-done.33.refs_2_
  102.2 2.7 %shard_map.190 = (f32[128,640]{1,0:T(8,128)S(1)}, bf16[128,640]{1,0:T(8,128)(2,1)S(1)}, bf16[128,640]{1,0:T(8,128)(2,1)S(1)}, bf16[128,640]{1,0:T(8,128)(2,1)S(1...) custom-call(bf16[128,640]{1,0:T(8,128)(2,1)S(1)} %get-tuple-element.166.refs_0_, ...), custom_call_target="tpu_custom_call" | custom-call | flops 3000000000 | bytes 20000000 | tf_op jit(solution)/shard_map/pallas_call | solution.py:204
  105.7 1.3 collective-permute-start.36
  107.0 1.4 collective-permute-start.37
  108.4 1.6 shard_map.191
  110.0 2.0 %collective-permute-done.35.come1_ref = bf16[128,640]{1,0:T(8,128)(2,1)S(1)} collective-permute-done((bf16[128,640]{1,0:T(8,128)(2,1)S(1)}, bf16[128,640]{1,0:T(8,128)(2,1)S(1)}, u32[]{:S(2)}, u32[]{:S(2)}) %collective-permute-start.35) | collective-permute-done | bytes 163872 | tf_op jit(solution)/shard_map/ppermute | solution.py:70
  112.0 2.7 %collective-permute-done.36.come2_ref = bf16[128,640]{1,0:T(8,128)(2,1)S(1)} collective-permute-done((bf16[128,640]{1,0:T(8,128)(2,1)S(1)}, bf16[128,640]{1,0:T(8,128)(2,1)S(1)}, u32[]{:S(2)}, u32[]{:S(2)}) %collective-permute-start.36) | collective-permute-done | bytes 163872 | tf_op jit(solution)/shard_map/ppermute | solution.py:70
  114.8 1.9 %shard_map.192 = (f32[128,640]{1,0:T(8,128)S(1)}, bf16[128,1024]{1,0:T(8,128)(2,1)S(1)}, bf16[16,32,640]{2,1,0:T(8,128)(2,1)S(1)}, bf16[16,32,640]{2,1,0:T(8,128...) custom-call(f32[128,640]{1,0:T(8,128)S(1)} %get-tuple-element.172.own_ref, ...), custom_call_target="tpu_custom_call" | custom-call | flops 3000000000 | bytes 20000000 | tf_op jit(solution)/shard_map/pallas_call | solution.py:204
  117.2 1.7 collective-permute-done.38
  120.0 1.3 collective-permute-start.44
  121.3 1.4 collective-permute-start.43
  123.6 1.3 collective-permute-start.41
  125.0 1.1 collective-permute-start.40
  126.2 6.3 %shard_map.193 = (bf16[16,48,640]{2,1,0:T(8,128)(2,1)S(1)}, bf16[16,48,640]{2,1,0:T(8,128)(2,1)S(1)}, bf16[512,512]{1,0:T(8,128)(2,1)S(1)}, bf16[512,512]{1,0:T(...) custom-call(bf16[128,1024]{1,0:T(8,128)(2,1)S(1)} %get-tuple-element, ...), custom_call_target="tpu_custom_call" | custom-call | flops 12000000000 | bytes 20000000 | tf_op jit(solution)/shard_map/pallas_call | solution.py:204
  134.3 2.6 %collective-permute-done.41.refs_7_ = bf16[192,640]{1,0:T(8,128)(2,1)S(1)} collective-permute-done((bf16[192,640]{1,0:T(8,128)(2,1)S(1)}, bf16[192,640]{1,0:T(8,128)(2,1)S(1)}, u32[]{:S(2)}, u32[]{:S(2)}) %collective-permute-start.41) | collective-permute-done | bytes 245792 | tf_op jit(solution)/shard_map/ppermute | solution.py:75
  139.9 1.8 %collective-permute-start.48 = (bf16[96,640]{1,0:T(8,128)(2,1)S(1)}, bf16[96,640]{1,0:T(8,128)(2,1)S(1)}, u32[]{:S(2)}, u32[]{:S(2)}) collective-permute-start(bf16[96,640]{1,0:T(8,128)(2,1)S(1)} %slice_bitcast_fusion.10), channel_id=1, source_target_pairs={{0,6},{1,7},{2,4},{3,5},{4,2},{5,3},{6,0},{7,1},{8,14},{9,15},{10,... | collective-permute-start | bytes 368648 | tf_op jit(solution)/shard_map/ppermute | solution.py:75
  141.8 1.2 fusion.4
  143.6 4.0 %collective-permute-done.48.refs_8_ = bf16[96,640]{1,0:T(8,128)(2,1)S(1)} collective-permute-done((bf16[96,640]{1,0:T(8,128)(2,1)S(1)}, bf16[96,640]{1,0:T(8,128)(2,1)S(1)}, u32[]{:S(2)}, u32[]{:S(2)}) %collective-permute-start.48) | collective-permute-done | bytes 122912 | tf_op jit(solution)/shard_map/ppermute | solution.py:75
  147.6 1.1 collective-permute-start.52
  149.5 1.7 collective-permute-start.53
  152.0 1.6 collective-permute-start.51
  154.8 2.2 %collective-permute-done.54 = bf16[128,512]{1,0:T(8,128)(2,1)S(1)} collective-permute-done((bf16[128,512]{1,0:T(8,128)(2,1)S(1)}, bf16[128,512]{1,0:T(8,128)(2,1)S(1)}, u32[]{:S(2)}, u32[]{:S(2)}) %collective-permute-start.54) | collective-permute-done | bytes 131104 | tf_op jit(solution)/shard_map/ppermute | solution.py:75
  157.0 5.3 %collective-permute-done.53 = bf16[128,512]{1,0:T(8,128)(2,1)S(1)} collective-permute-done((bf16[128,512]{1,0:T(8,128)(2,1)S(1)}, bf16[128,512]{1,0:T(8,128)(2,1)S(1)}, u32[]{:S(2)}, u32[]{:S(2)}) %collective-permute-start.53) | collective-permute-done | bytes 131104 | tf_op jit(solution)/shard_map/ppermute | solution.py:75
  162.4 3.0 %collective-permute-done.51 = bf16[4,56,640]{2,1,0:T(8,128)(2,1)S(1)} collective-permute-done((bf16[4,56,640]{2,1,0:T(8,128)(2,1)S(1)}, bf16[4,56,640]{2,1,0:T(8,128)(2,1)S(1)}, u32[]{:S(2)}, u32[]{:S(2)}) %collective-permute-start.51) | collective-permute-done | bytes 286752 | tf_op jit(solution)/shard_map/ppermute | solution.py:70
  165.4 1.4 collective-permute-done.50
  168.2 1.5 collective-permute-start.55
  170.7 2.1 %collective-permute-start.57 = (bf16[184,640]{1,0:T(8,128)(2,1)S(1)}, bf16[184,640]{1,0:T(8,128)(2,1)S(1)}, u32[]{:S(2)}, u32[]{:S(2)}) collective-permute-start(bf16[184,640]{1,0:T(8,128)(2,1)S(1)} %pad_maximum_fusion.5), channel_id=1, source_target_pairs={{0,6},{1,7},{2,4},{3,5},{4,2},{5,3},{6,0},{7,1},{8,14},{9,15},{10,... | collective-permute-start | bytes 706568 | tf_op jit(solution)/shard_map/ppermute | solution.py:75
  174.7 1.1 collective-permute-done.55.refs_2_
  175.8 4.8 %collective-permute-done.56.refs_3_ = bf16[88,640]{1,0:T(8,128)(2,1)S(1)} collective-permute-done((bf16[88,640]{1,0:T(8,128)(2,1)S(1)}, bf16[88,640]{1,0:T(8,128)(2,1)S(1)}, u32[]{:S(2)}, u32[]{:S(2)}) %collective-permute-start.56) | collective-permute-done | bytes 112672 | tf_op jit(solution)/shard_map/ppermute | solution.py:75
  (206 shorter events, 31.7 us)
Async XLA Ops:
  0.6 12.7 %copy-start.31 = (bf16[64,640]{1,0:T(8,128)(2,1)S(1)}, bf16[64,640]{1,0:T(8,128)(2,1)}, u32[]{:S(2)}) copy-start(bf16[64,640]{1,0:T(8,128)(2,1)} %param.19) | copy-start | bytes 245764
  0.7 12.7 %copy-start.32 = (bf16[64,640]{1,0:T(8,128)(2,1)S(1)}, bf16[64,640]{1,0:T(8,128)(2,1)}, u32[]{:S(2)}) copy-start(bf16[64,640]{1,0:T(8,128)(2,1)} %param.18) | copy-start | bytes 245764
  0.7 12.7 %copy-start.33 = (bf16[64,640]{1,0:T(8,128)(2,1)S(1)}, bf16[64,640]{1,0:T(8,128)(2,1)}, u32[]{:S(2)}) copy-start(bf16[64,640]{1,0:T(8,128)(2,1)} %param.17) | copy-start | bytes 245764
  4.3 9.1 %collective-permute-start.2 = (bf16[1,56,640]{2,1,0:T(8,128)(2,1)S(1)}, bf16[1,56,640]{2,1,0:T(8,128)(2,1)S(1)}, u32[]{:S(2)}, u32[]{:S(2)}) collective-permute-start(bf16[1,56,640]{2,1,0:T(8,128)(2,1)S(1)} %bitcast.115), channel_id=1, source_target_pairs={{0,6},{1,7},{2,4},{3,5},{4,2},{5,3},{6,0},{7,1},{8,14},{9,15},{10,... | collective-permute-start | bytes 215048 | tf_op jit(solution)/shard_map/ppermute | solution.py:75
  9.4 6.1 %collective-permute-start.1 = (bf16[1,56,640]{2,1,0:T(8,128)(2,1)S(1)}, bf16[1,56,640]{2,1,0:T(8,128)(2,1)S(1)}, u32[]{:S(2)}, u32[]{:S(2)}) collective-permute-start(bf16[1,56,640]{2,1,0:T(8,128)(2,1)S(1)} %bitcast.116), channel_id=1, source_target_pairs={{0,4},{1,5},{2,6},{3,7},{4,0},{5,1},{6,2},{7,3},{8,12},{9,13},{10,... | collective-permute-start | bytes 215048 | tf_op jit(solution)/shard_map/ppermute | solution.py:75
  9.4 6.1 %collective-permute-start = (bf16[1,56,640]{2,1,0:T(8,128)(2,1)S(1)}, bf16[1,56,640]{2,1,0:T(8,128)(2,1)S(1)}, u32[]{:S(2)}, u32[]{:S(2)}) collective-permute-start(bf16[1,56,640]{2,1,0:T(8,128)(2,1)S(1)} %bitcast.117), channel_id=1, source_target_pairs={{0,2},{1,3},{2,0},{3,1},{4,6},{5,7},{6,4},{7,5},{8,10},{9,11},{10,... | collective-permute-start | bytes 215048 | tf_op jit(solution)/shard_map/ppermute | solution.py:75
  15.6 7.0 %collective-permute-start.9 = (bf16[4,8,640]{2,1,0:T(8,128)(2,1)S(1)}, bf16[4,8,640]{2,1,0:T(8,128)(2,1)S(1)}, u32[]{:S(2)}, u32[]{:S(2)}) collective-permute-start(bf16[4,8,640]{2,1,0:T(8,128)(2,1)S(1)} %get-tuple-element.270), channel_id=1, source_target_pairs={{0,1},{1,0},{2,3},{3,2},{4,5},{5,4},{6,7},{7,6},{8,9},{9,8},{10,11... | collective-permute-start | bytes 122888 | tf_op jit(solution)/shard_map/ppermute | solution.py:75
  15.6 9.0 %collective-permute-start.8 = (bf16[1,128,640]{2,1,0:T(8,128)(2,1)S(1)}, bf16[1,128,640]{2,1,0:T(8,128)(2,1)S(1)}, u32[]{:S(2)}, u32[]{:S(2)}) collective-permute-start(bf16[1,128,640]{2,1,0:T(8,128)(2,1)S(1)} %bitcast.111), channel_id=1, source_target_pairs={{0,6},{1,7},{2,4},{3,5},{4,2},{5,3},{6,0},{7,1},{8,14},{9,15},{10,... | collective-permute-start | bytes 491528 | tf_op jit(solution)/shard_map/ppermute | solution.py:75
  18.4 14.8 %collective-permute-start.7 = (bf16[1,128,640]{2,1,0:T(8,128)(2,1)S(1)}, bf16[1,128,640]{2,1,0:T(8,128)(2,1)S(1)}, u32[]{:S(2)}, u32[]{:S(2)}) collective-permute-start(bf16[1,128,640]{2,1,0:T(8,128)(2,1)S(1)} %bitcast.112), channel_id=1, source_target_pairs={{0,4},{1,5},{2,6},{3,7},{4,0},{5,1},{6,2},{7,3},{8,12},{9,13},{10,... | collective-permute-start | bytes 491528 | tf_op jit(solution)/shard_map/ppermute | solution.py:75
  18.4 14.8 %collective-permute-start.6 = (bf16[1,128,640]{2,1,0:T(8,128)(2,1)S(1)}, bf16[1,128,640]{2,1,0:T(8,128)(2,1)S(1)}, u32[]{:S(2)}, u32[]{:S(2)}) collective-permute-start(bf16[1,128,640]{2,1,0:T(8,128)(2,1)S(1)} %bitcast.113), channel_id=1, source_target_pairs={{0,2},{1,3},{2,0},{3,1},{4,6},{5,7},{6,4},{7,5},{8,10},{9,11},{10,... | collective-permute-start | bytes 491528 | tf_op jit(solution)/shard_map/ppermute | solution.py:75
  20.1 13.3 %collective-permute-start.5 = (bf16[1,4,56,640]{3,2,1,0:T(8,128)(2,1)S(1)}, bf16[1,4,56,640]{3,2,1,0:T(8,128)(2,1)S(1)}, u32[]{:S(2)}, u32[]{:S(2)}) collective-permute-start(bf16[1,4,56,640]{3,2,1,0:T(8,128)(2,1)S(1)} %bitcast.100), channel_id=1, source_target_pairs={{0,24},{8,16},{16,8},{24,0},{1,25},{9,17},{17,9},{25,1},{2,26},{10... | collective-permute-start | bytes 860168 | tf_op jit(solution)/shard_map/ppermute | solution.py:70
  22.6 12.9 %collective-permute-start.4 = (bf16[1,4,56,640]{3,2,1,0:T(8,128)(2,1)S(1)}, bf16[1,4,56,640]{3,2,1,0:T(8,128)(2,1)S(1)}, u32[]{:S(2)}, u32[]{:S(2)}) collective-permute-start(bf16[1,4,56,640]{3,2,1,0:T(8,128)(2,1)S(1)} %bitcast.101), channel_id=1, source_target_pairs={{0,16},{8,24},{16,0},{24,8},{1,17},{9,25},{17,1},{25,9},{2,18},{10... | collective-permute-start | bytes 860168 | tf_op jit(solution)/shard_map/ppermute | solution.py:70
  24.6 10.9 %collective-permute-start.3 = (bf16[1,4,56,640]{3,2,1,0:T(8,128)(2,1)S(1)}, bf16[1,4,56,640]{3,2,1,0:T(8,128)(2,1)S(1)}, u32[]{:S(2)}, u32[]{:S(2)}) collective-permute-start(bf16[1,4,56,640]{3,2,1,0:T(8,128)(2,1)S(1)} %bitcast.102), channel_id=1, source_target_pairs={{0,8},{8,0},{16,24},{24,16},{1,9},{9,1},{17,25},{25,17},{2,10},{10... | collective-permute-start | bytes 860168 | tf_op jit(solution)/shard_map/ppermute | solution.py:70
  35.8 16.3 %copy-start.27 = (bf16[4,4,56,640]{3,2,1,0:T(8,128)(2,1)}, bf16[4,4,56,640]{3,2,1,0:T(8,128)(2,1)S(1)}, u32[]{:S(2)}) copy-start(bf16[4,4,56,640]{3,2,1,0:T(8,128)(2,1)S(1)} %pad_maximum_fusion) | copy-start | bytes 3440644
  35.8 9.3 %collective-permute-start.10 = (bf16[16,56,640]{2,1,0:T(8,128)(2,1)S(1)}, bf16[16,56,640]{2,1,0:T(8,128)(2,1)}, u32[]{:S(2)}, u32[]{:S(2)}) collective-permute-start(bf16[16,56,640]{2,1,0:T(8,128)(2,1)S(1)} %bitcast.104), channel_id=1, source_target_pairs={{0,1},{1,0},{2,3},{3,2},{4,5},{5,4},{6,7},{7,6},{8,9},{9,8},{10,11... | collective-permute-start | bytes 3440648 | tf_op jit(solution)/shard_map/ppermute | solution.py:75
  35.9 9.2 %collective-permute-start.11 = (bf16[512,640]{1,0:T(8,128)(2,1)S(1)}, bf16[512,640]{1,0:T(8,128)(2,1)S(1)}, u32[]{:S(2)}, u32[]{:S(2)}) collective-permute-start(bf16[512,640]{1,0:T(8,128)(2,1)S(1)} %bitcast.83), channel_id=1, source_target_pairs={{0,1},{1,0},{2,3},{3,2},{4,5},{5,4},{6,7},{7,6},{8,9},{9,8},{10,11... | collective-permute-start | bytes 1966088 | tf_op jit(solution)/shard_map/ppermute | solution.py:75
  36.4 5.9 %collective-permute-start.14 = (bf16[1,32,640]{2,1,0:T(8,128)(2,1)S(1)}, bf16[1,32,640]{2,1,0:T(8,128)(2,1)S(1)}, u32[]{:S(2)}, u32[]{:S(2)}) collective-permute-start(bf16[1,32,640]{2,1,0:T(8,128)(2,1)S(1)} %bitcast.119), channel_id=1, source_target_pairs={{0,6},{1,7},{2,4},{3,5},{4,2},{5,3},{6,0},{7,1},{8,14},{9,15},{10,... | collective-permute-start | bytes 122888 | tf_op jit(solution)/shard_map/ppermute | solution.py:75
  39.2 5.6 %collective-permute-start.13 = (bf16[1,32,640]{2,1,0:T(8,128)(2,1)S(1)}, bf16[1,32,640]{2,1,0:T(8,128)(2,1)S(1)}, u32[]{:S(2)}, u32[]{:S(2)}) collective-permute-start(bf16[1,32,640]{2,1,0:T(8,128)(2,1)S(1)} %bitcast.120), channel_id=1, source_target_pairs={{0,4},{1,5},{2,6},{3,7},{4,0},{5,1},{6,2},{7,3},{8,12},{9,13},{10,... | collective-permute-start | bytes 122888 | tf_op jit(solution)/shard_map/ppermute | solution.py:75
  41.0 4.0 %collective-permute-start.12 = (bf16[1,32,640]{2,1,0:T(8,128)(2,1)S(1)}, bf16[1,32,640]{2,1,0:T(8,128)(2,1)S(1)}, u32[]{:S(2)}, u32[]{:S(2)}) collective-permute-start(bf16[1,32,640]{2,1,0:T(8,128)(2,1)S(1)} %bitcast.121), channel_id=1, source_target_pairs={{0,2},{1,3},{2,0},{3,1},{4,6},{5,7},{6,4},{7,5},{8,10},{9,11},{10,... | collective-permute-start | bytes 122888 | tf_op jit(solution)/shard_map/ppermute | solution.py:75
  46.1 14.9 %collective-permute-start.19 = (bf16[1,4,32,640]{3,2,1,0:T(8,128)(2,1)S(1)}, bf16[1,4,32,640]{3,2,1,0:T(8,128)(2,1)S(1)}, u32[]{:S(2)}, u32[]{:S(2)}) collective-permute-start(bf16[1,4,32,640]{3,2,1,0:T(8,128)(2,1)S(1)} %bitcast.107), channel_id=1, source_target_pairs={{0,24},{8,16},{16,8},{24,0},{1,25},{9,17},{17,9},{25,1},{2,26},{10... | collective-permute-start | bytes 491528 | tf_op jit(solution)/shard_map/ppermute | solution.py:70
  48.6 12.4 %collective-permute-start.18 = (bf16[1,4,32,640]{3,2,1,0:T(8,128)(2,1)S(1)}, bf16[1,4,32,640]{3,2,1,0:T(8,128)(2,1)S(1)}, u32[]{:S(2)}, u32[]{:S(2)}) collective-permute-start(bf16[1,4,32,640]{3,2,1,0:T(8,128)(2,1)S(1)} %bitcast.108), channel_id=1, source_target_pairs={{0,16},{8,24},{16,0},{24,8},{1,17},{9,25},{17,1},{25,9},{2,18},{10... | collective-permute-start | bytes 491528 | tf_op jit(solution)/shard_map/ppermute | solution.py:70
  49.1 11.9 %collective-permute-start.17 = (bf16[1,4,32,640]{3,2,1,0:T(8,128)(2,1)S(1)}, bf16[1,4,32,640]{3,2,1,0:T(8,128)(2,1)S(1)}, u32[]{:S(2)}, u32[]{:S(2)}) collective-permute-start(bf16[1,4,32,640]{3,2,1,0:T(8,128)(2,1)S(1)} %bitcast.109), channel_id=1, source_target_pairs={{0,8},{8,0},{16,24},{24,16},{1,9},{9,1},{17,25},{25,17},{2,10},{10... | collective-permute-start | bytes 491528 | tf_op jit(solution)/shard_map/ppermute | solution.py:70
  49.7 12.1 %collective-permute-start.16 = (bf16[192,640]{1,0:T(8,128)(2,1)S(1)}, bf16[192,640]{1,0:T(8,128)(2,1)S(1)}, u32[]{:S(2)}, u32[]{:S(2)}) collective-permute-start(bf16[192,640]{1,0:T(8,128)(2,1)S(1)} %pad_maximum_fusion.4.refs_4_), channel_id=1, source_target_pairs={{0,4},{1,5},{2,6},{3,7},{4,0},{5,1},{6,2},{7,3},{8,12},{9,13},{10,... | collective-permute-start | bytes 737288 | tf_op jit(solution)/shard_map/ppermute | solution.py:75
  50.7 11.0 %collective-permute-start.15 = (bf16[192,640]{1,0:T(8,128)(2,1)S(1)}, bf16[192,640]{1,0:T(8,128)(2,1)S(1)}, u32[]{:S(2)}, u32[]{:S(2)}) collective-permute-start(bf16[192,640]{1,0:T(8,128)(2,1)S(1)} %pad_maximum_fusion.4.refs_4_), channel_id=1, source_target_pairs={{0,2},{1,3},{2,0},{3,1},{4,6},{5,7},{6,4},{7,5},{8,10},{9,11},{10,... | collective-permute-start | bytes 737288 | tf_op jit(solution)/shard_map/ppermute | solution.py:75
  61.0 53.7 %copy-start.14 = (bf16[128,1024]{1,0:T(8,128)(2,1)}, bf16[128,1024]{1,0:T(8,128)(2,1)S(1)}, u32[]{:S(2)}) copy-start(bf16[128,1024]{1,0:T(8,128)(2,1)S(1)} %get-tuple-element.146.attn_ref) | copy-start | bytes 786436
  61.8 2.9 %collective-permute-start.20 = (bf16[16,32,640]{2,1,0:T(8,128)(2,1)S(1)}, bf16[16,32,640]{2,1,0:T(8,128)(2,1)S(1)}, u32[]{:S(2)}, u32[]{:S(2)}) collective-permute-start(bf16[16,32,640]{2,1,0:T(8,128)(2,1)S(1)} %bitcast.86), channel_id=1, source_target_pairs={{0,1},{1,0},{2,3},{3,2},{4,5},{5,4},{6,7},{7,6},{8,9},{9,8},{10,11... | collective-permute-start | bytes 1966088 | tf_op jit(solution)/shard_map/ppermute | solution.py:75
  61.8 6.7 %collective-permute-start.26 = (bf16[192,640]{1,0:T(8,128)(2,1)S(1)}, bf16[192,640]{1,0:T(8,128)(2,1)S(1)}, u32[]{:S(2)}, u32[]{:S(2)}) collective-permute-start(bf16[192,640]{1,0:T(8,128)(2,1)S(1)} %collective-permute-done.15.refs_5_), channel_id=1, source_target_pairs={{0,1},{1,0},{2,3},{3,2},{4,5},{5,4},{6,7},{7,6},{8,9},{9,8},{10,11... | collective-permute-start | bytes 737288 | tf_op jit(solution)/shard_map/ppermute | solution.py:75
  62.3 6.7 %collective-permute-start.27 = (bf16[192,640]{1,0:T(8,128)(2,1)S(1)}, bf16[192,640]{1,0:T(8,128)(2,1)S(1)}, u32[]{:S(2)}, u32[]{:S(2)}) collective-permute-start(bf16[192,640]{1,0:T(8,128)(2,1)S(1)} %collective-permute-done.16.refs_6_), channel_id=1, source_target_pairs={{0,1},{1,0},{2,3},{3,2},{4,5},{5,4},{6,7},{7,6},{8,9},{9,8},{10,11... | collective-permute-start | bytes 737288 | tf_op jit(solution)/shard_map/ppermute | solution.py:75
  62.4 7.2 %collective-permute-start.25 = (bf16[192,640]{1,0:T(8,128)(2,1)S(1)}, bf16[192,640]{1,0:T(8,128)(2,1)S(1)}, u32[]{:S(2)}, u32[]{:S(2)}) collective-permute-start(bf16[192,640]{1,0:T(8,128)(2,1)S(1)} %pad_maximum_fusion.4.refs_4_), channel_id=1, source_target_pairs={{0,1},{1,0},{2,3},{3,2},{4,5},{5,4},{6,7},{7,6},{8,9},{9,8},{10,11... | collective-permute-start | bytes 737288 | tf_op jit(solution)/shard_map/ppermute | solution.py:75
  62.8 9.8 %collective-permute-start.24 = (bf16[192,640]{1,0:T(8,128)(2,1)S(1)}, bf16[192,640]{1,0:T(8,128)(2,1)S(1)}, u32[]{:S(2)}, u32[]{:S(2)}) collective-permute-start(bf16[192,640]{1,0:T(8,128)(2,1)S(1)} %pad_maximum_fusion.4.refs_4_), channel_id=1, source_target_pairs={{0,6},{1,7},{2,4},{3,5},{4,2},{5,3},{6,0},{7,1},{8,14},{9,15},{10,... | collective-permute-start | bytes 737288 | tf_op jit(solution)/shard_map/ppermute | solution.py:75
  66.0 25.8 %copy-start.7 = (f32[1,128,640]{2,1,0:T(8,128)S(1)}, f32[1,128,640]{2,1,0:T(8,128)}, u32[]{:S(2)}) copy-start(f32[1,128,640]{2,1,0:T(8,128)} %param.21) | copy-start | bytes 983044
  66.0 7.9 %collective-permute-start.23 = (bf16[128,640]{1,0:T(8,128)(2,1)S(1)}, bf16[128,640]{1,0:T(8,128)(2,1)S(1)}, u32[]{:S(2)}, u32[]{:S(2)}) collective-permute-start(bf16[128,640]{1,0:T(8,128)(2,1)S(1)} %get-tuple-element.152.refs_0_), channel_id=1, source_target_pairs={{0,24},{8,16},{16,8},{24,0},{1,25},{9,17},{17,9},{25,1},{2,26},{10... | collective-permute-start | bytes 491528 | tf_op jit(solution)/shard_map/ppermute | solution.py:70
  68.5 7.9 %collective-permute-start.22 = (bf16[128,640]{1,0:T(8,128)(2,1)S(1)}, bf16[128,640]{1,0:T(8,128)(2,1)S(1)}, u32[]{:S(2)}, u32[]{:S(2)}) collective-permute-start(bf16[128,640]{1,0:T(8,128)(2,1)S(1)} %get-tuple-element.152.refs_0_), channel_id=1, source_target_pairs={{0,16},{8,24},{16,0},{24,8},{1,17},{9,25},{17,1},{25,9},{2,18},{10... | collective-permute-start | bytes 491528 | tf_op jit(solution)/shard_map/ppermute | solution.py:70
  69.0 7.5 %collective-permute-start.21 = (bf16[128,640]{1,0:T(8,128)(2,1)S(1)}, bf16[128,640]{1,0:T(8,128)(2,1)S(1)}, u32[]{:S(2)}, u32[]{:S(2)}) collective-permute-start(bf16[128,640]{1,0:T(8,128)(2,1)S(1)} %get-tuple-element.152.refs_0_), channel_id=1, source_target_pairs={{0,8},{8,0},{16,24},{24,16},{1,9},{9,1},{17,25},{25,17},{2,10},{10... | collective-permute-start | bytes 491528 | tf_op jit(solution)/shard_map/ppermute | solution.py:70
  76.5 1.5 collective-permute-start.28
  80.7 7.1 %collective-permute-start.29 = (bf16[128,640]{1,0:T(8,128)(2,1)S(1)}, bf16[128,640]{1,0:T(8,128)(2,1)S(1)}, u32[]{:S(2)}, u32[]{:S(2)}) collective-permute-start(bf16[128,640]{1,0:T(8,128)(2,1)S(1)} %get-tuple-element.161), channel_id=1, source_target_pairs={{0,8},{8,0},{16,24},{24,16},{1,9},{9,1},{17,25},{25,17},{2,10},{10... | collective-permute-start | bytes 491528 | tf_op jit(solution)/shard_map/ppermute | solution.py:70
  82.2 9.5 %collective-permute-start.30 = (bf16[128,640]{1,0:T(8,128)(2,1)S(1)}, bf16[128,640]{1,0:T(8,128)(2,1)S(1)}, u32[]{:S(2)}, u32[]{:S(2)}) collective-permute-start(bf16[128,640]{1,0:T(8,128)(2,1)S(1)} %get-tuple-element.162), channel_id=1, source_target_pairs={{0,16},{8,24},{16,0},{24,8},{1,17},{9,25},{17,1},{25,9},{2,18},{10... | collective-permute-start | bytes 491528 | tf_op jit(solution)/shard_map/ppermute | solution.py:70
  83.0 8.7 %collective-permute-start.31 = (bf16[128,640]{1,0:T(8,128)(2,1)S(1)}, bf16[128,640]{1,0:T(8,128)(2,1)S(1)}, u32[]{:S(2)}, u32[]{:S(2)}) collective-permute-start(bf16[128,640]{1,0:T(8,128)(2,1)S(1)} %get-tuple-element.163), channel_id=1, source_target_pairs={{0,24},{8,16},{16,8},{24,0},{1,25},{9,17},{17,9},{25,1},{2,26},{10... | collective-permute-start | bytes 491528 | tf_op jit(solution)/shard_map/ppermute | solution.py:70
  92.7 7.8 %collective-permute-start.34 = (bf16[128,640]{1,0:T(8,128)(2,1)S(1)}, bf16[128,640]{1,0:T(8,128)(2,1)S(1)}, u32[]{:S(2)}, u32[]{:S(2)}) collective-permute-start(bf16[128,640]{1,0:T(8,128)(2,1)S(1)} %get-tuple-element.166.refs_0_), channel_id=1, source_target_pairs={{0,24},{8,16},{16,8},{24,0},{1,25},{9,17},{17,9},{25,1},{2,26},{10... | collective-permute-start | bytes 491528 | tf_op jit(solution)/shard_map/ppermute | solution.py:70
  94.1 8.1 %collective-permute-start.33 = (bf16[128,640]{1,0:T(8,128)(2,1)S(1)}, bf16[128,640]{1,0:T(8,128)(2,1)S(1)}, u32[]{:S(2)}, u32[]{:S(2)}) collective-permute-start(bf16[128,640]{1,0:T(8,128)(2,1)S(1)} %get-tuple-element.166.refs_0_), channel_id=1, source_target_pairs={{0,16},{8,24},{16,0},{24,8},{1,17},{9,25},{17,1},{25,9},{2,18},{10... | collective-permute-start | bytes 491528 | tf_op jit(solution)/shard_map/ppermute | solution.py:70
  94.7 7.5 %collective-permute-start.32 = (bf16[128,640]{1,0:T(8,128)(2,1)S(1)}, bf16[128,640]{1,0:T(8,128)(2,1)S(1)}, u32[]{:S(2)}, u32[]{:S(2)}) collective-permute-start(bf16[128,640]{1,0:T(8,128)(2,1)S(1)} %get-tuple-element.166.refs_0_), channel_id=1, source_target_pairs={{0,8},{8,0},{16,24},{24,16},{1,9},{9,1},{17,25},{25,17},{2,10},{10... | collective-permute-start | bytes 491528 | tf_op jit(solution)/shard_map/ppermute | solution.py:70
  104.8 7.2 %collective-permute-start.35 = (bf16[128,640]{1,0:T(8,128)(2,1)S(1)}, bf16[128,640]{1,0:T(8,128)(2,1)S(1)}, u32[]{:S(2)}, u32[]{:S(2)}) collective-permute-start(bf16[128,640]{1,0:T(8,128)(2,1)S(1)} %get-tuple-element.180), channel_id=1, source_target_pairs={{0,8},{8,0},{16,24},{24,16},{1,9},{9,1},{17,25},{25,17},{2,10},{10... | collective-permute-start | bytes 491528 | tf_op jit(solution)/shard_map/ppermute | solution.py:70
  105.7 9.0 %collective-permute-start.36 = (bf16[128,640]{1,0:T(8,128)(2,1)S(1)}, bf16[128,640]{1,0:T(8,128)(2,1)S(1)}, u32[]{:S(2)}, u32[]{:S(2)}) collective-permute-start(bf16[128,640]{1,0:T(8,128)(2,1)S(1)} %get-tuple-element.181), channel_id=1, source_target_pairs={{0,16},{8,24},{16,0},{24,8},{1,17},{9,25},{17,1},{25,9},{2,18},{10... | collective-permute-start | bytes 491528 | tf_op jit(solution)/shard_map/ppermute | solution.py:70
  107.0 7.7 %collective-permute-start.37 = (bf16[128,640]{1,0:T(8,128)(2,1)S(1)}, bf16[128,640]{1,0:T(8,128)(2,1)S(1)}, u32[]{:S(2)}, u32[]{:S(2)}) collective-permute-start(bf16[128,640]{1,0:T(8,128)(2,1)S(1)} %get-tuple-element.182), channel_id=1, source_target_pairs={{0,24},{8,16},{16,8},{24,0},{1,25},{9,17},{17,9},{25,1},{2,26},{10... | collective-permute-start | bytes 491528 | tf_op jit(solution)/shard_map/ppermute | solution.py:70
  114.7 4.4 %collective-permute-start.39 = (bf16[4,192,640]{2,1,0:T(8,128)(2,1)S(1)}, bf16[4,192,640]{2,1,0:T(8,128)(2,1)S(1)}, u32[]{:S(2)}, u32[]{:S(2)}) collective-permute-start(bf16[4,192,640]{2,1,0:T(8,128)(2,1)S(1)} %get-tuple-element.192), channel_id=1, source_target_pairs={{0,1},{1,0},{2,3},{3,2},{4,5},{5,4},{6,7},{7,6},{8,9},{9,8},{10,11... | collective-permute-start | bytes 2949128 | tf_op jit(solution)/shard_map/ppermute | solution.py:75
  116.6 2.3 %collective-permute-start.38 = (bf16[16,32,640]{2,1,0:T(8,128)(2,1)S(1)}, bf16[16,32,640]{2,1,0:T(8,128)(2,1)S(1)}, u32[]{:S(2)}, u32[]{:S(2)}) collective-permute-start(bf16[16,32,640]{2,1,0:T(8,128)(2,1)S(1)} %get-tuple-element.190), channel_id=1, source_target_pairs={{0,1},{1,0},{2,3},{3,2},{4,5},{5,4},{6,7},{7,6},{8,9},{9,8},{10,11... | collective-permute-start | bytes 1966088 | tf_op jit(solution)/shard_map/ppermute | solution.py:75
  120.0 14.3 %collective-permute-start.44 = (bf16[4,32,640]{2,1,0:T(8,128)(2,1)S(1)}, bf16[4,32,640]{2,1,0:T(8,128)(2,1)S(1)}, u32[]{:S(2)}, u32[]{:S(2)}) collective-permute-start(bf16[4,32,640]{2,1,0:T(8,128)(2,1)S(1)} %get-tuple-element.259), channel_id=1, source_target_pairs={{0,24},{8,16},{16,8},{24,0},{1,25},{9,17},{17,9},{25,1},{2,26},{10... | collective-permute-start | bytes 491528 | tf_op jit(solution)/shard_map/ppermute | solution.py:70
  121.3 13.0 %collective-permute-start.43 = (bf16[4,32,640]{2,1,0:T(8,128)(2,1)S(1)}, bf16[4,32,640]{2,1,0:T(8,128)(2,1)S(1)}, u32[]{:S(2)}, u32[]{:S(2)}) collective-permute-start(bf16[4,32,640]{2,1,0:T(8,128)(2,1)S(1)} %get-tuple-element.260), channel_id=1, source_target_pairs={{0,16},{8,24},{16,0},{24,8},{1,17},{9,25},{17,1},{25,9},{2,18},{10... | collective-permute-start | bytes 491528 | tf_op jit(solution)/shard_map/ppermute | solution.py:70
  122.6 11.6 %collective-permute-start.42 = (bf16[4,32,640]{2,1,0:T(8,128)(2,1)S(1)}, bf16[4,32,640]{2,1,0:T(8,128)(2,1)S(1)}, u32[]{:S(2)}, u32[]{:S(2)}) collective-permute-start(bf16[4,32,640]{2,1,0:T(8,128)(2,1)S(1)} %get-tuple-element.261), channel_id=1, source_target_pairs={{0,8},{8,0},{16,24},{24,16},{1,9},{9,1},{17,25},{25,17},{2,10},{10... | collective-permute-start | bytes 491528 | tf_op jit(solution)/shard_map/ppermute | solution.py:70
  123.6 13.3 %collective-permute-start.41 = (bf16[192,640]{1,0:T(8,128)(2,1)S(1)}, bf16[192,640]{1,0:T(8,128)(2,1)S(1)}, u32[]{:S(2)}, u32[]{:S(2)}) collective-permute-start(bf16[192,640]{1,0:T(8,128)(2,1)S(1)} %get-tuple-element.257), channel_id=1, source_target_pairs={{0,4},{1,5},{2,6},{3,7},{4,0},{5,1},{6,2},{7,3},{8,12},{9,13},{10,... | collective-permute-start | bytes 737288 | tf_op jit(solution)/shard_map/ppermute | solution.py:75
  125.0 12.4 %collective-permute-start.40 = (bf16[192,640]{1,0:T(8,128)(2,1)S(1)}, bf16[192,640]{1,0:T(8,128)(2,1)S(1)}, u32[]{:S(2)}, u32[]{:S(2)}) collective-permute-start(bf16[192,640]{1,0:T(8,128)(2,1)S(1)} %get-tuple-element.258), channel_id=1, source_target_pairs={{0,2},{1,3},{2,0},{3,1},{4,6},{5,7},{6,4},{7,5},{8,10},{9,11},{10,... | collective-permute-start | bytes 737288 | tf_op jit(solution)/shard_map/ppermute | solution.py:75
  138.2 4.9 %collective-permute-start.45 = (bf16[16,48,640]{2,1,0:T(8,128)(2,1)}, bf16[16,48,640]{2,1,0:T(8,128)(2,1)S(1)}, u32[]{:S(2)}, u32[]{:S(2)}) collective-permute-start(bf16[16,48,640]{2,1,0:T(8,128)(2,1)} %copy-done.10), channel_id=1, source_target_pairs={{0,1},{1,0},{2,3},{3,2},{4,5},{5,4},{6,7},{7,6},{8,9},{9,8},{10,11... | collective-permute-start | bytes 2949128 | tf_op jit(solution)/shard_map/ppermute | solution.py:75
  138.4 4.6 %collective-permute-start.46 = (bf16[16,96]{1,0:T(8,128)(2,1)S(1)}, bf16[16,96]{1,0:T(8,128)(2,1)S(1)}, u32[]{:S(2)}, u32[]{:S(2)}) collective-permute-start(bf16[16,96]{1,0:T(8,128)(2,1)S(1)} %slice.172), channel_id=1, source_target_pairs={{0,1},{1,0},{2,3},{3,2},{4,5},{5,4},{6,7},{7,6},{8,9},{9,8},{10,11... | collective-permute-start | bytes 9224 | tf_op jit(solution)/shard_map/ppermute | solution.py:75
  139.0 4.1 %collective-permute-start.47 = (bf16[512,512]{1,0:T(8,128)(2,1)}, bf16[512,512]{1,0:T(8,128)(2,1)S(1)}, u32[]{:S(2)}, u32[]{:S(2)}) collective-permute-start(bf16[512,512]{1,0:T(8,128)(2,1)} %copy-done.13), channel_id=1, source_target_pairs={{0,1},{1,0},{2,3},{3,2},{4,5},{5,4},{6,7},{7,6},{8,9},{9,8},{10,11... | collective-permute-start | bytes 1572872 | tf_op jit(solution)/shard_map/ppermute | solution.py:75
  139.9 7.6 %collective-permute-start.48 = (bf16[96,640]{1,0:T(8,128)(2,1)S(1)}, bf16[96,640]{1,0:T(8,128)(2,1)S(1)}, u32[]{:S(2)}, u32[]{:S(2)}) collective-permute-start(bf16[96,640]{1,0:T(8,128)(2,1)S(1)} %slice_bitcast_fusion.10), channel_id=1, source_target_pairs={{0,6},{1,7},{2,4},{3,5},{4,2},{5,3},{6,0},{7,1},{8,14},{9,15},{10,... | collective-permute-start | bytes 368648 | tf_op jit(solution)/shard_map/ppermute | solution.py:75
  147.6 6.9 %collective-permute-start.52 = (bf16[128,512]{1,0:T(8,128)(2,1)S(1)}, bf16[128,512]{1,0:T(8,128)(2,1)S(1)}, u32[]{:S(2)}, u32[]{:S(2)}) collective-permute-start(bf16[128,512]{1,0:T(8,128)(2,1)S(1)} %get-tuple-element.262), channel_id=1, source_target_pairs={{0,2},{1,3},{2,0},{3,1},{4,6},{5,7},{6,4},{7,5},{8,10},{9,11},{10,... | collective-permute-start | bytes 393224 | tf_op jit(solution)/shard_map/ppermute | solution.py:75
  148.7 8.3 %collective-permute-start.54 = (bf16[128,512]{1,0:T(8,128)(2,1)S(1)}, bf16[128,512]{1,0:T(8,128)(2,1)S(1)}, u32[]{:S(2)}, u32[]{:S(2)}) collective-permute-start(bf16[128,512]{1,0:T(8,128)(2,1)S(1)} %get-tuple-element.263), channel_id=1, source_target_pairs={{0,6},{1,7},{2,4},{3,5},{4,2},{5,3},{6,0},{7,1},{8,14},{9,15},{10,... | collective-permute-start | bytes 393224 | tf_op jit(solution)/shard_map/ppermute | solution.py:75
  149.5 12.8 %collective-permute-start.53 = (bf16[128,512]{1,0:T(8,128)(2,1)S(1)}, bf16[128,512]{1,0:T(8,128)(2,1)S(1)}, u32[]{:S(2)}, u32[]{:S(2)}) collective-permute-start(bf16[128,512]{1,0:T(8,128)(2,1)S(1)} %get-tuple-element.264), channel_id=1, source_target_pairs={{0,4},{1,5},{2,6},{3,7},{4,0},{5,1},{6,2},{7,3},{8,12},{9,13},{10,... | collective-permute-start | bytes 393224 | tf_op jit(solution)/shard_map/ppermute | solution.py:75
  151.2 11.1 %collective-permute-start.49 = (bf16[4,56,640]{2,1,0:T(8,128)(2,1)S(1)}, bf16[4,56,640]{2,1,0:T(8,128)(2,1)S(1)}, u32[]{:S(2)}, u32[]{:S(2)}) collective-permute-start(bf16[4,56,640]{2,1,0:T(8,128)(2,1)S(1)} %get-tuple-element.254), channel_id=1, source_target_pairs={{0,8},{8,0},{16,24},{24,16},{1,9},{9,1},{17,25},{25,17},{2,10},{10... | collective-permute-start | bytes 860168 | tf_op jit(solution)/shard_map/ppermute | solution.py:70
  152.0 13.3 %collective-permute-start.51 = (bf16[4,56,640]{2,1,0:T(8,128)(2,1)S(1)}, bf16[4,56,640]{2,1,0:T(8,128)(2,1)S(1)}, u32[]{:S(2)}, u32[]{:S(2)}) collective-permute-start(bf16[4,56,640]{2,1,0:T(8,128)(2,1)S(1)} %get-tuple-element.255), channel_id=1, source_target_pairs={{0,24},{8,16},{16,8},{24,0},{1,25},{9,17},{17,9},{25,1},{2,26},{10... | collective-permute-start | bytes 860168 | tf_op jit(solution)/shard_map/ppermute | solution.py:70
  154.5 12.2 %collective-permute-start.50 = (bf16[4,56,640]{2,1,0:T(8,128)(2,1)S(1)}, bf16[4,56,640]{2,1,0:T(8,128)(2,1)S(1)}, u32[]{:S(2)}, u32[]{:S(2)}) collective-permute-start(bf16[4,56,640]{2,1,0:T(8,128)(2,1)S(1)} %get-tuple-element.256), channel_id=1, source_target_pairs={{0,16},{8,24},{16,0},{24,8},{1,17},{9,25},{17,1},{25,9},{2,18},{10... | collective-permute-start | bytes 860168 | tf_op jit(solution)/shard_map/ppermute | solution.py:70
  168.2 7.6 %collective-permute-start.55 = (bf16[88,640]{1,0:T(8,128)(2,1)S(1)}, bf16[88,640]{1,0:T(8,128)(2,1)S(1)}, u32[]{:S(2)}, u32[]{:S(2)}) collective-permute-start(bf16[88,640]{1,0:T(8,128)(2,1)S(1)} %pad_maximum_fusion.7), channel_id=1, source_target_pairs={{0,2},{1,3},{2,0},{3,1},{4,6},{5,7},{6,4},{7,5},{8,10},{9,11},{10,... | collective-permute-start | bytes 337928 | tf_op jit(solution)/shard_map/ppermute | solution.py:75
  169.8 10.8 %collective-permute-start.56 = (bf16[88,640]{1,0:T(8,128)(2,1)S(1)}, bf16[88,640]{1,0:T(8,128)(2,1)S(1)}, u32[]{:S(2)}, u32[]{:S(2)}) collective-permute-start(bf16[88,640]{1,0:T(8,128)(2,1)S(1)} %pad_maximum_fusion.8), channel_id=1, source_target_pairs={{0,4},{1,5},{2,6},{3,7},{4,0},{5,1},{6,2},{7,3},{8,12},{9,13},{10,... | collective-permute-start | bytes 337928 | tf_op jit(solution)/shard_map/ppermute | solution.py:75
  170.7 9.9 %collective-permute-start.57 = (bf16[184,640]{1,0:T(8,128)(2,1)S(1)}, bf16[184,640]{1,0:T(8,128)(2,1)S(1)}, u32[]{:S(2)}, u32[]{:S(2)}) collective-permute-start(bf16[184,640]{1,0:T(8,128)(2,1)S(1)} %pad_maximum_fusion.5), channel_id=1, source_target_pairs={{0,6},{1,7},{2,4},{3,5},{4,2},{5,3},{6,0},{7,1},{8,14},{9,15},{10,... | collective-permute-start | bytes 706568 | tf_op jit(solution)/shard_map/ppermute | solution.py:75
  (29 other events, 174.8 us)

commit v5 on v4

--- a/solution.py
+++ b/solution.py
@@ -868,7 +868,7 @@
                 unit_in, near, far, first, other, owner_of, order_kv, scale_in, scale_query, scale_key,
                 cos_all, sine_all, key_index, row_index,
             ),
-            mebibytes=52,
+            mebibytes=56,
         )
     )
     attn_bf, feed_z1, feed_z2, out_own, feed = tie((attn_bf, feed_z1, feed_z2, out_own, feed))
@@ -985,7 +985,7 @@
             scale_query, scale_key, cos_all, sine_all, key_index, row_index, normed, normed_all,
             unit_in, near, far, owner_of, order_kv,
         ),
-        mebibytes=36,
+        mebibytes=48,
     )
     back = (packed, packed_far, g_near, g_far, grad_normed_q, grad_s_in, grad_s_query, grad_s_key)
     back, feed_come1, feed_come2, out_comes, g_out, g_feed = tie(

time: 184 us -> 182 us (0.989)
  local copies, waits for them, and re-layouts: 11.5 us -> 6.63 us
  Pallas kernels: 26.4 us -> 28.9 us
  waiting for transfers between devices: 68.5 us -> 66 us
  other arithmetic: 10.9 us -> 12.8 us
    ppermute x34, waiting for transfers between devices: 39.9 us -> 37.3 us  [swap_ctx(): lax.ppermute(block, 'ctx', [(place, place ^ bits) for place in range(coun...]
    pallas_call x9, Pallas kernels: 26.4 us -> 28.9 us  [call_kernel(): pl.pallas_call(body, out_shape=[jax.ShapeDtypeStruct(shape, dtype) for sh...]
    unnamed x72 -> x68, local copies, waits for them, and re-layouts: 3.91 us -> 1.41 us
  transfers between devices with their start and end apart: 58 -> 58, of which waited for: 31 -> 29; matrix products, arithmetic and copies ran while one was open for 6% -> 7% of each run, Pallas kernels for 11% -> 12%
where the time goes in v5:
time: 182 us; the launch traced here: 180 us
  waiting for transfers between devices  66 us (36%)
  starting transfers between devices  63.6 us (35%)
  Pallas kernels  28.9 us (16%)
  other arithmetic  12.8 us (7%)
  local copies, waits for them, and re-layouts  6.63 us (4%)
    ppermute x34, waiting for transfers between devices, swap_ctx(): lax.ppermute(block, 'ctx', [(place, place ^ bits) for place in range(coun...  37.3 us
    ppermute x34, starting transfers between devices, swap_ctx(): lax.ppermute(block, 'ctx', [(place, place ^ bits) for place in range(coun...  34.3 us
    ppermute x24, starting transfers between devices, swap_dp(): lax.ppermute(block, 'dp', [(place, place ^ bits) for place in range(count)])  29.3 us
    pallas_call x9, Pallas kernels, call_kernel(): pl.pallas_call(body, out_shape=[jax.ShapeDtypeStruct(shape, dtype) for sh...  28.9 us
    ppermute x24, waiting for transfers between devices, swap_dp(): lax.ppermute(block, 'dp', [(place, place ^ bits) for place in range(count)])  28.7 us
  transfers between devices with their start and end apart: 58, of which 29 were waited for; matrix products, arithmetic and copies ran while one was open for 7% of the time, Pallas kernels for 12%

profile of v5, /device:TPU:0, one launch (start us, length us, event | category | flops | bytes accessed | tf_op | source)
XLA Modules:
  0.0 180.1 jit_solution(11133212545072896977)
XLA Ops:
  2.1 2.2 %concatenate.37 = bf16[56,640]{1,0:T(8,128)(2,1)S(1)} concatenate(bf16[32,640]{1,0:T(8,128)(2,1)} %param.13, bf16[8,640]{1,0:T(8,128)(2,1)} %param.14, bf16[8,640]{1,0:T(8,128)(2,1)} %param.15, bf16[1,640]{1,0:T(2,128)(2,1)S(1)} %pad.19, bf16[1,640]{1,0:T(2,128)(2,1)S(1)} %pad.20, bf16[1,640]{1,0:T(2,128)(2,1)S(1)} %pad.21, bf16[5,640]{1,0:T(8,128)(2,1)S(1)} %broadcast_in_dim.72), dimensions={0} | concatenate | bytes 143360 | tf_op jit(solution)/shard_map/concatenate | solution.py:818
  4.3 5.1 %collective-permute-start.2 = (bf16[1,56,640]{2,1,0:T(8,128)(2,1)S(1)}, bf16[1,56,640]{2,1,0:T(8,128)(2,1)S(1)}, u32[]{:S(2)}, u32[]{:S(2)}) collective-permute-start(bf16[1,56,640]{2,1,0:T(8,128)(2,1)S(1)} %bitcast.115), channel_id=1, source_target_pairs={{0,6},{1,7},{2,4},{3,5},{4,2},{5,3},{6,0},{7,1},{8,14},{9,15},{10,... | collective-permute-start | bytes 215048 | tf_op jit(solution)/shard_map/ppermute | solution.py:75
  10.1 1.1 multiply_reduce_fusion.1
  11.4 1.8 %fusion.41 = (bf16[128,640]{1,0:T(8,128)(2,1)S(1)}, f32[128,640]{1,0:T(8,128)}) fusion(f32[128]{0:T(128)S(1)} %add_rsqrt_fusion, f32[1,128,640]{2,1,0:T(8,128)} %param.11), kind=kLoop, calls=%fused_computation.140 | loop fusion | flops 163840 | bytes 819712 | tf_op jit(solution)/shard_map/convert_element_type | solution.py:822
  14.1 1.3 collective-permute-done.1
  15.6 2.8 %collective-permute-start.8 = (bf16[1,128,640]{2,1,0:T(8,128)(2,1)S(1)}, bf16[1,128,640]{2,1,0:T(8,128)(2,1)S(1)}, u32[]{:S(2)}, u32[]{:S(2)}) collective-permute-start(bf16[1,128,640]{2,1,0:T(8,128)(2,1)S(1)} %bitcast.111), channel_id=1, source_target_pairs={{0,6},{1,7},{2,4},{3,5},{4,2},{5,3},{6,0},{7,1},{8,14},{9,15},{10,... | collective-permute-start | bytes 491528 | tf_op jit(solution)/shard_map/ppermute | solution.py:75
  18.4 1.7 collective-permute-start.6
  20.1 2.4 %collective-permute-start.5 = (bf16[1,4,56,640]{3,2,1,0:T(8,128)(2,1)S(1)}, bf16[1,4,56,640]{3,2,1,0:T(8,128)(2,1)S(1)}, u32[]{:S(2)}, u32[]{:S(2)}) collective-permute-start(bf16[1,4,56,640]{3,2,1,0:T(8,128)(2,1)S(1)} %bitcast.97), channel_id=1, source_target_pairs={{0,24},{8,16},{16,8},{24,0},{1,25},{9,17},{17,9},{25,1},{2,26},{10... | collective-permute-start | bytes 860168 | tf_op jit(solution)/shard_map/ppermute | solution.py:70
  23.1 1.6 collective-permute-done.8
  24.6 1.5 collective-permute-start.3
  26.1 3.0 %multiply_sine_fusion = (f32[1024,128]{1,0:T(8,128)}, f32[1024,128]{1,0:T(8,128)}) fusion(f32[128]{0:T(128)S(1)} %multiply_power_fusion, f32[1024]{0:T(1024)S(1)} %bitcast.125), kind=kLoop, calls=%fused_computation.11 | loop fusion | flops 131072 | bytes 1053184 | tf_op jit(solution)/shard_map/sin | solution.py:831
  29.2 4.1 %collective-permute-done.7 = bf16[1,128,640]{2,1,0:T(8,128)(2,1)S(1)} collective-permute-done((bf16[1,128,640]{2,1,0:T(8,128)(2,1)S(1)}, bf16[1,128,640]{2,1,0:T(8,128)(2,1)S(1)}, u32[]{:S(2)}, u32[]{:S(2)}) %collective-permute-start.7) | collective-permute-done | bytes 163872 | tf_op jit(solution)/shard_map/ppermute | solution.py:75
  33.4 2.1 %collective-permute-done.4 = bf16[1,4,56,640]{3,2,1,0:T(8,128)(2,1)S(1)} collective-permute-done((bf16[1,4,56,640]{3,2,1,0:T(8,128)(2,1)S(1)}, bf16[1,4,56,640]{3,2,1,0:T(8,128)(2,1)S(1)}, u32[]{:S(2)}, u32[]{:S(2)}) %collective-permute-start.4) | collective-permute-done | bytes 286752 | tf_op jit(solution)/shard_map/ppermute | solution.py:70
  37.0 2.7 %collective-permute-start.14 = (bf16[1,32,640]{2,1,0:T(8,128)(2,1)S(1)}, bf16[1,32,640]{2,1,0:T(8,128)(2,1)S(1)}, u32[]{:S(2)}, u32[]{:S(2)}) collective-permute-start(bf16[1,32,640]{2,1,0:T(8,128)(2,1)S(1)} %bitcast.119), channel_id=1, source_target_pairs={{0,6},{1,7},{2,4},{3,5},{4,2},{5,3},{6,0},{7,1},{8,14},{9,15},{10,... | collective-permute-start | bytes 122888 | tf_op jit(solution)/shard_map/ppermute | solution.py:75
  39.8 1.8 %collective-permute-start.13 = (bf16[1,32,640]{2,1,0:T(8,128)(2,1)S(1)}, bf16[1,32,640]{2,1,0:T(8,128)(2,1)S(1)}, u32[]{:S(2)}, u32[]{:S(2)}) collective-permute-start(bf16[1,32,640]{2,1,0:T(8,128)(2,1)S(1)} %bitcast.120), channel_id=1, source_target_pairs={{0,4},{1,5},{2,6},{3,7},{4,0},{5,1},{6,2},{7,3},{8,12},{9,13},{10,... | collective-permute-start | bytes 122888 | tf_op jit(solution)/shard_map/ppermute | solution.py:75
  42.9 2.4 %collective-permute-done.13 = bf16[1,32,640]{2,1,0:T(8,128)(2,1)S(1)} collective-permute-done((bf16[1,32,640]{2,1,0:T(8,128)(2,1)S(1)}, bf16[1,32,640]{2,1,0:T(8,128)(2,1)S(1)}, u32[]{:S(2)}, u32[]{:S(2)}) %collective-permute-start.13) | collective-permute-done | bytes 40992 | tf_op jit(solution)/shard_map/ppermute | solution.py:75
  47.3 2.4 %collective-permute-start.19 = (bf16[1,4,32,640]{3,2,1,0:T(8,128)(2,1)S(1)}, bf16[1,4,32,640]{3,2,1,0:T(8,128)(2,1)S(1)}, u32[]{:S(2)}, u32[]{:S(2)}) collective-permute-start(bf16[1,4,32,640]{3,2,1,0:T(8,128)(2,1)S(1)} %bitcast.104), channel_id=1, source_target_pairs={{0,24},{8,16},{16,8},{24,0},{1,25},{9,17},{17,9},{25,1},{2,26},{10... | collective-permute-start | bytes 491528 | tf_op jit(solution)/shard_map/ppermute | solution.py:70
  50.8 1.1 collective-permute-start.16
  51.8 1.3 collective-permute-start.15
  53.7 7.7 %shard_map.186 = (bf16[1024,640]{1,0:T(8,128)(2,1)}, bf16[512,640]{1,0:T(8,128)(2,1)}, bf16[128,640]{1,0:T(8,128)(2,1)}, bf16[1024,640]{1,0:T(8,128)(2,1)}, f32[...) custom-call(f32[128,640]{1,0:T(8,128)} %get-tuple-element.253.unit_r, ...), custom_call_target="tpu_custom_call" | custom-call | flops 12000000000 | bytes 20000000 | tf_op jit(solution)/shard_map/pallas_call | solution.py:204
  61.6 1.3 collective-permute-done.16.refs_6_
  63.9 1.7 collective-permute-start.24
  65.7 1.2 shard_map.187
  66.9 2.4 %collective-permute-start.23 = (bf16[128,640]{1,0:T(8,128)(2,1)S(1)}, bf16[128,640]{1,0:T(8,128)(2,1)S(1)}, u32[]{:S(2)}, u32[]{:S(2)}) collective-permute-start(bf16[128,640]{1,0:T(8,128)(2,1)S(1)} %get-tuple-element.152.refs_0_), channel_id=1, source_target_pairs={{0,24},{8,16},{16,8},{24,0},{1,25},{9,17},{17,9},{25,1},{2,26},{10... | collective-permute-start | bytes 491528 | tf_op jit(solution)/shard_map/ppermute | solution.py:70
  70.5 3.3 %collective-permute-done.24.refs_7_ = bf16[192,640]{1,0:T(8,128)(2,1)S(1)} collective-permute-done((bf16[192,640]{1,0:T(8,128)(2,1)S(1)}, bf16[192,640]{1,0:T(8,128)(2,1)S(1)}, u32[]{:S(2)}, u32[]{:S(2)}) %collective-permute-start.24) | collective-permute-done | bytes 245792 | tf_op jit(solution)/shard_map/ppermute | solution.py:75
  73.8 1.1 collective-permute-done.23.refs_3_
  74.9 2.4 %collective-permute-done.22.refs_2_ = bf16[128,640]{1,0:T(8,128)(2,1)S(1)} collective-permute-done((bf16[128,640]{1,0:T(8,128)(2,1)S(1)}, bf16[128,640]{1,0:T(8,128)(2,1)S(1)}, u32[]{:S(2)}, u32[]{:S(2)}) %collective-permute-start.22) | collective-permute-done | bytes 163872 | tf_op jit(solution)/shard_map/ppermute | solution.py:70
  77.3 1.5 collective-permute-done.28.refs_11_
  78.8 2.7 %shard_map.188 = (f32[128,640]{1,0:T(8,128)S(1)}, bf16[128,640]{1,0:T(8,128)(2,1)S(1)}, bf16[128,640]{1,0:T(8,128)(2,1)S(1)}, bf16[128,640]{1,0:T(8,128)(2,1)S(1...) custom-call(bf16[128,640]{1,0:T(8,128)(2,1)S(1)} %get-tuple-element., ...), custom_call_target="tpu_custom_call" | custom-call | flops 3000000000 | bytes 20000000 | tf_op jit(solution)/shard_map/pallas_call | solution.py:204
  81.5 1.6 collective-permute-start.29
  83.9 1.2 collective-permute-start.31
  85.1 3.5 %collective-permute-done.29.come1_ref = bf16[128,640]{1,0:T(8,128)(2,1)S(1)} collective-permute-done((bf16[128,640]{1,0:T(8,128)(2,1)S(1)}, bf16[128,640]{1,0:T(8,128)(2,1)S(1)}, u32[]{:S(2)}, u32[]{:S(2)}) %collective-permute-start.29) | collective-permute-done | bytes 163872 | tf_op jit(solution)/shard_map/ppermute | solution.py:70
  88.6 3.9 %collective-permute-done.30.come2_ref = bf16[128,640]{1,0:T(8,128)(2,1)S(1)} collective-permute-done((bf16[128,640]{1,0:T(8,128)(2,1)S(1)}, bf16[128,640]{1,0:T(8,128)(2,1)S(1)}, u32[]{:S(2)}, u32[]{:S(2)}) %collective-permute-start.30) | collective-permute-done | bytes 163872 | tf_op jit(solution)/shard_map/ppermute | solution.py:70
  93.5 1.4 collective-permute-start.34
  95.5 1.5 collective-permute-start.32
  97.0 4.3 %collective-permute-done.34.refs_3_ = bf16[128,640]{1,0:T(8,128)(2,1)S(1)} collective-permute-done((bf16[128,640]{1,0:T(8,128)(2,1)S(1)}, bf16[128,640]{1,0:T(8,128)(2,1)S(1)}, u32[]{:S(2)}, u32[]{:S(2)}) %collective-permute-start.34) | collective-permute-done | bytes 163872 | tf_op jit(solution)/shard_map/ppermute | solution.py:70
  101.3 1.7 collective-permute-done.33.refs_2_
  103.0 2.6 %shard_map.190 = (f32[128,640]{1,0:T(8,128)S(1)}, bf16[128,640]{1,0:T(8,128)(2,1)S(1)}, bf16[128,640]{1,0:T(8,128)(2,1)S(1)}, bf16[128,640]{1,0:T(8,128)(2,1)S(1...) custom-call(bf16[128,640]{1,0:T(8,128)(2,1)S(1)} %get-tuple-element.166.refs_0_, ...), custom_call_target="tpu_custom_call" | custom-call | flops 3000000000 | bytes 20000000 | tf_op jit(solution)/shard_map/pallas_call | solution.py:204
  106.5 1.3 collective-permute-start.36
  107.8 1.4 collective-permute-start.37
  109.1 1.6 shard_map.191
  110.8 2.0 %collective-permute-done.35.come1_ref = bf16[128,640]{1,0:T(8,128)(2,1)S(1)} collective-permute-done((bf16[128,640]{1,0:T(8,128)(2,1)S(1)}, bf16[128,640]{1,0:T(8,128)(2,1)S(1)}, u32[]{:S(2)}, u32[]{:S(2)}) %collective-permute-start.35) | collective-permute-done | bytes 163872 | tf_op jit(solution)/shard_map/ppermute | solution.py:70
  112.8 2.7 %collective-permute-done.36.come2_ref = bf16[128,640]{1,0:T(8,128)(2,1)S(1)} collective-permute-done((bf16[128,640]{1,0:T(8,128)(2,1)S(1)}, bf16[128,640]{1,0:T(8,128)(2,1)S(1)}, u32[]{:S(2)}, u32[]{:S(2)}) %collective-permute-start.36) | collective-permute-done | bytes 163872 | tf_op jit(solution)/shard_map/ppermute | solution.py:70
  115.5 1.8 %shard_map.192 = (f32[128,640]{1,0:T(8,128)S(1)}, bf16[128,1024]{1,0:T(8,128)(2,1)S(1)}, bf16[16,32,640]{2,1,0:T(8,128)(2,1)S(1)}, bf16[16,32,640]{2,1,0:T(8,128...) custom-call(f32[128,640]{1,0:T(8,128)S(1)} %get-tuple-element.172.own_ref, ...), custom_call_target="tpu_custom_call" | custom-call | flops 3000000000 | bytes 20000000 | tf_op jit(solution)/shard_map/pallas_call | solution.py:204
  117.9 1.7 collective-permute-done.38
  120.8 1.2 collective-permute-start.44
  122.0 1.3 collective-permute-start.43
  124.7 2.4 %collective-permute-start.40 = (bf16[192,640]{1,0:T(8,128)(2,1)S(1)}, bf16[192,640]{1,0:T(8,128)(2,1)S(1)}, u32[]{:S(2)}, u32[]{:S(2)}) collective-permute-start(bf16[192,640]{1,0:T(8,128)(2,1)S(1)} %get-tuple-element.258), channel_id=1, source_target_pairs={{0,2},{1,3},{2,0},{3,1},{4,6},{5,7},{6,4},{7,5},{8,10},{9,11},{10,... | collective-permute-start | bytes 737288 | tf_op jit(solution)/shard_map/ppermute | solution.py:75
  127.2 9.3 %shard_map.193 = (bf16[16,48,640]{2,1,0:T(8,128)(2,1)}, bf16[16,48,640]{2,1,0:T(8,128)(2,1)}, bf16[512,512]{1,0:T(8,128)(2,1)S(1)}, bf16[512,512]{1,0:T(8,128)(2...) custom-call(bf16[128,1024]{1,0:T(8,128)(2,1)S(1)} %get-tuple-element.194.g, ...), custom_call_target="tpu_custom_call" | custom-call | flops 12000000000 | bytes 20000000 | tf_op jit(solution)/shard_map/pallas_call | solution.py:204
  138.9 1.8 collective-permute-start.48
  140.6 1.2 fusion.4
  142.4 4.0 %collective-permute-done.48.refs_8_ = bf16[96,640]{1,0:T(8,128)(2,1)S(1)} collective-permute-done((bf16[96,640]{1,0:T(8,128)(2,1)S(1)}, bf16[96,640]{1,0:T(8,128)(2,1)S(1)}, u32[]{:S(2)}, u32[]{:S(2)}) %collective-permute-start.48) | collective-permute-done | bytes 122912 | tf_op jit(solution)/shard_map/ppermute | solution.py:75
  146.5 2.6 %collective-permute-start.54 = (bf16[128,512]{1,0:T(8,128)(2,1)S(1)}, bf16[128,512]{1,0:T(8,128)(2,1)S(1)}, u32[]{:S(2)}, u32[]{:S(2)}) collective-permute-start(bf16[128,512]{1,0:T(8,128)(2,1)S(1)} %get-tuple-element.263), channel_id=1, source_target_pairs={{0,6},{1,7},{2,4},{3,5},{4,2},{5,3},{6,0},{7,1},{8,14},{9,15},{10,... | collective-permute-start | bytes 393224 | tf_op jit(solution)/shard_map/ppermute | solution.py:75
  150.1 1.3 collective-permute-start.49
  151.4 1.4 collective-permute-start.51
  153.7 2.5 %collective-permute-done.54 = bf16[128,512]{1,0:T(8,128)(2,1)S(1)} collective-permute-done((bf16[128,512]{1,0:T(8,128)(2,1)S(1)}, bf16[128,512]{1,0:T(8,128)(2,1)S(1)}, u32[]{:S(2)}, u32[]{:S(2)}) %collective-permute-start.54) | collective-permute-done | bytes 131104 | tf_op jit(solution)/shard_map/ppermute | solution.py:75
  156.2 4.9 %collective-permute-done.53 = bf16[128,512]{1,0:T(8,128)(2,1)S(1)} collective-permute-done((bf16[128,512]{1,0:T(8,128)(2,1)S(1)}, bf16[128,512]{1,0:T(8,128)(2,1)S(1)}, u32[]{:S(2)}, u32[]{:S(2)}) %collective-permute-start.53) | collective-permute-done | bytes 131104 | tf_op jit(solution)/shard_map/ppermute | solution.py:75
  161.2 3.3 %collective-permute-done.51 = bf16[4,56,640]{2,1,0:T(8,128)(2,1)S(1)} collective-permute-done((bf16[4,56,640]{2,1,0:T(8,128)(2,1)S(1)}, bf16[4,56,640]{2,1,0:T(8,128)(2,1)S(1)}, u32[]{:S(2)}, u32[]{:S(2)}) %collective-permute-start.51) | collective-permute-done | bytes 286752 | tf_op jit(solution)/shard_map/ppermute | solution.py:70
  164.6 1.4 collective-permute-done.50
  166.6 1.3 collective-permute-start.55
  167.9 1.2 collective-permute-start.56
  169.1 2.1 %collective-permute-start.57 = (bf16[184,640]{1,0:T(8,128)(2,1)S(1)}, bf16[184,640]{1,0:T(8,128)(2,1)S(1)}, u32[]{:S(2)}, u32[]{:S(2)}) collective-permute-start(bf16[184,640]{1,0:T(8,128)(2,1)S(1)} %pad_maximum_fusion.5), channel_id=1, source_target_pairs={{0,6},{1,7},{2,4},{3,5},{4,2},{5,3},{6,0},{7,1},{8,14},{9,15},{10,... | collective-permute-start | bytes 706568 | tf_op jit(solution)/shard_map/ppermute | solution.py:75
  172.1 2.2 %collective-permute-done.55.refs_2_ = bf16[88,640]{1,0:T(8,128)(2,1)S(1)} collective-permute-done((bf16[88,640]{1,0:T(8,128)(2,1)S(1)}, bf16[88,640]{1,0:T(8,128)(2,1)S(1)}, u32[]{:S(2)}, u32[]{:S(2)}) %collective-permute-start.55) | collective-permute-done | bytes 112672 | tf_op jit(solution)/shard_map/ppermute | solution.py:75
  174.3 4.4 %collective-permute-done.56.refs_3_ = bf16[88,640]{1,0:T(8,128)(2,1)S(1)} collective-permute-done((bf16[88,640]{1,0:T(8,128)(2,1)S(1)}, bf16[88,640]{1,0:T(8,128)(2,1)S(1)}, u32[]{:S(2)}, u32[]{:S(2)}) %collective-permute-start.56) | collective-permute-done | bytes 112672 | tf_op jit(solution)/shard_map/ppermute | solution.py:75
  (202 shorter events, 26.5 us)
Async XLA Ops:
  0.6 13.4 %copy-start.27 = (bf16[64,640]{1,0:T(8,128)(2,1)S(1)}, bf16[64,640]{1,0:T(8,128)(2,1)}, u32[]{:S(2)}) copy-start(bf16[64,640]{1,0:T(8,128)(2,1)} %param.19) | copy-start | bytes 245764
  0.7 13.4 %copy-start.28 = (bf16[64,640]{1,0:T(8,128)(2,1)S(1)}, bf16[64,640]{1,0:T(8,128)(2,1)}, u32[]{:S(2)}) copy-start(bf16[64,640]{1,0:T(8,128)(2,1)} %param.18) | copy-start | bytes 245764
  4.3 9.8 %collective-permute-start.2 = (bf16[1,56,640]{2,1,0:T(8,128)(2,1)S(1)}, bf16[1,56,640]{2,1,0:T(8,128)(2,1)S(1)}, u32[]{:S(2)}, u32[]{:S(2)}) collective-permute-start(bf16[1,56,640]{2,1,0:T(8,128)(2,1)S(1)} %bitcast.115), channel_id=1, source_target_pairs={{0,6},{1,7},{2,4},{3,5},{4,2},{5,3},{6,0},{7,1},{8,14},{9,15},{10,... | collective-permute-start | bytes 215048 | tf_op jit(solution)/shard_map/ppermute | solution.py:75
  9.4 6.1 %collective-permute-start.1 = (bf16[1,56,640]{2,1,0:T(8,128)(2,1)S(1)}, bf16[1,56,640]{2,1,0:T(8,128)(2,1)S(1)}, u32[]{:S(2)}, u32[]{:S(2)}) collective-permute-start(bf16[1,56,640]{2,1,0:T(8,128)(2,1)S(1)} %bitcast.116), channel_id=1, source_target_pairs={{0,4},{1,5},{2,6},{3,7},{4,0},{5,1},{6,2},{7,3},{8,12},{9,13},{10,... | collective-permute-start | bytes 215048 | tf_op jit(solution)/shard_map/ppermute | solution.py:75
  9.4 6.1 %collective-permute-start = (bf16[1,56,640]{2,1,0:T(8,128)(2,1)S(1)}, bf16[1,56,640]{2,1,0:T(8,128)(2,1)S(1)}, u32[]{:S(2)}, u32[]{:S(2)}) collective-permute-start(bf16[1,56,640]{2,1,0:T(8,128)(2,1)S(1)} %bitcast.117), channel_id=1, source_target_pairs={{0,2},{1,3},{2,0},{3,1},{4,6},{5,7},{6,4},{7,5},{8,10},{9,11},{10,... | collective-permute-start | bytes 215048 | tf_op jit(solution)/shard_map/ppermute | solution.py:75
  11.2 34.5 %copy-start.7 = (s32[32]{0:T(128)}, s32[32]{0:T(128)S(1)}, u32[]{:S(2)}) copy-start(s32[32]{0:T(128)S(1)} %get-tuple-element.251.owner_ref) | copy-start | bytes 388
  15.6 7.0 %collective-permute-start.9 = (bf16[4,8,640]{2,1,0:T(8,128)(2,1)S(1)}, bf16[4,8,640]{2,1,0:T(8,128)(2,1)S(1)}, u32[]{:S(2)}, u32[]{:S(2)}) collective-permute-start(bf16[4,8,640]{2,1,0:T(8,128)(2,1)S(1)} %get-tuple-element.270), channel_id=1, source_target_pairs={{0,1},{1,0},{2,3},{3,2},{4,5},{5,4},{6,7},{7,6},{8,9},{9,8},{10,11... | collective-permute-start | bytes 122888 | tf_op jit(solution)/shard_map/ppermute | solution.py:75
  15.6 9.0 %collective-permute-start.8 = (bf16[1,128,640]{2,1,0:T(8,128)(2,1)S(1)}, bf16[1,128,640]{2,1,0:T(8,128)(2,1)S(1)}, u32[]{:S(2)}, u32[]{:S(2)}) collective-permute-start(bf16[1,128,640]{2,1,0:T(8,128)(2,1)S(1)} %bitcast.111), channel_id=1, source_target_pairs={{0,6},{1,7},{2,4},{3,5},{4,2},{5,3},{6,0},{7,1},{8,14},{9,15},{10,... | collective-permute-start | bytes 491528 | tf_op jit(solution)/shard_map/ppermute | solution.py:75
  18.4 14.8 %collective-permute-start.7 = (bf16[1,128,640]{2,1,0:T(8,128)(2,1)S(1)}, bf16[1,128,640]{2,1,0:T(8,128)(2,1)S(1)}, u32[]{:S(2)}, u32[]{:S(2)}) collective-permute-start(bf16[1,128,640]{2,1,0:T(8,128)(2,1)S(1)} %bitcast.112), channel_id=1, source_target_pairs={{0,4},{1,5},{2,6},{3,7},{4,0},{5,1},{6,2},{7,3},{8,12},{9,13},{10,... | collective-permute-start | bytes 491528 | tf_op jit(solution)/shard_map/ppermute | solution.py:75
  18.4 14.8 %collective-permute-start.6 = (bf16[1,128,640]{2,1,0:T(8,128)(2,1)S(1)}, bf16[1,128,640]{2,1,0:T(8,128)(2,1)S(1)}, u32[]{:S(2)}, u32[]{:S(2)}) collective-permute-start(bf16[1,128,640]{2,1,0:T(8,128)(2,1)S(1)} %bitcast.113), channel_id=1, source_target_pairs={{0,2},{1,3},{2,0},{3,1},{4,6},{5,7},{6,4},{7,5},{8,10},{9,11},{10,... | collective-permute-start | bytes 491528 | tf_op jit(solution)/shard_map/ppermute | solution.py:75
  20.1 13.3 %collective-permute-start.5 = (bf16[1,4,56,640]{3,2,1,0:T(8,128)(2,1)S(1)}, bf16[1,4,56,640]{3,2,1,0:T(8,128)(2,1)S(1)}, u32[]{:S(2)}, u32[]{:S(2)}) collective-permute-start(bf16[1,4,56,640]{3,2,1,0:T(8,128)(2,1)S(1)} %bitcast.97), channel_id=1, source_target_pairs={{0,24},{8,16},{16,8},{24,0},{1,25},{9,17},{17,9},{25,1},{2,26},{10... | collective-permute-start | bytes 860168 | tf_op jit(solution)/shard_map/ppermute | solution.py:70
  22.6 12.9 %collective-permute-start.4 = (bf16[1,4,56,640]{3,2,1,0:T(8,128)(2,1)S(1)}, bf16[1,4,56,640]{3,2,1,0:T(8,128)(2,1)S(1)}, u32[]{:S(2)}, u32[]{:S(2)}) collective-permute-start(bf16[1,4,56,640]{3,2,1,0:T(8,128)(2,1)S(1)} %bitcast.98), channel_id=1, source_target_pairs={{0,16},{8,24},{16,0},{24,8},{1,17},{9,25},{17,1},{25,9},{2,18},{10... | collective-permute-start | bytes 860168 | tf_op jit(solution)/shard_map/ppermute | solution.py:70
  24.6 10.9 %collective-permute-start.3 = (bf16[1,4,56,640]{3,2,1,0:T(8,128)(2,1)S(1)}, bf16[1,4,56,640]{3,2,1,0:T(8,128)(2,1)S(1)}, u32[]{:S(2)}, u32[]{:S(2)}) collective-permute-start(bf16[1,4,56,640]{3,2,1,0:T(8,128)(2,1)S(1)} %bitcast.99), channel_id=1, source_target_pairs={{0,8},{8,0},{16,24},{24,16},{1,9},{9,1},{17,25},{25,17},{2,10},{10... | collective-permute-start | bytes 860168 | tf_op jit(solution)/shard_map/ppermute | solution.py:70
  35.8 17.9 %copy-start.20 = (bf16[4,4,56,640]{3,2,1,0:T(8,128)(2,1)}, bf16[4,4,56,640]{3,2,1,0:T(8,128)(2,1)S(1)}, u32[]{:S(2)}) copy-start(bf16[4,4,56,640]{3,2,1,0:T(8,128)(2,1)S(1)} %pad_maximum_fusion) | copy-start | bytes 3440644
  35.8 9.9 %collective-permute-start.10 = (bf16[16,56,640]{2,1,0:T(8,128)(2,1)S(1)}, bf16[16,56,640]{2,1,0:T(8,128)(2,1)S(1)}, u32[]{:S(2)}, u32[]{:S(2)}) collective-permute-start(bf16[16,56,640]{2,1,0:T(8,128)(2,1)S(1)} %bitcast.101), channel_id=1, source_target_pairs={{0,1},{1,0},{2,3},{3,2},{4,5},{5,4},{6,7},{7,6},{8,9},{9,8},{10,11... | collective-permute-start | bytes 3440648 | tf_op jit(solution)/shard_map/ppermute | solution.py:75
  35.9 9.8 %collective-permute-start.11 = (bf16[512,640]{1,0:T(8,128)(2,1)S(1)}, bf16[512,640]{1,0:T(8,128)(2,1)S(1)}, u32[]{:S(2)}, u32[]{:S(2)}) collective-permute-start(bf16[512,640]{1,0:T(8,128)(2,1)S(1)} %bitcast.108), channel_id=1, source_target_pairs={{0,1},{1,0},{2,3},{3,2},{4,5},{5,4},{6,7},{7,6},{8,9},{9,8},{10,11... | collective-permute-start | bytes 1966088 | tf_op jit(solution)/shard_map/ppermute | solution.py:75
  37.0 5.9 %collective-permute-start.14 = (bf16[1,32,640]{2,1,0:T(8,128)(2,1)S(1)}, bf16[1,32,640]{2,1,0:T(8,128)(2,1)S(1)}, u32[]{:S(2)}, u32[]{:S(2)}) collective-permute-start(bf16[1,32,640]{2,1,0:T(8,128)(2,1)S(1)} %bitcast.119), channel_id=1, source_target_pairs={{0,6},{1,7},{2,4},{3,5},{4,2},{5,3},{6,0},{7,1},{8,14},{9,15},{10,... | collective-permute-start | bytes 122888 | tf_op jit(solution)/shard_map/ppermute | solution.py:75
  39.8 5.6 %collective-permute-start.13 = (bf16[1,32,640]{2,1,0:T(8,128)(2,1)S(1)}, bf16[1,32,640]{2,1,0:T(8,128)(2,1)S(1)}, u32[]{:S(2)}, u32[]{:S(2)}) collective-permute-start(bf16[1,32,640]{2,1,0:T(8,128)(2,1)S(1)} %bitcast.120), channel_id=1, source_target_pairs={{0,4},{1,5},{2,6},{3,7},{4,0},{5,1},{6,2},{7,3},{8,12},{9,13},{10,... | collective-permute-start | bytes 122888 | tf_op jit(solution)/shard_map/ppermute | solution.py:75
  41.6 4.0 %collective-permute-start.12 = (bf16[1,32,640]{2,1,0:T(8,128)(2,1)S(1)}, bf16[1,32,640]{2,1,0:T(8,128)(2,1)S(1)}, u32[]{:S(2)}, u32[]{:S(2)}) collective-permute-start(bf16[1,32,640]{2,1,0:T(8,128)(2,1)S(1)} %bitcast.121), channel_id=1, source_target_pairs={{0,2},{1,3},{2,0},{3,1},{4,6},{5,7},{6,4},{7,5},{8,10},{9,11},{10,... | collective-permute-start | bytes 122888 | tf_op jit(solution)/shard_map/ppermute | solution.py:75
  47.3 14.2 %collective-permute-start.19 = (bf16[1,4,32,640]{3,2,1,0:T(8,128)(2,1)S(1)}, bf16[1,4,32,640]{3,2,1,0:T(8,128)(2,1)S(1)}, u32[]{:S(2)}, u32[]{:S(2)}) collective-permute-start(bf16[1,4,32,640]{3,2,1,0:T(8,128)(2,1)S(1)} %bitcast.104), channel_id=1, source_target_pairs={{0,24},{8,16},{16,8},{24,0},{1,25},{9,17},{17,9},{25,1},{2,26},{10... | collective-permute-start | bytes 491528 | tf_op jit(solution)/shard_map/ppermute | solution.py:70
  49.7 11.8 %collective-permute-start.18 = (bf16[1,4,32,640]{3,2,1,0:T(8,128)(2,1)S(1)}, bf16[1,4,32,640]{3,2,1,0:T(8,128)(2,1)S(1)}, u32[]{:S(2)}, u32[]{:S(2)}) collective-permute-start(bf16[1,4,32,640]{3,2,1,0:T(8,128)(2,1)S(1)} %bitcast.105), channel_id=1, source_target_pairs={{0,16},{8,24},{16,0},{24,8},{1,17},{9,25},{17,1},{25,9},{2,18},{10... | collective-permute-start | bytes 491528 | tf_op jit(solution)/shard_map/ppermute | solution.py:70
  50.2 11.3 %collective-permute-start.17 = (bf16[1,4,32,640]{3,2,1,0:T(8,128)(2,1)S(1)}, bf16[1,4,32,640]{3,2,1,0:T(8,128)(2,1)S(1)}, u32[]{:S(2)}, u32[]{:S(2)}) collective-permute-start(bf16[1,4,32,640]{3,2,1,0:T(8,128)(2,1)S(1)} %bitcast.106), channel_id=1, source_target_pairs={{0,8},{8,0},{16,24},{24,16},{1,9},{9,1},{17,25},{25,17},{2,10},{10... | collective-permute-start | bytes 491528 | tf_op jit(solution)/shard_map/ppermute | solution.py:70
  50.8 12.1 %collective-permute-start.16 = (bf16[192,640]{1,0:T(8,128)(2,1)S(1)}, bf16[192,640]{1,0:T(8,128)(2,1)S(1)}, u32[]{:S(2)}, u32[]{:S(2)}) collective-permute-start(bf16[192,640]{1,0:T(8,128)(2,1)S(1)} %pad_maximum_fusion.4.refs_4_), channel_id=1, source_target_pairs={{0,4},{1,5},{2,6},{3,7},{4,0},{5,1},{6,2},{7,3},{8,12},{9,13},{10,... | collective-permute-start | bytes 737288 | tf_op jit(solution)/shard_map/ppermute | solution.py:75
  51.8 11.0 %collective-permute-start.15 = (bf16[192,640]{1,0:T(8,128)(2,1)S(1)}, bf16[192,640]{1,0:T(8,128)(2,1)S(1)}, u32[]{:S(2)}, u32[]{:S(2)}) collective-permute-start(bf16[192,640]{1,0:T(8,128)(2,1)S(1)} %pad_maximum_fusion.4.refs_4_), channel_id=1, source_target_pairs={{0,2},{1,3},{2,0},{3,1},{4,6},{5,7},{6,4},{7,5},{8,10},{9,11},{10,... | collective-permute-start | bytes 737288 | tf_op jit(solution)/shard_map/ppermute | solution.py:75
  62.9 2.7 %collective-permute-start.20 = (bf16[16,32,640]{2,1,0:T(8,128)(2,1)S(1)}, bf16[16,32,640]{2,1,0:T(8,128)(2,1)S(1)}, u32[]{:S(2)}, u32[]{:S(2)}) collective-permute-start(bf16[16,32,640]{2,1,0:T(8,128)(2,1)S(1)} %bitcast.83), channel_id=1, source_target_pairs={{0,1},{1,0},{2,3},{3,2},{4,5},{5,4},{6,7},{7,6},{8,9},{9,8},{10,11... | collective-permute-start | bytes 1966088 | tf_op jit(solution)/shard_map/ppermute | solution.py:75
  62.9 6.4 %collective-permute-start.26 = (bf16[192,640]{1,0:T(8,128)(2,1)S(1)}, bf16[192,640]{1,0:T(8,128)(2,1)S(1)}, u32[]{:S(2)}, u32[]{:S(2)}) collective-permute-start(bf16[192,640]{1,0:T(8,128)(2,1)S(1)} %collective-permute-done.15.refs_5_), channel_id=1, source_target_pairs={{0,1},{1,0},{2,3},{3,2},{4,5},{5,4},{6,7},{7,6},{8,9},{9,8},{10,11... | collective-permute-start | bytes 737288 | tf_op jit(solution)/shard_map/ppermute | solution.py:75
  63.4 6.5 %collective-permute-start.27 = (bf16[192,640]{1,0:T(8,128)(2,1)S(1)}, bf16[192,640]{1,0:T(8,128)(2,1)S(1)}, u32[]{:S(2)}, u32[]{:S(2)}) collective-permute-start(bf16[192,640]{1,0:T(8,128)(2,1)S(1)} %collective-permute-done.16.refs_6_), channel_id=1, source_target_pairs={{0,1},{1,0},{2,3},{3,2},{4,5},{5,4},{6,7},{7,6},{8,9},{9,8},{10,11... | collective-permute-start | bytes 737288 | tf_op jit(solution)/shard_map/ppermute | solution.py:75
  63.4 7.1 %collective-permute-start.25 = (bf16[192,640]{1,0:T(8,128)(2,1)S(1)}, bf16[192,640]{1,0:T(8,128)(2,1)S(1)}, u32[]{:S(2)}, u32[]{:S(2)}) collective-permute-start(bf16[192,640]{1,0:T(8,128)(2,1)S(1)} %pad_maximum_fusion.4.refs_4_), channel_id=1, source_target_pairs={{0,1},{1,0},{2,3},{3,2},{4,5},{5,4},{6,7},{7,6},{8,9},{9,8},{10,11... | collective-permute-start | bytes 737288 | tf_op jit(solution)/shard_map/ppermute | solution.py:75
  63.9 9.8 %collective-permute-start.24 = (bf16[192,640]{1,0:T(8,128)(2,1)S(1)}, bf16[192,640]{1,0:T(8,128)(2,1)S(1)}, u32[]{:S(2)}, u32[]{:S(2)}) collective-permute-start(bf16[192,640]{1,0:T(8,128)(2,1)S(1)} %pad_maximum_fusion.4.refs_4_), channel_id=1, source_target_pairs={{0,6},{1,7},{2,4},{3,5},{4,2},{5,3},{6,0},{7,1},{8,14},{9,15},{10,... | collective-permute-start | bytes 737288 | tf_op jit(solution)/shard_map/ppermute | solution.py:75
  66.9 25.7 %copy-start.5 = (f32[1,128,640]{2,1,0:T(8,128)S(1)}, f32[1,128,640]{2,1,0:T(8,128)}, u32[]{:S(2)}) copy-start(f32[1,128,640]{2,1,0:T(8,128)} %param.21) | copy-start | bytes 983044
  66.9 8.0 %collective-permute-start.23 = (bf16[128,640]{1,0:T(8,128)(2,1)S(1)}, bf16[128,640]{1,0:T(8,128)(2,1)S(1)}, u32[]{:S(2)}, u32[]{:S(2)}) collective-permute-start(bf16[128,640]{1,0:T(8,128)(2,1)S(1)} %get-tuple-element.152.refs_0_), channel_id=1, source_target_pairs={{0,24},{8,16},{16,8},{24,0},{1,25},{9,17},{17,9},{25,1},{2,26},{10... | collective-permute-start | bytes 491528 | tf_op jit(solution)/shard_map/ppermute | solution.py:70
  69.3 7.9 %collective-permute-start.22 = (bf16[128,640]{1,0:T(8,128)(2,1)S(1)}, bf16[128,640]{1,0:T(8,128)(2,1)S(1)}, u32[]{:S(2)}, u32[]{:S(2)}) collective-permute-start(bf16[128,640]{1,0:T(8,128)(2,1)S(1)} %get-tuple-element.152.refs_0_), channel_id=1, source_target_pairs={{0,16},{8,24},{16,0},{24,8},{1,17},{9,25},{17,1},{25,9},{2,18},{10... | collective-permute-start | bytes 491528 | tf_op jit(solution)/shard_map/ppermute | solution.py:70
  69.9 7.4 %collective-permute-start.21 = (bf16[128,640]{1,0:T(8,128)(2,1)S(1)}, bf16[128,640]{1,0:T(8,128)(2,1)S(1)}, u32[]{:S(2)}, u32[]{:S(2)}) collective-permute-start(bf16[128,640]{1,0:T(8,128)(2,1)S(1)} %get-tuple-element.152.refs_0_), channel_id=1, source_target_pairs={{0,8},{8,0},{16,24},{24,16},{1,9},{9,1},{17,25},{25,17},{2,10},{10... | collective-permute-start | bytes 491528 | tf_op jit(solution)/shard_map/ppermute | solution.py:70
  77.3 1.5 collective-permute-start.28
  81.5 7.1 %collective-permute-start.29 = (bf16[128,640]{1,0:T(8,128)(2,1)S(1)}, bf16[128,640]{1,0:T(8,128)(2,1)S(1)}, u32[]{:S(2)}, u32[]{:S(2)}) collective-permute-start(bf16[128,640]{1,0:T(8,128)(2,1)S(1)} %get-tuple-element.161), channel_id=1, source_target_pairs={{0,8},{8,0},{16,24},{24,16},{1,9},{9,1},{17,25},{25,17},{2,10},{10... | collective-permute-start | bytes 491528 | tf_op jit(solution)/shard_map/ppermute | solution.py:70
  83.1 9.5 %collective-permute-start.30 = (bf16[128,640]{1,0:T(8,128)(2,1)S(1)}, bf16[128,640]{1,0:T(8,128)(2,1)S(1)}, u32[]{:S(2)}, u32[]{:S(2)}) collective-permute-start(bf16[128,640]{1,0:T(8,128)(2,1)S(1)} %get-tuple-element.162), channel_id=1, source_target_pairs={{0,16},{8,24},{16,0},{24,8},{1,17},{9,25},{17,1},{25,9},{2,18},{10... | collective-permute-start | bytes 491528 | tf_op jit(solution)/shard_map/ppermute | solution.py:70
  83.9 8.7 %collective-permute-start.31 = (bf16[128,640]{1,0:T(8,128)(2,1)S(1)}, bf16[128,640]{1,0:T(8,128)(2,1)S(1)}, u32[]{:S(2)}, u32[]{:S(2)}) collective-permute-start(bf16[128,640]{1,0:T(8,128)(2,1)S(1)} %get-tuple-element.163), channel_id=1, source_target_pairs={{0,24},{8,16},{16,8},{24,0},{1,25},{9,17},{17,9},{25,1},{2,26},{10... | collective-permute-start | bytes 491528 | tf_op jit(solution)/shard_map/ppermute | solution.py:70
  93.5 7.8 %collective-permute-start.34 = (bf16[128,640]{1,0:T(8,128)(2,1)S(1)}, bf16[128,640]{1,0:T(8,128)(2,1)S(1)}, u32[]{:S(2)}, u32[]{:S(2)}) collective-permute-start(bf16[128,640]{1,0:T(8,128)(2,1)S(1)} %get-tuple-element.166.refs_0_), channel_id=1, source_target_pairs={{0,24},{8,16},{16,8},{24,0},{1,25},{9,17},{17,9},{25,1},{2,26},{10... | collective-permute-start | bytes 491528 | tf_op jit(solution)/shard_map/ppermute | solution.py:70
  94.9 8.1 %collective-permute-start.33 = (bf16[128,640]{1,0:T(8,128)(2,1)S(1)}, bf16[128,640]{1,0:T(8,128)(2,1)S(1)}, u32[]{:S(2)}, u32[]{:S(2)}) collective-permute-start(bf16[128,640]{1,0:T(8,128)(2,1)S(1)} %get-tuple-element.166.refs_0_), channel_id=1, source_target_pairs={{0,16},{8,24},{16,0},{24,8},{1,17},{9,25},{17,1},{25,9},{2,18},{10... | collective-permute-start | bytes 491528 | tf_op jit(solution)/shard_map/ppermute | solution.py:70
  95.5 7.5 %collective-permute-start.32 = (bf16[128,640]{1,0:T(8,128)(2,1)S(1)}, bf16[128,640]{1,0:T(8,128)(2,1)S(1)}, u32[]{:S(2)}, u32[]{:S(2)}) collective-permute-start(bf16[128,640]{1,0:T(8,128)(2,1)S(1)} %get-tuple-element.166.refs_0_), channel_id=1, source_target_pairs={{0,8},{8,0},{16,24},{24,16},{1,9},{9,1},{17,25},{25,17},{2,10},{10... | collective-permute-start | bytes 491528 | tf_op jit(solution)/shard_map/ppermute | solution.py:70
  105.6 7.2 %collective-permute-start.35 = (bf16[128,640]{1,0:T(8,128)(2,1)S(1)}, bf16[128,640]{1,0:T(8,128)(2,1)S(1)}, u32[]{:S(2)}, u32[]{:S(2)}) collective-permute-start(bf16[128,640]{1,0:T(8,128)(2,1)S(1)} %get-tuple-element.180), channel_id=1, source_target_pairs={{0,8},{8,0},{16,24},{24,16},{1,9},{9,1},{17,25},{25,17},{2,10},{10... | collective-permute-start | bytes 491528 | tf_op jit(solution)/shard_map/ppermute | solution.py:70
  106.5 9.0 %collective-permute-start.36 = (bf16[128,640]{1,0:T(8,128)(2,1)S(1)}, bf16[128,640]{1,0:T(8,128)(2,1)S(1)}, u32[]{:S(2)}, u32[]{:S(2)}) collective-permute-start(bf16[128,640]{1,0:T(8,128)(2,1)S(1)} %get-tuple-element.181), channel_id=1, source_target_pairs={{0,16},{8,24},{16,0},{24,8},{1,17},{9,25},{17,1},{25,9},{2,18},{10... | collective-permute-start | bytes 491528 | tf_op jit(solution)/shard_map/ppermute | solution.py:70
  107.8 7.7 %collective-permute-start.37 = (bf16[128,640]{1,0:T(8,128)(2,1)S(1)}, bf16[128,640]{1,0:T(8,128)(2,1)S(1)}, u32[]{:S(2)}, u32[]{:S(2)}) collective-permute-start(bf16[128,640]{1,0:T(8,128)(2,1)S(1)} %get-tuple-element.182), channel_id=1, source_target_pairs={{0,24},{8,16},{16,8},{24,0},{1,25},{9,17},{17,9},{25,1},{2,26},{10... | collective-permute-start | bytes 491528 | tf_op jit(solution)/shard_map/ppermute | solution.py:70
  115.5 4.3 %collective-permute-start.39 = (bf16[4,192,640]{2,1,0:T(8,128)(2,1)S(1)}, bf16[4,192,640]{2,1,0:T(8,128)(2,1)S(1)}, u32[]{:S(2)}, u32[]{:S(2)}) collective-permute-start(bf16[4,192,640]{2,1,0:T(8,128)(2,1)S(1)} %get-tuple-element.192), channel_id=1, source_target_pairs={{0,1},{1,0},{2,3},{3,2},{4,5},{5,4},{6,7},{7,6},{8,9},{9,8},{10,11... | collective-permute-start | bytes 2949128 | tf_op jit(solution)/shard_map/ppermute | solution.py:75
  117.4 2.3 %collective-permute-start.38 = (bf16[16,32,640]{2,1,0:T(8,128)(2,1)S(1)}, bf16[16,32,640]{2,1,0:T(8,128)(2,1)S(1)}, u32[]{:S(2)}, u32[]{:S(2)}) collective-permute-start(bf16[16,32,640]{2,1,0:T(8,128)(2,1)S(1)} %get-tuple-element.190), channel_id=1, source_target_pairs={{0,1},{1,0},{2,3},{3,2},{4,5},{5,4},{6,7},{7,6},{8,9},{9,8},{10,11... | collective-permute-start | bytes 1966088 | tf_op jit(solution)/shard_map/ppermute | solution.py:75
  120.8 15.8 %collective-permute-start.44 = (bf16[4,32,640]{2,1,0:T(8,128)(2,1)S(1)}, bf16[4,32,640]{2,1,0:T(8,128)(2,1)S(1)}, u32[]{:S(2)}, u32[]{:S(2)}) collective-permute-start(bf16[4,32,640]{2,1,0:T(8,128)(2,1)S(1)} %get-tuple-element.259), channel_id=1, source_target_pairs={{0,24},{8,16},{16,8},{24,0},{1,25},{9,17},{17,9},{25,1},{2,26},{10... | collective-permute-start | bytes 491528 | tf_op jit(solution)/shard_map/ppermute | solution.py:70
  122.0 14.6 %collective-permute-start.43 = (bf16[4,32,640]{2,1,0:T(8,128)(2,1)S(1)}, bf16[4,32,640]{2,1,0:T(8,128)(2,1)S(1)}, u32[]{:S(2)}, u32[]{:S(2)}) collective-permute-start(bf16[4,32,640]{2,1,0:T(8,128)(2,1)S(1)} %get-tuple-element.260), channel_id=1, source_target_pairs={{0,16},{8,24},{16,0},{24,8},{1,17},{9,25},{17,1},{25,9},{2,18},{10... | collective-permute-start | bytes 491528 | tf_op jit(solution)/shard_map/ppermute | solution.py:70
  123.4 13.2 %collective-permute-start.42 = (bf16[4,32,640]{2,1,0:T(8,128)(2,1)S(1)}, bf16[4,32,640]{2,1,0:T(8,128)(2,1)S(1)}, u32[]{:S(2)}, u32[]{:S(2)}) collective-permute-start(bf16[4,32,640]{2,1,0:T(8,128)(2,1)S(1)} %get-tuple-element.261), channel_id=1, source_target_pairs={{0,8},{8,0},{16,24},{24,16},{1,9},{9,1},{17,25},{25,17},{2,10},{10... | collective-permute-start | bytes 491528 | tf_op jit(solution)/shard_map/ppermute | solution.py:70
  124.4 13.2 %collective-permute-start.41 = (bf16[192,640]{1,0:T(8,128)(2,1)S(1)}, bf16[192,640]{1,0:T(8,128)(2,1)S(1)}, u32[]{:S(2)}, u32[]{:S(2)}) collective-permute-start(bf16[192,640]{1,0:T(8,128)(2,1)S(1)} %get-tuple-element.257), channel_id=1, source_target_pairs={{0,4},{1,5},{2,6},{3,7},{4,0},{5,1},{6,2},{7,3},{8,12},{9,13},{10,... | collective-permute-start | bytes 737288 | tf_op jit(solution)/shard_map/ppermute | solution.py:75
  124.7 13.0 %collective-permute-start.40 = (bf16[192,640]{1,0:T(8,128)(2,1)S(1)}, bf16[192,640]{1,0:T(8,128)(2,1)S(1)}, u32[]{:S(2)}, u32[]{:S(2)}) collective-permute-start(bf16[192,640]{1,0:T(8,128)(2,1)S(1)} %get-tuple-element.258), channel_id=1, source_target_pairs={{0,2},{1,3},{2,0},{3,1},{4,6},{5,7},{6,4},{7,5},{8,10},{9,11},{10,... | collective-permute-start | bytes 737288 | tf_op jit(solution)/shard_map/ppermute | solution.py:75
  138.0 4.1 %collective-permute-start.45 = (bf16[16,48,640]{2,1,0:T(8,128)(2,1)}, bf16[16,48,640]{2,1,0:T(8,128)(2,1)S(1)}, u32[]{:S(2)}, u32[]{:S(2)}) collective-permute-start(bf16[16,48,640]{2,1,0:T(8,128)(2,1)} %get-tuple-element.216), channel_id=1, source_target_pairs={{0,1},{1,0},{2,3},{3,2},{4,5},{5,4},{6,7},{7,6},{8,9},{9,8},{10,11... | collective-permute-start | bytes 2949128 | tf_op jit(solution)/shard_map/ppermute | solution.py:75
  138.2 3.7 %collective-permute-start.46 = (bf16[16,96]{1,0:T(8,128)(2,1)S(1)}, bf16[16,96]{1,0:T(8,128)(2,1)S(1)}, u32[]{:S(2)}, u32[]{:S(2)}) collective-permute-start(bf16[16,96]{1,0:T(8,128)(2,1)S(1)} %slice.172), channel_id=1, source_target_pairs={{0,1},{1,0},{2,3},{3,2},{4,5},{5,4},{6,7},{7,6},{8,9},{9,8},{10,11... | collective-permute-start | bytes 9224 | tf_op jit(solution)/shard_map/ppermute | solution.py:75
  138.8 3.1 %collective-permute-start.47 = (bf16[512,512]{1,0:T(8,128)(2,1)S(1)}, bf16[512,512]{1,0:T(8,128)(2,1)S(1)}, u32[]{:S(2)}, u32[]{:S(2)}) collective-permute-start(bf16[512,512]{1,0:T(8,128)(2,1)S(1)} %get-tuple-element.224), channel_id=1, source_target_pairs={{0,1},{1,0},{2,3},{3,2},{4,5},{5,4},{6,7},{7,6},{8,9},{9,8},{10,11... | collective-permute-start | bytes 1572872 | tf_op jit(solution)/shard_map/ppermute | solution.py:75
  138.9 7.5 %collective-permute-start.48 = (bf16[96,640]{1,0:T(8,128)(2,1)S(1)}, bf16[96,640]{1,0:T(8,128)(2,1)S(1)}, u32[]{:S(2)}, u32[]{:S(2)}) collective-permute-start(bf16[96,640]{1,0:T(8,128)(2,1)S(1)} %slice_bitcast_fusion.10), channel_id=1, source_target_pairs={{0,6},{1,7},{2,4},{3,5},{4,2},{5,3},{6,0},{7,1},{8,14},{9,15},{10,... | collective-permute-start | bytes 368648 | tf_op jit(solution)/shard_map/ppermute | solution.py:75
  146.4 6.4 %collective-permute-start.52 = (bf16[128,512]{1,0:T(8,128)(2,1)S(1)}, bf16[128,512]{1,0:T(8,128)(2,1)S(1)}, u32[]{:S(2)}, u32[]{:S(2)}) collective-permute-start(bf16[128,512]{1,0:T(8,128)(2,1)S(1)} %get-tuple-element.262), channel_id=1, source_target_pairs={{0,2},{1,3},{2,0},{3,1},{4,6},{5,7},{6,4},{7,5},{8,10},{9,11},{10,... | collective-permute-start | bytes 393224 | tf_op jit(solution)/shard_map/ppermute | solution.py:75
  146.5 9.7 %collective-permute-start.54 = (bf16[128,512]{1,0:T(8,128)(2,1)S(1)}, bf16[128,512]{1,0:T(8,128)(2,1)S(1)}, u32[]{:S(2)}, u32[]{:S(2)}) collective-permute-start(bf16[128,512]{1,0:T(8,128)(2,1)S(1)} %get-tuple-element.263), channel_id=1, source_target_pairs={{0,6},{1,7},{2,4},{3,5},{4,2},{5,3},{6,0},{7,1},{8,14},{9,15},{10,... | collective-permute-start | bytes 393224 | tf_op jit(solution)/shard_map/ppermute | solution.py:75
  149.1 12.0 %collective-permute-start.53 = (bf16[128,512]{1,0:T(8,128)(2,1)S(1)}, bf16[128,512]{1,0:T(8,128)(2,1)S(1)}, u32[]{:S(2)}, u32[]{:S(2)}) collective-permute-start(bf16[128,512]{1,0:T(8,128)(2,1)S(1)} %get-tuple-element.264), channel_id=1, source_target_pairs={{0,4},{1,5},{2,6},{3,7},{4,0},{5,1},{6,2},{7,3},{8,12},{9,13},{10,... | collective-permute-start | bytes 393224 | tf_op jit(solution)/shard_map/ppermute | solution.py:75
  150.1 16.0 %copy-start.22 = (bf16[512,640]{1,0:T(8,128)(2,1)S(1)}, bf16[512,640]{1,0:T(8,128)(2,1)}, u32[]{:S(2)}) copy-start(bf16[512,640]{1,0:T(8,128)(2,1)} %get-tuple-element.202.wkv_ref) | copy-start | bytes 1966084
  150.1 11.2 %collective-permute-start.49 = (bf16[4,56,640]{2,1,0:T(8,128)(2,1)S(1)}, bf16[4,56,640]{2,1,0:T(8,128)(2,1)S(1)}, u32[]{:S(2)}, u32[]{:S(2)}) collective-permute-start(bf16[4,56,640]{2,1,0:T(8,128)(2,1)S(1)} %get-tuple-element.254), channel_id=1, source_target_pairs={{0,8},{8,0},{16,24},{24,16},{1,9},{9,1},{17,25},{25,17},{2,10},{10... | collective-permute-start | bytes 860168 | tf_op jit(solution)/shard_map/ppermute | solution.py:70
  151.4 13.2 %collective-permute-start.51 = (bf16[4,56,640]{2,1,0:T(8,128)(2,1)S(1)}, bf16[4,56,640]{2,1,0:T(8,128)(2,1)S(1)}, u32[]{:S(2)}, u32[]{:S(2)}) collective-permute-start(bf16[4,56,640]{2,1,0:T(8,128)(2,1)S(1)} %get-tuple-element.255), channel_id=1, source_target_pairs={{0,24},{8,16},{16,8},{24,0},{1,25},{9,17},{17,9},{25,1},{2,26},{10... | collective-permute-start | bytes 860168 | tf_op jit(solution)/shard_map/ppermute | solution.py:70
  152.8 13.1 %collective-permute-start.50 = (bf16[4,56,640]{2,1,0:T(8,128)(2,1)S(1)}, bf16[4,56,640]{2,1,0:T(8,128)(2,1)S(1)}, u32[]{:S(2)}, u32[]{:S(2)}) collective-permute-start(bf16[4,56,640]{2,1,0:T(8,128)(2,1)S(1)} %get-tuple-element.256), channel_id=1, source_target_pairs={{0,16},{8,24},{16,0},{24,8},{1,17},{9,25},{17,1},{25,9},{2,18},{10... | collective-permute-start | bytes 860168 | tf_op jit(solution)/shard_map/ppermute | solution.py:70
  166.6 7.8 %collective-permute-start.55 = (bf16[88,640]{1,0:T(8,128)(2,1)S(1)}, bf16[88,640]{1,0:T(8,128)(2,1)S(1)}, u32[]{:S(2)}, u32[]{:S(2)}) collective-permute-start(bf16[88,640]{1,0:T(8,128)(2,1)S(1)} %pad_maximum_fusion.7), channel_id=1, source_target_pairs={{0,2},{1,3},{2,0},{3,1},{4,6},{5,7},{6,4},{7,5},{8,10},{9,11},{10,... | collective-permute-start | bytes 337928 | tf_op jit(solution)/shard_map/ppermute | solution.py:75
  167.9 10.8 %collective-permute-start.56 = (bf16[88,640]{1,0:T(8,128)(2,1)S(1)}, bf16[88,640]{1,0:T(8,128)(2,1)S(1)}, u32[]{:S(2)}, u32[]{:S(2)}) collective-permute-start(bf16[88,640]{1,0:T(8,128)(2,1)S(1)} %pad_maximum_fusion.8), channel_id=1, source_target_pairs={{0,4},{1,5},{2,6},{3,7},{4,0},{5,1},{6,2},{7,3},{8,12},{9,13},{10,... | collective-permute-start | bytes 337928 | tf_op jit(solution)/shard_map/ppermute | solution.py:75
  169.1 9.6 %collective-permute-start.57 = (bf16[184,640]{1,0:T(8,128)(2,1)S(1)}, bf16[184,640]{1,0:T(8,128)(2,1)S(1)}, u32[]{:S(2)}, u32[]{:S(2)}) collective-permute-start(bf16[184,640]{1,0:T(8,128)(2,1)S(1)} %pad_maximum_fusion.5), channel_id=1, source_target_pairs={{0,6},{1,7},{2,4},{3,5},{4,2},{5,3},{6,0},{7,1},{8,14},{9,15},{10,... | collective-permute-start | bytes 706568 | tf_op jit(solution)/shard_map/ppermute | solution.py:75
  (27 other events, 158.8 us)
